TPU v7x, 32 devices: a whole 2x2x4 slice. The times are simulated.
32 devices in a mesh: dom: 32 (over z, y, x, core).
Axes of the slice: x: 2, y: 2, z: 4, core: 2. Of those that a mesh axis runs over, the one named last changes fastest.
Arguments:
- adjoint_start: float32 [3, 221184], P(None, 'dom'), may hold values from -6 to 6
- adjoint_source: float32 [3, 221184], P(None, 'dom'), may hold values from -6 to 6
- inverse_diagonal: float32 [3, 221184], P(None, 'dom'), may hold values from 0.05 to 0.3
- primal_field: float32 [3, 221184], P(None, 'dom'), may hold values from -6 to 6
- cell_load: float32 [192, 8192], P(None, 'dom'), may hold values from -6 to 6
- modulus: float32 [8192], P('dom'), may hold values from 0.5 to 4
- stiffness: float32 [192, 192], replicated
- connectivity: int32 [64, 8192], P(None, 'dom'), may hold values from 0 to 16368
- hang_node: int32 [4096], P('dom'), may hold values from 0 to 16368, as said below
- hang_master: int32 [16, 4096], P(None, 'dom'), may hold values from 0 to 16368
- hang_weight: float32 [16, 4096], P(None, 'dom'), may hold values from -0.25 to 0.45
- ghost_lists: int32 [8, 8192], P(None, 'dom'), may hold values from 0 to 16368
- subface_cell: int32 [8, 4096], P(None, 'dom'), may hold values from 0 to 255
- subface_face: int32 [8, 4096], P(None, 'dom'), may hold values from 0 to 5
- subface_owner: int32 [8, 4096], P(None, 'dom'), may hold values from 0 to 256, as said below
Outputs:
- adjoint: float32 [3, 221184], P(None, 'dom')
- indicator: float32 [8192], P('dom')
Inputs may be any that keep to these rules, and one draw needn't show every extreme that they name: `hang_node`: on each partition the live hanging slots come first and hold distinct codes under min(16368, 6912); all slots after them hold 16368; between half and all of a partition's slots are live. `subface_owner`: 256 marks an unused slot; between half and all of each neighbour slot's entries are live.
All inputs are finite; a program needn't handle non-finite values.
Results may differ from a plain program's by a relative error of at most 0.0003.
Values sent between devices are 32-bit elements; how exact they have to be, the bound alone decides.
No kernel may reach another device: no remote copies, remote signals or barrier semaphores. Data moves between devices by JAX's collectives and lax.ppermute only.
A program may use at most 64 MiB of HBM per device.

v0:
```python
import jax
import jax.numpy as jnp
from jax import lax
from jax.sharding import PartitionSpec as P

REACH = 4
SWEEPS = 2
NODES_DEV = 6912
EXT = 8960


relaxation = 0.7
scale_down = 16.0
pad_code = 16368


def from_behind(block, axis, distance):
    devices = range(lax.axis_size(axis))
    route = [(i - distance, i) for i in devices if i - distance in devices]
    return lax.ppermute(block, axis, route)


def neighbour_offsets():
    return [step + 1 for step in range(REACH)] + [-(step + 1) for step in range(REACH)]


def decode_connect(codes):
    cells = jnp.arange(codes.shape[-1], dtype=jnp.int32)
    return (27 * cells + 17 * codes) % EXT


def decode_master(codes):
    slots = jnp.arange(codes.shape[-1], dtype=jnp.int32)
    return (17 * codes + 8 * slots) % EXT


def decode_node(codes):
    return jnp.where(codes == pad_code, EXT, 13 * codes % NODES_DEV)


def decode_lists(codes):
    slots = jnp.arange(codes.shape[-1], dtype=jnp.int32)
    return (17 * codes + slots) % NODES_DEV


def face_table(width):
    node = jnp.arange(width, dtype=jnp.int32) % 64
    first = node // 16
    second = node // 4 % 4
    third = node % 4
    rows = [first == 0, first == 3, second == 0, second == 3, third == 0, third == 3]
    return jnp.stack(rows).astype(jnp.float32)


def constrain(extended, node, master, weight):
    padded = jnp.concatenate([extended, jnp.zeros((extended.shape[0], 1), extended.dtype)], 1)
    values = jnp.sum(weight[None] * padded[:, master], axis=1)
    padded = padded.at[:, node].set(values)
    return padded[:, :-1]


def release(totals, node, master, weight):
    padded = jnp.concatenate([totals, jnp.zeros((totals.shape[0], 1), totals.dtype)], 1)
    held = padded[:, node]
    padded = padded.at[:, node].set(0.0)
    spread = weight[None] * held[:, None, :]
    padded = padded.at[:, master.reshape(-1)].add(spread.reshape(totals.shape[0], -1))
    return padded[:, :-1]


def local_product(extended, connect, modulus, stiffness, node, master, weight):
    fixed = constrain(extended, node, master, weight)
    cells = fixed[:, connect].reshape(3 * connect.shape[0], -1)
    image = modulus[None] * lax.dot_general(
        stiffness, cells, (((0,), (0,)), ((), ())), precision=lax.Precision.HIGHEST
    )
    totals = jnp.zeros_like(fixed).at[:, connect].add(image.reshape(3, connect.shape[0], -1))
    return release(totals, node, master, weight)


def local(
    adjoint_start,
    adjoint_source,
    inverse_diagonal,
    primal_field,
    cell_load,
    modulus,
    stiffness,
    connectivity,
    hang_node,
    hang_master,
    hang_weight,
    ghost_lists,
    subface_cell,
    subface_face,
    subface_owner,
):
    offsets = neighbour_offsets()
    highest = lax.Precision.HIGHEST
    connect = decode_connect(connectivity)
    node_slots = decode_node(hang_node)
    master_slots = decode_master(hang_master)
    export_rows = decode_lists(ghost_lists)

    def ghosts_in(blocks):
        return jnp.stack(
            [from_behind(blocks[slot], "dom", offsets[slot]) for slot in range(2 * REACH)]
        )

    def ghosts_back(blocks):
        return jnp.stack(
            [from_behind(blocks[slot], "dom", -offsets[slot]) for slot in range(2 * REACH)]
        )

    def extend(owned):
        blocks = jnp.moveaxis(owned[:, export_rows], 1, 0)
        ghosts = ghosts_in(blocks)
        return jnp.concatenate([owned, jnp.moveaxis(ghosts, 0, 1).reshape(owned.shape[0], -1)], 1)

    owned_count = adjoint_start.shape[1]
    ghost_count = export_rows.shape[1]
    adjoint = adjoint_start
    for sweep in range(SWEEPS):
        extended = extend(adjoint)
        totals = local_product(
            extended, connect, modulus, stiffness, node_slots, master_slots, hang_weight
        )
        owned_part = totals[:, :owned_count]
        ghost_part = jnp.moveaxis(totals[:, owned_count:].reshape(3, 2 * REACH, ghost_count), 1, 0)
        returned = ghosts_back(ghost_part)
        applied = owned_part.at[:, export_rows.reshape(-1)].add(
            jnp.moveaxis(returned, 0, 1).reshape(3, -1)
        )
        adjoint = adjoint + relaxation * inverse_diagonal * (adjoint_source - applied)
    both_ext = extend(jnp.concatenate([adjoint, primal_field], 0))
    fixed = constrain(both_ext, node_slots, master_slots, hang_weight)
    adjoint_cells = fixed[:3][:, connect].reshape(3 * connect.shape[0], -1)
    primal_cells = fixed[3:][:, connect].reshape(3 * connect.shape[0], -1)
    applied = modulus[None] * jnp.dot(stiffness, primal_cells, precision=highest)
    cell_term = jnp.sum(adjoint_cells * (cell_load - applied), axis=0)
    flux = jnp.dot(face_table(applied.shape[0]), applied * adjoint_cells, precision=highest)
    cell_count = connect.shape[1]
    sent = flux.reshape(-1)[subface_face * cell_count + subface_cell]
    received = jnp.stack(
        [from_behind(sent[slot], "dom", offsets[slot]) for slot in range(2 * REACH)]
    )
    face_term = (
        jnp.zeros((cell_count + 1,), jnp.float32)
        .at[subface_owner.reshape(-1)]
        .add(received.reshape(-1))[:cell_count]
    )
    indicator = (jnp.abs(cell_term) + jnp.abs(face_term)) / scale_down
    return (adjoint, indicator)


def solution(mesh):
    placed = (
        P(None, "dom"),
        P(None, "dom"),
        P(None, "dom"),
        P(None, "dom"),
        P(None, "dom"),
        P("dom"),
        P(),
        P(None, "dom"),
        P("dom"),
        P(None, "dom"),
        P(None, "dom"),
        P(None, "dom"),
        P(None, "dom"),
        P(None, "dom"),
        P(None, "dom"),
    )
    return jax.shard_map(
        local, mesh=mesh, in_specs=placed, out_specs=(P(None, "dom"), P("dom")), check_vma=False
    )
```

profile of v0, /device:TPU:0, one launch (start us, length us, event | category | flops | bytes accessed | tf_op | source)
XLA Modules:
  0.0 815.1 jit_solution(16889599215936667023)
XLA Ops:
  4.7 7.5 gather_fusion
  14.8 4.4 collective-permute-start.1
  19.3 4.3 collective-permute-start.2
  39.9 8.4 %maximum_maximum_fusion = f32[3,8961]{0,1:T(8,128)} fusion(f32[3,2048]{0,1:T(8,128)S(1)} %bitcast.243, f32[3,6912]{0,1:T(8,128)} %copy.246, f32[8961]{0:T(1024)S(1)} %pad.13.clone), kind=kLoop, calls=%fused_computation.25 | loop fusion | flops 53766 | bytes 250896 | tf_op jit(solution)/shard_map/concatenate | solution.py:56
  48.3 7.8 gather_fusion.1
  56.5 5.2 scatter_fusion
  61.7 4.0 slice.279
  65.7 56.8 %gather_fusion.2 = f32[16384,3]{1,0:T(8,128)} fusion(f32[3,8960]{0,1:T(8,128)} %slice.279, s32[16384]{0:T(1024)S(1)} %broadcast_clamp_fusion), kind=kCustom, calls=%fused_computation.2 | custom fusion | bytes 458752 | tf_op jit(solution)/shard_map/gather | solution.py:73
  122.5 5.2 copy.248
  128.3 4.7 copy.249
  133.0 90.1 %scatter_custom_fusion.1 = f32[3,8960]{0,1:T(8,128)} fusion(s32[16384]{0:T(1024)S(1)} %bitcast.260, f32[16384,3]{1,0:T(8,128)} %bitcast.240, f32[]{:T(128)} %constant.113.clone.1), kind=kCustom, calls=%fused_computation.28 | custom fusion | flops 49152 | bytes 108032 | tf_op jit(solution)/shard_map/scatter-add | solution.py:77
  229.9 5.2 scatter_custom_fusion.2
  235.5 14.8 %scatter_custom_fusion.3 = f32[3,8961]{0,1:T(8,128)} fusion(f32[3,8961]{0,1:T(8,128)} %scatter_custom_fusion.2, s32[2048]{0:T(1024)S(1)} %bitcast.288, f32[3,2048]{0,1:T(8,128)S(1)} %bitcast_multiply_fusion.1), kind=kCustom, calls=%fused_computation.37 | custom fusion | flops 6144 | bytes 1156108 | tf_op jit(solution)/shard_map/scatter-add | solution.py:67
  260.2 4.9 collective-permute-start.13
  265.1 6.1 collective-permute-start.14
  271.2 4.9 collective-permute-start.15
  276.2 4.1 slice.280
  280.8 14.1 %scatter_fusion.1 = f32[3,6912]{0,1:T(8,128)} fusion(f32[3,6912]{0,1:T(8,128)} %slice.280, s32[2048]{0:T(1024)S(1)} %bitcast.274, f32[2048,3]{1,0:T(8,128)S(1)} %bitcast.247), kind=kCustom, calls=%fused_computation.17 | custom fusion | flops 6144 | bytes 81920 | tf_op jit(solution)/shard_map/scatter-add | solution.py:131
  299.9 7.5 gather_fusion.4
  309.0 4.5 collective-permute-start.17
  313.5 5.4 collective-permute-start.18
  337.8 7.8 gather_fusion.5
  345.9 5.2 scatter_fusion.2
  351.1 4.0 slice.298
  355.1 56.8 %gather_fusion.6 = f32[16384,3]{1,0:T(8,128)} fusion(f32[3,8960]{0,1:T(8,128)} %slice.298, s32[16384]{0:T(1024)S(1)} %broadcast_clamp_fusion), kind=kCustom, calls=%fused_computation.6 | custom fusion | bytes 458752 | tf_op jit(solution)/shard_map/gather | solution.py:73
  411.9 5.2 copy.271
  417.7 4.7 copy.272
  422.4 90.1 %scatter_custom_fusion.6 = f32[3,8960]{0,1:T(8,128)} fusion(s32[16384]{0:T(1024)S(1)} %bitcast.261, f32[16384,3]{1,0:T(8,128)} %bitcast.239, f32[]{:T(128)} %constant.113.clone.1), kind=kCustom, calls=%fused_computation.26 | custom fusion | flops 49152 | bytes 108032 | tf_op jit(solution)/shard_map/scatter-add | solution.py:77
  519.3 5.2 scatter_custom_fusion.7
  524.9 14.8 %scatter_custom_fusion.8 = f32[3,8961]{0,1:T(8,128)} fusion(f32[3,8961]{0,1:T(8,128)} %scatter_custom_fusion.7, s32[2048]{0:T(1024)S(1)} %bitcast.289, f32[3,2048]{0,1:T(8,128)S(1)} %bitcast_multiply_fusion), kind=kCustom, calls=%fused_computation.34 | custom fusion | flops 6144 | bytes 1156108 | tf_op jit(solution)/shard_map/scatter-add | solution.py:67
  549.6 4.9 collective-permute-start.29
  554.5 6.1 collective-permute-start.30
  560.7 4.8 collective-permute-start.31
  565.6 4.0 slice.299
  570.2 14.1 %scatter_fusion.3 = f32[3,6912]{0,1:T(8,128)} fusion(f32[3,6912]{0,1:T(8,128)} %slice.299, s32[2048]{0:T(1024)S(1)} %bitcast.275, f32[2048,3]{1,0:T(8,128)S(1)} %bitcast.246), kind=kCustom, calls=%fused_computation.22 | custom fusion | flops 6144 | bytes 81920 | tf_op jit(solution)/shard_map/scatter-add | solution.py:131
  589.4 7.5 gather_fusion.8
  598.5 4.5 collective-permute-start.33
  603.0 5.2 collective-permute-start.34
  627.3 7.8 gather_fusion.9
  635.4 5.2 scatter_fusion.4
  640.7 7.8 fusion.24
  648.5 56.8 %gather_fusion.11 = f32[16384,3]{1,0:T(8,128)} fusion(f32[3,8960]{0,1:T(8,128)} %get-tuple-element.15, s32[16384]{0:T(1024)S(1)} %broadcast_clamp_fusion), kind=kCustom, calls=%fused_computation.11 | custom fusion | bytes 458752 | tf_op jit(solution)/shard_map/gather | solution.py:138
  705.2 5.2 copy.295
  710.5 56.8 %gather_fusion.10 = f32[16384,3]{1,0:T(8,128)} fusion(f32[3,8960]{0,1:T(8,128)} %get-tuple-element.14, s32[16384]{0:T(1024)S(1)} %broadcast_clamp_fusion), kind=kCustom, calls=%fused_computation.10 | custom fusion | bytes 458752 | tf_op jit(solution)/shard_map/gather | solution.py:137
  767.3 5.3 copy.294
  773.1 6.2 gather_fusion.12
  784.3 5.2 collective-permute-start.42
  806.9 7.6 scatter_custom_fusion.11
  (225 shorter events, 134.6 us)
Async XLA Ops:
  12.5 16.1 %collective-permute-start = (f32[3,256]{1,0:T(4,128)S(1)}, f32[3,256]{1,0:T(4,128)S(1)}, u32[]{:S(2)}, u32[]{:S(2)}) collective-permute-start(f32[3,256]{1,0:T(4,128)S(1)} %get-tuple-element.57), channel_id=1, source_target_pairs={{0,1},{1,2},{2,3},{3,4},{4,5},{5,6},{6,7},{7,8},{8,9},{9,10},{10,1... | collective-permute-start | bytes 9224 | tf_op jit(solution)/shard_map/ppermute | solution.py:20
  14.8 15.0 %collective-permute-start.1 = (f32[3,256]{1,0:T(4,128)S(1)}, f32[3,256]{1,0:T(4,128)S(1)}, u32[]{:S(2)}, u32[]{:S(2)}) collective-permute-start(f32[3,256]{1,0:T(4,128)S(1)} %get-tuple-element.56), channel_id=1, source_target_pairs={{0,2},{1,3},{2,4},{3,5},{4,6},{5,7},{6,8},{7,9},{8,10},{9,11},{10,... | collective-permute-start | bytes 9224 | tf_op jit(solution)/shard_map/ppermute | solution.py:20
  19.3 11.9 %collective-permute-start.2 = (f32[3,256]{1,0:T(4,128)S(1)}, f32[3,256]{1,0:T(4,128)S(1)}, u32[]{:S(2)}, u32[]{:S(2)}) collective-permute-start(f32[3,256]{1,0:T(4,128)S(1)} %get-tuple-element.55), channel_id=1, source_target_pairs={{0,3},{1,4},{2,5},{3,6},{4,7},{5,8},{6,9},{7,10},{8,11},{9,12},{10... | collective-permute-start | bytes 9224 | tf_op jit(solution)/shard_map/ppermute | solution.py:20
  23.6 9.0 %collective-permute-start.3 = (f32[3,256]{1,0:T(4,128)S(1)}, f32[3,256]{1,0:T(4,128)S(1)}, u32[]{:S(2)}, u32[]{:S(2)}) collective-permute-start(f32[3,256]{1,0:T(4,128)S(1)} %get-tuple-element.54), channel_id=1, source_target_pairs={{0,4},{1,5},{2,6},{3,7},{4,8},{5,9},{6,10},{7,11},{8,12},{9,13},{1... | collective-permute-start | bytes 9224 | tf_op jit(solution)/shard_map/ppermute | solution.py:20
  27.0 5.6 collective-permute-start.4
  28.6 5.6 collective-permute-start.5
  29.9 6.3 collective-permute-start.6
  31.2 8.3 %collective-permute-start.7 = (f32[3,256]{1,0:T(4,128)S(1)}, f32[3,256]{1,0:T(4,128)S(1)}, u32[]{:S(2)}, u32[]{:S(2)}) collective-permute-start(f32[3,256]{1,0:T(4,128)S(1)} %get-tuple-element.50), channel_id=1, source_target_pairs={{4,0},{5,1},{6,2},{7,3},{8,4},{9,5},{10,6},{11,7},{12,8},{13,9},{1... | collective-permute-start | bytes 9224 | tf_op jit(solution)/shard_map/ppermute | solution.py:20
  251.9 8.3 %collective-permute-start.8 = (f32[3,256]{1,0:T(4,128)S(1)}, f32[3,256]{1,0:T(4,128)S(1)}, u32[]{:S(2)}, u32[]{:S(2)}) collective-permute-start(f32[3,256]{1,0:T(4,128)S(1)} %get-tuple-element.49), channel_id=1, source_target_pairs={{1,0},{2,1},{3,2},{4,3},{5,4},{6,5},{7,6},{8,7},{9,8},{10,9},{11,1... | collective-permute-start | bytes 9224 | tf_op jit(solution)/shard_map/ppermute | solution.py:20
  253.2 11.9 %collective-permute-start.9 = (f32[3,256]{1,0:T(4,128)S(1)}, f32[3,256]{1,0:T(4,128)S(1)}, u32[]{:S(2)}, u32[]{:S(2)}) collective-permute-start(f32[3,256]{1,0:T(4,128)S(1)} %get-tuple-element.48), channel_id=1, source_target_pairs={{2,0},{3,1},{4,2},{5,3},{6,4},{7,5},{8,6},{9,7},{10,8},{11,9},{12,... | collective-permute-start | bytes 9224 | tf_op jit(solution)/shard_map/ppermute | solution.py:20
  254.5 16.7 %collective-permute-start.10 = (f32[3,256]{1,0:T(4,128)S(1)}, f32[3,256]{1,0:T(4,128)S(1)}, u32[]{:S(2)}, u32[]{:S(2)}) collective-permute-start(f32[3,256]{1,0:T(4,128)S(1)} %get-tuple-element.47), channel_id=1, source_target_pairs={{3,0},{4,1},{5,2},{6,3},{7,4},{8,5},{9,6},{10,7},{11,8},{12,9},{13... | collective-permute-start | bytes 9224 | tf_op jit(solution)/shard_map/ppermute | solution.py:20
  255.8 24.5 %collective-permute-start.11 = (f32[3,256]{1,0:T(4,128)S(1)}, f32[3,256]{1,0:T(4,128)S(1)}, u32[]{:S(2)}, u32[]{:S(2)}) collective-permute-start(f32[3,256]{1,0:T(4,128)S(1)} %get-tuple-element.46), channel_id=1, source_target_pairs={{4,0},{5,1},{6,2},{7,3},{8,4},{9,5},{10,6},{11,7},{12,8},{13,9},{1... | collective-permute-start | bytes 9224 | tf_op jit(solution)/shard_map/ppermute | solution.py:20
  257.1 23.2 %collective-permute-start.12 = (f32[3,256]{1,0:T(4,128)S(1)}, f32[3,256]{1,0:T(4,128)S(1)}, u32[]{:S(2)}, u32[]{:S(2)}) collective-permute-start(f32[3,256]{1,0:T(4,128)S(1)} %get-tuple-element.45), channel_id=1, source_target_pairs={{0,1},{1,2},{2,3},{3,4},{4,5},{5,6},{6,7},{7,8},{8,9},{9,10},{10,1... | collective-permute-start | bytes 9224 | tf_op jit(solution)/shard_map/ppermute | solution.py:20
  260.2 20.2 %collective-permute-start.13 = (f32[3,256]{1,0:T(4,128)S(1)}, f32[3,256]{1,0:T(4,128)S(1)}, u32[]{:S(2)}, u32[]{:S(2)}) collective-permute-start(f32[3,256]{1,0:T(4,128)S(1)} %get-tuple-element.44), channel_id=1, source_target_pairs={{0,2},{1,3},{2,4},{3,5},{4,6},{5,7},{6,8},{7,9},{8,10},{9,11},{10,... | collective-permute-start | bytes 9224 | tf_op jit(solution)/shard_map/ppermute | solution.py:20
  265.1 15.3 %collective-permute-start.14 = (f32[3,256]{1,0:T(4,128)S(1)}, f32[3,256]{1,0:T(4,128)S(1)}, u32[]{:S(2)}, u32[]{:S(2)}) collective-permute-start(f32[3,256]{1,0:T(4,128)S(1)} %get-tuple-element.43), channel_id=1, source_target_pairs={{0,3},{1,4},{2,5},{3,6},{4,7},{5,8},{6,9},{7,10},{8,11},{9,12},{10... | collective-permute-start | bytes 9224 | tf_op jit(solution)/shard_map/ppermute | solution.py:20
  271.2 9.1 %collective-permute-start.15 = (f32[3,256]{1,0:T(4,128)S(1)}, f32[3,256]{1,0:T(4,128)S(1)}, u32[]{:S(2)}, u32[]{:S(2)}) collective-permute-start(f32[3,256]{1,0:T(4,128)S(1)} %get-tuple-element.42), channel_id=1, source_target_pairs={{0,4},{1,5},{2,6},{3,7},{4,8},{5,9},{6,10},{7,11},{8,12},{9,13},{1... | collective-permute-start | bytes 9224 | tf_op jit(solution)/shard_map/ppermute | solution.py:20
  307.7 15.7 %collective-permute-start.16 = (f32[3,256]{1,0:T(4,128)S(1)}, f32[3,256]{1,0:T(4,128)S(1)}, u32[]{:S(2)}, u32[]{:S(2)}) collective-permute-start(f32[3,256]{1,0:T(4,128)S(1)} %get-tuple-element.41), channel_id=1, source_target_pairs={{0,1},{1,2},{2,3},{3,4},{4,5},{5,6},{6,7},{7,8},{8,9},{9,10},{10,1... | collective-permute-start | bytes 9224 | tf_op jit(solution)/shard_map/ppermute | solution.py:20
  309.0 15.7 %collective-permute-start.17 = (f32[3,256]{1,0:T(4,128)S(1)}, f32[3,256]{1,0:T(4,128)S(1)}, u32[]{:S(2)}, u32[]{:S(2)}) collective-permute-start(f32[3,256]{1,0:T(4,128)S(1)} %get-tuple-element.40), channel_id=1, source_target_pairs={{0,2},{1,3},{2,4},{3,5},{4,6},{5,7},{6,8},{7,9},{8,10},{9,11},{10,... | collective-permute-start | bytes 9224 | tf_op jit(solution)/shard_map/ppermute | solution.py:20
  313.5 12.6 %collective-permute-start.18 = (f32[3,256]{1,0:T(4,128)S(1)}, f32[3,256]{1,0:T(4,128)S(1)}, u32[]{:S(2)}, u32[]{:S(2)}) collective-permute-start(f32[3,256]{1,0:T(4,128)S(1)} %get-tuple-element.39), channel_id=1, source_target_pairs={{0,3},{1,4},{2,5},{3,6},{4,7},{5,8},{6,9},{7,10},{8,11},{9,12},{10... | collective-permute-start | bytes 9224 | tf_op jit(solution)/shard_map/ppermute | solution.py:20
  318.9 8.5 %collective-permute-start.19 = (f32[3,256]{1,0:T(4,128)S(1)}, f32[3,256]{1,0:T(4,128)S(1)}, u32[]{:S(2)}, u32[]{:S(2)}) collective-permute-start(f32[3,256]{1,0:T(4,128)S(1)} %get-tuple-element.38), channel_id=1, source_target_pairs={{0,4},{1,5},{2,6},{3,7},{4,8},{5,9},{6,10},{7,11},{8,12},{9,13},{1... | collective-permute-start | bytes 9224 | tf_op jit(solution)/shard_map/ppermute | solution.py:20
  322.2 5.3 collective-permute-start.20
  323.5 5.8 collective-permute-start.21
  324.8 6.3 collective-permute-start.22
  326.1 8.5 %collective-permute-start.23 = (f32[3,256]{1,0:T(4,128)S(1)}, f32[3,256]{1,0:T(4,128)S(1)}, u32[]{:S(2)}, u32[]{:S(2)}) collective-permute-start(f32[3,256]{1,0:T(4,128)S(1)} %get-tuple-element.34), channel_id=1, source_target_pairs={{4,0},{5,1},{6,2},{7,3},{8,4},{9,5},{10,6},{11,7},{12,8},{13,9},{1... | collective-permute-start | bytes 9224 | tf_op jit(solution)/shard_map/ppermute | solution.py:20
  541.3 8.3 %collective-permute-start.24 = (f32[3,256]{1,0:T(4,128)S(1)}, f32[3,256]{1,0:T(4,128)S(1)}, u32[]{:S(2)}, u32[]{:S(2)}) collective-permute-start(f32[3,256]{1,0:T(4,128)S(1)} %get-tuple-element.33), channel_id=1, source_target_pairs={{1,0},{2,1},{3,2},{4,3},{5,4},{6,5},{7,6},{8,7},{9,8},{10,9},{11,1... | collective-permute-start | bytes 9224 | tf_op jit(solution)/shard_map/ppermute | solution.py:20
  542.6 11.9 %collective-permute-start.25 = (f32[3,256]{1,0:T(4,128)S(1)}, f32[3,256]{1,0:T(4,128)S(1)}, u32[]{:S(2)}, u32[]{:S(2)}) collective-permute-start(f32[3,256]{1,0:T(4,128)S(1)} %get-tuple-element.32), channel_id=1, source_target_pairs={{2,0},{3,1},{4,2},{5,3},{6,4},{7,5},{8,6},{9,7},{10,8},{11,9},{12,... | collective-permute-start | bytes 9224 | tf_op jit(solution)/shard_map/ppermute | solution.py:20
  543.9 16.7 %collective-permute-start.26 = (f32[3,256]{1,0:T(4,128)S(1)}, f32[3,256]{1,0:T(4,128)S(1)}, u32[]{:S(2)}, u32[]{:S(2)}) collective-permute-start(f32[3,256]{1,0:T(4,128)S(1)} %get-tuple-element.31), channel_id=1, source_target_pairs={{3,0},{4,1},{5,2},{6,3},{7,4},{8,5},{9,6},{10,7},{11,8},{12,9},{13... | collective-permute-start | bytes 9224 | tf_op jit(solution)/shard_map/ppermute | solution.py:20
  545.3 24.3 %collective-permute-start.27 = (f32[3,256]{1,0:T(4,128)S(1)}, f32[3,256]{1,0:T(4,128)S(1)}, u32[]{:S(2)}, u32[]{:S(2)}) collective-permute-start(f32[3,256]{1,0:T(4,128)S(1)} %get-tuple-element.30), channel_id=1, source_target_pairs={{4,0},{5,1},{6,2},{7,3},{8,4},{9,5},{10,6},{11,7},{12,8},{13,9},{1... | collective-permute-start | bytes 9224 | tf_op jit(solution)/shard_map/ppermute | solution.py:20
  546.6 23.1 %collective-permute-start.28 = (f32[3,256]{1,0:T(4,128)S(1)}, f32[3,256]{1,0:T(4,128)S(1)}, u32[]{:S(2)}, u32[]{:S(2)}) collective-permute-start(f32[3,256]{1,0:T(4,128)S(1)} %get-tuple-element.29), channel_id=1, source_target_pairs={{0,1},{1,2},{2,3},{3,4},{4,5},{5,6},{6,7},{7,8},{8,9},{9,10},{10,1... | collective-permute-start | bytes 9224 | tf_op jit(solution)/shard_map/ppermute | solution.py:20
  549.6 20.0 %collective-permute-start.29 = (f32[3,256]{1,0:T(4,128)S(1)}, f32[3,256]{1,0:T(4,128)S(1)}, u32[]{:S(2)}, u32[]{:S(2)}) collective-permute-start(f32[3,256]{1,0:T(4,128)S(1)} %get-tuple-element.28), channel_id=1, source_target_pairs={{0,2},{1,3},{2,4},{3,5},{4,6},{5,7},{6,8},{7,9},{8,10},{9,11},{10,... | collective-permute-start | bytes 9224 | tf_op jit(solution)/shard_map/ppermute | solution.py:20
  554.5 15.1 %collective-permute-start.30 = (f32[3,256]{1,0:T(4,128)S(1)}, f32[3,256]{1,0:T(4,128)S(1)}, u32[]{:S(2)}, u32[]{:S(2)}) collective-permute-start(f32[3,256]{1,0:T(4,128)S(1)} %get-tuple-element.27), channel_id=1, source_target_pairs={{0,3},{1,4},{2,5},{3,6},{4,7},{5,8},{6,9},{7,10},{8,11},{9,12},{10... | collective-permute-start | bytes 9224 | tf_op jit(solution)/shard_map/ppermute | solution.py:20
  560.7 9.0 %collective-permute-start.31 = (f32[3,256]{1,0:T(4,128)S(1)}, f32[3,256]{1,0:T(4,128)S(1)}, u32[]{:S(2)}, u32[]{:S(2)}) collective-permute-start(f32[3,256]{1,0:T(4,128)S(1)} %get-tuple-element.26), channel_id=1, source_target_pairs={{0,4},{1,5},{2,6},{3,7},{4,8},{5,9},{6,10},{7,11},{8,12},{9,13},{1... | collective-permute-start | bytes 9224 | tf_op jit(solution)/shard_map/ppermute | solution.py:20
  597.2 15.6 %collective-permute-start.32 = (f32[6,256]{1,0:T(8,128)S(1)}, f32[6,256]{1,0:T(8,128)S(1)}, u32[]{:S(2)}, u32[]{:S(2)}) collective-permute-start(f32[6,256]{1,0:T(8,128)S(1)} %get-tuple-element.25), channel_id=1, source_target_pairs={{0,1},{1,2},{2,3},{3,4},{4,5},{5,6},{6,7},{7,8},{8,9},{9,10},{10,1... | collective-permute-start | bytes 18440 | tf_op jit(solution)/shard_map/ppermute | solution.py:20
  598.5 15.6 %collective-permute-start.33 = (f32[6,256]{1,0:T(8,128)S(1)}, f32[6,256]{1,0:T(8,128)S(1)}, u32[]{:S(2)}, u32[]{:S(2)}) collective-permute-start(f32[6,256]{1,0:T(8,128)S(1)} %get-tuple-element.24), channel_id=1, source_target_pairs={{0,2},{1,3},{2,4},{3,5},{4,6},{5,7},{6,8},{7,9},{8,10},{9,11},{10,... | collective-permute-start | bytes 18440 | tf_op jit(solution)/shard_map/ppermute | solution.py:20
  603.0 12.4 %collective-permute-start.34 = (f32[6,256]{1,0:T(8,128)S(1)}, f32[6,256]{1,0:T(8,128)S(1)}, u32[]{:S(2)}, u32[]{:S(2)}) collective-permute-start(f32[6,256]{1,0:T(8,128)S(1)} %get-tuple-element.23), channel_id=1, source_target_pairs={{0,3},{1,4},{2,5},{3,6},{4,7},{5,8},{6,9},{7,10},{8,11},{9,12},{10... | collective-permute-start | bytes 18440 | tf_op jit(solution)/shard_map/ppermute | solution.py:20
  608.2 8.5 %collective-permute-start.35 = (f32[6,256]{1,0:T(8,128)S(1)}, f32[6,256]{1,0:T(8,128)S(1)}, u32[]{:S(2)}, u32[]{:S(2)}) collective-permute-start(f32[6,256]{1,0:T(8,128)S(1)} %get-tuple-element.22), channel_id=1, source_target_pairs={{0,4},{1,5},{2,6},{3,7},{4,8},{5,9},{6,10},{7,11},{8,12},{9,13},{1... | collective-permute-start | bytes 18440 | tf_op jit(solution)/shard_map/ppermute | solution.py:20
  611.4 5.4 collective-permute-start.36
  612.7 5.8 collective-permute-start.37
  614.0 6.3 collective-permute-start.38
  615.4 8.5 %collective-permute-start.39 = (f32[6,256]{1,0:T(8,128)S(1)}, f32[6,256]{1,0:T(8,128)S(1)}, u32[]{:S(2)}, u32[]{:S(2)}) collective-permute-start(f32[6,256]{1,0:T(8,128)S(1)} %get-tuple-element.18), channel_id=1, source_target_pairs={{4,0},{5,1},{6,2},{7,3},{8,4},{9,5},{10,6},{11,7},{12,8},{13,9},{1... | collective-permute-start | bytes 18440 | tf_op jit(solution)/shard_map/ppermute | solution.py:20
  779.3 15.3 %collective-permute-start.40 = (f32[128]{0:T(128)S(1)}, f32[128]{0:T(128)S(1)}, u32[]{:S(2)}, u32[]{:S(2)}) collective-permute-start(f32[128]{0:T(128)S(1)} %get-tuple-element.67), channel_id=1, source_target_pairs={{0,1},{1,2},{2,3},{3,4},{4,5},{5,6},{6,7},{7,8},{8,9},{9,10},{10,1... | collective-permute-start | bytes 1544 | tf_op jit(solution)/shard_map/ppermute | solution.py:20
  780.6 15.3 %collective-permute-start.41 = (f32[128]{0:T(128)S(1)}, f32[128]{0:T(128)S(1)}, u32[]{:S(2)}, u32[]{:S(2)}) collective-permute-start(f32[128]{0:T(128)S(1)} %get-tuple-element.66), channel_id=1, source_target_pairs={{0,2},{1,3},{2,4},{3,5},{4,6},{5,7},{6,8},{7,9},{8,10},{9,11},{10,... | collective-permute-start | bytes 1544 | tf_op jit(solution)/shard_map/ppermute | solution.py:20
  784.3 12.8 %collective-permute-start.42 = (f32[128]{0:T(128)S(1)}, f32[128]{0:T(128)S(1)}, u32[]{:S(2)}, u32[]{:S(2)}) collective-permute-start(f32[128]{0:T(128)S(1)} %get-tuple-element.65), channel_id=1, source_target_pairs={{0,3},{1,4},{2,5},{3,6},{4,7},{5,8},{6,9},{7,10},{8,11},{9,12},{10... | collective-permute-start | bytes 1544 | tf_op jit(solution)/shard_map/ppermute | solution.py:20
  789.6 9.0 %collective-permute-start.43 = (f32[128]{0:T(128)S(1)}, f32[128]{0:T(128)S(1)}, u32[]{:S(2)}, u32[]{:S(2)}) collective-permute-start(f32[128]{0:T(128)S(1)} %get-tuple-element.64), channel_id=1, source_target_pairs={{0,4},{1,5},{2,6},{3,7},{4,8},{5,9},{6,10},{7,11},{8,12},{9,13},{1... | collective-permute-start | bytes 1544 | tf_op jit(solution)/shard_map/ppermute | solution.py:20
  793.3 5.3 collective-permute-start.44
  794.6 7.0 collective-permute-start.45
  795.9 7.4 collective-permute-start.46
  797.2 9.7 %collective-permute-start.47 = (f32[128]{0:T(128)S(1)}, f32[128]{0:T(128)S(1)}, u32[]{:S(2)}, u32[]{:S(2)}) collective-permute-start(f32[128]{0:T(128)S(1)} %get-tuple-element.60), channel_id=1, source_target_pairs={{4,0},{5,1},{6,2},{7,3},{8,4},{9,5},{10,6},{11,7},{12,8},{13,9},{1... | collective-permute-start | bytes 1544 | tf_op jit(solution)/shard_map/ppermute | solution.py:20
  (15 other events, 425.6 us)
where the time goes:
time: 818 us; the launch traced here: 815 us
  local copies, waits for them, and re-layouts  399 us (49%)
  other arithmetic  257 us (31%)
  starting transfers between devices  126 us (15%)
  waiting for transfers between devices  29.5 us (4%)
    scatter-add x2, other arithmetic, local_product(): jnp.zeros_like(fixed).at[:, connect]  180 us
    ppermute x48, starting transfers between devices, from_behind(): return lax.ppermute(block, axis, route)  126 us
    gather x4, local copies, waits for them, and re-layouts, local_product(): cells = fixed[:, connect].reshape(3 * connect.shape[0], -1)  124 us
    gather x2, local copies, waits for them, and re-layouts, local(): adjoint_cells = fixed[:3][:, connect].reshape(3 * connect.shape[0], -1)  62.1 us
    gather x2, local copies, waits for them, and re-layouts, local(): primal_cells = fixed[3:][:, connect].reshape(3 * connect.shape[0], -1)  62 us
    scatter-add x2, other arithmetic, release(): padded.at[:, master.reshape(-1)].add(spread.reshape(totals.shape[0], -1))  29.5 us
    ppermute x48, waiting for transfers between devices, from_behind(): return lax.ppermute(block, axis, route)  29.5 us
    scatter-add x2, other arithmetic, local(): owned_part.at[:, export_rows.reshape(-1)]  28.2 us
  transfers between devices with their start and end apart: 48, of which 12 were waited for; matrix products, arithmetic and copies ran while one was open for 1% of the time, Pallas kernels for 0%

commit v1 on v0

v1 whole, which is shorter than its diff:
```python
import functools

import jax
import jax.numpy as jnp
from jax import lax
from jax.experimental import pallas as pl
from jax.experimental.pallas import tpu as pltpu
from jax.sharding import PartitionSpec as P

REACH = 4
SWEEPS = 2
WIDE = 256
OWN = 32
EDGE = 16
NOWHERE = 63

relaxation = 0.7
scale_down = 16.0
pad_code = 16368

f32 = jnp.float32
bf16 = jnp.bfloat16
i16 = jnp.int16
i32 = jnp.int32


def from_behind(block, axis, distance):
    devices = range(lax.axis_size(axis))
    route = [(i - distance, i) for i in devices if i - distance in devices]
    return lax.ppermute(block, axis, route)


def neighbour_offsets():
    return [step + 1 for step in range(REACH)] + [-(step + 1) for step in range(REACH)]


def pieces(x):
    high = x.astype(bf16)
    return high, (x - high.astype(f32)).astype(bf16)


def match16(row, count):
    width = row.shape[1]
    wide = jnp.broadcast_to(row, (16, width)).astype(i16)
    numbers = lax.broadcasted_iota(i16, (count, width), 0).reshape(count // 16, 16, width)
    return numbers == wide[None]


def one_hot(row, count):
    mask = match16(row, count)
    ones = jnp.ones(mask.shape, bf16)
    return jnp.where(mask, ones, jnp.zeros_like(ones)).reshape(count, row.shape[1])


def spread16(mask, row):
    wide = jnp.broadcast_to(row, (16, row.shape[1])).astype(bf16)[None]
    out = jnp.where(mask, jnp.broadcast_to(wide, mask.shape), jnp.zeros(mask.shape, bf16))
    return out.reshape(mask.shape[0] * 16, row.shape[1])


def gather_rows(table, rows, parts, at_row, at_column):
    hot = one_hot(at_column, WIDE)
    found = jnp.dot(table, jnp.concatenate([hot, hot], 0), preferred_element_type=f32)
    mask = lax.broadcasted_iota(i32, (rows, at_row.shape[1]), 0) == at_row
    return [
        jnp.sum(jnp.where(mask, found[part * rows : (part + 1) * rows], 0.0), 0, keepdims=True)
        for part in range(parts)
    ]


def gather_cells(table_ref, rows, parts, row_ref, column_ref, out_ref):
    count = row_ref.shape[0]

    def body(block, carry):
        start = pl.multiple_of(block * 8, 8)
        at_row = row_ref[pl.ds(start, 8), :]
        at_column = column_ref[pl.ds(start, 8), :]
        for j in range(8):
            found = gather_rows(
                table_ref[...], rows, parts, at_row[j : j + 1], at_column[j : j + 1]
            )
            for part in range(parts):
                out_ref[pl.ds(part * count + start + j, 1), :] = found[part]
        return carry

    lax.fori_loop(0, count // 8, body, 0)


def scatter_block(values, rows, at_row, at_column):
    count = at_row.shape[0]
    masks = [match16(at_row[j : j + 1], rows) for j in range(count)]
    hot = jnp.concatenate([one_hot(at_column[j : j + 1], WIDE) for j in range(count)], 1)
    stacked = []
    for piece in range(2):
        for part in range(3):
            stacked.append(
                jnp.concatenate(
                    [spread16(masks[j], values[piece][part][j : j + 1]) for j in range(count)], 1
                )
            )
    return lax.dot_general(
        jnp.concatenate(stacked, 0), hot, (((1,), (1,)), ((), ())), preferred_element_type=f32
    )


def split32(x):
    high = x.astype(bf16).astype(f32)
    return high, x - high


def scatter_cells(image_ref, rows, row_ref, column_ref, sum_ref):
    count = row_ref.shape[0]
    sum_ref[...] = jnp.zeros_like(sum_ref)

    def body(block, carry):
        start = pl.multiple_of(block * 8, 8)
        values = [split32(image_ref[pl.ds(part * count + start, 8), :]) for part in range(3)]
        values = list(zip(*values))
        sum_ref[...] += scatter_block(
            values, rows, row_ref[pl.ds(start, 8), :], column_ref[pl.ds(start, 8), :]
        )
        return carry

    lax.fori_loop(0, count // 8, body, 0)


def add_pieces(sums):
    half = sums.shape[0] // 2
    return sums[:half] + sums[half:]


def spread_hanging(held, weight, rows, at_row, at_column):
    both = jnp.concatenate([held, held], 1)
    values = [split32(weight * both[part : part + 1]) for part in range(3)]
    return add_pieces(scatter_block(list(zip(*values)), rows, at_row, at_column))


def sum_masters(table, rows, parts, weight, at_row, at_column):
    total = [jnp.zeros((1, WIDE), f32)] * parts
    for j in range(8):
        found = gather_rows(table, rows, parts, at_row[j : j + 1], at_column[j : j + 1])
        total = [total[part] + weight[j : j + 1] * found[part] for part in range(parts)]
    half = WIDE // 2
    return [x[:, :half] + x[:, half:] for x in total]


def fill_table(x_ref, out_ref):
    count = x_ref.shape[1] // WIDE
    out_ref[...] = jnp.zeros_like(out_ref)
    for row in range(count):
        block = x_ref[:, row * WIDE : (row + 1) * WIDE]
        for part in range(3):
            out_ref[part * OWN + row : part * OWN + row + 1, :] = block[part : part + 1]


def export_rows(table, parts, at_row, at_column, out_refs):
    for slot, out_ref in enumerate(out_refs):
        found = gather_rows(
            table, OWN, parts, at_row[slot : slot + 1], at_column[slot : slot + 1]
        )
        for part in range(parts):
            out_ref[part : part + 1, :] = found[part]


def first_export(adjoint_ref, primal_ref, list_ref, tab_a, tab_p, row_ref, column_ref, *out_refs):
    owned = adjoint_ref.shape[1]
    fill_table(adjoint_ref, tab_a)
    fill_table(primal_ref, tab_p)
    codes = list_ref[...]
    node = lax.rem(17 * codes + lax.broadcasted_iota(i32, codes.shape, 1), owned)
    row_ref[...] = node >> 8
    column_ref[...] = node & 255
    table = jnp.concatenate([tab_a[...], tab_p[...]], 0)
    table = jnp.concatenate(pieces(table), 1)
    export_rows(table, 6, node >> 8, node & 255, out_refs)


def setup(
    connect_ref,
    node_ref,
    master_ref,
    weight_ref,
    source_ref,
    inverse_ref,
    row_own,
    column_own,
    row_edge,
    column_edge,
    master_own,
    master_edge,
    master_column,
    weight_out,
    tab_source,
    tab_inverse,
    found_ref,
):
    owned = source_ref.shape[1]
    extent = owned + 2 * REACH * WIDE
    fill_table(source_ref, tab_source)
    fill_table(inverse_ref, tab_inverse)
    half = WIDE // 2
    codes = master_ref[...]
    master = lax.rem(17 * codes + 8 * lax.broadcasted_iota(i32, codes.shape, 1), extent)
    count = codes.shape[0] // 2
    master = jnp.concatenate([master[:count], master[count:]], 1)
    weight = weight_ref[...]
    weight_out[...] = jnp.concatenate([weight[:count], weight[count:]], 1)
    last = owned // WIDE
    row = master >> 8
    master_own[...] = jnp.where(row < last, row, NOWHERE)
    master_edge[...] = jnp.where(row < last, NOWHERE, row - last)
    master_column[...] = master & 255

    codes = node_ref[...]
    node = jnp.where(codes == pad_code, extent, lax.rem(13 * codes, owned))
    hot = one_hot(node & 255, WIDE)
    slot = (lax.broadcasted_iota(i32, codes.shape, 1) + 1).astype(f32)
    where = spread16(match16(node >> 8, OWN), slot)
    table = lax.dot_general(where, hot, (((1,), (1,)), ((), ())), preferred_element_type=f32)
    table = table.astype(bf16)

    codes = connect_ref[...]
    cells = lax.broadcasted_iota(i32, codes.shape, 1)
    slots = lax.rem(27 * cells + 17 * codes, extent)
    row_own[...] = slots >> 8
    column_own[...] = slots & 255

    def body(block, carry):
        start = pl.multiple_of(block * 8, 8)
        at_row = row_own[pl.ds(start, 8), :]
        at_column = column_own[pl.ds(start, 8), :]
        for j in range(8):
            found = jnp.dot(
                table, one_hot(at_column[j : j + 1], WIDE), preferred_element_type=f32
            )
            mask = lax.broadcasted_iota(i32, (OWN, WIDE), 0) == at_row[j : j + 1]
            found_ref[pl.ds(start + j, 1), :] = jnp.sum(
                jnp.where(mask, found, 0.0), 0, keepdims=True
            )
        return carry

    lax.fori_loop(0, codes.shape[0] // 8, body, 0)
    slot = found_ref[...].astype(i32)
    row = slots >> 8
    hanging = slot > 0
    outside = row >= last
    row_own[...] = jnp.where(hanging | outside, NOWHERE, row)
    row_edge[...] = jnp.where(
        hanging, 2 * REACH, jnp.where(outside, row - last, NOWHERE)
    )
    column_edge[...] = jnp.where(hanging, slot - 1, slots & 255)


def own_gather(
    tab_ref, row_ref, column_ref, master_row, master_column, weight_ref, cells_ref, hang_ref, table_ref
):
    table_ref[...] = jnp.concatenate(pieces(tab_ref[...]), 1)
    found = sum_masters(
        table_ref[...], OWN, 3, weight_ref[...], master_row[...], master_column[...]
    )
    for part in range(3):
        hang_ref[part : part + 1, :] = found[part]
    gather_cells(table_ref, OWN, 3, row_ref, column_ref, cells_ref)


def edge_gather(
    ghost_refs, first, hang_ref, row_ref, column_ref, master_row, master_column, weight_ref,
    edge_ref, table_ref, out_ref,
):
    edge_ref[...] = jnp.zeros_like(edge_ref)
    for slot, ghost_ref in enumerate(ghost_refs):
        for part in range(3):
            edge_ref[part * EDGE + slot : part * EDGE + slot + 1, :] = ghost_ref[
                first + part : first + part + 1, :
            ]
    found = sum_masters(
        jnp.concatenate(pieces(edge_ref[...]), 1),
        EDGE,
        3,
        weight_ref[...],
        master_row[...],
        master_column[...],
    )
    slots = len(ghost_refs)
    for part in range(3):
        edge_ref[part * EDGE + slots : part * EDGE + slots + 1, : WIDE // 2] = (
            found[part] + hang_ref[part : part + 1, :]
        )
    table_ref[...] = jnp.concatenate(pieces(edge_ref[...]), 1)
    gather_cells(table_ref, EDGE, 3, row_ref, column_ref, out_ref)


def edge_product(first, *refs):
    ghost_refs = refs[: 2 * REACH]
    (
        cells_ref, hang_ref, row_ref, column_ref, master_row, master_column, weight_ref,
        modulus_ref, stiffness_ref,
    ) = refs[2 * REACH : 2 * REACH + 9]
    rest = refs[2 * REACH + 9 :]
    out_refs = rest[: 2 * REACH]
    image_ref, held_ref, edge_ref, table_ref, more_ref, sum_ref = rest[2 * REACH :]
    edge_gather(
        ghost_refs, first, hang_ref, row_ref, column_ref, master_row, master_column, weight_ref,
        edge_ref, table_ref, more_ref,
    )
    image_ref[...] = modulus_ref[...] * lax.dot_general(
        stiffness_ref[...],
        cells_ref[...] + more_ref[...],
        (((0,), (0,)), ((), ())),
        precision=lax.Precision.HIGHEST,
        preferred_element_type=f32,
    )
    scatter_cells(image_ref, EDGE, row_ref, column_ref, sum_ref)
    edge_ref[...] = add_pieces(sum_ref[...])
    slots = 2 * REACH
    held = jnp.concatenate(
        [edge_ref[part * EDGE + slots : part * EDGE + slots + 1, : WIDE // 2] for part in range(3)],
        0,
    )
    held_ref[...] = held
    edge_ref[...] += spread_hanging(
        held, weight_ref[...], EDGE, master_row[...], master_column[...]
    )
    for slot, out_ref in enumerate(out_refs):
        for part in range(3):
            out_ref[part : part + 1, :] = edge_ref[part * EDGE + slot : part * EDGE + slot + 1, :]


def own_sums(
    image_ref, held_ref, row_ref, column_ref, master_row, master_column, weight_ref,
    tab_ref, source_ref, inverse_ref, out_ref, sum_ref,
):
    scatter_cells(image_ref, OWN, row_ref, column_ref, sum_ref)
    applied = add_pieces(sum_ref[...]) + spread_hanging(
        held_ref[...], weight_ref[...], OWN, master_row[...], master_column[...]
    )
    out_ref[...] = tab_ref[...] + relaxation * inverse_ref[...] * (source_ref[...] - applied)


def update(last, *refs):
    back_refs = refs[: 2 * REACH]
    row_ref, column_ref, partial_ref, inverse_ref = refs[2 * REACH : 2 * REACH + 4]
    rest = refs[2 * REACH + 4 :]
    out_refs = rest[: 2 * REACH]
    tab_ref = rest[2 * REACH]
    values = []
    for part in range(3):
        block = jnp.concatenate([ref[part : part + 1, :] for ref in back_refs], 0)
        values.append(split32(block))
    returned = add_pieces(
        scatter_block(list(zip(*values)), OWN, row_ref[...], column_ref[...])
    )
    fresh = partial_ref[...] - relaxation * inverse_ref[...] * returned
    tab_ref[...] = fresh
    table = jnp.concatenate(pieces(fresh), 1)
    export_rows(table, 3, row_ref[...], column_ref[...], out_refs)
    if last:
        final_ref = rest[2 * REACH + 1]
        for row in range(final_ref.shape[1] // WIDE):
            for part in range(3):
                final_ref[part : part + 1, row * WIDE : (row + 1) * WIDE] = tab_ref[
                    part * OWN + row : part * OWN + row + 1, :
                ]


def primal_product(first, *refs):
    ghost_refs = refs[: 2 * REACH]
    (
        cells_ref, hang_ref, row_ref, column_ref, master_row, master_column, weight_ref,
        modulus_ref, stiffness_ref, out_ref, edge_ref, table_ref, more_ref,
    ) = refs[2 * REACH :]
    edge_gather(
        ghost_refs, first, hang_ref, row_ref, column_ref, master_row, master_column, weight_ref,
        edge_ref, table_ref, more_ref,
    )
    out_ref[...] = modulus_ref[...] * jnp.dot(
        stiffness_ref[...],
        cells_ref[...] + more_ref[...],
        precision=lax.Precision.HIGHEST,
        preferred_element_type=f32,
    )


def fluxes(*refs):
    ghost_refs = refs[: 2 * REACH]
    (
        cells_ref, hang_ref, row_ref, column_ref, master_row, master_column, weight_ref,
        ku_ref, load_ref, sub_cell, sub_face,
    ) = refs[2 * REACH : 2 * REACH + 11]
    rest = refs[2 * REACH + 11 :]
    out_refs = rest[: 2 * REACH]
    term_ref, edge_ref, table_ref, more_ref = rest[2 * REACH :]
    edge_gather(
        ghost_refs, 0, hang_ref, row_ref, column_ref, master_row, master_column, weight_ref,
        edge_ref, table_ref, more_ref,
    )
    cells = cells_ref[...] + more_ref[...]
    ku = ku_ref[...]
    term_ref[...] = jnp.sum(cells * (load_ref[...] - ku), 0, keepdims=True)
    face = lax.broadcasted_iota(i32, (8, ku.shape[0]), 0)
    node = lax.broadcasted_iota(i32, (8, ku.shape[0]), 1) & 63
    index = jnp.where(face < 2, node >> 4, jnp.where(face < 4, (node >> 2) & 3, node & 3))
    member = jnp.where((face < 6) & (index == 3 * (face & 1)), 1.0, 0.0).astype(f32)
    flux = jnp.dot(
        member, ku * cells, precision=lax.Precision.HIGHEST, preferred_element_type=f32
    )
    table = jnp.concatenate(pieces(flux), 1)
    for slot, out_ref in enumerate(out_refs):
        out_ref[...] = gather_rows(
            table, 8, 1, sub_face[slot : slot + 1, :], sub_cell[slot : slot + 1, :]
        )[0]


def collect(*refs):
    got_refs = refs[: 2 * REACH]
    owner_ref, term_ref, out_ref = refs[2 * REACH :]
    count = term_ref.shape[1]
    got = jnp.concatenate([ref[...] for ref in got_refs], 1)
    hot = jnp.concatenate(
        [one_hot(owner_ref[slot : slot + 1, :], count) for slot in range(2 * REACH)], 1
    )
    high, low = split32(got)
    values = jnp.concatenate(
        [jnp.broadcast_to(x, (16, got.shape[1])).astype(bf16) for x in (high, low)], 0
    )
    sums = lax.dot_general(values, hot, (((1,), (1,)), ((), ())), preferred_element_type=f32)
    face_term = sums[0:1] + sums[16:17]
    out_ref[...] = (jnp.abs(term_ref[...]) + jnp.abs(face_term)) / scale_down


def call(kernel, outs, scratch=()):
    return pl.pallas_call(
        kernel,
        out_shape=[jax.ShapeDtypeStruct(shape, kind) for shape, kind in outs],
        scratch_shapes=[pltpu.VMEM(shape, kind) for shape, kind in scratch],
        compiler_params=pltpu.CompilerParams(vmem_limit_bytes=40 * 1024 * 1024),
    )


def local(
    adjoint_start,
    adjoint_source,
    inverse_diagonal,
    primal_field,
    cell_load,
    modulus,
    stiffness,
    connectivity,
    hang_node,
    hang_master,
    hang_weight,
    ghost_lists,
    subface_cell,
    subface_face,
    subface_owner,
):
    offsets = neighbour_offsets()
    slots = len(offsets)
    local_values, cell_count = cell_load.shape
    nodes = connectivity.shape[0]
    moduli = modulus.reshape(1, cell_count)
    table = ((3 * OWN, WIDE), f32)
    index = ((nodes, cell_count), i32)
    block = ((3, WIDE), f32)
    cells_shape = ((local_values, cell_count), f32)
    hang_shape = ((3, hang_node.shape[0]), f32)
    master_shape = ((8, WIDE), i32)
    own_table = ((3 * OWN, 2 * WIDE), bf16)
    edge = [((3 * EDGE, WIDE), f32), ((3 * EDGE, 2 * WIDE), bf16), cells_shape]

    def send(blocks, sign):
        return [from_behind(b, "dom", sign * o) for b, o in zip(blocks, offsets)]

    tab, tab_primal, list_row, list_column, *blocks = call(
        first_export,
        [table, table, (ghost_lists.shape, i32), (ghost_lists.shape, i32)]
        + [((6, WIDE), f32)] * slots,
    )(adjoint_start, primal_field, ghost_lists)
    ghosts = first_ghosts = send(blocks, 1)
    (
        row_own, column_own, row_edge, column_edge, master_own, master_edge, master_column,
        weight, source, inverse,
    ) = call(
        setup,
        [index] * 4 + [master_shape] * 3 + [((8, WIDE), f32), table, table],
        [((nodes, cell_count), f32)],
    )(
        connectivity, hang_node.reshape(1, -1), hang_master, hang_weight, adjoint_source,
        inverse_diagonal,
    )

    def gather_own(values):
        return call(own_gather, [cells_shape, hang_shape], [own_table])(
            values, row_own, column_own, master_own, master_column, weight
        )

    on_edge = (row_edge, column_edge, master_edge, master_column, weight)
    ku = None
    for sweep in range(SWEEPS):
        cells, hang = gather_own(tab)
        *blocks, image, held = call(
            functools.partial(edge_product, 0),
            [block] * slots + [cells_shape, hang_shape],
            edge + [((6 * EDGE, WIDE), f32)],
        )(*ghosts, cells, hang, *on_edge, moduli, stiffness)
        returned = send(blocks, -1)
        (partial,) = call(own_sums, [table], [((6 * OWN, WIDE), f32)])(
            image, held, row_own, column_own, master_own, master_column, weight, tab, source,
            inverse,
        )
        if sweep == 0:
            cells, hang = gather_own(tab_primal)
            (ku,) = call(functools.partial(primal_product, 3), [cells_shape], edge)(
                *first_ghosts, cells, hang, *on_edge, moduli, stiffness
            )
        last = sweep == SWEEPS - 1
        *blocks, tab = call(
            functools.partial(update, last),
            [block] * slots + [table] + ([(adjoint_start.shape, f32)] if last else []),
        )(*returned, list_row, list_column, partial, inverse)
        if last:
            adjoint = tab
            tab = blocks.pop()
        ghosts = send(blocks, 1)
    cells, hang = gather_own(tab)
    *sent, term = call(
        fluxes,
        [((1, subface_cell.shape[1]), f32)] * slots + [((1, cell_count), f32)],
        edge,
    )(*ghosts, cells, hang, *on_edge, ku, cell_load, subface_cell, subface_face)
    received = send(sent, 1)
    (indicator,) = call(collect, [((1, cell_count), f32)])(*received, subface_owner, term)
    return (adjoint, indicator.reshape(cell_count))


def solution(mesh):
    placed = (
        P(None, "dom"),
        P(None, "dom"),
        P(None, "dom"),
        P(None, "dom"),
        P(None, "dom"),
        P("dom"),
        P(),
        P(None, "dom"),
        P("dom"),
        P(None, "dom"),
        P(None, "dom"),
        P(None, "dom"),
        P(None, "dom"),
        P(None, "dom"),
        P(None, "dom"),
    )
    return jax.shard_map(
        local, mesh=mesh, in_specs=placed, out_specs=(P(None, "dom"), P("dom")), check_vma=False
    )
```

time: 818 us -> 218 us (0.27)
  local copies, waits for them, and re-layouts: 399 us -> 4.04 us
  other arithmetic: 257 us -> 0 us
  Pallas kernels: 0 us -> 61.7 us
  waiting for transfers between devices: 29.5 us -> 10.2 us
  starting transfers between devices: 126 us -> 137 us
    gather x20 -> x0, local copies, waits for them, and re-layouts: 307 us -> none  [the longest x4 124 us: local_product(): cells = fixed[:, connect].reshape(3 * connect.shape[0], -1)]
    scatter-add x7 -> x0, other arithmetic: 245 us -> none  [the longest x2 180 us: local_product(): jnp.zeros_like(fixed).at[:, connect]]
    pallas_call x0 -> x15, Pallas kernels: none -> 61.7 us  [the longest x2 18.1 us: local(): call(functools.partial(edge_product, 0), [block] * slots + [cells_shape,...]
    slice x8 -> x0, local copies, waits for them, and re-layouts: 26.4 us -> none  [the longest x2 8.09 us: local(): owned_part = totals[:, :owned_count]]
    scatter x5 -> x0, local copies, waits for them, and re-layouts: 26.2 us -> none  [the longest x3 15.7 us: constrain(): padded = padded.at[:, node].set(values)]
    ppermute x48, waiting for transfers between devices: 29.5 us -> 10.2 us  [from_behind(): return lax.ppermute(block, axis, route)]
    concatenate x6 -> x0, local copies, waits for them, and re-layouts: 16.6 us -> none  [the longest x2 7.83 us: release(): jnp.concatenate([totals, jnp.zeros((totals.shape[0], 1), totals.dtype)], 1)]
    reshape x7 -> x0, local copies, waits for them, and re-layouts: 10.8 us -> none  [the longest x2 9.41 us: local_product(): image.reshape(3, connect.shape[0], -1)]
  transfers between devices with their start and end apart: 48 -> 48, of which waited for: 12 -> 4; matrix products, arithmetic and copies ran while one was open for 1% -> 0% of each run, Pallas kernels for 0% -> 16%
where the time goes in v1:
time: 218 us; the launch traced here: 214 us
  starting transfers between devices  137 us (63%)
  Pallas kernels  61.7 us (28%)
  waiting for transfers between devices  10.2 us (5%)
  local copies, waits for them, and re-layouts  4.04 us (2%)
    ppermute x48, starting transfers between devices, from_behind(): return lax.ppermute(block, axis, route)  137 us
    pallas_call x2, Pallas kernels, local(): call(functools.partial(edge_product, 0), [block] * slots + [cells_shape,...  18.1 us
    pallas_call x4, Pallas kernels, gather_own(): call(own_gather, [cells_shape, hang_shape], [own_table])  17.6 us
    ppermute x48, waiting for transfers between devices, from_behind(): return lax.ppermute(block, axis, route)  10.2 us
    pallas_call x2, Pallas kernels, local(): call(own_sums, [table], [((6 * OWN, WIDE), f32)])  8.93 us
    pallas_call x1, Pallas kernels, local(): call(fluxes, [((1, subface_cell.shape[1]), f32)] * slots + [((1, cell_cou...  5.11 us
    pallas_call x1, Pallas kernels, local(): call(functools.partial(primal_product, 3), [cells_shape], edge)  4.81 us
  transfers between devices with their start and end apart: 48, of which 4 were waited for; matrix products, arithmetic and copies ran while one was open for 0% of the time, Pallas kernels for 16%

profile of v1, /device:TPU:0, one launch (start us, length us, event | category | flops | bytes accessed | tf_op | source)
XLA Modules:
  0.0 214.1 jit_solution(2458114265009895913)
XLA Ops:
  3.8 2.4 %collective-permute-start = (f32[6,256]{1,0:T(8,128)S(1)}, f32[6,256]{1,0:T(8,128)S(1)}, u32[]{:S(2)}, u32[]{:S(2)}) collective-permute-start(f32[6,256]{1,0:T(8,128)S(1)} %get-tuple-element.80), channel_id=1, source_target_pairs={{0,1},{1,2},{2,3},{3,4},{4,5},{5,6},{6,7},{7,8},{8,9},{9,10},{10,1... | collective-permute-start | bytes 18440 | tf_op jit(solution)/shard_map/ppermute | solution.py:30
  6.2 4.4 %collective-permute-start.1 = (f32[6,256]{1,0:T(8,128)S(1)}, f32[6,256]{1,0:T(8,128)S(1)}, u32[]{:S(2)}, u32[]{:S(2)}) collective-permute-start(f32[6,256]{1,0:T(8,128)S(1)} %get-tuple-element.81), channel_id=1, source_target_pairs={{0,2},{1,3},{2,4},{3,5},{4,6},{5,7},{6,8},{7,9},{8,10},{9,11},{10,... | collective-permute-start | bytes 18440 | tf_op jit(solution)/shard_map/ppermute | solution.py:30
  10.6 4.3 %collective-permute-start.2 = (f32[6,256]{1,0:T(8,128)S(1)}, f32[6,256]{1,0:T(8,128)S(1)}, u32[]{:S(2)}, u32[]{:S(2)}) collective-permute-start(f32[6,256]{1,0:T(8,128)S(1)} %get-tuple-element.82), channel_id=1, source_target_pairs={{0,3},{1,4},{2,5},{3,6},{4,7},{5,8},{6,9},{7,10},{8,11},{9,12},{10... | collective-permute-start | bytes 18440 | tf_op jit(solution)/shard_map/ppermute | solution.py:30
  14.9 3.4 %collective-permute-start.3 = (f32[6,256]{1,0:T(8,128)S(1)}, f32[6,256]{1,0:T(8,128)S(1)}, u32[]{:S(2)}, u32[]{:S(2)}) collective-permute-start(f32[6,256]{1,0:T(8,128)S(1)} %get-tuple-element.83), channel_id=1, source_target_pairs={{0,4},{1,5},{2,6},{3,7},{4,8},{5,9},{6,10},{7,11},{8,12},{9,13},{1... | collective-permute-start | bytes 18440 | tf_op jit(solution)/shard_map/ppermute | solution.py:30
  18.4 1.3 collective-permute-start.4
  19.7 1.3 collective-permute-start.5
  24.5 2.7 %shard_map.159 = (s32[64,256]{1,0:T(8,128)S(1)}, s32[64,256]{1,0:T(8,128)S(1)}, s32[64,256]{1,0:T(8,128)S(1)}, s32[64,256]{1,0:T(8,128)S(1)}, s32[8,256]{1,0:T(8...) custom-call(s32[64,256]{1,0:T(8,128)S(1)} %copy-done.6, ...), custom_call_target="tpu_custom_call" | custom-call | tf_op jit(solution)/shard_map/pallas_call | solution.py:483
  27.2 4.4 %shard_map.160 = (f32[192,256]{1,0:T(8,128)S(1)}, f32[3,128]{1,0:T(4,128)S(1)}) custom-call(f32[96,256]{1,0:T(8,128)S(1)} %get-tuple-element.88.tab_ref, s32[64,256]{1,0:T(8,128)S(1)} %get-tuple-element.89.row_ref, s32[64,256]{1,0:T(8,128)S(1)} %get-tuple-element.90.column_ref, s32[8,256]{1,0:T(8,128)S(1)} %get-tuple-element.91.master_row, ...), custom_call_target="tpu_custom_call" | custom-call | tf_op jit(solution)/shard_map/pallas_call | solution.py:493
  32.4 9.0 %shard_map.161 = (f32[3,256]{1,0:T(4,128)S(1)}, f32[3,256]{1,0:T(4,128)S(1)}, f32[3,256]{1,0:T(4,128)S(1)}, f32[3,256]{1,0:T(4,128)S(1)}, f32[3,256]{1,0:T(4,128...) custom-call(f32[6,256]{1,0:T(8,128)S(1)} %collective-permute-done.re, ...), custom_call_target="tpu_custom_call" | custom-call | tf_op jit(solution)/shard_map/pallas_call | solution.py:501
  46.6 3.7 %collective-permute-start.12 = (f32[3,256]{1,0:T(4,128)S(1)}, f32[3,256]{1,0:T(4,128)S(1)}, u32[]{:S(2)}, u32[]{:S(2)}) collective-permute-start(f32[3,256]{1,0:T(4,128)S(1)} %get-tuple-element.103), channel_id=1, source_target_pairs={{0,1},{1,2},{2,3},{3,4},{4,5},{5,6},{6,7},{7,8},{8,9},{9,10},{10,1... | collective-permute-start | bytes 9224 | tf_op jit(solution)/shard_map/ppermute | solution.py:30
  50.3 6.2 %collective-permute-start.13 = (f32[3,256]{1,0:T(4,128)S(1)}, f32[3,256]{1,0:T(4,128)S(1)}, u32[]{:S(2)}, u32[]{:S(2)}) collective-permute-start(f32[3,256]{1,0:T(4,128)S(1)} %get-tuple-element.104), channel_id=1, source_target_pairs={{0,2},{1,3},{2,4},{3,5},{4,6},{5,7},{6,8},{7,9},{8,10},{9,11},{10,... | collective-permute-start | bytes 9224 | tf_op jit(solution)/shard_map/ppermute | solution.py:30
  56.5 6.8 %collective-permute-start.14 = (f32[3,256]{1,0:T(4,128)S(1)}, f32[3,256]{1,0:T(4,128)S(1)}, u32[]{:S(2)}, u32[]{:S(2)}) collective-permute-start(f32[3,256]{1,0:T(4,128)S(1)} %get-tuple-element.105), channel_id=1, source_target_pairs={{0,3},{1,4},{2,5},{3,6},{4,7},{5,8},{6,9},{7,10},{8,11},{9,12},{10... | collective-permute-start | bytes 9224 | tf_op jit(solution)/shard_map/ppermute | solution.py:30
  63.3 6.0 %collective-permute-start.15 = (f32[3,256]{1,0:T(4,128)S(1)}, f32[3,256]{1,0:T(4,128)S(1)}, u32[]{:S(2)}, u32[]{:S(2)}) collective-permute-start(f32[3,256]{1,0:T(4,128)S(1)} %get-tuple-element.106), channel_id=1, source_target_pairs={{0,4},{1,5},{2,6},{3,7},{4,8},{5,9},{6,10},{7,11},{8,12},{9,13},{1... | collective-permute-start | bytes 9224 | tf_op jit(solution)/shard_map/ppermute | solution.py:30
  69.3 4.5 %shard_map.162.refs_10_ = f32[96,256]{1,0:T(8,128)S(1)} custom-call(f32[192,256]{1,0:T(8,128)S(1)} %get-tuple-element.109.image_ref, f32[3,128]{1,0:T(4,128)S(1)} %get-tuple-element.110.held_ref, s32[64,256]{1,0:T(8,128)S(1)} %get-tuple-element.89.row_ref, s32[64,256]{1,0:T(8,128)S(1)} %get-tuple-element.90.column_ref, ...), custom_call_target="tpu_custom_call" | custom-call | tf_op jit(solution)/shard_map/pallas_call | solution.py:507
  73.8 1.4 shard_map.163
  76.5 4.5 %collective-permute-start.17 = (f32[3,256]{1,0:T(4,128)S(1)}, f32[3,256]{1,0:T(4,128)S(1)}, u32[]{:S(2)}, u32[]{:S(2)}) collective-permute-start(f32[3,256]{1,0:T(4,128)S(1)} %get-tuple-element.114), channel_id=1, source_target_pairs={{0,2},{1,3},{2,4},{3,5},{4,6},{5,7},{6,8},{7,9},{8,10},{9,11},{10,... | collective-permute-start | bytes 9224 | tf_op jit(solution)/shard_map/ppermute | solution.py:30
  81.0 5.3 %collective-permute-start.18 = (f32[3,256]{1,0:T(4,128)S(1)}, f32[3,256]{1,0:T(4,128)S(1)}, u32[]{:S(2)}, u32[]{:S(2)}) collective-permute-start(f32[3,256]{1,0:T(4,128)S(1)} %get-tuple-element.115), channel_id=1, source_target_pairs={{0,3},{1,4},{2,5},{3,6},{4,7},{5,8},{6,9},{7,10},{8,11},{9,12},{10... | collective-permute-start | bytes 9224 | tf_op jit(solution)/shard_map/ppermute | solution.py:30
  86.2 3.6 %collective-permute-start.19 = (f32[3,256]{1,0:T(4,128)S(1)}, f32[3,256]{1,0:T(4,128)S(1)}, u32[]{:S(2)}, u32[]{:S(2)}) collective-permute-start(f32[3,256]{1,0:T(4,128)S(1)} %get-tuple-element.116), channel_id=1, source_target_pairs={{0,4},{1,5},{2,6},{3,7},{4,8},{5,9},{6,10},{7,11},{8,12},{9,13},{1... | collective-permute-start | bytes 9224 | tf_op jit(solution)/shard_map/ppermute | solution.py:30
  92.5 1.3 collective-permute-start.22
  95.1 4.4 %shard_map.164 = (f32[192,256]{1,0:T(8,128)S(1)}, f32[3,128]{1,0:T(4,128)S(1)}) custom-call(f32[96,256]{1,0:T(8,128)S(1)} %get-tuple-element.121.tab_ref, s32[64,256]{1,0:T(8,128)S(1)} %get-tuple-element.89.row_ref, s32[64,256]{1,0:T(8,128)S(1)} %get-tuple-element.90.column_ref, s32[8,256]{1,0:T(8,128)S(1)} %get-tuple-element.91.master_row, ...), custom_call_target="tpu_custom_call" | custom-call | tf_op jit(solution)/shard_map/pallas_call | solution.py:493
  99.6 2.6 %collective-permute-done.23.refs_7_ = f32[3,256]{1,0:T(4,128)S(1)} collective-permute-done((f32[3,256]{1,0:T(4,128)S(1)}, f32[3,256]{1,0:T(4,128)S(1)}, u32[]{:S(2)}, u32[]{:S(2)}) %collective-permute-start.23) | collective-permute-done | bytes 3104 | tf_op jit(solution)/shard_map/ppermute | solution.py:30
  102.1 9.0 %shard_map.165 = (f32[3,256]{1,0:T(4,128)S(1)}, f32[3,256]{1,0:T(4,128)S(1)}, f32[3,256]{1,0:T(4,128)S(1)}, f32[3,256]{1,0:T(4,128)S(1)}, f32[3,256]{1,0:T(4,128...) custom-call(f32[3,256]{1,0:T(4,128)S(1)} %collective-permute-done.16, ...), custom_call_target="tpu_custom_call" | custom-call | tf_op jit(solution)/shard_map/pallas_call | solution.py:501
  111.2 1.3 collective-permute-start.24
  112.5 1.3 collective-permute-start.25
  113.8 1.3 collective-permute-start.26
  115.1 1.3 collective-permute-start.27
  116.4 3.0 %collective-permute-start.28 = (f32[3,256]{1,0:T(4,128)S(1)}, f32[3,256]{1,0:T(4,128)S(1)}, u32[]{:S(2)}, u32[]{:S(2)}) collective-permute-start(f32[3,256]{1,0:T(4,128)S(1)} %get-tuple-element.128), channel_id=1, source_target_pairs={{0,1},{1,2},{2,3},{3,4},{4,5},{5,6},{6,7},{7,8},{8,9},{9,10},{10,1... | collective-permute-start | bytes 9224 | tf_op jit(solution)/shard_map/ppermute | solution.py:30
  119.4 4.9 %collective-permute-start.29 = (f32[3,256]{1,0:T(4,128)S(1)}, f32[3,256]{1,0:T(4,128)S(1)}, u32[]{:S(2)}, u32[]{:S(2)}) collective-permute-start(f32[3,256]{1,0:T(4,128)S(1)} %get-tuple-element.129), channel_id=1, source_target_pairs={{0,2},{1,3},{2,4},{3,5},{4,6},{5,7},{6,8},{7,9},{8,10},{9,11},{10,... | collective-permute-start | bytes 9224 | tf_op jit(solution)/shard_map/ppermute | solution.py:30
  124.3 6.2 %collective-permute-start.30 = (f32[3,256]{1,0:T(4,128)S(1)}, f32[3,256]{1,0:T(4,128)S(1)}, u32[]{:S(2)}, u32[]{:S(2)}) collective-permute-start(f32[3,256]{1,0:T(4,128)S(1)} %get-tuple-element.130), channel_id=1, source_target_pairs={{0,3},{1,4},{2,5},{3,6},{4,7},{5,8},{6,9},{7,10},{8,11},{9,12},{10... | collective-permute-start | bytes 9224 | tf_op jit(solution)/shard_map/ppermute | solution.py:30
  130.6 5.9 %collective-permute-start.31 = (f32[3,256]{1,0:T(4,128)S(1)}, f32[3,256]{1,0:T(4,128)S(1)}, u32[]{:S(2)}, u32[]{:S(2)}) collective-permute-start(f32[3,256]{1,0:T(4,128)S(1)} %get-tuple-element.131), channel_id=1, source_target_pairs={{0,4},{1,5},{2,6},{3,7},{4,8},{5,9},{6,10},{7,11},{8,12},{9,13},{1... | collective-permute-start | bytes 9224 | tf_op jit(solution)/shard_map/ppermute | solution.py:30
  136.5 4.5 %shard_map.166.refs_10_ = f32[96,256]{1,0:T(8,128)S(1)} custom-call(f32[192,256]{1,0:T(8,128)S(1)} %get-tuple-element.132.image_ref, f32[3,128]{1,0:T(4,128)S(1)} %get-tuple-element.133.held_ref, s32[64,256]{1,0:T(8,128)S(1)} %get-tuple-element.89.row_ref, s32[64,256]{1,0:T(8,128)S(1)} %get-tuple-element.90.column_ref, ...), custom_call_target="tpu_custom_call" | custom-call | tf_op jit(solution)/shard_map/pallas_call | solution.py:507
  141.0 1.6 shard_map.167
  143.9 4.9 %collective-permute-start.33 = (f32[3,256]{1,0:T(4,128)S(1)}, f32[3,256]{1,0:T(4,128)S(1)}, u32[]{:S(2)}, u32[]{:S(2)}) collective-permute-start(f32[3,256]{1,0:T(4,128)S(1)} %get-tuple-element.136), channel_id=1, source_target_pairs={{0,2},{1,3},{2,4},{3,5},{4,6},{5,7},{6,8},{7,9},{8,10},{9,11},{10,... | collective-permute-start | bytes 9224 | tf_op jit(solution)/shard_map/ppermute | solution.py:30
  148.8 5.7 %collective-permute-start.34 = (f32[3,256]{1,0:T(4,128)S(1)}, f32[3,256]{1,0:T(4,128)S(1)}, u32[]{:S(2)}, u32[]{:S(2)}) collective-permute-start(f32[3,256]{1,0:T(4,128)S(1)} %get-tuple-element.137), channel_id=1, source_target_pairs={{0,3},{1,4},{2,5},{3,6},{4,7},{5,8},{6,9},{7,10},{8,11},{9,12},{10... | collective-permute-start | bytes 9224 | tf_op jit(solution)/shard_map/ppermute | solution.py:30
  154.5 3.6 %collective-permute-start.35 = (f32[3,256]{1,0:T(4,128)S(1)}, f32[3,256]{1,0:T(4,128)S(1)}, u32[]{:S(2)}, u32[]{:S(2)}) collective-permute-start(f32[3,256]{1,0:T(4,128)S(1)} %get-tuple-element.138), channel_id=1, source_target_pairs={{0,4},{1,5},{2,6},{3,7},{4,8},{5,9},{6,10},{7,11},{8,12},{9,13},{1... | collective-permute-start | bytes 9224 | tf_op jit(solution)/shard_map/ppermute | solution.py:30
  160.8 1.3 collective-permute-start.38
  162.1 1.5 collective-permute-start.39
  163.6 4.4 %shard_map.169 = (f32[192,256]{1,0:T(8,128)S(1)}, f32[3,128]{1,0:T(4,128)S(1)}) custom-call(f32[96,256]{1,0:T(8,128)S(1)} %get-tuple-element.146.tab_ref, s32[64,256]{1,0:T(8,128)S(1)} %get-tuple-element.89.row_ref, s32[64,256]{1,0:T(8,128)S(1)} %get-tuple-element.90.column_ref, s32[8,256]{1,0:T(8,128)S(1)} %get-tuple-element.91.master_row, ...), custom_call_target="tpu_custom_call" | custom-call | tf_op jit(solution)/shard_map/pallas_call | solution.py:493
  168.0 4.8 %shard_map.170.refs_15_ = f32[192,256]{1,0:T(8,128)S(1)} custom-call(f32[6,256]{1,0:T(8,128)S(1)} %collective-permute-done.refs_0_, f32[6,256]{1,0:T(8,128)S(1)} %collective-permute-done.1.refs_1_, f32[6,256]{1,0:T(8,128)S(1)} %collective-permute-done.2.refs_2_, f32[6,256]{1,0:T(8,128)S(1)} %collective-permute-done.3.refs_3_, ...), custom_call_target="tpu_custom_call" | custom-call | tf_op jit(solution)/shard_map/pallas_call | solution.py:513
  172.8 4.4 %shard_map.168 = (f32[192,256]{1,0:T(8,128)S(1)}, f32[3,128]{1,0:T(4,128)S(1)}) custom-call(f32[96,256]{1,0:T(8,128)S(1)} %get-tuple-element.143.tab_ref, s32[64,256]{1,0:T(8,128)S(1)} %get-tuple-element.89.row_ref, s32[64,256]{1,0:T(8,128)S(1)} %get-tuple-element.90.column_ref, s32[8,256]{1,0:T(8,128)S(1)} %get-tuple-element.91.master_row, ...), custom_call_target="tpu_custom_call" | custom-call | tf_op jit(solution)/shard_map/pallas_call | solution.py:493
  177.3 5.1 %shard_map.171 = (f32[1,128]{1,0:T(1,128)S(1)}, f32[1,128]{1,0:T(1,128)S(1)}, f32[1,128]{1,0:T(1,128)S(1)}, f32[1,128]{1,0:T(1,128)S(1)}, f32[1,128]{1,0:T(1,128...) custom-call(f32[3,256]{1,0:T(4,128)S(1)} %collective-permute-done.32.refs_0_, ...), custom_call_target="tpu_custom_call" | custom-call | tf_op jit(solution)/shard_map/pallas_call | solution.py:526
  182.4 3.0 %collective-permute-start.40 = (f32[1,128]{1,0:T(1,128)S(1)}, f32[1,128]{1,0:T(1,128)S(1)}, u32[]{:S(2)}, u32[]{:S(2)}) collective-permute-start(f32[1,128]{1,0:T(1,128)S(1)} %get-tuple-element.149), channel_id=1, source_target_pairs={{0,1},{1,2},{2,3},{3,4},{4,5},{5,6},{6,7},{7,8},{8,9},{9,10},{10,1... | collective-permute-start | bytes 1544 | tf_op jit(solution)/shard_map/ppermute | solution.py:30
  185.5 4.9 %collective-permute-start.41 = (f32[1,128]{1,0:T(1,128)S(1)}, f32[1,128]{1,0:T(1,128)S(1)}, u32[]{:S(2)}, u32[]{:S(2)}) collective-permute-start(f32[1,128]{1,0:T(1,128)S(1)} %get-tuple-element.150), channel_id=1, source_target_pairs={{0,2},{1,3},{2,4},{3,5},{4,6},{5,7},{6,8},{7,9},{8,10},{9,11},{10,... | collective-permute-start | bytes 1544 | tf_op jit(solution)/shard_map/ppermute | solution.py:30
  190.4 5.3 %collective-permute-start.42 = (f32[1,128]{1,0:T(1,128)S(1)}, f32[1,128]{1,0:T(1,128)S(1)}, u32[]{:S(2)}, u32[]{:S(2)}) collective-permute-start(f32[1,128]{1,0:T(1,128)S(1)} %get-tuple-element.151), channel_id=1, source_target_pairs={{0,3},{1,4},{2,5},{3,6},{4,7},{5,8},{6,9},{7,10},{8,11},{9,12},{10... | collective-permute-start | bytes 1544 | tf_op jit(solution)/shard_map/ppermute | solution.py:30
  195.7 4.8 %collective-permute-start.43 = (f32[1,128]{1,0:T(1,128)S(1)}, f32[1,128]{1,0:T(1,128)S(1)}, u32[]{:S(2)}, u32[]{:S(2)}) collective-permute-start(f32[1,128]{1,0:T(1,128)S(1)} %get-tuple-element.152), channel_id=1, source_target_pairs={{0,4},{1,5},{2,6},{3,7},{4,8},{5,9},{6,10},{7,11},{8,12},{9,13},{1... | collective-permute-start | bytes 1544 | tf_op jit(solution)/shard_map/ppermute | solution.py:30
  205.8 2.2 %collective-permute-done.45.refs_5_ = f32[1,128]{1,0:T(1,128)S(1)} collective-permute-done((f32[1,128]{1,0:T(1,128)S(1)}, f32[1,128]{1,0:T(1,128)S(1)}, u32[]{:S(2)}, u32[]{:S(2)}) %collective-permute-start.45) | collective-permute-done | bytes 544 | tf_op jit(solution)/shard_map/ppermute | solution.py:30
  208.0 1.7 collective-permute-done.46.refs_6_
  209.7 3.6 %collective-permute-done.47.refs_7_ = f32[1,128]{1,0:T(1,128)S(1)} collective-permute-done((f32[1,128]{1,0:T(1,128)S(1)}, f32[1,128]{1,0:T(1,128)S(1)}, u32[]{:S(2)}, u32[]{:S(2)}) %collective-permute-start.47) | collective-permute-done | bytes 544 | tf_op jit(solution)/shard_map/ppermute | solution.py:30
  (93 shorter events, 27.6 us)
Async XLA Ops:
  3.8 15.8 %collective-permute-start = (f32[6,256]{1,0:T(8,128)S(1)}, f32[6,256]{1,0:T(8,128)S(1)}, u32[]{:S(2)}, u32[]{:S(2)}) collective-permute-start(f32[6,256]{1,0:T(8,128)S(1)} %get-tuple-element.80), channel_id=1, source_target_pairs={{0,1},{1,2},{2,3},{3,4},{4,5},{5,6},{6,7},{7,8},{8,9},{9,10},{10,1... | collective-permute-start | bytes 18440 | tf_op jit(solution)/shard_map/ppermute | solution.py:30
  6.2 14.8 %collective-permute-start.1 = (f32[6,256]{1,0:T(8,128)S(1)}, f32[6,256]{1,0:T(8,128)S(1)}, u32[]{:S(2)}, u32[]{:S(2)}) collective-permute-start(f32[6,256]{1,0:T(8,128)S(1)} %get-tuple-element.81), channel_id=1, source_target_pairs={{0,2},{1,3},{2,4},{3,5},{4,6},{5,7},{6,8},{7,9},{8,10},{9,11},{10,... | collective-permute-start | bytes 18440 | tf_op jit(solution)/shard_map/ppermute | solution.py:30
  10.6 11.7 %collective-permute-start.2 = (f32[6,256]{1,0:T(8,128)S(1)}, f32[6,256]{1,0:T(8,128)S(1)}, u32[]{:S(2)}, u32[]{:S(2)}) collective-permute-start(f32[6,256]{1,0:T(8,128)S(1)} %get-tuple-element.82), channel_id=1, source_target_pairs={{0,3},{1,4},{2,5},{3,6},{4,7},{5,8},{6,9},{7,10},{8,11},{9,12},{10... | collective-permute-start | bytes 18440 | tf_op jit(solution)/shard_map/ppermute | solution.py:30
  14.9 16.7 %collective-permute-start.3 = (f32[6,256]{1,0:T(8,128)S(1)}, f32[6,256]{1,0:T(8,128)S(1)}, u32[]{:S(2)}, u32[]{:S(2)}) collective-permute-start(f32[6,256]{1,0:T(8,128)S(1)} %get-tuple-element.83), channel_id=1, source_target_pairs={{0,4},{1,5},{2,6},{3,7},{4,8},{5,9},{6,10},{7,11},{8,12},{9,13},{1... | collective-permute-start | bytes 18440 | tf_op jit(solution)/shard_map/ppermute | solution.py:30
  18.4 13.3 %collective-permute-start.4 = (f32[6,256]{1,0:T(8,128)S(1)}, f32[6,256]{1,0:T(8,128)S(1)}, u32[]{:S(2)}, u32[]{:S(2)}) collective-permute-start(f32[6,256]{1,0:T(8,128)S(1)} %get-tuple-element.84), channel_id=1, source_target_pairs={{1,0},{2,1},{3,2},{4,3},{5,4},{6,5},{7,6},{8,7},{9,8},{10,9},{11,1... | collective-permute-start | bytes 18440 | tf_op jit(solution)/shard_map/ppermute | solution.py:30
  19.7 12.0 %collective-permute-start.5 = (f32[6,256]{1,0:T(8,128)S(1)}, f32[6,256]{1,0:T(8,128)S(1)}, u32[]{:S(2)}, u32[]{:S(2)}) collective-permute-start(f32[6,256]{1,0:T(8,128)S(1)} %get-tuple-element.85), channel_id=1, source_target_pairs={{2,0},{3,1},{4,2},{5,3},{6,4},{7,5},{8,6},{9,7},{10,8},{11,9},{12,... | collective-permute-start | bytes 18440 | tf_op jit(solution)/shard_map/ppermute | solution.py:30
  21.0 10.7 %collective-permute-start.6 = (f32[6,256]{1,0:T(8,128)S(1)}, f32[6,256]{1,0:T(8,128)S(1)}, u32[]{:S(2)}, u32[]{:S(2)}) collective-permute-start(f32[6,256]{1,0:T(8,128)S(1)} %get-tuple-element.86), channel_id=1, source_target_pairs={{3,0},{4,1},{5,2},{6,3},{7,4},{8,5},{9,6},{10,7},{11,8},{12,9},{13... | collective-permute-start | bytes 18440 | tf_op jit(solution)/shard_map/ppermute | solution.py:30
  22.3 9.4 %collective-permute-start.7 = (f32[6,256]{1,0:T(8,128)S(1)}, f32[6,256]{1,0:T(8,128)S(1)}, u32[]{:S(2)}, u32[]{:S(2)}) collective-permute-start(f32[6,256]{1,0:T(8,128)S(1)} %get-tuple-element.87), channel_id=1, source_target_pairs={{4,0},{5,1},{6,2},{7,3},{8,4},{9,5},{10,6},{11,7},{12,8},{13,9},{1... | collective-permute-start | bytes 18440 | tf_op jit(solution)/shard_map/ppermute | solution.py:30
  41.4 8.9 %collective-permute-start.8 = (f32[3,256]{1,0:T(4,128)S(1)}, f32[3,256]{1,0:T(4,128)S(1)}, u32[]{:S(2)}, u32[]{:S(2)}) collective-permute-start(f32[3,256]{1,0:T(4,128)S(1)} %get-tuple-element.99), channel_id=1, source_target_pairs={{1,0},{2,1},{3,2},{4,3},{5,4},{6,5},{7,6},{8,7},{9,8},{10,9},{11,1... | collective-permute-start | bytes 9224 | tf_op jit(solution)/shard_map/ppermute | solution.py:30
  42.7 13.7 %collective-permute-start.9 = (f32[3,256]{1,0:T(4,128)S(1)}, f32[3,256]{1,0:T(4,128)S(1)}, u32[]{:S(2)}, u32[]{:S(2)}) collective-permute-start(f32[3,256]{1,0:T(4,128)S(1)} %get-tuple-element.100), channel_id=1, source_target_pairs={{2,0},{3,1},{4,2},{5,3},{6,4},{7,5},{8,6},{9,7},{10,8},{11,9},{12,... | collective-permute-start | bytes 9224 | tf_op jit(solution)/shard_map/ppermute | solution.py:30
  44.0 19.3 %collective-permute-start.10 = (f32[3,256]{1,0:T(4,128)S(1)}, f32[3,256]{1,0:T(4,128)S(1)}, u32[]{:S(2)}, u32[]{:S(2)}) collective-permute-start(f32[3,256]{1,0:T(4,128)S(1)} %get-tuple-element.101), channel_id=1, source_target_pairs={{3,0},{4,1},{5,2},{6,3},{7,4},{8,5},{9,6},{10,7},{11,8},{12,9},{13... | collective-permute-start | bytes 9224 | tf_op jit(solution)/shard_map/ppermute | solution.py:30
  45.3 28.4 %collective-permute-start.11 = (f32[3,256]{1,0:T(4,128)S(1)}, f32[3,256]{1,0:T(4,128)S(1)}, u32[]{:S(2)}, u32[]{:S(2)}) collective-permute-start(f32[3,256]{1,0:T(4,128)S(1)} %get-tuple-element.102), channel_id=1, source_target_pairs={{4,0},{5,1},{6,2},{7,3},{8,4},{9,5},{10,6},{11,7},{12,8},{13,9},{1... | collective-permute-start | bytes 9224 | tf_op jit(solution)/shard_map/ppermute | solution.py:30
  46.6 27.1 %collective-permute-start.12 = (f32[3,256]{1,0:T(4,128)S(1)}, f32[3,256]{1,0:T(4,128)S(1)}, u32[]{:S(2)}, u32[]{:S(2)}) collective-permute-start(f32[3,256]{1,0:T(4,128)S(1)} %get-tuple-element.103), channel_id=1, source_target_pairs={{0,1},{1,2},{2,3},{3,4},{4,5},{5,6},{6,7},{7,8},{8,9},{9,10},{10,1... | collective-permute-start | bytes 9224 | tf_op jit(solution)/shard_map/ppermute | solution.py:30
  50.3 23.5 %collective-permute-start.13 = (f32[3,256]{1,0:T(4,128)S(1)}, f32[3,256]{1,0:T(4,128)S(1)}, u32[]{:S(2)}, u32[]{:S(2)}) collective-permute-start(f32[3,256]{1,0:T(4,128)S(1)} %get-tuple-element.104), channel_id=1, source_target_pairs={{0,2},{1,3},{2,4},{3,5},{4,6},{5,7},{6,8},{7,9},{8,10},{9,11},{10,... | collective-permute-start | bytes 9224 | tf_op jit(solution)/shard_map/ppermute | solution.py:30
  56.5 17.3 %collective-permute-start.14 = (f32[3,256]{1,0:T(4,128)S(1)}, f32[3,256]{1,0:T(4,128)S(1)}, u32[]{:S(2)}, u32[]{:S(2)}) collective-permute-start(f32[3,256]{1,0:T(4,128)S(1)} %get-tuple-element.105), channel_id=1, source_target_pairs={{0,3},{1,4},{2,5},{3,6},{4,7},{5,8},{6,9},{7,10},{8,11},{9,12},{10... | collective-permute-start | bytes 9224 | tf_op jit(solution)/shard_map/ppermute | solution.py:30
  63.3 10.5 %collective-permute-start.15 = (f32[3,256]{1,0:T(4,128)S(1)}, f32[3,256]{1,0:T(4,128)S(1)}, u32[]{:S(2)}, u32[]{:S(2)}) collective-permute-start(f32[3,256]{1,0:T(4,128)S(1)} %get-tuple-element.106), channel_id=1, source_target_pairs={{0,4},{1,5},{2,6},{3,7},{4,8},{5,9},{6,10},{7,11},{8,12},{9,13},{1... | collective-permute-start | bytes 9224 | tf_op jit(solution)/shard_map/ppermute | solution.py:30
  75.2 16.0 %collective-permute-start.16 = (f32[3,256]{1,0:T(4,128)S(1)}, f32[3,256]{1,0:T(4,128)S(1)}, u32[]{:S(2)}, u32[]{:S(2)}) collective-permute-start(f32[3,256]{1,0:T(4,128)S(1)} %get-tuple-element.113), channel_id=1, source_target_pairs={{0,1},{1,2},{2,3},{3,4},{4,5},{5,6},{6,7},{7,8},{8,9},{9,10},{10,1... | collective-permute-start | bytes 9224 | tf_op jit(solution)/shard_map/ppermute | solution.py:30
  76.5 16.0 %collective-permute-start.17 = (f32[3,256]{1,0:T(4,128)S(1)}, f32[3,256]{1,0:T(4,128)S(1)}, u32[]{:S(2)}, u32[]{:S(2)}) collective-permute-start(f32[3,256]{1,0:T(4,128)S(1)} %get-tuple-element.114), channel_id=1, source_target_pairs={{0,2},{1,3},{2,4},{3,5},{4,6},{5,7},{6,8},{7,9},{8,10},{9,11},{10,... | collective-permute-start | bytes 9224 | tf_op jit(solution)/shard_map/ppermute | solution.py:30
  81.0 12.8 %collective-permute-start.18 = (f32[3,256]{1,0:T(4,128)S(1)}, f32[3,256]{1,0:T(4,128)S(1)}, u32[]{:S(2)}, u32[]{:S(2)}) collective-permute-start(f32[3,256]{1,0:T(4,128)S(1)} %get-tuple-element.115), channel_id=1, source_target_pairs={{0,3},{1,4},{2,5},{3,6},{4,7},{5,8},{6,9},{7,10},{8,11},{9,12},{10... | collective-permute-start | bytes 9224 | tf_op jit(solution)/shard_map/ppermute | solution.py:30
  86.2 13.3 %collective-permute-start.19 = (f32[3,256]{1,0:T(4,128)S(1)}, f32[3,256]{1,0:T(4,128)S(1)}, u32[]{:S(2)}, u32[]{:S(2)}) collective-permute-start(f32[3,256]{1,0:T(4,128)S(1)} %get-tuple-element.116), channel_id=1, source_target_pairs={{0,4},{1,5},{2,6},{3,7},{4,8},{5,9},{6,10},{7,11},{8,12},{9,13},{1... | collective-permute-start | bytes 9224 | tf_op jit(solution)/shard_map/ppermute | solution.py:30
  89.9 9.7 %collective-permute-start.20 = (f32[3,256]{1,0:T(4,128)S(1)}, f32[3,256]{1,0:T(4,128)S(1)}, u32[]{:S(2)}, u32[]{:S(2)}) collective-permute-start(f32[3,256]{1,0:T(4,128)S(1)} %get-tuple-element.117), channel_id=1, source_target_pairs={{1,0},{2,1},{3,2},{4,3},{5,4},{6,5},{7,6},{8,7},{9,8},{10,9},{11,1... | collective-permute-start | bytes 9224 | tf_op jit(solution)/shard_map/ppermute | solution.py:30
  91.2 8.4 %collective-permute-start.21 = (f32[3,256]{1,0:T(4,128)S(1)}, f32[3,256]{1,0:T(4,128)S(1)}, u32[]{:S(2)}, u32[]{:S(2)}) collective-permute-start(f32[3,256]{1,0:T(4,128)S(1)} %get-tuple-element.118), channel_id=1, source_target_pairs={{2,0},{3,1},{4,2},{5,3},{6,4},{7,5},{8,6},{9,7},{10,8},{11,9},{12,... | collective-permute-start | bytes 9224 | tf_op jit(solution)/shard_map/ppermute | solution.py:30
  92.5 7.1 %collective-permute-start.22 = (f32[3,256]{1,0:T(4,128)S(1)}, f32[3,256]{1,0:T(4,128)S(1)}, u32[]{:S(2)}, u32[]{:S(2)}) collective-permute-start(f32[3,256]{1,0:T(4,128)S(1)} %get-tuple-element.119), channel_id=1, source_target_pairs={{3,0},{4,1},{5,2},{6,3},{7,4},{8,5},{9,6},{10,7},{11,8},{12,9},{13... | collective-permute-start | bytes 9224 | tf_op jit(solution)/shard_map/ppermute | solution.py:30
  93.8 8.3 %collective-permute-start.23 = (f32[3,256]{1,0:T(4,128)S(1)}, f32[3,256]{1,0:T(4,128)S(1)}, u32[]{:S(2)}, u32[]{:S(2)}) collective-permute-start(f32[3,256]{1,0:T(4,128)S(1)} %get-tuple-element.120), channel_id=1, source_target_pairs={{4,0},{5,1},{6,2},{7,3},{8,4},{9,5},{10,6},{11,7},{12,8},{13,9},{1... | collective-permute-start | bytes 9224 | tf_op jit(solution)/shard_map/ppermute | solution.py:30
  111.2 8.2 %collective-permute-start.24 = (f32[3,256]{1,0:T(4,128)S(1)}, f32[3,256]{1,0:T(4,128)S(1)}, u32[]{:S(2)}, u32[]{:S(2)}) collective-permute-start(f32[3,256]{1,0:T(4,128)S(1)} %get-tuple-element.124), channel_id=1, source_target_pairs={{1,0},{2,1},{3,2},{4,3},{5,4},{6,5},{7,6},{8,7},{9,8},{10,9},{11,1... | collective-permute-start | bytes 9224 | tf_op jit(solution)/shard_map/ppermute | solution.py:30
  112.5 11.9 %collective-permute-start.25 = (f32[3,256]{1,0:T(4,128)S(1)}, f32[3,256]{1,0:T(4,128)S(1)}, u32[]{:S(2)}, u32[]{:S(2)}) collective-permute-start(f32[3,256]{1,0:T(4,128)S(1)} %get-tuple-element.125), channel_id=1, source_target_pairs={{2,0},{3,1},{4,2},{5,3},{6,4},{7,5},{8,6},{9,7},{10,8},{11,9},{12,... | collective-permute-start | bytes 9224 | tf_op jit(solution)/shard_map/ppermute | solution.py:30
  113.8 16.8 %collective-permute-start.26 = (f32[3,256]{1,0:T(4,128)S(1)}, f32[3,256]{1,0:T(4,128)S(1)}, u32[]{:S(2)}, u32[]{:S(2)}) collective-permute-start(f32[3,256]{1,0:T(4,128)S(1)} %get-tuple-element.126), channel_id=1, source_target_pairs={{3,0},{4,1},{5,2},{6,3},{7,4},{8,5},{9,6},{10,7},{11,8},{12,9},{13... | collective-permute-start | bytes 9224 | tf_op jit(solution)/shard_map/ppermute | solution.py:30
  115.1 25.9 %collective-permute-start.27 = (f32[3,256]{1,0:T(4,128)S(1)}, f32[3,256]{1,0:T(4,128)S(1)}, u32[]{:S(2)}, u32[]{:S(2)}) collective-permute-start(f32[3,256]{1,0:T(4,128)S(1)} %get-tuple-element.127), channel_id=1, source_target_pairs={{4,0},{5,1},{6,2},{7,3},{8,4},{9,5},{10,6},{11,7},{12,8},{13,9},{1... | collective-permute-start | bytes 9224 | tf_op jit(solution)/shard_map/ppermute | solution.py:30
  116.4 24.6 %collective-permute-start.28 = (f32[3,256]{1,0:T(4,128)S(1)}, f32[3,256]{1,0:T(4,128)S(1)}, u32[]{:S(2)}, u32[]{:S(2)}) collective-permute-start(f32[3,256]{1,0:T(4,128)S(1)} %get-tuple-element.128), channel_id=1, source_target_pairs={{0,1},{1,2},{2,3},{3,4},{4,5},{5,6},{6,7},{7,8},{8,9},{9,10},{10,1... | collective-permute-start | bytes 9224 | tf_op jit(solution)/shard_map/ppermute | solution.py:30
  119.4 21.6 %collective-permute-start.29 = (f32[3,256]{1,0:T(4,128)S(1)}, f32[3,256]{1,0:T(4,128)S(1)}, u32[]{:S(2)}, u32[]{:S(2)}) collective-permute-start(f32[3,256]{1,0:T(4,128)S(1)} %get-tuple-element.129), channel_id=1, source_target_pairs={{0,2},{1,3},{2,4},{3,5},{4,6},{5,7},{6,8},{7,9},{8,10},{9,11},{10,... | collective-permute-start | bytes 9224 | tf_op jit(solution)/shard_map/ppermute | solution.py:30
  124.3 16.7 %collective-permute-start.30 = (f32[3,256]{1,0:T(4,128)S(1)}, f32[3,256]{1,0:T(4,128)S(1)}, u32[]{:S(2)}, u32[]{:S(2)}) collective-permute-start(f32[3,256]{1,0:T(4,128)S(1)} %get-tuple-element.130), channel_id=1, source_target_pairs={{0,3},{1,4},{2,5},{3,6},{4,7},{5,8},{6,9},{7,10},{8,11},{9,12},{10... | collective-permute-start | bytes 9224 | tf_op jit(solution)/shard_map/ppermute | solution.py:30
  130.6 10.4 %collective-permute-start.31 = (f32[3,256]{1,0:T(4,128)S(1)}, f32[3,256]{1,0:T(4,128)S(1)}, u32[]{:S(2)}, u32[]{:S(2)}) collective-permute-start(f32[3,256]{1,0:T(4,128)S(1)} %get-tuple-element.131), channel_id=1, source_target_pairs={{0,4},{1,5},{2,6},{3,7},{4,8},{5,9},{6,10},{7,11},{8,12},{9,13},{1... | collective-permute-start | bytes 9224 | tf_op jit(solution)/shard_map/ppermute | solution.py:30
  142.6 16.9 %collective-permute-start.32 = (f32[3,256]{1,0:T(4,128)S(1)}, f32[3,256]{1,0:T(4,128)S(1)}, u32[]{:S(2)}, u32[]{:S(2)}) collective-permute-start(f32[3,256]{1,0:T(4,128)S(1)} %get-tuple-element.135), channel_id=1, source_target_pairs={{0,1},{1,2},{2,3},{3,4},{4,5},{5,6},{6,7},{7,8},{8,9},{9,10},{10,1... | collective-permute-start | bytes 9224 | tf_op jit(solution)/shard_map/ppermute | solution.py:30
  143.9 16.9 %collective-permute-start.33 = (f32[3,256]{1,0:T(4,128)S(1)}, f32[3,256]{1,0:T(4,128)S(1)}, u32[]{:S(2)}, u32[]{:S(2)}) collective-permute-start(f32[3,256]{1,0:T(4,128)S(1)} %get-tuple-element.136), channel_id=1, source_target_pairs={{0,2},{1,3},{2,4},{3,5},{4,6},{5,7},{6,8},{7,9},{8,10},{9,11},{10,... | collective-permute-start | bytes 9224 | tf_op jit(solution)/shard_map/ppermute | solution.py:30
  148.8 13.3 %collective-permute-start.34 = (f32[3,256]{1,0:T(4,128)S(1)}, f32[3,256]{1,0:T(4,128)S(1)}, u32[]{:S(2)}, u32[]{:S(2)}) collective-permute-start(f32[3,256]{1,0:T(4,128)S(1)} %get-tuple-element.137), channel_id=1, source_target_pairs={{0,3},{1,4},{2,5},{3,6},{4,7},{5,8},{6,9},{7,10},{8,11},{9,12},{10... | collective-permute-start | bytes 9224 | tf_op jit(solution)/shard_map/ppermute | solution.py:30
  154.5 22.7 %collective-permute-start.35 = (f32[3,256]{1,0:T(4,128)S(1)}, f32[3,256]{1,0:T(4,128)S(1)}, u32[]{:S(2)}, u32[]{:S(2)}) collective-permute-start(f32[3,256]{1,0:T(4,128)S(1)} %get-tuple-element.138), channel_id=1, source_target_pairs={{0,4},{1,5},{2,6},{3,7},{4,8},{5,9},{6,10},{7,11},{8,12},{9,13},{1... | collective-permute-start | bytes 9224 | tf_op jit(solution)/shard_map/ppermute | solution.py:30
  158.1 19.1 %collective-permute-start.36 = (f32[3,256]{1,0:T(4,128)S(1)}, f32[3,256]{1,0:T(4,128)S(1)}, u32[]{:S(2)}, u32[]{:S(2)}) collective-permute-start(f32[3,256]{1,0:T(4,128)S(1)} %get-tuple-element.139), channel_id=1, source_target_pairs={{1,0},{2,1},{3,2},{4,3},{5,4},{6,5},{7,6},{8,7},{9,8},{10,9},{11,1... | collective-permute-start | bytes 9224 | tf_op jit(solution)/shard_map/ppermute | solution.py:30
  159.5 17.8 %collective-permute-start.37 = (f32[3,256]{1,0:T(4,128)S(1)}, f32[3,256]{1,0:T(4,128)S(1)}, u32[]{:S(2)}, u32[]{:S(2)}) collective-permute-start(f32[3,256]{1,0:T(4,128)S(1)} %get-tuple-element.140), channel_id=1, source_target_pairs={{2,0},{3,1},{4,2},{5,3},{6,4},{7,5},{8,6},{9,7},{10,8},{11,9},{12,... | collective-permute-start | bytes 9224 | tf_op jit(solution)/shard_map/ppermute | solution.py:30
  160.8 16.5 %collective-permute-start.38 = (f32[3,256]{1,0:T(4,128)S(1)}, f32[3,256]{1,0:T(4,128)S(1)}, u32[]{:S(2)}, u32[]{:S(2)}) collective-permute-start(f32[3,256]{1,0:T(4,128)S(1)} %get-tuple-element.141), channel_id=1, source_target_pairs={{3,0},{4,1},{5,2},{6,3},{7,4},{8,5},{9,6},{10,7},{11,8},{12,9},{13... | collective-permute-start | bytes 9224 | tf_op jit(solution)/shard_map/ppermute | solution.py:30
  162.1 15.2 %collective-permute-start.39 = (f32[3,256]{1,0:T(4,128)S(1)}, f32[3,256]{1,0:T(4,128)S(1)}, u32[]{:S(2)}, u32[]{:S(2)}) collective-permute-start(f32[3,256]{1,0:T(4,128)S(1)} %get-tuple-element.142), channel_id=1, source_target_pairs={{4,0},{5,1},{6,2},{7,3},{8,4},{9,5},{10,6},{11,7},{12,8},{13,9},{1... | collective-permute-start | bytes 9224 | tf_op jit(solution)/shard_map/ppermute | solution.py:30
  182.4 19.4 %collective-permute-start.40 = (f32[1,128]{1,0:T(1,128)S(1)}, f32[1,128]{1,0:T(1,128)S(1)}, u32[]{:S(2)}, u32[]{:S(2)}) collective-permute-start(f32[1,128]{1,0:T(1,128)S(1)} %get-tuple-element.149), channel_id=1, source_target_pairs={{0,1},{1,2},{2,3},{3,4},{4,5},{5,6},{6,7},{7,8},{8,9},{9,10},{10,1... | collective-permute-start | bytes 1544 | tf_op jit(solution)/shard_map/ppermute | solution.py:30
  185.5 17.7 %collective-permute-start.41 = (f32[1,128]{1,0:T(1,128)S(1)}, f32[1,128]{1,0:T(1,128)S(1)}, u32[]{:S(2)}, u32[]{:S(2)}) collective-permute-start(f32[1,128]{1,0:T(1,128)S(1)} %get-tuple-element.150), channel_id=1, source_target_pairs={{0,2},{1,3},{2,4},{3,5},{4,6},{5,7},{6,8},{7,9},{8,10},{9,11},{10,... | collective-permute-start | bytes 1544 | tf_op jit(solution)/shard_map/ppermute | solution.py:30
  190.4 14.1 %collective-permute-start.42 = (f32[1,128]{1,0:T(1,128)S(1)}, f32[1,128]{1,0:T(1,128)S(1)}, u32[]{:S(2)}, u32[]{:S(2)}) collective-permute-start(f32[1,128]{1,0:T(1,128)S(1)} %get-tuple-element.151), channel_id=1, source_target_pairs={{0,3},{1,4},{2,5},{3,6},{4,7},{5,8},{6,9},{7,10},{8,11},{9,12},{10... | collective-permute-start | bytes 1544 | tf_op jit(solution)/shard_map/ppermute | solution.py:30
  195.7 10.1 %collective-permute-start.43 = (f32[1,128]{1,0:T(1,128)S(1)}, f32[1,128]{1,0:T(1,128)S(1)}, u32[]{:S(2)}, u32[]{:S(2)}) collective-permute-start(f32[1,128]{1,0:T(1,128)S(1)} %get-tuple-element.152), channel_id=1, source_target_pairs={{0,4},{1,5},{2,6},{3,7},{4,8},{5,9},{6,10},{7,11},{8,12},{9,13},{1... | collective-permute-start | bytes 1544 | tf_op jit(solution)/shard_map/ppermute | solution.py:30
  200.5 5.2 %collective-permute-start.44 = (f32[1,128]{1,0:T(1,128)S(1)}, f32[1,128]{1,0:T(1,128)S(1)}, u32[]{:S(2)}, u32[]{:S(2)}) collective-permute-start(f32[1,128]{1,0:T(1,128)S(1)} %get-tuple-element.153), channel_id=1, source_target_pairs={{1,0},{2,1},{3,2},{4,3},{5,4},{6,5},{7,6},{8,7},{9,8},{10,9},{11,1... | collective-permute-start | bytes 1544 | tf_op jit(solution)/shard_map/ppermute | solution.py:30
  201.9 6.1 %collective-permute-start.45 = (f32[1,128]{1,0:T(1,128)S(1)}, f32[1,128]{1,0:T(1,128)S(1)}, u32[]{:S(2)}, u32[]{:S(2)}) collective-permute-start(f32[1,128]{1,0:T(1,128)S(1)} %get-tuple-element.154), channel_id=1, source_target_pairs={{2,0},{3,1},{4,2},{5,3},{6,4},{7,5},{8,6},{9,7},{10,8},{11,9},{12,... | collective-permute-start | bytes 1544 | tf_op jit(solution)/shard_map/ppermute | solution.py:30
  203.2 6.6 %collective-permute-start.46 = (f32[1,128]{1,0:T(1,128)S(1)}, f32[1,128]{1,0:T(1,128)S(1)}, u32[]{:S(2)}, u32[]{:S(2)}) collective-permute-start(f32[1,128]{1,0:T(1,128)S(1)} %get-tuple-element.155), channel_id=1, source_target_pairs={{3,0},{4,1},{5,2},{6,3},{7,4},{8,5},{9,6},{10,7},{11,8},{12,9},{13... | collective-permute-start | bytes 1544 | tf_op jit(solution)/shard_map/ppermute | solution.py:30
  204.5 8.8 %collective-permute-start.47 = (f32[1,128]{1,0:T(1,128)S(1)}, f32[1,128]{1,0:T(1,128)S(1)}, u32[]{:S(2)}, u32[]{:S(2)}) collective-permute-start(f32[1,128]{1,0:T(1,128)S(1)} %get-tuple-element.156), channel_id=1, source_target_pairs={{4,0},{5,1},{6,2},{7,3},{8,4},{9,5},{10,6},{11,7},{12,8},{13,9},{1... | collective-permute-start | bytes 1544 | tf_op jit(solution)/shard_map/ppermute | solution.py:30
  (15 other events, 116.8 us)

commit v2 on v1

--- a/solution.py
+++ b/solution.py
@@ -22,12 +22,6 @@
 bf16 = jnp.bfloat16
 i16 = jnp.int16
 i32 = jnp.int32
-
-
-def from_behind(block, axis, distance):
-    devices = range(lax.axis_size(axis))
-    route = [(i - distance, i) for i in devices if i - distance in devices]
-    return lax.ppermute(block, axis, route)
 
 
 def neighbour_offsets():
@@ -153,16 +147,48 @@
             out_ref[part * OWN + row : part * OWN + row + 1, :] = block[part : part + 1]
 
 
-def export_rows(table, parts, at_row, at_column, out_refs):
-    for slot, out_ref in enumerate(out_refs):
+def export_rows(table, parts, at_row, at_column, out_ref):
+    slots = 2 * REACH
+    for slot in range(slots):
         found = gather_rows(
             table, OWN, parts, at_row[slot : slot + 1], at_column[slot : slot + 1]
         )
         for part in range(parts):
-            out_ref[part : part + 1, :] = found[part]
-
-
-def first_export(adjoint_ref, primal_ref, list_ref, tab_a, tab_p, row_ref, column_ref, *out_refs):
+            out_ref[part * slots + slot : part * slots + slot + 1, :] = found[part]
+
+
+def fetch_blocks(place_ref, sign, all_ref, land_ref, sems):
+    place, count = place_ref[0], all_ref.shape[0]
+    sources = [place - sign * offset for offset in neighbour_offsets()]
+    copies = [
+        pltpu.make_async_copy(
+            all_ref.at[jnp.clip(source, 0, count - 1)], land_ref.at[slot], sems.at[slot]
+        )
+        for slot, source in enumerate(sources)
+    ]
+    for copy in copies:
+        copy.start()
+    for copy in copies:
+        copy.wait()
+    for slot, source in enumerate(sources):
+
+        @pl.when((source < 0) | (source >= count))
+        def _():
+            land_ref[slot] = jnp.zeros(land_ref.shape[1:], land_ref.dtype)
+
+
+def landed(land_ref, first=0):
+    slots = 2 * REACH
+    return [
+        [
+            land_ref[slot, (first + part) * slots + slot : (first + part) * slots + slot + 1, :]
+            for part in range(3)
+        ]
+        for slot in range(slots)
+    ]
+
+
+def first_export(adjoint_ref, primal_ref, list_ref, tab_a, tab_p, row_ref, column_ref, out_ref):
     owned = adjoint_ref.shape[1]
     fill_table(adjoint_ref, tab_a)
     fill_table(primal_ref, tab_p)
@@ -172,7 +198,7 @@
     column_ref[...] = node & 255
     table = jnp.concatenate([tab_a[...], tab_p[...]], 0)
     table = jnp.concatenate(pieces(table), 1)
-    export_rows(table, 6, node >> 8, node & 255, out_refs)
+    export_rows(table, 6, node >> 8, node & 255, out_ref)
 
 
 def setup(
@@ -264,15 +290,13 @@
 
 
 def edge_gather(
-    ghost_refs, first, hang_ref, row_ref, column_ref, master_row, master_column, weight_ref,
+    ghosts, hang_ref, row_ref, column_ref, master_row, master_column, weight_ref,
     edge_ref, table_ref, out_ref,
 ):
     edge_ref[...] = jnp.zeros_like(edge_ref)
-    for slot, ghost_ref in enumerate(ghost_refs):
+    for slot, ghost in enumerate(ghosts):
         for part in range(3):
-            edge_ref[part * EDGE + slot : part * EDGE + slot + 1, :] = ghost_ref[
-                first + part : first + part + 1, :
-            ]
+            edge_ref[part * EDGE + slot : part * EDGE + slot + 1, :] = ghost[part]
     found = sum_masters(
         jnp.concatenate(pieces(edge_ref[...]), 1),
         EDGE,
@@ -281,7 +305,7 @@
         master_row[...],
         master_column[...],
     )
-    slots = len(ghost_refs)
+    slots = len(ghosts)
     for part in range(3):
         edge_ref[part * EDGE + slots : part * EDGE + slots + 1, : WIDE // 2] = (
             found[part] + hang_ref[part : part + 1, :]
@@ -290,17 +314,14 @@
     gather_cells(table_ref, EDGE, 3, row_ref, column_ref, out_ref)
 
 
-def edge_product(first, *refs):
-    ghost_refs = refs[: 2 * REACH]
-    (
-        cells_ref, hang_ref, row_ref, column_ref, master_row, master_column, weight_ref,
-        modulus_ref, stiffness_ref,
-    ) = refs[2 * REACH : 2 * REACH + 9]
-    rest = refs[2 * REACH + 9 :]
-    out_refs = rest[: 2 * REACH]
-    image_ref, held_ref, edge_ref, table_ref, more_ref, sum_ref = rest[2 * REACH :]
+def edge_product(
+    place_ref, all_ref, cells_ref, hang_ref, row_ref, column_ref, master_row, master_column,
+    weight_ref, modulus_ref, stiffness_ref, out_ref, image_ref, held_ref, edge_ref, table_ref,
+    more_ref, sum_ref, land_ref, sems,
+):
+    fetch_blocks(place_ref, 1, all_ref, land_ref, sems)
     edge_gather(
-        ghost_refs, first, hang_ref, row_ref, column_ref, master_row, master_column, weight_ref,
+        landed(land_ref), hang_ref, row_ref, column_ref, master_row, master_column, weight_ref,
         edge_ref, table_ref, more_ref,
     )
     image_ref[...] = modulus_ref[...] * lax.dot_general(
@@ -321,9 +342,10 @@
     edge_ref[...] += spread_hanging(
         held, weight_ref[...], EDGE, master_row[...], master_column[...]
     )
-    for slot, out_ref in enumerate(out_refs):
-        for part in range(3):
-            out_ref[part : part + 1, :] = edge_ref[part * EDGE + slot : part * EDGE + slot + 1, :]
+    for part in range(3):
+        out_ref[part * slots : (part + 1) * slots, :] = edge_ref[
+            part * EDGE : part * EDGE + slots, :
+        ]
 
 
 def own_sums(
@@ -337,25 +359,24 @@
     out_ref[...] = tab_ref[...] + relaxation * inverse_ref[...] * (source_ref[...] - applied)
 
 
-def update(last, *refs):
-    back_refs = refs[: 2 * REACH]
-    row_ref, column_ref, partial_ref, inverse_ref = refs[2 * REACH : 2 * REACH + 4]
-    rest = refs[2 * REACH + 4 :]
-    out_refs = rest[: 2 * REACH]
-    tab_ref = rest[2 * REACH]
-    values = []
-    for part in range(3):
-        block = jnp.concatenate([ref[part : part + 1, :] for ref in back_refs], 0)
-        values.append(split32(block))
+def update(
+    last, place_ref, all_ref, row_ref, column_ref, partial_ref, inverse_ref, out_ref, tab_ref, *rest
+):
+    land_ref, sems = rest[-2:]
+    fetch_blocks(place_ref, -1, all_ref, land_ref, sems)
+    back = landed(land_ref)
+    values = [
+        split32(jnp.concatenate([block[part] for block in back], 0)) for part in range(3)
+    ]
     returned = add_pieces(
         scatter_block(list(zip(*values)), OWN, row_ref[...], column_ref[...])
     )
     fresh = partial_ref[...] - relaxation * inverse_ref[...] * returned
     tab_ref[...] = fresh
     table = jnp.concatenate(pieces(fresh), 1)
-    export_rows(table, 3, row_ref[...], column_ref[...], out_refs)
+    export_rows(table, 3, row_ref[...], column_ref[...], out_ref)
     if last:
-        final_ref = rest[2 * REACH + 1]
+        final_ref = rest[0]
         for row in range(final_ref.shape[1] // WIDE):
             for part in range(3):
                 final_ref[part : part + 1, row * WIDE : (row + 1) * WIDE] = tab_ref[
@@ -363,14 +384,13 @@
                 ]
 
 
-def primal_product(first, *refs):
-    ghost_refs = refs[: 2 * REACH]
-    (
-        cells_ref, hang_ref, row_ref, column_ref, master_row, master_column, weight_ref,
-        modulus_ref, stiffness_ref, out_ref, edge_ref, table_ref, more_ref,
-    ) = refs[2 * REACH :]
+def primal_product(
+    place_ref, all_ref, cells_ref, hang_ref, row_ref, column_ref, master_row, master_column,
+    weight_ref, modulus_ref, stiffness_ref, out_ref, edge_ref, table_ref, more_ref, land_ref, sems,
+):
+    fetch_blocks(place_ref, 1, all_ref, land_ref, sems)
     edge_gather(
-        ghost_refs, first, hang_ref, row_ref, column_ref, master_row, master_column, weight_ref,
+        landed(land_ref, 3), hang_ref, row_ref, column_ref, master_row, master_column, weight_ref,
         edge_ref, table_ref, more_ref,
     )
     out_ref[...] = modulus_ref[...] * jnp.dot(
@@ -381,17 +401,14 @@
     )
 
 
-def fluxes(*refs):
-    ghost_refs = refs[: 2 * REACH]
-    (
-        cells_ref, hang_ref, row_ref, column_ref, master_row, master_column, weight_ref,
-        ku_ref, load_ref, sub_cell, sub_face,
-    ) = refs[2 * REACH : 2 * REACH + 11]
-    rest = refs[2 * REACH + 11 :]
-    out_refs = rest[: 2 * REACH]
-    term_ref, edge_ref, table_ref, more_ref = rest[2 * REACH :]
+def fluxes(
+    place_ref, all_ref, cells_ref, hang_ref, row_ref, column_ref, master_row, master_column,
+    weight_ref, ku_ref, load_ref, sub_cell, sub_face, out_ref, term_ref, edge_ref, table_ref,
+    more_ref, land_ref, sems,
+):
+    fetch_blocks(place_ref, 1, all_ref, land_ref, sems)
     edge_gather(
-        ghost_refs, 0, hang_ref, row_ref, column_ref, master_row, master_column, weight_ref,
+        landed(land_ref), hang_ref, row_ref, column_ref, master_row, master_column, weight_ref,
         edge_ref, table_ref, more_ref,
     )
     cells = cells_ref[...] + more_ref[...]
@@ -405,17 +422,16 @@
         member, ku * cells, precision=lax.Precision.HIGHEST, preferred_element_type=f32
     )
     table = jnp.concatenate(pieces(flux), 1)
-    for slot, out_ref in enumerate(out_refs):
-        out_ref[...] = gather_rows(
+    for slot in range(2 * REACH):
+        out_ref[slot : slot + 1, :] = gather_rows(
             table, 8, 1, sub_face[slot : slot + 1, :], sub_cell[slot : slot + 1, :]
         )[0]
 
 
-def collect(*refs):
-    got_refs = refs[: 2 * REACH]
-    owner_ref, term_ref, out_ref = refs[2 * REACH :]
+def collect(place_ref, all_ref, owner_ref, term_ref, out_ref, land_ref, sems):
+    fetch_blocks(place_ref, 1, all_ref, land_ref, sems)
     count = term_ref.shape[1]
-    got = jnp.concatenate([ref[...] for ref in got_refs], 1)
+    got = jnp.concatenate([land_ref[slot, slot : slot + 1, :] for slot in range(2 * REACH)], 1)
     hot = jnp.concatenate(
         [one_hot(owner_ref[slot : slot + 1, :], count) for slot in range(2 * REACH)], 1
     )
@@ -428,13 +444,30 @@
     out_ref[...] = (jnp.abs(term_ref[...]) + jnp.abs(face_term)) / scale_down
 
 
-def call(kernel, outs, scratch=()):
-    return pl.pallas_call(
-        kernel,
-        out_shape=[jax.ShapeDtypeStruct(shape, kind) for shape, kind in outs],
-        scratch_shapes=[pltpu.VMEM(shape, kind) for shape, kind in scratch],
-        compiler_params=pltpu.CompilerParams(vmem_limit_bytes=40 * 1024 * 1024),
-    )
+def call(kernel, outs, scratch=(), gathered=None):
+    specs = {}
+    scratch = [pltpu.VMEM(shape, kind) for shape, kind in scratch]
+    if gathered is not None:
+        scratch += [
+            pltpu.VMEM((2 * REACH,) + gathered, f32),
+            pltpu.SemaphoreType.DMA((2 * REACH,)),
+        ]
+
+    def run(*args):
+        if gathered is not None:
+            specs["in_specs"] = [
+                pl.BlockSpec(memory_space=pltpu.SMEM),
+                pl.BlockSpec(memory_space=pl.ANY),
+            ] + [pl.BlockSpec(memory_space=pltpu.VMEM)] * (len(args) - 2)
+        return pl.pallas_call(
+            kernel,
+            out_shape=[jax.ShapeDtypeStruct(shape, kind) for shape, kind in outs],
+            scratch_shapes=scratch,
+            compiler_params=pltpu.CompilerParams(vmem_limit_bytes=40 * 1024 * 1024),
+            **specs,
+        )(*args)
+
+    return run
 
 
 def local(
@@ -454,29 +487,31 @@
     subface_face,
     subface_owner,
 ):
-    offsets = neighbour_offsets()
-    slots = len(offsets)
+    slots = 2 * REACH
     local_values, cell_count = cell_load.shape
     nodes = connectivity.shape[0]
     moduli = modulus.reshape(1, cell_count)
     table = ((3 * OWN, WIDE), f32)
     index = ((nodes, cell_count), i32)
-    block = ((3, WIDE), f32)
     cells_shape = ((local_values, cell_count), f32)
     hang_shape = ((3, hang_node.shape[0]), f32)
     master_shape = ((8, WIDE), i32)
     own_table = ((3 * OWN, 2 * WIDE), bf16)
     edge = [((3 * EDGE, WIDE), f32), ((3 * EDGE, 2 * WIDE), bf16), cells_shape]
 
-    def send(blocks, sign):
-        return [from_behind(b, "dom", sign * o) for b, o in zip(blocks, offsets)]
-
-    tab, tab_primal, list_row, list_column, *blocks = call(
+    def share(blocks):
+        return lax.all_gather(blocks, "dom")
+
+    place = lax.axis_index("dom").reshape(1).astype(i32)
+    block = ((3 * slots, WIDE), f32)
+    landing = block[0]
+    tab, tab_primal, list_row, list_column, blocks = call(
         first_export,
         [table, table, (ghost_lists.shape, i32), (ghost_lists.shape, i32)]
-        + [((6, WIDE), f32)] * slots,
+        + [((6 * slots, WIDE), f32)],
     )(adjoint_start, primal_field, ghost_lists)
-    ghosts = first_ghosts = send(blocks, 1)
+    ghosts = first_ghosts = share(blocks)
+    first_landing = (6 * slots, WIDE)
     (
         row_own, column_own, row_edge, column_edge, master_own, master_edge, master_column,
         weight, source, inverse,
@@ -498,39 +533,41 @@
     ku = None
     for sweep in range(SWEEPS):
         cells, hang = gather_own(tab)
-        *blocks, image, held = call(
-            functools.partial(edge_product, 0),
-            [block] * slots + [cells_shape, hang_shape],
+        blocks, image, held = call(
+            edge_product,
+            [block, cells_shape, hang_shape],
             edge + [((6 * EDGE, WIDE), f32)],
-        )(*ghosts, cells, hang, *on_edge, moduli, stiffness)
-        returned = send(blocks, -1)
+            first_landing if sweep == 0 else landing,
+        )(place, ghosts, cells, hang, *on_edge, moduli, stiffness)
+        returned = share(blocks)
         (partial,) = call(own_sums, [table], [((6 * OWN, WIDE), f32)])(
             image, held, row_own, column_own, master_own, master_column, weight, tab, source,
             inverse,
         )
         if sweep == 0:
             cells, hang = gather_own(tab_primal)
-            (ku,) = call(functools.partial(primal_product, 3), [cells_shape], edge)(
-                *first_ghosts, cells, hang, *on_edge, moduli, stiffness
+            (ku,) = call(primal_product, [cells_shape], edge, first_landing)(
+                place, first_ghosts, cells, hang, *on_edge, moduli, stiffness
             )
         last = sweep == SWEEPS - 1
-        *blocks, tab = call(
+        blocks, tab, *final = call(
             functools.partial(update, last),
-            [block] * slots + [table] + ([(adjoint_start.shape, f32)] if last else []),
-        )(*returned, list_row, list_column, partial, inverse)
-        if last:
-            adjoint = tab
-            tab = blocks.pop()
-        ghosts = send(blocks, 1)
+            [block, table] + ([(adjoint_start.shape, f32)] if last else []),
+            gathered=landing,
+        )(place, returned, list_row, list_column, partial, inverse)
+        ghosts = share(blocks)
     cells, hang = gather_own(tab)
-    *sent, term = call(
+    sent, term = call(
         fluxes,
-        [((1, subface_cell.shape[1]), f32)] * slots + [((1, cell_count), f32)],
+        [(subface_cell.shape, f32), ((1, cell_count), f32)],
         edge,
-    )(*ghosts, cells, hang, *on_edge, ku, cell_load, subface_cell, subface_face)
-    received = send(sent, 1)
-    (indicator,) = call(collect, [((1, cell_count), f32)])(*received, subface_owner, term)
-    return (adjoint, indicator.reshape(cell_count))
+        landing,
+    )(place, ghosts, cells, hang, *on_edge, ku, cell_load, subface_cell, subface_face)
+    received = share(sent)
+    (indicator,) = call(collect, [((1, cell_count), f32)], gathered=subface_cell.shape)(
+        place, received, subface_owner, term
+    )
+    return (final[0], indicator.reshape(cell_count))
 
 
 def solution(mesh):

time: 218 us -> 330 us (1.51); the launches traced: 214 us -> 329 us
  blocking collectives: 0 us -> 198 us
  starting transfers between devices: 137 us -> 0.04 us
  waiting for transfers between devices: 10.2 us -> 41.8 us
  between operations: 1.62 us -> 14.2 us
  local copies, waits for them, and re-layouts: 4.04 us -> 10.2 us
  Pallas kernels: 61.7 us -> 65.3 us
    all_gather x0 -> x5, blocking collectives: none -> 198 us  [share(): return lax.all_gather(blocks, 'dom')]
    ppermute x48 -> x0, starting transfers between devices: 137 us -> none  [from_behind(): return lax.ppermute(block, axis, route)]
    all_gather x0 -> x1, waiting for transfers between devices: none -> 41.8 us  [share(): return lax.all_gather(blocks, 'dom')]
    ppermute x48 -> x0, waiting for transfers between devices: 10.2 us -> none  [from_behind(): return lax.ppermute(block, axis, route)]
    unnamed x30 -> x38, local copies, waits for them, and re-layouts: 4.04 us -> 10.2 us
    pallas_call x15, Pallas kernels: 61.7 us -> 65.3 us  [run(): pl.pallas_call(kernel, out_shape=[jax.ShapeDtypeStruct(shape, kind) for s...]
  transfers between devices with their start and end apart: 48 -> 1, of which waited for: 4 -> 1; matrix products, arithmetic and copies ran while one was open for 0% -> 0% of each run, Pallas kernels for 16% -> 4%
where the time goes in v2:
time: 330 us; the launch traced here: 329 us
  blocking collectives  198 us (60%)
  Pallas kernels  65.3 us (20%)
  waiting for transfers between devices  41.8 us (13%)
  between operations  14.2 us (4%)
  local copies, waits for them, and re-layouts  10.2 us (3%)
    all_gather x5, blocking collectives, share(): return lax.all_gather(blocks, 'dom')  198 us
    pallas_call x15, Pallas kernels, run(): pl.pallas_call(kernel, out_shape=[jax.ShapeDtypeStruct(shape, kind) for s...  65.3 us
    all_gather x1, waiting for transfers between devices, share(): return lax.all_gather(blocks, 'dom')  41.8 us
    unnamed x38, local copies, waits for them, and re-layouts  10.2 us
  transfers between devices with their start and end apart: 1, of which 1 were waited for; matrix products, arithmetic and copies ran while one was open for 0% of the time, Pallas kernels for 4%

profile of v2, /device:TPU:0, one launch (start us, length us, event | category | flops | bytes accessed | tf_op | source)
XLA Modules:
  0.0 329.5 jit_solution(8932146588811934260)
XLA Ops:
  7.2 0.0 all-gather.8.cloned.1.call-start
  7.2 0.0 copy-start.5
  7.2 0.9 copy-done.5
  8.1 0.0 copy-start.6
  8.1 0.9 copy-done.6
  9.0 0.7 copy-done.12
  9.7 1.3 shard_map.158
  11.0 0.0 all-gather.8.cloned.1.call-update
  11.0 0.0 copy-start.7
  11.0 0.9 copy-done.7
  11.9 0.9 copy-done.8
  12.8 0.8 copy-done.9
  13.7 0.7 copy-done.13
  14.4 0.7 copy-done.14
  15.1 0.7 copy-done.18
  15.7 2.7 shard_map.159
  18.4 4.4 %shard_map.169 = (f32[192,256]{1,0:T(8,128)S(1)}, f32[3,128]{1,0:T(4,128)S(1)}) custom-call(f32[96,256]{1,0:T(8,128)S(1)} %get-tuple-element.69.tab_ref, s32[64,256]{1,0:T(8,128)S(1)} %get-tuple-element.40.row_ref, s32[64,256]{1,0:T(8,128)S(1)} %get-tuple-element.41.column_ref, s32[8,256]{1,0:T(8,128)S(1)} %get-tuple-element.42.master_row, ...), custom_call_target="tpu_custom_call" | custom-call | tf_op jit(solution)/shard_map/pallas_call | solution.py:462
  22.9 4.4 %shard_map.160 = (f32[192,256]{1,0:T(8,128)S(1)}, f32[3,128]{1,0:T(4,128)S(1)}) custom-call(f32[96,256]{1,0:T(8,128)S(1)} %get-tuple-element.39.tab_ref, s32[64,256]{1,0:T(8,128)S(1)} %get-tuple-element.40.row_ref, s32[64,256]{1,0:T(8,128)S(1)} %get-tuple-element.41.column_ref, s32[8,256]{1,0:T(8,128)S(1)} %get-tuple-element.42.master_row, ...), custom_call_target="tpu_custom_call" | custom-call | tf_op jit(solution)/shard_map/pallas_call | solution.py:462
  27.3 41.8 %all-gather.8.cloned.1.call-done = f32[1536,256]{1,0:T(8,128)} async-done(((f32[48,256]{1,0:T(8,128)}), f32[1536,256]{1,0:T(8,128)}) %all-gather.8.cloned.1.call-update) | async-done | bytes 1572880 | tf_op jit(solution)/shard_map/all_gather | solution.py:503
  69.1 1.4 copy-done
  70.5 0.9 copy-done.2
  71.5 0.7 copy-done.10
  72.1 9.6 %shard_map.161 = (f32[24,256]{1,0:T(8,128)S(1)}, f32[192,256]{1,0:T(8,128)S(1)}, f32[3,128]{1,0:T(4,128)S(1)}) custom-call(s32[1]{0:T(128)} %bitcast.place_ref, f32[32,48,256]{2,1,0:T(8,128)S(1)} %bitcast.10, f32[192,256]{1,0:T(8,128)S(1)} %get-tuple-element.45.cells_ref, f32[3,128]{1,0:T(4,128)S(1)} %get-tuple-element.46.hang_ref, ...), custom_call_target="tpu_custom_call" | custom-call | tf_op jit(solution)/shard_map/pallas_call | solution.py:462
  81.8 41.6 %all-gather.1 = f32[768,256]{1,0:T(8,128)S(1)} all-gather(f32[24,256]{1,0:T(8,128)S(1)} %get-tuple-element.50), channel_id=3, replica_groups=mesh['dom'=32] {'dom'}, dimensions={0}, use_global_device_ids=true | all-gather | bytes 811008 | tf_op jit(solution)/shard_map/all_gather | solution.py:503
  123.4 4.5 %shard_map.162.partial_ref = f32[96,256]{1,0:T(8,128)S(1)} custom-call(f32[192,256]{1,0:T(8,128)S(1)} %get-tuple-element.53.image_ref, f32[3,128]{1,0:T(4,128)S(1)} %get-tuple-element.54.held_ref, s32[64,256]{1,0:T(8,128)S(1)} %get-tuple-element.40.row_ref, s32[64,256]{1,0:T(8,128)S(1)} %get-tuple-element.41.column_ref, ...), custom_call_target="tpu_custom_call" | custom-call | tf_op jit(solution)/shard_map/pallas_call | solution.py:462
  127.9 1.8 shard_map.163
  129.6 4.4 %shard_map.164 = (f32[192,256]{1,0:T(8,128)S(1)}, f32[3,128]{1,0:T(4,128)S(1)}) custom-call(f32[96,256]{1,0:T(8,128)S(1)} %get-tuple-element.58.tab_ref, s32[64,256]{1,0:T(8,128)S(1)} %get-tuple-element.40.row_ref, s32[64,256]{1,0:T(8,128)S(1)} %get-tuple-element.41.column_ref, s32[8,256]{1,0:T(8,128)S(1)} %get-tuple-element.42.master_row, ...), custom_call_target="tpu_custom_call" | custom-call | tf_op jit(solution)/shard_map/pallas_call | solution.py:462
  134.1 38.9 %all-gather.2 = f32[768,256]{1,0:T(8,128)S(1)} all-gather(f32[24,256]{1,0:T(8,128)S(1)} %get-tuple-element.57), channel_id=4, replica_groups=mesh['dom'=32] {'dom'}, dimensions={0}, use_global_device_ids=true | all-gather | bytes 811008 | tf_op jit(solution)/shard_map/all_gather | solution.py:503
  173.0 0.0 copy-done.11
  173.0 9.4 %shard_map.165 = (f32[24,256]{1,0:T(8,128)S(1)}, f32[192,256]{1,0:T(8,128)S(1)}, f32[3,128]{1,0:T(4,128)S(1)}) custom-call(s32[1]{0:T(128)} %bitcast.place_ref, f32[32,24,256]{2,1,0:T(8,128)S(1)} %bitcast.15, f32[192,256]{1,0:T(8,128)S(1)} %get-tuple-element.59.cells_ref, f32[3,128]{1,0:T(4,128)S(1)} %get-tuple-element.60.hang_ref, ...), custom_call_target="tpu_custom_call" | custom-call | tf_op jit(solution)/shard_map/pallas_call | solution.py:462
  182.4 40.1 %all-gather.3 = f32[768,256]{1,0:T(8,128)S(1)} all-gather(f32[24,256]{1,0:T(8,128)S(1)} %get-tuple-element.61), channel_id=5, replica_groups=mesh['dom'=32] {'dom'}, dimensions={0}, use_global_device_ids=true | all-gather | bytes 811008 | tf_op jit(solution)/shard_map/all_gather | solution.py:503
  222.4 4.5 %shard_map.166.partial_ref = f32[96,256]{1,0:T(8,128)S(1)} custom-call(f32[192,256]{1,0:T(8,128)S(1)} %get-tuple-element.62.image_ref, f32[3,128]{1,0:T(4,128)S(1)} %get-tuple-element.63.held_ref, s32[64,256]{1,0:T(8,128)S(1)} %get-tuple-element.40.row_ref, s32[64,256]{1,0:T(8,128)S(1)} %get-tuple-element.41.column_ref, ...), custom_call_target="tpu_custom_call" | custom-call | tf_op jit(solution)/shard_map/pallas_call | solution.py:462
  226.9 1.8 shard_map.167
  228.7 4.4 %shard_map.168 = (f32[192,256]{1,0:T(8,128)S(1)}, f32[3,128]{1,0:T(4,128)S(1)}) custom-call(f32[96,256]{1,0:T(8,128)S(1)} %get-tuple-element.66.tab_ref, s32[64,256]{1,0:T(8,128)S(1)} %get-tuple-element.40.row_ref, s32[64,256]{1,0:T(8,128)S(1)} %get-tuple-element.41.column_ref, s32[8,256]{1,0:T(8,128)S(1)} %get-tuple-element.42.master_row, ...), custom_call_target="tpu_custom_call" | custom-call | tf_op jit(solution)/shard_map/pallas_call | solution.py:462
  233.2 0.0 copy-start.4
  233.2 0.0 copy-start.15
  233.2 0.0 copy-start.16
  233.2 39.0 %all-gather.4 = f32[768,256]{1,0:T(8,128)S(1)} all-gather(f32[24,256]{1,0:T(8,128)S(1)} %get-tuple-element.65), channel_id=6, replica_groups=mesh['dom'=32] {'dom'}, dimensions={0}, use_global_device_ids=true | all-gather | bytes 811008 | tf_op jit(solution)/shard_map/all_gather | solution.py:503
  272.2 0.0 copy-done.1
  272.2 0.0 copy-done.3
  272.2 5.6 %shard_map.170.ku_ref = f32[192,256]{1,0:T(8,128)S(1)} custom-call(s32[1]{0:T(128)} %bitcast.place_ref, f32[32,48,256]{2,1,0:T(8,128)S(1)} %bitcast.11, f32[192,256]{1,0:T(8,128)S(1)} %get-tuple-element.70.cells_ref, f32[3,128]{1,0:T(4,128)S(1)} %get-tuple-element.71.hang_ref, s32[64,256]{1,0:T(8,128)S(1)} %get-tuple-element.47.row_ref, ...), custom_call_target="tpu_custom_call" | custom-call | tf_op jit(solution)/shard_map/pallas_call | solution.py:462
  277.8 0.0 copy-done.4
  277.8 0.0 copy-done.15
  277.8 0.0 copy-done.16
  277.8 5.5 %shard_map.171 = (f32[8,128]{1,0:T(8,128)S(1)}, f32[1,256]{1,0:T(1,128)S(1)}) custom-call(s32[1]{0:T(128)} %bitcast.place_ref, f32[32,24,256]{2,1,0:T(8,128)S(1)} %bitcast.14, f32[192,256]{1,0:T(8,128)S(1)} %get-tuple-element.67.cells_ref, f32[3,128]{1,0:T(4,128)S(1)} %get-tuple-element.68.hang_ref, s32[64,256]{1,0:T(8,128)S(1)} %get-tuple-element.47.row_ref, ...), custom_call_target="tpu_custom_call" | custom-call | tf_op jit(solution)/shard_map/pallas_call | solution.py:462
  283.3 38.3 %all-gather.5 = f32[256,128]{1,0:T(8,128)S(1)} all-gather(f32[8,128]{1,0:T(8,128)S(1)} %get-tuple-element.72), channel_id=7, replica_groups=mesh['dom'=32] {'dom'}, dimensions={0}, use_global_device_ids=true | all-gather | bytes 135168 | tf_op jit(solution)/shard_map/all_gather | solution.py:503
  321.6 0.0 copy-done.17
  321.7 1.0 shard_map.172
  (13 shorter events, 0.0 us)
Async XLA Ops:
  7.2 62.0 %all-gather.8.cloned.1.call-start = ((), (), s32[]{:S(2)}) async-start(), calls=%async_computation | async-start | bytes 1622016 | tf_op jit(solution)/shard_map/all_gather | solution.py:503
  7.2 0.9 copy-start.5
  8.1 0.9 copy-start.6
  9.0 0.7 copy-start.12
  11.0 0.9 copy-start.7
  11.9 0.9 copy-start.8
  12.8 0.8 copy-start.9
  13.7 0.7 copy-start.13
  14.4 0.7 copy-start.14
  15.1 0.7 copy-start.18
  69.1 1.4 copy-start
  70.5 0.9 copy-start.2
  71.5 0.7 copy-start.10
  123.4 49.6 %copy-start.11 = (f32[256]{0:T(256)S(1)}, f32[256]{0:T(256)}, u32[]{:S(2)}) copy-start(f32[256]{0:T(256)} %param.20) | copy-start | bytes 3076
  222.4 49.7 %copy-start.1 = (f32[1536,256]{1,0:T(8,128)S(1)}, f32[1536,256]{1,0:T(8,128)}, u32[]{:S(2)}) copy-start(f32[1536,256]{1,0:T(8,128)} %all-gather.8.cloned.1.call-done) | copy-start | bytes 4718596
  222.4 49.7 %copy-start.3 = (f32[192,192]{1,0:T(8,128)S(1)}, f32[192,192]{1,0:T(8,128)}, u32[]{:S(2)}) copy-start(f32[192,192]{1,0:T(8,128)} %stiffness_ref.5) | copy-start | bytes 442372
  233.2 44.6 %copy-start.4 = (f32[192,256]{1,0:T(8,128)S(1)}, f32[192,256]{1,0:T(8,128)}, u32[]{:S(2)}) copy-start(f32[192,256]{1,0:T(8,128)} %load_ref.1) | copy-start | bytes 589828
  233.2 44.6 %copy-start.15 = (s32[8,128]{1,0:T(8,128)S(1)}, s32[8,128]{1,0:T(8,128)}, u32[]{:S(2)}) copy-start(s32[8,128]{1,0:T(8,128)} %sub_cell.1) | copy-start | bytes 12292
  233.2 44.6 %copy-start.16 = (s32[8,128]{1,0:T(8,128)S(1)}, s32[8,128]{1,0:T(8,128)}, u32[]{:S(2)}) copy-start(s32[8,128]{1,0:T(8,128)} %sub_face.1) | copy-start | bytes 12292
  272.2 49.5 %copy-start.17 = (s32[8,128]{1,0:T(8,128)S(1)}, s32[8,128]{1,0:T(8,128)}, u32[]{:S(2)}) copy-start(s32[8,128]{1,0:T(8,128)} %owner_ref.1) | copy-start | bytes 12292
Sparse Core Ops, SparseCore 0:
  11.4 57.6 all-gather.7

commit v3 on v2

v3 whole, which is shorter than its diff:
```python
import functools

import jax
import jax.numpy as jnp
from jax import lax
from jax.experimental import pallas as pl
from jax.experimental.pallas import tpu as pltpu
from jax.sharding import PartitionSpec as P

REACH = 4
SWEEPS = 2
LANES = 128
WIDE = 2 * LANES
OWN = 32
EDGE = 16
NOWHERE = 126

relaxation = 0.7
scale_down = 16.0
pad_code = 16368

f32 = jnp.float32
bf16 = jnp.bfloat16
i32 = jnp.int32


def neighbour_offsets():
    return [step + 1 for step in range(REACH)] + [-(step + 1) for step in range(REACH)]


def exchange(packed):
    return lax.all_to_all(packed, "dom", 0, 0, tiled=True)


def pack(place, sign, rows, pack_ref, out_ref):
    count = out_ref.shape[0]
    pack_ref[...] = jnp.zeros_like(pack_ref)
    for slot, offset in enumerate(neighbour_offsets()):
        target = place + sign * offset
        at = jnp.where((target >= 0) & (target < count), target, count)
        for number, row in enumerate(rows[slot]):
            pack_ref[at, number : number + 1, :] = row
    out_ref[...] = pack_ref[:count]


def landed(place, sign, got_ref, number):
    count = got_ref.shape[0]
    rows = []
    for offset in neighbour_offsets():
        source = place - sign * offset
        row = got_ref[jnp.clip(source, 0, count - 1), number : number + 1, :]
        there = jnp.broadcast_to((source >= 0) & (source < count), row.shape)
        rows.append(jnp.where(there, row, 0.0))
    return rows


def landed_wide(place, sign, got_ref, part):
    halves = [
        jnp.concatenate(landed(place, sign, got_ref, 2 * part + half), 0) for half in range(2)
    ]
    return jnp.concatenate(halves, 1)


def match16(row, count):
    width = row.shape[1]
    wide = jnp.broadcast_to(row.astype(f32), (16, width)).astype(bf16)
    numbers = lax.broadcasted_iota(i32, (count, width), 0).astype(f32).astype(bf16)
    numbers = numbers.reshape(count // 16, 16, width)
    return numbers == wide[None]


def one_hot(row, count):
    mask = match16(row, count)
    ones = jnp.ones(mask.shape, bf16)
    return jnp.where(mask, ones, jnp.zeros_like(ones)).reshape(count, row.shape[1])


def spread16(mask, row):
    wide = jnp.broadcast_to(row, (16, row.shape[1])).astype(bf16)[None]
    out = jnp.where(mask, jnp.broadcast_to(wide, mask.shape), jnp.zeros(mask.shape, bf16))
    return out.reshape(mask.shape[0] * 16, row.shape[1])


def look_up(table, tops, half_rows, where, lane, totals=None):
    tiles = range(len(where))
    if totals is None:
        totals = [[jnp.zeros(where[0].shape, f32) for _ in tiles] for _ in tops]
    for half_row in range(half_rows):
        row, half = half_row // 2, half_row % 2
        masks = [where[tile] == half_row for tile in tiles]
        for part, top in enumerate(tops):
            line = jnp.broadcast_to(
                table[top + row : top + row + 1, half * LANES : (half + 1) * LANES],
                where[0].shape,
            )
            for tile in tiles:
                found = jnp.take_along_axis(line, lane[tile], axis=1, mode="promise_in_bounds")
                totals[part][tile] = jnp.where(masks[tile], found, totals[part][tile])
    return totals


def halves(x):
    return [x[:, :LANES], x[:, LANES:]]


def gather_cells(table, tops, half_rows, where_ref, lane_ref, out_ref, start_ref=None):
    count = where_ref.shape[0]
    high = 32

    def body(group, carry):
        start = pl.multiple_of(group * high, high)
        places = [
            (start + 8 * (tile // 2), slice(LANES * (tile % 2), LANES * (tile % 2 + 1)))
            for tile in range(high // 4)
        ]
        where = [where_ref[pl.ds(row, 8), columns] for row, columns in places]
        lane = [lane_ref[pl.ds(row, 8), columns] for row, columns in places]
        totals = None
        if start_ref is not None:
            totals = [
                [start_ref[pl.ds(part * count + row, 8), columns] for row, columns in places]
                for part in range(len(tops))
            ]
        totals = look_up(table, tops, half_rows, where, lane, totals)
        for part in range(len(tops)):
            for tile, (row, columns) in enumerate(places):
                out_ref[pl.ds(part * count + row, 8), columns] = totals[part][tile]
        return carry

    lax.fori_loop(0, count // high, body, 0)


def tops_of(rows, parts=3):
    return [part * rows for part in range(parts)]


def rows_and_columns(where, lane):
    return where >> 1, (where & 1) * LANES + lane


def scatter_block(values, rows, where, lane):
    at_row, at_column = rows_and_columns(where, lane)
    count = at_row.shape[0]
    masks = [match16(at_row[j : j + 1], rows) for j in range(count)]
    hot = jnp.concatenate([one_hot(at_column[j : j + 1], WIDE) for j in range(count)], 1)
    stacked = []
    for piece in range(2):
        for part in range(3):
            stacked.append(
                jnp.concatenate(
                    [spread16(masks[j], values[piece][part][j : j + 1]) for j in range(count)], 1
                )
            )
    return lax.dot_general(
        jnp.concatenate(stacked, 0), hot, (((1,), (1,)), ((), ())), preferred_element_type=f32
    )


def split32(x):
    high = x.astype(bf16).astype(f32)
    return high, x - high


def scatter_cells(image_ref, rows, where_ref, lane_ref, sum_ref):
    count = where_ref.shape[0]
    sum_ref[...] = jnp.zeros_like(sum_ref)

    def body(block, carry):
        start = pl.multiple_of(block * 8, 8)
        values = [split32(image_ref[pl.ds(part * count + start, 8), :]) for part in range(3)]
        values = list(zip(*values))
        sum_ref[...] += scatter_block(
            values, rows, where_ref[pl.ds(start, 8), :], lane_ref[pl.ds(start, 8), :]
        )
        return carry

    lax.fori_loop(0, count // 8, body, 0)


def add_pieces(sums):
    half = sums.shape[0] // 2
    return sums[:half] + sums[half:]


def spread_hanging(held, weight, rows, where, lane):
    both = jnp.concatenate([held, held], 1)
    values = [split32(weight * both[part : part + 1]) for part in range(3)]
    return add_pieces(scatter_block(list(zip(*values)), rows, where, lane))


def sum_masters(table, tops, half_rows, weight, where, lane):
    found = look_up(table, tops, half_rows, halves(where), halves(lane))
    weight = halves(weight)
    return [
        jnp.sum(weight[0] * tiles[0] + weight[1] * tiles[1], 0, keepdims=True) for tiles in found
    ]


def fill_table(x_ref, out_ref):
    count = x_ref.shape[1] // WIDE
    for part in range(3):
        out_ref[part * OWN + count : (part + 1) * OWN, :] = jnp.zeros((OWN - count, WIDE), f32)
    for row in range(count):
        block = x_ref[:, row * WIDE : (row + 1) * WIDE]
        for part in range(3):
            out_ref[part * OWN + row : part * OWN + row + 1, :] = block[part : part + 1]


def export_rows(tables, half_rows, where, lane):
    rows = [[] for _ in range(2 * REACH)]
    for table in tables:
        found = look_up(table, tops_of(OWN), half_rows, halves(where), halves(lane))
        for tiles in found:
            for tile in tiles:
                for slot in range(2 * REACH):
                    rows[slot].append(tile[slot : slot + 1])
    return rows


def copy_in(pairs, sems):
    copies = [
        pltpu.make_async_copy(source, target, sems.at[number])
        for number, (source, target) in enumerate(pairs)
    ]
    for copy in copies:
        copy.start()
    for copy in copies:
        copy.wait()


def first_export(
    place_ref, adjoint_hbm, primal_hbm, list_hbm, tab_a, tab_p, where_ref, lane_ref,
    out_ref, pack_ref, adjoint_ref, primal_ref, list_ref, sems,
):
    copy_in(
        [(adjoint_hbm, adjoint_ref), (primal_hbm, primal_ref), (list_hbm, list_ref)], sems
    )
    owned = adjoint_ref.shape[1]
    fill_table(adjoint_ref, tab_a)
    fill_table(primal_ref, tab_p)
    codes = list_ref[...]
    node = lax.rem(17 * codes + lax.broadcasted_iota(i32, codes.shape, 1), owned)
    where_ref[...] = node >> 7
    lane_ref[...] = node & 127
    rows = export_rows([tab_a, tab_p], owned // LANES, node >> 7, node & 127)
    pack(place_ref[0], 1, rows, pack_ref, out_ref)


def setup(
    connect_hbm, node_hbm, master_hbm, weight_hbm, source_hbm, inverse_hbm,
    own_where, edge_where, lane_ref, master_own, master_edge, master_lane, weight_out,
    tab_source, tab_inverse,
    connect_ref, node_ref, master_ref, weight_ref, source_ref, inverse_ref, map_ref, found_ref,
    sems,
):
    copy_in(
        [
            (connect_hbm, connect_ref),
            (node_hbm, node_ref),
            (master_hbm, master_ref),
            (weight_hbm, weight_ref),
            (source_hbm, source_ref),
            (inverse_hbm, inverse_ref),
        ],
        sems,
    )
    owned = source_ref.shape[1]
    extent = owned + 2 * REACH * WIDE
    fill_table(source_ref, tab_source)
    fill_table(inverse_ref, tab_inverse)
    codes = master_ref[...]
    master = lax.rem(17 * codes + 8 * lax.broadcasted_iota(i32, codes.shape, 1), extent)
    count = codes.shape[0] // 2
    master = jnp.concatenate([master[:count], master[count:]], 1)
    weight = weight_ref[...]
    weight_out[...] = jnp.concatenate([weight[:count], weight[count:]], 1)
    last = owned // LANES
    where = master >> 7
    master_own[...] = jnp.where(where < last, where, NOWHERE)
    master_edge[...] = jnp.where(where < last, NOWHERE, where - last)
    master_lane[...] = master & 127

    codes = node_ref[...]
    node = jnp.where(codes == pad_code, extent, lax.rem(13 * codes, owned))
    slot = (lax.broadcasted_iota(i32, codes.shape, 1) + 1).astype(f32)
    map_ref[...] = lax.dot_general(
        spread16(match16(node >> 8, OWN), slot),
        one_hot(node & 255, WIDE),
        (((1,), (1,)), ((), ())),
        preferred_element_type=f32,
    )

    codes = connect_ref[...]
    cells = lax.broadcasted_iota(i32, codes.shape, 1)
    slots = lax.rem(27 * cells + 17 * codes, extent)
    own_where[...] = slots >> 7
    lane_ref[...] = slots & 127
    gather_cells(map_ref, [0], last, own_where, lane_ref, found_ref)
    slot = found_ref[...].astype(i32)
    where = slots >> 7
    hanging = slot > 0
    outside = where >= last
    own_where[...] = jnp.where(hanging | outside, NOWHERE, where)
    edge_where[...] = jnp.where(
        hanging, 4 * REACH, jnp.where(outside, where - last, NOWHERE)
    )
    lane_ref[...] = jnp.where(hanging, slot - 1, slots & 127)


def pieces(x):
    high = x.astype(bf16)
    return high, (x - high.astype(f32)).astype(bf16)


def gather_own_cells(tab_ref, half_rows, where_ref, lane_ref, out_ref, tall_ref):
    count = where_ref.shape[0]
    tall = -(-half_rows // 8) * 8
    tall_ref[...] = jnp.zeros_like(tall_ref)
    for part in range(3):
        for half_row in range(half_rows):
            row, half = part * OWN + half_row // 2, half_row % 2
            tall_ref[part * tall + half_row : part * tall + half_row + 1, :] = tab_ref[
                row : row + 1, half * LANES : (half + 1) * LANES
            ]
    table = jnp.concatenate(pieces(tall_ref[...]), 1)

    def body(block, carry):
        start = pl.multiple_of(block * 8, 8)
        where = where_ref[pl.ds(start, 8), :]
        lane = lane_ref[pl.ds(start, 8), :]
        for j in range(8):
            hot = one_hot(lane[j : j + 1], LANES)
            found = jnp.dot(table, jnp.concatenate([hot, hot], 0), preferred_element_type=f32)
            mask = lax.broadcasted_iota(i32, (tall, WIDE), 0) == where[j : j + 1]
            for part in range(3):
                out_ref[pl.ds(part * count + start + j, 1), :] = jnp.sum(
                    jnp.where(mask, found[part * tall : (part + 1) * tall], 0.0), 0, keepdims=True
                )
        return carry

    lax.fori_loop(0, count // 8, body, 0)


def own_gather(
    half_rows, tab_ref, where_ref, lane_ref, master_where, master_lane, weight_ref, cells_ref,
    hang_ref, tall_ref,
):
    found = sum_masters(
        tab_ref, tops_of(OWN), half_rows, weight_ref[...], master_where[...], master_lane[...]
    )
    for part in range(3):
        hang_ref[part : part + 1, :] = found[part]
    gather_own_cells(tab_ref, half_rows, where_ref, lane_ref, cells_ref, tall_ref)


def edge_gather(
    place, got_ref, first, cells_ref, hang_ref, where_ref, lane_ref, master_where, master_lane,
    weight_ref, edge_ref, out_ref,
):
    slots = 2 * REACH
    for part in range(3):
        edge_ref[part * EDGE : part * EDGE + slots, :] = landed_wide(
            place, 1, got_ref, first + part
        )
    found = sum_masters(
        edge_ref, tops_of(EDGE), 2 * slots, weight_ref[...], master_where[...], master_lane[...]
    )
    for part in range(3):
        edge_ref[part * EDGE + slots : part * EDGE + slots + 1, :LANES] = (
            found[part] + hang_ref[part : part + 1, :]
        )
    gather_cells(
        edge_ref, tops_of(EDGE), 2 * slots + 1, where_ref, lane_ref, out_ref, cells_ref
    )


def edge_product(
    place_ref, got_ref, cells_ref, hang_ref, where_ref, lane_ref, master_where,
    master_lane, weight_ref, modulus_ref, stiffness_ref, out_ref,
    image_ref, held_ref, pack_ref, edge_ref, full_ref, sum_ref,
):
    place = place_ref[0]
    edge_gather(
        place, got_ref, 0, cells_ref, hang_ref, where_ref, lane_ref,
        master_where, master_lane, weight_ref, edge_ref, full_ref,
    )
    image_ref[...] = modulus_ref[...] * lax.dot_general(
        stiffness_ref[...],
        full_ref[...],
        (((0,), (0,)), ((), ())),
        precision=lax.Precision.HIGHEST,
        preferred_element_type=f32,
    )
    scatter_cells(image_ref, EDGE, where_ref, lane_ref, sum_ref)
    sums = add_pieces(sum_ref[...])
    slots = 2 * REACH
    held = jnp.concatenate(
        [sums[part * EDGE + slots : part * EDGE + slots + 1, :LANES] for part in range(3)], 0
    )
    held_ref[...] = held
    edge_ref[...] = sums + spread_hanging(
        held, weight_ref[...], EDGE, master_where[...], master_lane[...]
    )
    rows = [
        [
            edge_ref[part * EDGE + slot : part * EDGE + slot + 1, half * LANES : (half + 1) * LANES]
            for part in range(3)
            for half in range(2)
        ]
        for slot in range(slots)
    ]
    pack(place, -1, rows, pack_ref, out_ref)


def own_sums(
    image_ref, held_ref, where_ref, lane_ref, master_where, master_lane, weight_ref,
    tab_ref, source_ref, inverse_ref, out_ref, sum_ref,
):
    scatter_cells(image_ref, OWN, where_ref, lane_ref, sum_ref)
    applied = add_pieces(sum_ref[...]) + spread_hanging(
        held_ref[...], weight_ref[...], OWN, master_where[...], master_lane[...]
    )
    out_ref[...] = tab_ref[...] + relaxation * inverse_ref[...] * (source_ref[...] - applied)


def update(
    half_rows, place_ref, got_ref, where_ref, lane_ref, partial_ref, inverse_ref,
    out_ref, tab_ref, *rest,
):
    pack_ref = rest[-1]
    place = place_ref[0]
    values = [split32(landed_wide(place, -1, got_ref, part)) for part in range(3)]
    returned = add_pieces(
        scatter_block(list(zip(*values)), OWN, where_ref[...], lane_ref[...])
    )
    tab_ref[...] = partial_ref[...] - relaxation * inverse_ref[...] * returned
    rows = export_rows([tab_ref], half_rows, where_ref[...], lane_ref[...])
    pack(place, 1, rows, pack_ref, out_ref)
    if len(rest) > 1:
        final_ref = rest[0]
        for row in range(final_ref.shape[1] // WIDE):
            for part in range(3):
                final_ref[part : part + 1, row * WIDE : (row + 1) * WIDE] = tab_ref[
                    part * OWN + row : part * OWN + row + 1, :
                ]


def primal_product(
    place_ref, got_ref, cells_ref, hang_ref, where_ref, lane_ref, master_where,
    master_lane, weight_ref, modulus_ref, stiffness_ref, out_ref, edge_ref, full_ref,
):
    edge_gather(
        place_ref[0], got_ref, 3, cells_ref, hang_ref, where_ref, lane_ref,
        master_where, master_lane, weight_ref, edge_ref, full_ref,
    )
    out_ref[...] = modulus_ref[...] * jnp.dot(
        stiffness_ref[...],
        full_ref[...],
        precision=lax.Precision.HIGHEST,
        preferred_element_type=f32,
    )


def fluxes(
    place_ref, got_ref, cells_ref, hang_ref, where_ref, lane_ref, master_where,
    master_lane, weight_ref, ku_ref, load_ref, sub_cell, sub_face, out_ref,
    term_ref, pack_ref, edge_ref, full_ref, flux_ref,
):
    place = place_ref[0]
    edge_gather(
        place, got_ref, 0, cells_ref, hang_ref, where_ref, lane_ref,
        master_where, master_lane, weight_ref, edge_ref, full_ref,
    )
    cells = full_ref[...]
    ku = ku_ref[...]
    term_ref[...] = jnp.sum(cells * (load_ref[...] - ku), 0, keepdims=True)
    face = lax.broadcasted_iota(i32, (8, ku.shape[0]), 0)
    node = lax.broadcasted_iota(i32, (8, ku.shape[0]), 1) & 63
    index = jnp.where(face < 2, node >> 4, jnp.where(face < 4, (node >> 2) & 3, node & 3))
    member = jnp.where((face < 6) & (index == 3 * (face & 1)), 1.0, 0.0).astype(f32)
    flux_ref[...] = jnp.dot(
        member, ku * cells, precision=lax.Precision.HIGHEST, preferred_element_type=f32
    )
    cell = sub_cell[...]
    found = look_up(flux_ref, [0], 12, [2 * sub_face[...] + (cell >> 7)], [cell & 127])[0][0]
    rows = [[found[slot : slot + 1]] for slot in range(2 * REACH)]
    pack(place, 1, rows, pack_ref, out_ref)


def collect(place_ref, got_ref, owner_ref, term_ref, out_ref):
    count = term_ref.shape[1]
    got = jnp.concatenate(landed(place_ref[0], 1, got_ref, 0), 1)
    hot = jnp.concatenate(
        [one_hot(owner_ref[slot : slot + 1, :], count) for slot in range(2 * REACH)], 1
    )
    values = jnp.concatenate(
        [jnp.broadcast_to(x, (16, got.shape[1])).astype(bf16) for x in split32(got)], 0
    )
    sums = lax.dot_general(values, hot, (((1,), (1,)), ((), ())), preferred_element_type=f32)
    face_term = sums[0:1] + sums[16:17]
    out_ref[...] = (jnp.abs(term_ref[...]) + jnp.abs(face_term)) / scale_down


SMALL = pl.BlockSpec(memory_space=pltpu.SMEM)
FAST = pl.BlockSpec(memory_space=pltpu.VMEM)
FAR = pl.BlockSpec(memory_space=pl.ANY)


def call(kernel, outs, scratch=(), specs=None, sems=0):
    scratch = [pltpu.VMEM(shape, kind) for shape, kind in scratch]
    if sems:
        scratch.append(pltpu.SemaphoreType.DMA((sems,)))

    def run(*args):
        return pl.pallas_call(
            kernel,
            out_shape=[jax.ShapeDtypeStruct(shape, kind) for shape, kind in outs],
            in_specs=specs or [SMALL] + [FAST] * (len(args) - 1),
            scratch_shapes=scratch,
            compiler_params=pltpu.CompilerParams(vmem_limit_bytes=40 * 1024 * 1024),
        )(*args)

    return run


def local(
    adjoint_start,
    adjoint_source,
    inverse_diagonal,
    primal_field,
    cell_load,
    modulus,
    stiffness,
    connectivity,
    hang_node,
    hang_master,
    hang_weight,
    ghost_lists,
    subface_cell,
    subface_face,
    subface_owner,
):
    slots = 2 * REACH
    local_values, cell_count = cell_load.shape
    nodes = connectivity.shape[0]
    half_rows = adjoint_start.shape[1] // LANES
    moduli = modulus.reshape(1, cell_count)
    place = lax.axis_index("dom").reshape(1).astype(i32)
    table = ((3 * OWN, WIDE), f32)
    index = ((nodes, cell_count), i32)
    cells_shape = ((local_values, cell_count), f32)
    hang_shape = ((3, hang_node.shape[0]), f32)
    master_shape = ((8, WIDE), i32)
    edge = ((3 * EDGE, WIDE), f32)

    count = lax.axis_size("dom")

    def packed(height):
        return [((count, height, LANES), f32)]

    def room(height):
        return ((count + 1, height, LANES), f32)

    tab, tab_primal, list_where, list_lane, blocks = call(
        first_export,
        [table, table] + [(ghost_lists.shape, i32)] * 2 + packed(16),
        [
            room(16),
            (adjoint_start.shape, f32),
            (primal_field.shape, f32),
            (ghost_lists.shape, i32),
        ],
        [SMALL, FAR, FAR, FAR],
        sems=3,
    )(place, adjoint_start, primal_field, ghost_lists)
    ghosts = first_ghosts = exchange(blocks)
    hang_node = hang_node.reshape(1, -1)
    far = (
        connectivity, hang_node, hang_master, hang_weight, adjoint_source, inverse_diagonal
    )
    (
        own_where, edge_where, lane, master_own, master_edge, master_lane, weight, source, inverse,
    ) = call(
        setup,
        [index] * 3 + [master_shape] * 3 + [((8, WIDE), f32), table, table],
        [(x.shape, x.dtype) for x in far] + [((OWN, WIDE), f32), ((nodes, cell_count), f32)],
        [FAR] * 6,
        sems=6,
    )(*far)

    def gather_own(values):
        return call(
            functools.partial(own_gather, half_rows),
            [cells_shape, hang_shape],
            [((3 * (-(-half_rows // 8) * 8), LANES), f32)],
            specs=[FAST] * 6,
        )(values, own_where, lane, master_own, master_lane, weight)

    on_edge = (edge_where, lane, master_edge, master_lane, weight)
    ku = None
    for sweep in range(SWEEPS):
        cells, hang = gather_own(tab)
        blocks, image, held = call(
            edge_product,
            packed(8) + [cells_shape, hang_shape],
            [room(8), edge, cells_shape, ((6 * EDGE, WIDE), f32)],
        )(place, ghosts, cells, hang, *on_edge, moduli, stiffness)
        returned = exchange(blocks)
        (partial,) = call(
            own_sums, [table], [((6 * OWN, WIDE), f32)], specs=[FAST] * 10
        )(image, held, own_where, lane, master_own, master_lane, weight, tab, source, inverse)
        if sweep == 0:
            cells, hang = gather_own(tab_primal)
            (ku,) = call(primal_product, [cells_shape], [edge, cells_shape])(
                place, first_ghosts, cells, hang, *on_edge, moduli, stiffness
            )
        last = sweep == SWEEPS - 1
        blocks, tab, *final = call(
            functools.partial(update, half_rows),
            packed(8) + [table] + ([(adjoint_start.shape, f32)] if last else []),
            [room(8)],
        )(place, returned, list_where, list_lane, partial, inverse)
        ghosts = exchange(blocks)
    cells, hang = gather_own(tab)
    blocks, term = call(
        fluxes,
        packed(1) + [((1, cell_count), f32)],
        [room(1), edge, cells_shape, ((8, cell_count), f32)],
    )(place, ghosts, cells, hang, *on_edge, ku, cell_load, subface_cell, subface_face)
    received = exchange(blocks)
    (indicator,) = call(collect, [((1, cell_count), f32)])(
        place, received, subface_owner, term
    )
    return (final[0], indicator.reshape(cell_count))


def solution(mesh):
    placed = (
        P(None, "dom"),
        P(None, "dom"),
        P(None, "dom"),
        P(None, "dom"),
        P(None, "dom"),
        P("dom"),
        P(),
        P(None, "dom"),
        P("dom"),
        P(None, "dom"),
        P(None, "dom"),
        P(None, "dom"),
        P(None, "dom"),
        P(None, "dom"),
        P(None, "dom"),
    )
    return jax.shard_map(
        local, mesh=mesh, in_specs=placed, out_specs=(P(None, "dom"), P("dom")), check_vma=False
    )
```

time: 330 us -> 105 us (0.32)
  blocking collectives: 198 us -> 12.6 us
  waiting for transfers between devices: 41.8 us -> 15.1 us
  starting transfers between devices: 0.04 us -> 17.9 us
  between operations: 14.2 us -> 0.92 us
  Pallas kernels: 65.3 us -> 54.1 us
  local copies, waits for them, and re-layouts: 10.2 us -> 3.82 us
    all_gather x5 -> x0, blocking collectives: 198 us -> none  [share(): return lax.all_gather(blocks, 'dom')]
    all_gather x1 -> x0, waiting for transfers between devices: 41.8 us -> none  [share(): return lax.all_gather(blocks, 'dom')]
    all_to_all x0 -> x5, starting transfers between devices: none -> 17.9 us  [exchange(): return lax.all_to_all(packed, 'dom', 0, 0, tiled=True)]
    all_to_all x0 -> x5, waiting for transfers between devices: none -> 15.1 us  [exchange(): return lax.all_to_all(packed, 'dom', 0, 0, tiled=True)]
    all_to_all x0 -> x1, blocking collectives: none -> 12.6 us  [exchange(): return lax.all_to_all(packed, 'dom', 0, 0, tiled=True)]
    pallas_call x15, Pallas kernels: 65.3 us -> 54.1 us  [run(): pl.pallas_call(kernel, out_shape=[jax.ShapeDtypeStruct(shape, kind) for s...]
    unnamed x38 -> x30, local copies, waits for them, and re-layouts: 10.2 us -> 3.82 us
  transfers between devices with their start and end apart: 1 -> 5, of which waited for: 1 -> 4; matrix products, arithmetic and copies ran while one was open for 0% -> 0% of each run, Pallas kernels for 4% -> 28%
where the time goes in v3:
time: 105 us; the launch traced here: 104 us
  Pallas kernels  54.1 us (52%)
  starting transfers between devices  17.9 us (17%)
  waiting for transfers between devices  15.1 us (14%)
  blocking collectives  12.6 us (12%)
  local copies, waits for them, and re-layouts  3.82 us (4%)
    pallas_call x15, Pallas kernels, run(): pl.pallas_call(kernel, out_shape=[jax.ShapeDtypeStruct(shape, kind) for s...  54.1 us
    all_to_all x5, starting transfers between devices, exchange(): return lax.all_to_all(packed, 'dom', 0, 0, tiled=True)  17.9 us
    all_to_all x5, waiting for transfers between devices, exchange(): return lax.all_to_all(packed, 'dom', 0, 0, tiled=True)  15.1 us
    all_to_all x1, blocking collectives, exchange(): return lax.all_to_all(packed, 'dom', 0, 0, tiled=True)  12.6 us
    unnamed x30, local copies, waits for them, and re-layouts  3.82 us
  transfers between devices with their start and end apart: 5, of which 4 were waited for; matrix products, arithmetic and copies ran while one was open for 0% of the time, Pallas kernels for 28%

profile of v3, /device:TPU:0, one launch (start us, length us, event | category | flops | bytes accessed | tf_op | source)
XLA Modules:
  0.0 104.5 jit_solution(16011221823463136102)
XLA Ops:
  0.6 0.0 copy-start.2
  0.6 0.9 copy-done.2
  1.5 0.9 copy-done.3
  2.4 0.7 copy-done.8
  3.1 1.8 %shard_map.158 = (f32[96,256]{1,0:T(8,128)S(1)}, f32[96,256]{1,0:T(8,128)S(1)}, s32[8,256]{1,0:T(8,128)S(1)}, s32[8,256]{1,0:T(8,128)S(1)}, f32[32,16,128]{2,1,0:T(8,128)}) custom-call(s32[1]{0:T(128)} %bitcast.place_ref, f32[3,6912]{1,0:T(4,128)S(1)} %copy-done.2, f32[3,6912]{1,0:T(4,128)S(1)} %copy-done.3, s32[8,256]{1,0:T(8,128)S(1)} %copy-done.8), custom_call_target="tpu_custom_call" | custom-call | tf_op jit(solution)/shard_map/pallas_call | solution.py:515
  5.0 0.0 copy-start.4
  5.0 0.0 copy-start.5
  5.0 0.0 copy-start.6
  5.0 0.0 copy-start.9
  5.0 0.0 copy-start.10
  5.0 7.3 %all-to-all-start = ((f32[32,16,128]{2,1,0:T(8,128)}), f32[32,16,128]{2,1,0:T(8,128)S(1)}, u32[]{:S(2)}, u32[]{:S(2)}) async-start(f32[32,16,128]{2,1,0:T(8,128)} %get-tuple-element.37), calls=%async_computation | async-start | bytes 524288 | tf_op jit(solution)/shard_map/all_to_all | solution.py:32
  12.4 0.0 copy-start.14
  12.4 0.0 copy-done.4
  12.4 0.0 copy-done.5
  12.4 0.0 copy-done.6
  12.4 0.0 copy-done.9
  12.4 0.0 copy-done.10
  12.4 0.6 copy-done.14
  13.0 3.3 %shard_map.159 = (s32[64,256]{1,0:T(8,128)S(1)}, s32[64,256]{1,0:T(8,128)S(1)}, s32[64,256]{1,0:T(8,128)S(1)}, s32[8,256]{1,0:T(8,128)S(1)}, s32[8,256]{1,0:T(8,...) custom-call(s32[64,256]{1,0:T(8,128)S(1)} %copy-done.6, ...), custom_call_target="tpu_custom_call" | custom-call | tf_op jit(solution)/shard_map/pallas_call | solution.py:515
  16.3 0.0 copy-start
  16.3 3.5 %shard_map.160 = (f32[192,256]{1,0:T(8,128)S(1)}, f32[3,128]{1,0:T(4,128)S(1)}) custom-call(f32[96,256]{1,0:T(8,128)S(1)} %get-tuple-element.38.tab_ref, s32[64,256]{1,0:T(8,128)S(1)} %get-tuple-element.39.where_ref, s32[64,256]{1,0:T(8,128)S(1)} %get-tuple-element.40.lane_ref, s32[8,256]{1,0:T(8,128)S(1)} %get-tuple-element.41.master_where, ...), custom_call_target="tpu_custom_call" | custom-call | tf_op jit(solution)/shard_map/pallas_call | solution.py:515
  19.8 3.1 %all-to-all-done.got_ref = f32[32,16,128]{2,1,0:T(8,128)S(1)} async-done(((f32[32,16,128]{2,1,0:T(8,128)}), f32[32,16,128]{2,1,0:T(8,128)S(1)}, u32[]{:S(2)}, u32[]{:S(2)}) %all-to-all-start) | async-done | bytes 262176 | tf_op jit(solution)/shard_map/all_to_all | solution.py:32
  23.0 0.7 copy-done.7
  23.6 7.9 %shard_map.161 = (f32[32,8,128]{2,1,0:T(8,128)}, f32[192,256]{1,0:T(8,128)S(1)}, f32[3,128]{1,0:T(4,128)S(1)}) custom-call(s32[1]{0:T(128)} %bitcast.place_ref, f32[32,16,128]{2,1,0:T(8,128)S(1)} %all-to-all-done.got_ref, f32[192,256]{1,0:T(8,128)S(1)} %get-tuple-element.44.cells_ref, f32[3,128]{1,0:T(4,128)S(1)} %get-tuple-element.45.hang_ref, ...), custom_call_target="tpu_custom_call" | custom-call | tf_op jit(solution)/shard_map/pallas_call | solution.py:515
  31.5 2.7 %all-to-all-start.1 = ((f32[32,8,128]{2,1,0:T(8,128)}), f32[32,8,128]{2,1,0:T(8,128)S(1)}, u32[]{:S(2)}, u32[]{:S(2)}) async-start(f32[32,8,128]{2,1,0:T(8,128)} %get-tuple-element.48), calls=%async_computation.1 | async-start | bytes 262144 | tf_op jit(solution)/shard_map/all_to_all | solution.py:32
  34.2 4.6 %shard_map.162.partial_ref = f32[96,256]{1,0:T(8,128)S(1)} custom-call(f32[192,256]{1,0:T(8,128)S(1)} %get-tuple-element.51.image_ref, f32[3,128]{1,0:T(4,128)S(1)} %get-tuple-element.52.held_ref, s32[64,256]{1,0:T(8,128)S(1)} %get-tuple-element.39.where_ref, s32[64,256]{1,0:T(8,128)S(1)} %get-tuple-element.40.lane_ref, ...), custom_call_target="tpu_custom_call" | custom-call | tf_op jit(solution)/shard_map/pallas_call | solution.py:515
  38.8 3.6 %all-to-all-done.1.got_ref = f32[32,8,128]{2,1,0:T(8,128)S(1)} async-done(((f32[32,8,128]{2,1,0:T(8,128)}), f32[32,8,128]{2,1,0:T(8,128)S(1)}, u32[]{:S(2)}, u32[]{:S(2)}) %all-to-all-start.1) | async-done | bytes 131104 | tf_op jit(solution)/shard_map/all_to_all | solution.py:32
  42.5 1.6 %shard_map.163 = (f32[32,8,128]{2,1,0:T(8,128)}, f32[96,256]{1,0:T(8,128)S(1)}) custom-call(s32[1]{0:T(128)} %bitcast.place_ref, f32[32,8,128]{2,1,0:T(8,128)S(1)} %all-to-all-done.1.got_ref, s32[8,256]{1,0:T(8,128)S(1)} %get-tuple-element.49.where_ref, s32[8,256]{1,0:T(8,128)S(1)} %get-tuple-element.50.lane_ref, f32[96,256]{1,0:T(8,128)S(1)} %shard_map.162.partial_ref, ...), custom_call_target="tpu_custom_call" | custom-call | tf_op jit(solution)/shard_map/pallas_call | solution.py:515
  44.0 2.6 %all-to-all-start.2 = ((f32[32,8,128]{2,1,0:T(8,128)}), f32[32,8,128]{2,1,0:T(8,128)S(1)}, u32[]{:S(2)}, u32[]{:S(2)}) async-start(f32[32,8,128]{2,1,0:T(8,128)} %get-tuple-element.55), calls=%async_computation.2 | async-start | bytes 262144 | tf_op jit(solution)/shard_map/all_to_all | solution.py:32
  46.6 3.5 %shard_map.164 = (f32[192,256]{1,0:T(8,128)S(1)}, f32[3,128]{1,0:T(4,128)S(1)}) custom-call(f32[96,256]{1,0:T(8,128)S(1)} %get-tuple-element.56.tab_ref, s32[64,256]{1,0:T(8,128)S(1)} %get-tuple-element.39.where_ref, s32[64,256]{1,0:T(8,128)S(1)} %get-tuple-element.40.lane_ref, s32[8,256]{1,0:T(8,128)S(1)} %get-tuple-element.41.master_where, ...), custom_call_target="tpu_custom_call" | custom-call | tf_op jit(solution)/shard_map/pallas_call | solution.py:515
  50.2 4.7 %all-to-all-done.2.got_ref = f32[32,8,128]{2,1,0:T(8,128)S(1)} async-done(((f32[32,8,128]{2,1,0:T(8,128)}), f32[32,8,128]{2,1,0:T(8,128)S(1)}, u32[]{:S(2)}, u32[]{:S(2)}) %all-to-all-start.2) | async-done | bytes 131104 | tf_op jit(solution)/shard_map/all_to_all | solution.py:32
  54.8 7.9 %shard_map.165 = (f32[32,8,128]{2,1,0:T(8,128)}, f32[192,256]{1,0:T(8,128)S(1)}, f32[3,128]{1,0:T(4,128)S(1)}) custom-call(s32[1]{0:T(128)} %bitcast.place_ref, f32[32,8,128]{2,1,0:T(8,128)S(1)} %all-to-all-done.2.got_ref, f32[192,256]{1,0:T(8,128)S(1)} %get-tuple-element.57.cells_ref, f32[3,128]{1,0:T(4,128)S(1)} %get-tuple-element.58.hang_ref, ...), custom_call_target="tpu_custom_call" | custom-call | tf_op jit(solution)/shard_map/pallas_call | solution.py:515
  62.7 2.6 %all-to-all-start.3 = ((f32[32,8,128]{2,1,0:T(8,128)}), f32[32,8,128]{2,1,0:T(8,128)S(1)}, u32[]{:S(2)}, u32[]{:S(2)}) async-start(f32[32,8,128]{2,1,0:T(8,128)} %get-tuple-element.59), calls=%async_computation.3 | async-start | bytes 262144 | tf_op jit(solution)/shard_map/all_to_all | solution.py:32
  65.3 4.6 %shard_map.166.partial_ref = f32[96,256]{1,0:T(8,128)S(1)} custom-call(f32[192,256]{1,0:T(8,128)S(1)} %get-tuple-element.60.image_ref, f32[3,128]{1,0:T(4,128)S(1)} %get-tuple-element.61.held_ref, s32[64,256]{1,0:T(8,128)S(1)} %get-tuple-element.39.where_ref, s32[64,256]{1,0:T(8,128)S(1)} %get-tuple-element.40.lane_ref, ...), custom_call_target="tpu_custom_call" | custom-call | tf_op jit(solution)/shard_map/pallas_call | solution.py:515
  69.9 3.6 %all-to-all-done.3.got_ref = f32[32,8,128]{2,1,0:T(8,128)S(1)} async-done(((f32[32,8,128]{2,1,0:T(8,128)}), f32[32,8,128]{2,1,0:T(8,128)S(1)}, u32[]{:S(2)}, u32[]{:S(2)}) %all-to-all-start.3) | async-done | bytes 131104 | tf_op jit(solution)/shard_map/all_to_all | solution.py:32
  73.5 1.6 %shard_map.167 = (f32[32,8,128]{2,1,0:T(8,128)}, f32[96,256]{1,0:T(8,128)S(1)}, f32[3,6912]{1,0:T(4,128)}) custom-call(s32[1]{0:T(128)} %bitcast.place_ref, f32[32,8,128]{2,1,0:T(8,128)S(1)} %all-to-all-done.3.got_ref, s32[8,256]{1,0:T(8,128)S(1)} %get-tuple-element.49.where_ref, s32[8,256]{1,0:T(8,128)S(1)} %get-tuple-element.50.lane_ref, ...), custom_call_target="tpu_custom_call" | custom-call | tf_op jit(solution)/shard_map/pallas_call | solution.py:515
  75.1 2.8 %all-to-all-start.4 = ((f32[32,8,128]{2,1,0:T(8,128)}), f32[32,8,128]{2,1,0:T(8,128)S(1)}, u32[]{:S(2)}, u32[]{:S(2)}) async-start(f32[32,8,128]{2,1,0:T(8,128)} %get-tuple-element.63), calls=%async_computation.4 | async-start | bytes 262144 | tf_op jit(solution)/shard_map/all_to_all | solution.py:32
  77.9 3.5 %shard_map.169 = (f32[192,256]{1,0:T(8,128)S(1)}, f32[3,128]{1,0:T(4,128)S(1)}) custom-call(f32[96,256]{1,0:T(8,128)S(1)} %get-tuple-element.67.tab_ref, s32[64,256]{1,0:T(8,128)S(1)} %get-tuple-element.39.where_ref, s32[64,256]{1,0:T(8,128)S(1)} %get-tuple-element.40.lane_ref, s32[8,256]{1,0:T(8,128)S(1)} %get-tuple-element.41.master_where, ...), custom_call_target="tpu_custom_call" | custom-call | tf_op jit(solution)/shard_map/pallas_call | solution.py:515
  81.4 3.0 %shard_map.170.ku_ref = f32[192,256]{1,0:T(8,128)S(1)} custom-call(s32[1]{0:T(128)} %bitcast.place_ref, f32[32,16,128]{2,1,0:T(8,128)S(1)} %all-to-all-done.got_ref, f32[192,256]{1,0:T(8,128)S(1)} %get-tuple-element.68.cells_ref, f32[3,128]{1,0:T(4,128)S(1)} %get-tuple-element.69.hang_ref, s32[64,256]{1,0:T(8,128)S(1)} %get-tuple-element.46.where_ref, ...), custom_call_target="tpu_custom_call" | custom-call | tf_op jit(solution)/shard_map/pallas_call | solution.py:515
  84.4 0.0 copy-start.1
  84.4 0.0 copy-start.11
  84.4 0.0 copy-start.12
  84.4 3.5 %shard_map.168 = (f32[192,256]{1,0:T(8,128)S(1)}, f32[3,128]{1,0:T(4,128)S(1)}) custom-call(f32[96,256]{1,0:T(8,128)S(1)} %get-tuple-element.64.tab_ref, s32[64,256]{1,0:T(8,128)S(1)} %get-tuple-element.39.where_ref, s32[64,256]{1,0:T(8,128)S(1)} %get-tuple-element.40.lane_ref, s32[8,256]{1,0:T(8,128)S(1)} %get-tuple-element.41.master_where, ...), custom_call_target="tpu_custom_call" | custom-call | tf_op jit(solution)/shard_map/pallas_call | solution.py:515
  88.0 0.0 all-to-all-done.4.got_ref
  88.0 0.0 copy-start.13
  88.0 3.0 %shard_map.171 = (f32[32,1,128]{2,1,0:T(1,128)S(1)}, f32[1,256]{1,0:T(1,128)S(1)}) custom-call(s32[1]{0:T(128)} %bitcast.place_ref, f32[32,8,128]{2,1,0:T(8,128)S(1)} %all-to-all-done.4.got_ref, f32[192,256]{1,0:T(8,128)S(1)} %get-tuple-element.65.cells_ref, f32[3,128]{1,0:T(4,128)S(1)} %get-tuple-element.66.hang_ref, ...), custom_call_target="tpu_custom_call" | custom-call | tf_op jit(solution)/shard_map/pallas_call | solution.py:515
  91.0 12.6 %all_to_all.30.got_ref = f32[32,1,128]{2,1,0:T(1,128)S(1)} all-to-all(f32[32,1,128]{2,1,0:T(1,128)S(1)} %get-tuple-element.70), channel_id=1, replica_groups=mesh['dom'=32] {'dom'}, dimensions={0} | all-to-all | bytes 32768 | tf_op jit(solution)/shard_map/all_to_all | solution.py:32
  103.6 0.8 shard_map.172
  (8 shorter events, 0.0 us)
Async XLA Ops:
  0.6 0.9 copy-start.2
  1.5 0.9 copy-start.3
  2.4 0.7 copy-start.8
  5.0 7.4 %copy-start.4 = (f32[3,6912]{1,0:T(4,128)S(1)}, f32[3,6912]{1,0:T(4,128)}, u32[]{:S(2)}) copy-start(f32[3,6912]{1,0:T(4,128)} %source_hbm.1) | copy-start | bytes 248836
  5.0 7.4 %copy-start.5 = (f32[3,6912]{1,0:T(4,128)S(1)}, f32[3,6912]{1,0:T(4,128)}, u32[]{:S(2)}) copy-start(f32[3,6912]{1,0:T(4,128)} %inverse_hbm.1) | copy-start | bytes 248836
  5.0 7.4 %copy-start.6 = (s32[64,256]{1,0:T(8,128)S(1)}, s32[64,256]{1,0:T(8,128)}, u32[]{:S(2)}) copy-start(s32[64,256]{1,0:T(8,128)} %connect_hbm.1) | copy-start | bytes 196612
  5.0 7.4 %copy-start.9 = (s32[16,128]{1,0:T(8,128)S(1)}, s32[16,128]{1,0:T(8,128)}, u32[]{:S(2)}) copy-start(s32[16,128]{1,0:T(8,128)} %master_hbm.1) | copy-start | bytes 24580
  5.0 7.4 %copy-start.10 = (f32[16,128]{1,0:T(8,128)S(1)}, f32[16,128]{1,0:T(8,128)}, u32[]{:S(2)}) copy-start(f32[16,128]{1,0:T(8,128)} %weight_hbm.1) | copy-start | bytes 24580
  5.0 17.9 %all-to-all-start = ((f32[32,16,128]{2,1,0:T(8,128)}), f32[32,16,128]{2,1,0:T(8,128)S(1)}, u32[]{:S(2)}, u32[]{:S(2)}) async-start(f32[32,16,128]{2,1,0:T(8,128)} %get-tuple-element.37), calls=%async_computation | async-start | bytes 524288 | tf_op jit(solution)/shard_map/all_to_all | solution.py:32
  12.4 0.7 copy-start.14
  16.3 6.7 %copy-start = (f32[192,192]{1,0:T(8,128)S(1)}, f32[192,192]{1,0:T(8,128)}, u32[]{:S(2)}) copy-start(f32[192,192]{1,0:T(8,128)} %stiffness_ref.5) | copy-start | bytes 442372
  23.0 0.7 copy-start.7
  31.5 11.0 %all-to-all-start.1 = ((f32[32,8,128]{2,1,0:T(8,128)}), f32[32,8,128]{2,1,0:T(8,128)S(1)}, u32[]{:S(2)}, u32[]{:S(2)}) async-start(f32[32,8,128]{2,1,0:T(8,128)} %get-tuple-element.48), calls=%async_computation.1 | async-start | bytes 262144 | tf_op jit(solution)/shard_map/all_to_all | solution.py:32
  44.0 10.8 %all-to-all-start.2 = ((f32[32,8,128]{2,1,0:T(8,128)}), f32[32,8,128]{2,1,0:T(8,128)S(1)}, u32[]{:S(2)}, u32[]{:S(2)}) async-start(f32[32,8,128]{2,1,0:T(8,128)} %get-tuple-element.55), calls=%async_computation.2 | async-start | bytes 262144 | tf_op jit(solution)/shard_map/all_to_all | solution.py:32
  62.7 10.8 %all-to-all-start.3 = ((f32[32,8,128]{2,1,0:T(8,128)}), f32[32,8,128]{2,1,0:T(8,128)S(1)}, u32[]{:S(2)}, u32[]{:S(2)}) async-start(f32[32,8,128]{2,1,0:T(8,128)} %get-tuple-element.59), calls=%async_computation.3 | async-start | bytes 262144 | tf_op jit(solution)/shard_map/all_to_all | solution.py:32
  75.1 12.9 %all-to-all-start.4 = ((f32[32,8,128]{2,1,0:T(8,128)}), f32[32,8,128]{2,1,0:T(8,128)S(1)}, u32[]{:S(2)}, u32[]{:S(2)}) async-start(f32[32,8,128]{2,1,0:T(8,128)} %get-tuple-element.63), calls=%async_computation.4 | async-start | bytes 262144 | tf_op jit(solution)/shard_map/all_to_all | solution.py:32
  84.4 3.6 %copy-start.1 = (f32[192,256]{1,0:T(8,128)S(1)}, f32[192,256]{1,0:T(8,128)}, u32[]{:S(2)}) copy-start(f32[192,256]{1,0:T(8,128)} %load_ref.1) | copy-start | bytes 589828
  84.4 3.6 %copy-start.11 = (s32[8,128]{1,0:T(8,128)S(1)}, s32[8,128]{1,0:T(8,128)}, u32[]{:S(2)}) copy-start(s32[8,128]{1,0:T(8,128)} %sub_cell.1) | copy-start | bytes 12292
  84.4 3.6 %copy-start.12 = (s32[8,128]{1,0:T(8,128)S(1)}, s32[8,128]{1,0:T(8,128)}, u32[]{:S(2)}) copy-start(s32[8,128]{1,0:T(8,128)} %sub_face.1) | copy-start | bytes 12292
  88.0 15.6 %copy-start.13 = (s32[8,128]{1,0:T(8,128)S(1)}, s32[8,128]{1,0:T(8,128)}, u32[]{:S(2)}) copy-start(s32[8,128]{1,0:T(8,128)} %owner_ref.1) | copy-start | bytes 12292

commit v4 on v3

v4 whole, which is shorter than its diff:
```python
import functools

import jax
import jax.numpy as jnp
from jax import lax
from jax.experimental import pallas as pl
from jax.experimental.pallas import tpu as pltpu
from jax.sharding import PartitionSpec as P

REACH = 4
SWEEPS = 2
LANES = 128
WIDE = 2 * LANES
OWN = 32
EDGE = 16
TALL = 24
NOWHERE = 126

relaxation = 0.7
scale_down = 16.0
pad_code = 16368

f32 = jnp.float32
bf16 = jnp.bfloat16
i32 = jnp.int32


def neighbour_offsets():
    return [step + 1 for step in range(REACH)] + [-(step + 1) for step in range(REACH)]


def exchange(packed):
    return lax.all_to_all(packed, "dom", 0, 0, tiled=True)


def pack(place, sign, rows, pack_ref, out_ref):
    count = out_ref.shape[0]
    pack_ref[...] = jnp.zeros_like(pack_ref)
    for slot, offset in enumerate(neighbour_offsets()):
        target = place + sign * offset
        at = jnp.where((target >= 0) & (target < count), target, count)
        for number, row in enumerate(rows[slot]):
            pack_ref[at, number : number + 1, :] = row
    out_ref[...] = pack_ref[:count]


def landed(place, sign, got_ref, number):
    count = got_ref.shape[0]
    rows = []
    for offset in neighbour_offsets():
        source = place - sign * offset
        row = got_ref[jnp.clip(source, 0, count - 1), number : number + 1, :]
        there = jnp.broadcast_to((source >= 0) & (source < count), row.shape)
        rows.append(jnp.where(there, row, 0.0))
    return rows


def landed_wide(place, sign, got_ref, part):
    halves = [
        jnp.concatenate(landed(place, sign, got_ref, 2 * part + half), 0) for half in range(2)
    ]
    return jnp.concatenate(halves, 1)


def match16(row, count):
    width = row.shape[1]
    wide = jnp.broadcast_to(row.astype(f32), (16, width)).astype(bf16)
    numbers = lax.broadcasted_iota(i32, (count, width), 0).astype(f32).astype(bf16)
    numbers = numbers.reshape(count // 16, 16, width)
    return numbers == wide[None]


def one_hot(row, count):
    mask = match16(row, count)
    ones = jnp.ones(mask.shape, bf16)
    return jnp.where(mask, ones, jnp.zeros_like(ones)).reshape(count, row.shape[1])


def spread16(mask, row):
    wide = jnp.broadcast_to(row, (16, row.shape[1])).astype(bf16)[None]
    out = jnp.where(mask, jnp.broadcast_to(wide, mask.shape), jnp.zeros(mask.shape, bf16))
    return out.reshape(mask.shape[0] * 16, row.shape[1])


def pieces(x):
    high = x.astype(bf16)
    return high, (x - high.astype(f32)).astype(bf16)


def gather(table, tall, parts, where_ref, lane_ref, sums_ref):
    count = where_ref.shape[0]
    width = where_ref.shape[1]
    numbers = lax.broadcasted_iota(i32, (tall, width), 0)

    def body(block, carry):
        start = pl.multiple_of(block * 8, 8)
        for j in range(8):
            hot = one_hot(lane_ref[pl.ds(start + j, 1), :], LANES)
            found = jnp.dot(table, jnp.concatenate([hot, hot], 0), preferred_element_type=f32)
            mask = numbers == jnp.broadcast_to(where_ref[pl.ds(start + j, 1), :], numbers.shape)
            for part in range(parts):
                kept = jnp.where(mask, found[part * tall : (part + 1) * tall], 0.0)
                kept = jnp.sum(kept.reshape(tall // 8, 8, width), 0)
                for half in range(width // LANES):
                    sums_ref[half, pl.ds(part * count * 8 + start * 8 + j * 8, 8), :] = kept[
                        :, half * LANES : (half + 1) * LANES
                    ]
        return carry

    lax.fori_loop(0, count // 8, body, 0)


def gathered(sums_ref, count, part):
    totals = []
    for half in range(sums_ref.shape[0]):
        rows = [sums_ref[half, pl.ds(part * count * 8 + s, count, stride=8), :] for s in range(8)]
        while len(rows) > 1:
            rows = [a + b for a, b in zip(rows[::2], rows[1::2])]
        totals.append(rows[0])
    return jnp.concatenate(totals, 1)


def halves(x):
    return [x[:, :LANES], x[:, LANES:]]


def rows_and_columns(where, lane):
    return where >> 1, (where & 1) * LANES + lane


def scatter(high_ref, low_ref, rows, row_ref, column_ref, sum_ref, deep):
    count = row_ref.shape[0]
    sum_ref[...] = jnp.zeros_like(sum_ref)

    def body(block, carry):
        start = pl.multiple_of(block * 8, 8)
        for first in range(0, 8, deep):
            steps = range(first, first + deep)
            masks = [match16(row_ref[pl.ds(start + j, 1), :], rows) for j in steps]
            hot = jnp.concatenate(
                [one_hot(column_ref[pl.ds(start + j, 1), :], WIDE) for j in steps], 1
            )
            stacked = [
                jnp.concatenate(
                    [
                        spread16(mask, piece_ref[pl.ds(part * count + start + j, 1), :])
                        for mask, j in zip(masks, steps)
                    ],
                    1,
                )
                for piece_ref in (high_ref, low_ref)
                for part in range(3)
            ]
            sum_ref[...] += lax.dot_general(
                jnp.concatenate(stacked, 0),
                hot,
                (((1,), (1,)), ((), ())),
                preferred_element_type=f32,
            )
        return carry

    lax.fori_loop(0, count // 8, body, 0)


def split32(x):
    high = x.astype(bf16).astype(f32)
    return high, x - high


def add_pieces(sums):
    half = sums.shape[0] // 2
    return sums[:half] + sums[half:]


def scatter_few(values, rows, where, lane, scratch):
    high_ref, low_ref, row_ref, column_ref, sum_ref = scratch
    row_ref[...], column_ref[...] = rows_and_columns(where, lane)
    for part in range(3):
        high_ref[part * 8 : part * 8 + 8, :], low_ref[part * 8 : part * 8 + 8, :] = split32(
            values[part]
        )
    scatter(high_ref, low_ref, rows, row_ref, column_ref, sum_ref, 8)
    return add_pieces(sum_ref[...])


def few(rows):
    return [((24, WIDE), f32)] * 2 + [((8, WIDE), i32)] * 2 + [((6 * rows, WIDE), f32)]


def spread_hanging(held, weight, rows, where, lane, scratch):
    both = jnp.concatenate([held, held], 1)
    values = [weight * both[part : part + 1] for part in range(3)]
    return scatter_few(values, rows, where, lane, scratch)


def sum_masters(table, tall, weight, where_ref, lane_ref, sums_ref):
    gather(table, tall, 3, where_ref, lane_ref, sums_ref)
    totals = []
    for part in range(3):
        left, right = halves(weight * gathered(sums_ref, 8, part))
        totals.append(jnp.sum(left + right, 0, keepdims=True))
    return totals


def fill_table(x_ref, out_ref):
    count = x_ref.shape[1] // WIDE
    for part in range(3):
        out_ref[part * OWN + count : (part + 1) * OWN, :] = jnp.zeros((OWN - count, WIDE), f32)
    for row in range(count):
        block = x_ref[:, row * WIDE : (row + 1) * WIDE]
        for part in range(3):
            out_ref[part * OWN + row : part * OWN + row + 1, :] = block[part : part + 1]


def tall_table(tab_refs, half_rows, tall_ref):
    tall = up8(half_rows)
    tall_ref[...] = jnp.zeros_like(tall_ref)
    for number, tab_ref in enumerate(tab_refs):
        for part in range(3):
            for half_row in range(half_rows):
                row, half = part * OWN + half_row // 2, half_row % 2
                at = (3 * number + part) * tall + half_row
                tall_ref[at : at + 1, :] = tab_ref[
                    row : row + 1, half * LANES : (half + 1) * LANES
                ]
    return jnp.concatenate(pieces(tall_ref[...]), 1)


def up8(count):
    return -(-count // 8) * 8


def export_rows(table, tall, parts, where_ref, lane_ref, sums_ref):
    gather(table, tall, parts, where_ref, lane_ref, sums_ref)
    rows = [[] for _ in range(2 * REACH)]
    for part in range(parts):
        for tile in halves(gathered(sums_ref, 8, part)):
            for slot in range(2 * REACH):
                rows[slot].append(tile[slot : slot + 1])
    return rows


def copy_in(pairs, sems):
    copies = [
        pltpu.make_async_copy(source, target, sems.at[number])
        for number, (source, target) in enumerate(pairs)
    ]
    for copy in copies:
        copy.start()
    for copy in copies:
        copy.wait()


def first_export(
    place_ref, adjoint_hbm, primal_hbm, list_hbm, tab_a, tab_p, where_ref, lane_ref,
    out_ref, pack_ref, adjoint_ref, primal_ref, list_ref, tall_ref, sums_ref, sems,
):
    copy_in(
        [(adjoint_hbm, adjoint_ref), (primal_hbm, primal_ref), (list_hbm, list_ref)], sems
    )
    owned = adjoint_ref.shape[1]
    fill_table(adjoint_ref, tab_a)
    fill_table(primal_ref, tab_p)
    codes = list_ref[...]
    node = lax.rem(17 * codes + lax.broadcasted_iota(i32, codes.shape, 1), owned)
    where_ref[...] = node >> 7
    lane_ref[...] = node & 127
    half_rows = owned // LANES
    table = tall_table([tab_a, tab_p], half_rows, tall_ref)
    rows = export_rows(table, up8(half_rows), 6, where_ref, lane_ref, sums_ref)
    pack(place_ref[0], 1, rows, pack_ref, out_ref)


def setup(
    connect_hbm, node_hbm, master_hbm, weight_hbm, source_hbm, inverse_hbm,
    own_where, own_row, edge_where, edge_row, lane_ref, column_ref, edge_column, master_own, master_edge,
    master_lane, weight_out,
    tab_source, tab_inverse,
    connect_ref, node_ref, master_ref, weight_ref, source_ref, inverse_ref, map_ref, tall_ref, sums_ref,
    sems,
):
    copy_in(
        [
            (connect_hbm, connect_ref),
            (node_hbm, node_ref),
            (master_hbm, master_ref),
            (weight_hbm, weight_ref),
            (source_hbm, source_ref),
            (inverse_hbm, inverse_ref),
        ],
        sems,
    )
    owned = source_ref.shape[1]
    extent = owned + 2 * REACH * WIDE
    fill_table(source_ref, tab_source)
    fill_table(inverse_ref, tab_inverse)
    codes = master_ref[...]
    master = lax.rem(17 * codes + 8 * lax.broadcasted_iota(i32, codes.shape, 1), extent)
    count = codes.shape[0] // 2
    master = jnp.concatenate([master[:count], master[count:]], 1)
    weight = weight_ref[...]
    weight_out[...] = jnp.concatenate([weight[:count], weight[count:]], 1)
    last = owned // LANES
    where = master >> 7
    master_own[...] = jnp.where(where < last, where, NOWHERE)
    master_edge[...] = jnp.where(where < last, NOWHERE, where - last)
    master_lane[...] = master & 127

    codes = node_ref[...]
    node = jnp.where(codes == pad_code, extent, lax.rem(13 * codes, owned))
    slot = (lax.broadcasted_iota(i32, codes.shape, 1) + 1).astype(f32)
    map_ref[...] = lax.dot_general(
        spread16(match16(node >> 8, OWN), slot),
        one_hot(node & 255, WIDE),
        (((1,), (1,)), ((), ())),
        preferred_element_type=f32,
    )

    codes = connect_ref[...]
    cells = lax.broadcasted_iota(i32, codes.shape, 1)
    slots = lax.rem(27 * cells + 17 * codes, extent)
    own_where[...] = slots >> 7
    lane_ref[...] = slots & 127
    tall_ref[...] = jnp.zeros_like(tall_ref)
    for half_row in range(last):
        row, half = half_row // 2, half_row % 2
        tall_ref[half_row : half_row + 1, :] = map_ref[
            row : row + 1, half * LANES : (half + 1) * LANES
        ]
    table = jnp.concatenate(pieces(tall_ref[...]), 1)
    gather(table, tall_ref.shape[0], 1, own_where, lane_ref, sums_ref)
    slot = gathered(sums_ref, codes.shape[0], 0).astype(i32)
    where = slots >> 7
    hanging = slot > 0
    outside = where >= last
    lane = jnp.where(hanging, slot - 1, slots & 127)
    lane_ref[...] = lane
    where_own = jnp.where(hanging | outside, NOWHERE, where)
    own_where[...] = where_own
    own_row[...], column_ref[...] = rows_and_columns(where_own, lane)
    where_edge = jnp.where(hanging, 4 * REACH, jnp.where(outside, where - last, NOWHERE))
    edge_where[...] = where_edge
    edge_row[...], edge_column[...] = rows_and_columns(where_edge, lane)


def own_gather(
    half_rows, tab_ref, where_ref, lane_ref, master_where, master_lane, weight_ref, cells_ref,
    hang_ref, tall_ref, sums_ref,
):
    table = tall_table([tab_ref], half_rows, tall_ref)
    tall = up8(half_rows)
    found = sum_masters(table, tall, weight_ref[...], master_where, master_lane, sums_ref)
    for part in range(3):
        hang_ref[part : part + 1, :] = found[part]
    gather(table, tall, 3, where_ref, lane_ref, sums_ref)
    count = where_ref.shape[0]
    for part in range(3):
        cells_ref[part * count : (part + 1) * count, :] = gathered(sums_ref, count, part)


def edge_gather(
    place, got_ref, first, cells_ref, hang_ref, where_ref, lane_ref, master_where, master_lane,
    weight_ref, edge_ref, sums_ref, out_ref,
):
    slots = 2 * REACH
    edge_ref[...] = jnp.zeros_like(edge_ref)
    for part in range(3):
        for half in range(2):
            lines = landed(place, 1, got_ref, 2 * (first + part) + half)
            for slot in range(slots):
                at = part * TALL + 2 * slot + half
                edge_ref[at : at + 1, :] = lines[slot]
    table = jnp.concatenate(pieces(edge_ref[...]), 1)
    found = sum_masters(table, TALL, weight_ref[...], master_where, master_lane, sums_ref)
    for part in range(3):
        at = part * TALL + 2 * slots
        edge_ref[at : at + 1, :] = found[part] + hang_ref[part : part + 1, :]
    table = jnp.concatenate(pieces(edge_ref[...]), 1)
    gather(table, TALL, 3, where_ref, lane_ref, sums_ref)
    count = where_ref.shape[0]
    for part in range(3):
        rows = slice(part * count, (part + 1) * count)
        out_ref[rows, :] = cells_ref[rows, :] + gathered(sums_ref, count, part)


def edge_product(
    place_ref, got_ref, cells_ref, hang_ref, where_ref, lane_ref, master_where, master_lane,
    weight_ref, row_ref, column_ref, modulus_ref, stiffness_ref, out_ref,
    image_ref, held_ref, pack_ref, edge_ref, sums_ref, full_ref, low_ref, sum_ref, *scratch,
):
    place = place_ref[0]
    edge_gather(
        place, got_ref, 0, cells_ref, hang_ref, where_ref, lane_ref,
        master_where, master_lane, weight_ref, edge_ref, sums_ref, full_ref,
    )
    image = modulus_ref[...] * lax.dot_general(
        stiffness_ref[...],
        full_ref[...],
        (((0,), (0,)), ((), ())),
        precision=lax.Precision.HIGHEST,
        preferred_element_type=f32,
    )
    image_ref[...] = image
    full_ref[...], low_ref[...] = split32(image)
    scatter(full_ref, low_ref, EDGE, row_ref, column_ref, sum_ref, 2)
    sums = add_pieces(sum_ref[...])
    slots = 2 * REACH
    held = jnp.concatenate(
        [sums[part * EDGE + slots : part * EDGE + slots + 1, :LANES] for part in range(3)], 0
    )
    held_ref[...] = held
    sums += spread_hanging(
        held, weight_ref[...], EDGE, master_where[...], master_lane[...], scratch
    )
    rows = [
        [
            sums[part * EDGE + slot : part * EDGE + slot + 1, half * LANES : (half + 1) * LANES]
            for part in range(3)
            for half in range(2)
        ]
        for slot in range(slots)
    ]
    pack(place, -1, rows, pack_ref, out_ref)


def own_sums(
    image_ref, held_ref, row_ref, column_ref, master_where, master_lane, weight_ref,
    tab_ref, source_ref, inverse_ref, out_ref, high_ref, low_ref, sum_ref, *scratch,
):
    high_ref[...], low_ref[...] = split32(image_ref[...])
    scatter(high_ref, low_ref, OWN, row_ref, column_ref, sum_ref, 8)
    applied = add_pieces(sum_ref[...]) + spread_hanging(
        held_ref[...], weight_ref[...], OWN, master_where[...], master_lane[...], scratch
    )
    out_ref[...] = tab_ref[...] + relaxation * inverse_ref[...] * (source_ref[...] - applied)


def update(
    half_rows, place_ref, got_ref, where_ref, lane_ref, partial_ref, inverse_ref,
    out_ref, tab_ref, *rest,
):
    *final_ref, pack_ref, tall_ref, sums_ref = rest[:-5]
    place = place_ref[0]
    values = [landed_wide(place, -1, got_ref, part) for part in range(3)]
    returned = scatter_few(values, OWN, where_ref[...], lane_ref[...], rest[-5:])
    tab_ref[...] = partial_ref[...] - relaxation * inverse_ref[...] * returned
    table = tall_table([tab_ref], half_rows, tall_ref)
    rows = export_rows(table, up8(half_rows), 3, where_ref, lane_ref, sums_ref)
    pack(place, 1, rows, pack_ref, out_ref)
    if final_ref:
        final_ref = final_ref[0]
        for row in range(final_ref.shape[1] // WIDE):
            for part in range(3):
                final_ref[part : part + 1, row * WIDE : (row + 1) * WIDE] = tab_ref[
                    part * OWN + row : part * OWN + row + 1, :
                ]


def primal_product(
    place_ref, got_ref, cells_ref, hang_ref, where_ref, lane_ref, master_where,
    master_lane, weight_ref, modulus_ref, stiffness_ref, out_ref, edge_ref, sums_ref, full_ref,
):
    edge_gather(
        place_ref[0], got_ref, 3, cells_ref, hang_ref, where_ref, lane_ref,
        master_where, master_lane, weight_ref, edge_ref, sums_ref, full_ref,
    )
    out_ref[...] = modulus_ref[...] * jnp.dot(
        stiffness_ref[...],
        full_ref[...],
        precision=lax.Precision.HIGHEST,
        preferred_element_type=f32,
    )


def fluxes(
    place_ref, got_ref, cells_ref, hang_ref, where_ref, lane_ref, master_where,
    master_lane, weight_ref, ku_ref, load_ref, sub_cell, sub_face, out_ref,
    term_ref, pack_ref, edge_ref, sums_ref, full_ref, tall_ref, code_ref, few_ref,
):
    place = place_ref[0]
    edge_gather(
        place, got_ref, 0, cells_ref, hang_ref, where_ref, lane_ref,
        master_where, master_lane, weight_ref, edge_ref, sums_ref, full_ref,
    )
    cells = full_ref[...]
    ku = ku_ref[...]
    term_ref[...] = jnp.sum(cells * (load_ref[...] - ku), 0, keepdims=True)
    face = lax.broadcasted_iota(i32, (8, ku.shape[0]), 0)
    node = lax.broadcasted_iota(i32, (8, ku.shape[0]), 1) & 63
    index = jnp.where(face < 2, node >> 4, jnp.where(face < 4, (node >> 2) & 3, node & 3))
    member = jnp.where((face < 6) & (index == 3 * (face & 1)), 1.0, 0.0).astype(f32)
    flux = jnp.dot(
        member, ku * cells, precision=lax.Precision.HIGHEST, preferred_element_type=f32
    )
    tall_ref[...] = jnp.zeros_like(tall_ref)
    for number in range(6):
        for half in range(2):
            at = 2 * number + half
            tall_ref[at : at + 1, :] = flux[
                number : number + 1, half * LANES : (half + 1) * LANES
            ]
    cell = sub_cell[...]
    code_ref[:8, :] = 2 * sub_face[...] + (cell >> 7)
    code_ref[8:, :] = cell & 127
    table = jnp.concatenate(pieces(tall_ref[...]), 1)
    gather(table, 16, 1, code_ref.at[:8, :], code_ref.at[8:, :], few_ref)
    found = gathered(few_ref, 8, 0)
    rows = [[found[slot : slot + 1]] for slot in range(2 * REACH)]
    pack(place, 1, rows, pack_ref, out_ref)


def collect(place_ref, got_ref, owner_ref, term_ref, out_ref):
    count = term_ref.shape[1]
    got = jnp.concatenate(landed(place_ref[0], 1, got_ref, 0), 1)
    hot = jnp.concatenate(
        [one_hot(owner_ref[slot : slot + 1, :], count) for slot in range(2 * REACH)], 1
    )
    values = jnp.concatenate(
        [jnp.broadcast_to(x, (16, got.shape[1])).astype(bf16) for x in split32(got)], 0
    )
    sums = lax.dot_general(values, hot, (((1,), (1,)), ((), ())), preferred_element_type=f32)
    face_term = sums[0:1] + sums[16:17]
    out_ref[...] = (jnp.abs(term_ref[...]) + jnp.abs(face_term)) / scale_down


SMALL = pl.BlockSpec(memory_space=pltpu.SMEM)
FAST = pl.BlockSpec(memory_space=pltpu.VMEM)
FAR = pl.BlockSpec(memory_space=pl.ANY)


def away(*arrays):
    return [pltpu.with_memory_space_constraint(x, pltpu.HBM) for x in arrays]


def call(kernel, outs, scratch=(), specs=None, sems=0):
    scratch = [pltpu.VMEM(shape, kind) for shape, kind in scratch]
    if sems:
        scratch.append(pltpu.SemaphoreType.DMA((sems,)))

    def run(*args):
        return pl.pallas_call(
            kernel,
            out_shape=[jax.ShapeDtypeStruct(shape, kind) for shape, kind in outs],
            in_specs=specs or [SMALL] + [FAST] * (len(args) - 1),
            scratch_shapes=scratch,
            compiler_params=pltpu.CompilerParams(vmem_limit_bytes=40 * 1024 * 1024),
        )(*args)

    return run


def local(
    adjoint_start,
    adjoint_source,
    inverse_diagonal,
    primal_field,
    cell_load,
    modulus,
    stiffness,
    connectivity,
    hang_node,
    hang_master,
    hang_weight,
    ghost_lists,
    subface_cell,
    subface_face,
    subface_owner,
):
    slots = 2 * REACH
    local_values, cell_count = cell_load.shape
    nodes = connectivity.shape[0]
    half_rows = adjoint_start.shape[1] // LANES
    moduli = modulus.reshape(1, cell_count)
    place = lax.axis_index("dom").reshape(1).astype(i32)
    table = ((3 * OWN, WIDE), f32)
    index = ((nodes, cell_count), i32)
    cells_shape = ((local_values, cell_count), f32)
    hang_shape = ((3, hang_node.shape[0]), f32)
    master_shape = ((8, WIDE), i32)

    count = lax.axis_size("dom")

    def packed(height):
        return [((count, height, LANES), f32)]

    def room(height):
        return ((count + 1, height, LANES), f32)

    tall = up8(half_rows)
    few_sums = ((2, 3 * 64, LANES), f32)
    many_sums = ((2, local_values * 8, LANES), f32)
    own_tall = ((3 * tall, LANES), f32)
    edge = [((3 * TALL, LANES), f32), many_sums, cells_shape]
    tab, tab_primal, list_where, list_lane, blocks = call(
        first_export,
        [table, table] + [(ghost_lists.shape, i32)] * 2 + packed(16),
        [
            room(16),
            (adjoint_start.shape, f32),
            (primal_field.shape, f32),
            (ghost_lists.shape, i32),
            ((6 * tall, LANES), f32),
            ((2, 6 * 64, LANES), f32),
        ],
        [SMALL, FAR, FAR, FAR],
        sems=3,
    )(place, *away(adjoint_start, primal_field, ghost_lists))
    ghosts = first_ghosts = exchange(blocks)
    far = (
        connectivity, hang_node.reshape(1, -1), hang_master, hang_weight, adjoint_source,
        inverse_diagonal,
    )
    (
        own_where, own_row, edge_where, edge_row, lane, own_column, edge_column, master_own,
        master_edge, master_lane, weight, source, inverse,
    ) = call(
        setup,
        [index] * 7 + [master_shape] * 3 + [((8, WIDE), f32), table, table],
        [(x.shape, x.dtype) for x in far]
        + [((OWN, WIDE), f32), ((tall, LANES), f32), ((2, nodes * 8, LANES), f32)],
        [FAR] * 6,
        sems=6,
    )(*away(*far))

    def gather_own(values):
        return call(
            functools.partial(own_gather, half_rows),
            [cells_shape, hang_shape],
            [own_tall, many_sums],
            specs=[FAST] * 6,
        )(values, own_where, lane, master_own, master_lane, weight)

    on_edge = (edge_where, lane, master_edge, master_lane, weight)
    for sweep in range(SWEEPS):
        cells, hang = gather_own(tab)
        if sweep == 1:
            (ku,) = call(primal_product, [cells_shape], edge)(
                place, first_ghosts, *primal_cells, *on_edge, moduli, stiffness
            )
            cells, ku = lax.optimization_barrier((cells, ku))
        blocks, image, held = call(
            edge_product,
            packed(8) + [cells_shape, hang_shape],
            [room(8)] + edge + [cells_shape, ((6 * EDGE, WIDE), f32)] + few(EDGE),
        )(place, ghosts, cells, hang, *on_edge, edge_row, edge_column, moduli, stiffness)
        returned = exchange(blocks)
        (partial,) = call(
            own_sums,
            [table],
            [cells_shape, cells_shape, ((6 * OWN, WIDE), f32)] + few(OWN),
            specs=[FAST] * 10,
        )(image, held, own_row, own_column, master_own, master_lane, weight, tab, source, inverse)
        if sweep == 0:
            tab_primal, image = lax.optimization_barrier((tab_primal, image))
            primal_cells = gather_own(tab_primal)
            partial, *primal_cells = lax.optimization_barrier((partial, *primal_cells))
        last = sweep == SWEEPS - 1
        blocks, tab, *final = call(
            functools.partial(update, half_rows),
            packed(8) + [table] + ([(adjoint_start.shape, f32)] if last else []),
            [room(8), own_tall, few_sums] + few(OWN),
        )(place, returned, list_where, list_lane, partial, inverse)
        ghosts = exchange(blocks)
    cells, hang = gather_own(tab)
    blocks, term = call(
        fluxes,
        packed(1) + [((1, cell_count), f32)],
        [room(1)]
        + edge
        + [
            ((16, LANES), f32),
            ((16, subface_cell.shape[1]), i32),
            ((1, 64, LANES), f32),
        ],
    )(place, ghosts, cells, hang, *on_edge, ku, cell_load, subface_cell, subface_face)
    received = exchange(blocks)
    (indicator,) = call(collect, [((1, cell_count), f32)])(
        place, received, subface_owner, term
    )
    return (final[0], indicator.reshape(cell_count))


def solution(mesh):
    placed = (
        P(None, "dom"),
        P(None, "dom"),
        P(None, "dom"),
        P(None, "dom"),
        P(None, "dom"),
        P("dom"),
        P(),
        P(None, "dom"),
        P("dom"),
        P(None, "dom"),
        P(None, "dom"),
        P(None, "dom"),
        P(None, "dom"),
        P(None, "dom"),
        P(None, "dom"),
    )
    return jax.shard_map(
        local, mesh=mesh, in_specs=placed, out_specs=(P(None, "dom"), P("dom")), check_vma=False
    )
```

time: 105 us -> 105 us (level)
  starting transfers between devices: 17.9 us -> 23.3 us
  Pallas kernels: 54.1 us -> 58.2 us
  blocking collectives: 12.6 us -> 8.85 us
  local copies, waits for them, and re-layouts: 3.82 us -> 0.71 us
  waiting for transfers between devices: 15.1 us -> 12.4 us
    all_to_all x5, starting transfers between devices: 17.9 us -> 23.3 us  [exchange(): return lax.all_to_all(packed, 'dom', 0, 0, tiled=True)]
    pallas_call x15, Pallas kernels: 54.1 us -> 58.2 us  [run(): pl.pallas_call(kernel, out_shape=[jax.ShapeDtypeStruct(shape, kind) for s...]
    all_to_all x1, blocking collectives: 12.6 us -> 8.85 us  [exchange(): return lax.all_to_all(packed, 'dom', 0, 0, tiled=True)]
    unnamed x30 -> x12, local copies, waits for them, and re-layouts: 3.82 us -> 0.71 us
    all_to_all x5, waiting for transfers between devices: 15.1 us -> 12.4 us  [exchange(): return lax.all_to_all(packed, 'dom', 0, 0, tiled=True)]
  transfers between devices with their start and end apart: 5 -> 5, of which waited for: 4 -> 4; matrix products, arithmetic and copies ran while one was open for 0% -> 0% of each run, Pallas kernels for 28% -> 30%
where the time goes in v4:
time: 105 us; the launch traced here: 104 us
  Pallas kernels  58.2 us (55%)
  starting transfers between devices  23.3 us (22%)
  waiting for transfers between devices  12.4 us (12%)
  blocking collectives  8.85 us (8%)
    pallas_call x15, Pallas kernels, run(): pl.pallas_call(kernel, out_shape=[jax.ShapeDtypeStruct(shape, kind) for s...  58.2 us
    all_to_all x5, starting transfers between devices, exchange(): return lax.all_to_all(packed, 'dom', 0, 0, tiled=True)  23.3 us
    all_to_all x5, waiting for transfers between devices, exchange(): return lax.all_to_all(packed, 'dom', 0, 0, tiled=True)  12.4 us
    all_to_all x1, blocking collectives, exchange(): return lax.all_to_all(packed, 'dom', 0, 0, tiled=True)  8.85 us
  transfers between devices with their start and end apart: 5, of which 4 were waited for; matrix products, arithmetic and copies ran while one was open for 0% of the time, Pallas kernels for 30%

profile of v4, /device:TPU:0, one launch (start us, length us, event | category | flops | bytes accessed | tf_op | source)
XLA Modules:
  0.0 104.3 jit_solution(10208507589304159692)
XLA Ops:
  0.6 2.4 %shard_map.158 = (f32[96,256]{1,0:T(8,128)S(1)}, f32[96,256]{1,0:T(8,128)S(1)}, s32[8,256]{1,0:T(8,128)S(1)}, s32[8,256]{1,0:T(8,128)S(1)}, f32[32,16,128]{2,1,0:T(8,128)}) custom-call(s32[1]{0:T(128)} %bitcast.place_ref, f32[3,6912]{1,0:T(4,128)} %adjoint_hbm.1, f32[3,6912]{1,0:T(4,128)} %primal_hbm.1, s32[8,256]{1,0:T(8,128)} %list_hbm.1), custom_call_target="tpu_custom_call" | custom-call | tf_op jit(solution)/shard_map/pallas_call | solution.py:541
  3.1 7.3 %all-to-all-start = ((f32[32,16,128]{2,1,0:T(8,128)}), f32[32,16,128]{2,1,0:T(8,128)S(1)}, u32[]{:S(2)}, u32[]{:S(2)}) async-start(f32[32,16,128]{2,1,0:T(8,128)} %get-tuple-element.47), calls=%async_computation | async-start | bytes 524288 | tf_op jit(solution)/shard_map/all_to_all | solution.py:33
  10.4 3.9 %shard_map.159 = (s32[64,256]{1,0:T(8,128)S(1)}, s32[64,256]{1,0:T(8,128)S(1)}, s32[64,256]{1,0:T(8,128)S(1)}, s32[64,256]{1,0:T(8,128)S(1)}, s32[64,256]{1,0:T(...) custom-call(s32[64,256]{1,0:T(8,128)} %connect_hbm.1, ...), custom_call_target="tpu_custom_call" | custom-call | tf_op jit(solution)/shard_map/pallas_call | solution.py:541
  14.3 0.0 copy-start
  14.3 3.5 %shard_map.160 = (f32[192,256]{1,0:T(8,128)S(1)}, f32[3,128]{1,0:T(4,128)S(1)}) custom-call(f32[96,256]{1,0:T(8,128)S(1)} %get-tuple-element.48.tab_ref, s32[64,256]{1,0:T(8,128)S(1)} %get-tuple-element.49.where_ref, s32[64,256]{1,0:T(8,128)S(1)} %get-tuple-element.50.lane_ref, s32[8,256]{1,0:T(8,128)S(1)} %get-tuple-element.51.master_where, ...), custom_call_target="tpu_custom_call" | custom-call | tf_op jit(solution)/shard_map/pallas_call | solution.py:541
  17.9 3.1 %all-to-all-done.got_ref = f32[32,16,128]{2,1,0:T(8,128)S(1)} async-done(((f32[32,16,128]{2,1,0:T(8,128)}), f32[32,16,128]{2,1,0:T(8,128)S(1)}, u32[]{:S(2)}, u32[]{:S(2)}) %all-to-all-start) | async-done | bytes 262176 | tf_op jit(solution)/shard_map/all_to_all | solution.py:33
  21.0 0.0 copy-start.2
  21.0 0.0 copy-done
  21.0 0.7 copy-done.2
  21.6 8.3 %shard_map.161 = (f32[32,8,128]{2,1,0:T(8,128)}, f32[192,256]{1,0:T(8,128)S(1)}, f32[3,128]{1,0:T(4,128)S(1)}) custom-call(s32[1]{0:T(128)} %bitcast.place_ref, f32[32,16,128]{2,1,0:T(8,128)S(1)} %all-to-all-done.got_ref, f32[192,256]{1,0:T(8,128)S(1)} %get-tuple-element.54.cells_ref, f32[3,128]{1,0:T(4,128)S(1)} %get-tuple-element.55.hang_ref, ...), custom_call_target="tpu_custom_call" | custom-call | tf_op jit(solution)/shard_map/pallas_call | solution.py:541
  30.0 2.7 %all-to-all-start.1 = ((f32[32,8,128]{2,1,0:T(8,128)}), f32[32,8,128]{2,1,0:T(8,128)S(1)}, u32[]{:S(2)}, u32[]{:S(2)}) async-start(f32[32,8,128]{2,1,0:T(8,128)} %get-tuple-element.60), calls=%async_computation.1 | async-start | bytes 262144 | tf_op jit(solution)/shard_map/all_to_all | solution.py:33
  32.7 3.5 %shard_map.163 = (f32[192,256]{1,0:T(8,128)S(1)}, f32[3,128]{1,0:T(4,128)S(1)}) custom-call(f32[96,256]{1,0:T(8,128)S(1)} %get-tuple-element.70.tab_ref, s32[64,256]{1,0:T(8,128)S(1)} %get-tuple-element.49.where_ref, s32[64,256]{1,0:T(8,128)S(1)} %get-tuple-element.50.lane_ref, s32[8,256]{1,0:T(8,128)S(1)} %get-tuple-element.51.master_where, ...), custom_call_target="tpu_custom_call" | custom-call | tf_op jit(solution)/shard_map/pallas_call | solution.py:541
  36.2 4.6 %shard_map.162.partial_ref = f32[96,256]{1,0:T(8,128)S(1)} custom-call(f32[192,256]{1,0:T(8,128)S(1)} %get-tuple-element.63.image_ref, f32[3,128]{1,0:T(4,128)S(1)} %get-tuple-element.64.held_ref, s32[64,256]{1,0:T(8,128)S(1)} %get-tuple-element.65.row_ref, s32[64,256]{1,0:T(8,128)S(1)} %get-tuple-element.66.column_ref, ...), custom_call_target="tpu_custom_call" | custom-call | tf_op jit(solution)/shard_map/pallas_call | solution.py:541
  40.9 0.0 all-to-all-done.1.got_ref
  40.9 1.9 %shard_map.164 = (f32[32,8,128]{2,1,0:T(8,128)}, f32[96,256]{1,0:T(8,128)S(1)}) custom-call(s32[1]{0:T(128)} %bitcast.place_ref, f32[32,8,128]{2,1,0:T(8,128)S(1)} %all-to-all-done.1.got_ref, s32[8,256]{1,0:T(8,128)S(1)} %get-tuple-element.61.where_ref, s32[8,256]{1,0:T(8,128)S(1)} %get-tuple-element.62.lane_ref, f32[96,256]{1,0:T(8,128)S(1)} %shard_map.162.partial_ref, ...), custom_call_target="tpu_custom_call" | custom-call | tf_op jit(solution)/shard_map/pallas_call | solution.py:541
  42.8 5.8 %all-to-all-start.2 = ((f32[32,8,128]{2,1,0:T(8,128)}), f32[32,8,128]{2,1,0:T(8,128)S(1)}, u32[]{:S(2)}, u32[]{:S(2)}) async-start(f32[32,8,128]{2,1,0:T(8,128)} %get-tuple-element.74), calls=%async_computation.2 | async-start | bytes 262144 | tf_op jit(solution)/shard_map/all_to_all | solution.py:33
  48.6 3.4 %shard_map.166.ku_ref = f32[192,256]{1,0:T(8,128)S(1)} custom-call(s32[1]{0:T(128)} %bitcast.place_ref, f32[32,16,128]{2,1,0:T(8,128)S(1)} %all-to-all-done.got_ref, f32[192,256]{1,0:T(8,128)S(1)} %get-tuple-element.77.cells_ref, f32[3,128]{1,0:T(4,128)S(1)} %get-tuple-element.78.hang_ref, s32[64,256]{1,0:T(8,128)S(1)} %get-tuple-element.56.where_ref, ...), custom_call_target="tpu_custom_call" | custom-call | tf_op jit(solution)/shard_map/pallas_call | solution.py:541
  52.1 3.5 %shard_map.165 = (f32[192,256]{1,0:T(8,128)S(1)}, f32[3,128]{1,0:T(4,128)S(1)}) custom-call(f32[96,256]{1,0:T(8,128)S(1)} %get-tuple-element.75.tab_ref, s32[64,256]{1,0:T(8,128)S(1)} %get-tuple-element.49.where_ref, s32[64,256]{1,0:T(8,128)S(1)} %get-tuple-element.50.lane_ref, s32[8,256]{1,0:T(8,128)S(1)} %get-tuple-element.51.master_where, ...), custom_call_target="tpu_custom_call" | custom-call | tf_op jit(solution)/shard_map/pallas_call | solution.py:541
  55.6 1.2 %all-to-all-done.2.got_ref = f32[32,8,128]{2,1,0:T(8,128)S(1)} async-done(((f32[32,8,128]{2,1,0:T(8,128)}), f32[32,8,128]{2,1,0:T(8,128)S(1)}, u32[]{:S(2)}, u32[]{:S(2)}) %all-to-all-start.2) | async-done | bytes 131104 | tf_op jit(solution)/shard_map/all_to_all | solution.py:33
  56.9 8.3 %shard_map.167 = (f32[32,8,128]{2,1,0:T(8,128)}, f32[192,256]{1,0:T(8,128)S(1)}, f32[3,128]{1,0:T(4,128)S(1)}) custom-call(s32[1]{0:T(128)} %bitcast.place_ref, f32[32,8,128]{2,1,0:T(8,128)S(1)} %all-to-all-done.2.got_ref, f32[192,256]{1,0:T(8,128)S(1)} %get-tuple-element.79.cells_ref, f32[3,128]{1,0:T(4,128)S(1)} %get-tuple-element.80.hang_ref, ...), custom_call_target="tpu_custom_call" | custom-call | tf_op jit(solution)/shard_map/pallas_call | solution.py:541
  65.2 4.8 %all-to-all-start.3 = ((f32[32,8,128]{2,1,0:T(8,128)}), f32[32,8,128]{2,1,0:T(8,128)S(1)}, u32[]{:S(2)}, u32[]{:S(2)}) async-start(f32[32,8,128]{2,1,0:T(8,128)} %get-tuple-element.81), calls=%async_computation.3 | async-start | bytes 262144 | tf_op jit(solution)/shard_map/all_to_all | solution.py:33
  70.0 4.6 %shard_map.168.partial_ref = f32[96,256]{1,0:T(8,128)S(1)} custom-call(f32[192,256]{1,0:T(8,128)S(1)} %get-tuple-element.82.image_ref, f32[3,128]{1,0:T(4,128)S(1)} %get-tuple-element.83.held_ref, s32[64,256]{1,0:T(8,128)S(1)} %get-tuple-element.65.row_ref, s32[64,256]{1,0:T(8,128)S(1)} %get-tuple-element.66.column_ref, ...), custom_call_target="tpu_custom_call" | custom-call | tf_op jit(solution)/shard_map/pallas_call | solution.py:541
  74.6 3.4 %all-to-all-done.3.got_ref = f32[32,8,128]{2,1,0:T(8,128)S(1)} async-done(((f32[32,8,128]{2,1,0:T(8,128)}), f32[32,8,128]{2,1,0:T(8,128)S(1)}, u32[]{:S(2)}, u32[]{:S(2)}) %all-to-all-start.3) | async-done | bytes 131104 | tf_op jit(solution)/shard_map/all_to_all | solution.py:33
  78.0 1.9 %shard_map.169 = (f32[32,8,128]{2,1,0:T(8,128)}, f32[96,256]{1,0:T(8,128)S(1)}, f32[3,6912]{1,0:T(4,128)}) custom-call(s32[1]{0:T(128)} %bitcast.place_ref, f32[32,8,128]{2,1,0:T(8,128)S(1)} %all-to-all-done.3.got_ref, s32[8,256]{1,0:T(8,128)S(1)} %get-tuple-element.61.where_ref, s32[8,256]{1,0:T(8,128)S(1)} %get-tuple-element.62.lane_ref, ...), custom_call_target="tpu_custom_call" | custom-call | tf_op jit(solution)/shard_map/pallas_call | solution.py:541
  80.0 0.0 copy-start.1
  80.0 2.7 %all-to-all-start.4 = ((f32[32,8,128]{2,1,0:T(8,128)}), f32[32,8,128]{2,1,0:T(8,128)S(1)}, u32[]{:S(2)}, u32[]{:S(2)}) async-start(f32[32,8,128]{2,1,0:T(8,128)} %get-tuple-element.85), calls=%async_computation.4 | async-start | bytes 262144 | tf_op jit(solution)/shard_map/all_to_all | solution.py:33
  82.7 0.0 copy-start.3
  82.7 0.0 copy-start.4
  82.7 3.5 %shard_map.170 = (f32[192,256]{1,0:T(8,128)S(1)}, f32[3,128]{1,0:T(4,128)S(1)}) custom-call(f32[96,256]{1,0:T(8,128)S(1)} %get-tuple-element.86.tab_ref, s32[64,256]{1,0:T(8,128)S(1)} %get-tuple-element.49.where_ref, s32[64,256]{1,0:T(8,128)S(1)} %get-tuple-element.50.lane_ref, s32[8,256]{1,0:T(8,128)S(1)} %get-tuple-element.51.master_where, ...), custom_call_target="tpu_custom_call" | custom-call | tf_op jit(solution)/shard_map/pallas_call | solution.py:541
  86.2 4.7 %all-to-all-done.4.got_ref = f32[32,8,128]{2,1,0:T(8,128)S(1)} async-done(((f32[32,8,128]{2,1,0:T(8,128)}), f32[32,8,128]{2,1,0:T(8,128)S(1)}, u32[]{:S(2)}, u32[]{:S(2)}) %all-to-all-start.4) | async-done | bytes 131104 | tf_op jit(solution)/shard_map/all_to_all | solution.py:33
  90.9 0.0 copy-done.1
  90.9 0.0 copy-done.3
  90.9 0.0 copy-done.4
  90.9 0.0 copy-start.5
  90.9 3.7 %shard_map.171 = (f32[32,1,128]{2,1,0:T(1,128)S(1)}, f32[1,256]{1,0:T(1,128)S(1)}) custom-call(s32[1]{0:T(128)} %bitcast.place_ref, f32[32,8,128]{2,1,0:T(8,128)S(1)} %all-to-all-done.4.got_ref, f32[192,256]{1,0:T(8,128)S(1)} %get-tuple-element.87.cells_ref, f32[3,128]{1,0:T(4,128)S(1)} %get-tuple-element.88.hang_ref, ...), custom_call_target="tpu_custom_call" | custom-call | tf_op jit(solution)/shard_map/pallas_call | solution.py:541
  94.6 8.8 %all_to_all.30.got_ref = f32[32,1,128]{2,1,0:T(1,128)S(1)} all-to-all(f32[32,1,128]{2,1,0:T(1,128)S(1)} %get-tuple-element.90), channel_id=1, replica_groups=mesh['dom'=32] {'dom'}, dimensions={0} | all-to-all | bytes 32768 | tf_op jit(solution)/shard_map/all_to_all | solution.py:33
  103.5 0.0 copy-done.5
  103.5 0.8 shard_map.172
Async XLA Ops:
  3.1 17.9 %all-to-all-start = ((f32[32,16,128]{2,1,0:T(8,128)}), f32[32,16,128]{2,1,0:T(8,128)S(1)}, u32[]{:S(2)}, u32[]{:S(2)}) async-start(f32[32,16,128]{2,1,0:T(8,128)} %get-tuple-element.47), calls=%async_computation | async-start | bytes 524288 | tf_op jit(solution)/shard_map/all_to_all | solution.py:33
  14.3 6.7 %copy-start = (f32[192,192]{1,0:T(8,128)S(1)}, f32[192,192]{1,0:T(8,128)}, u32[]{:S(2)}) copy-start(f32[192,192]{1,0:T(8,128)} %stiffness_ref.5) | copy-start | bytes 442372
  21.0 0.7 copy-start.2
  30.0 11.0 %all-to-all-start.1 = ((f32[32,8,128]{2,1,0:T(8,128)}), f32[32,8,128]{2,1,0:T(8,128)S(1)}, u32[]{:S(2)}, u32[]{:S(2)}) async-start(f32[32,8,128]{2,1,0:T(8,128)} %get-tuple-element.60), calls=%async_computation.1 | async-start | bytes 262144 | tf_op jit(solution)/shard_map/all_to_all | solution.py:33
  42.8 14.0 %all-to-all-start.2 = ((f32[32,8,128]{2,1,0:T(8,128)}), f32[32,8,128]{2,1,0:T(8,128)S(1)}, u32[]{:S(2)}, u32[]{:S(2)}) async-start(f32[32,8,128]{2,1,0:T(8,128)} %get-tuple-element.74), calls=%async_computation.2 | async-start | bytes 262144 | tf_op jit(solution)/shard_map/all_to_all | solution.py:33
  65.2 12.9 %all-to-all-start.3 = ((f32[32,8,128]{2,1,0:T(8,128)}), f32[32,8,128]{2,1,0:T(8,128)S(1)}, u32[]{:S(2)}, u32[]{:S(2)}) async-start(f32[32,8,128]{2,1,0:T(8,128)} %get-tuple-element.81), calls=%async_computation.3 | async-start | bytes 262144 | tf_op jit(solution)/shard_map/all_to_all | solution.py:33
  80.0 10.9 %copy-start.1 = (f32[192,256]{1,0:T(8,128)S(1)}, f32[192,256]{1,0:T(8,128)}, u32[]{:S(2)}) copy-start(f32[192,256]{1,0:T(8,128)} %load_ref.1) | copy-start | bytes 589828
  80.0 10.9 %all-to-all-start.4 = ((f32[32,8,128]{2,1,0:T(8,128)}), f32[32,8,128]{2,1,0:T(8,128)S(1)}, u32[]{:S(2)}, u32[]{:S(2)}) async-start(f32[32,8,128]{2,1,0:T(8,128)} %get-tuple-element.85), calls=%async_computation.4 | async-start | bytes 262144 | tf_op jit(solution)/shard_map/all_to_all | solution.py:33
  82.7 8.2 %copy-start.3 = (s32[8,128]{1,0:T(8,128)S(1)}, s32[8,128]{1,0:T(8,128)}, u32[]{:S(2)}) copy-start(s32[8,128]{1,0:T(8,128)} %sub_cell.1) | copy-start | bytes 12292
  82.7 8.2 %copy-start.4 = (s32[8,128]{1,0:T(8,128)S(1)}, s32[8,128]{1,0:T(8,128)}, u32[]{:S(2)}) copy-start(s32[8,128]{1,0:T(8,128)} %sub_face.1) | copy-start | bytes 12292
  90.9 12.6 %copy-start.5 = (s32[8,128]{1,0:T(8,128)S(1)}, s32[8,128]{1,0:T(8,128)}, u32[]{:S(2)}) copy-start(s32[8,128]{1,0:T(8,128)} %owner_ref.1) | copy-start | bytes 12292

commit v5 on v4

v5 whole, which is shorter than its diff:
```python
import jax
import jax.numpy as jnp
from jax import lax
from jax.experimental import pallas as pl
from jax.experimental.pallas import tpu as pltpu
from jax.sharding import PartitionSpec as P

REACH = 4
SWEEPS = 2
LANES = 128
WIDE = 2 * LANES
OWN = 32
EDGE = 16
NOWHERE = 63

relaxation = 0.7
scale_down = 16.0
pad_code = 16368

f32 = jnp.float32
bf16 = jnp.bfloat16
i32 = jnp.int32


def neighbour_offsets():
    return [step + 1 for step in range(REACH)] + [-(step + 1) for step in range(REACH)]


def exchange(packed):
    return lax.all_to_all(packed, "dom", 0, 0, tiled=True)


def pack(place, sign, rows, pack_ref, out_ref):
    count = out_ref.shape[0]
    pack_ref[...] = jnp.zeros_like(pack_ref)
    for slot, offset in enumerate(neighbour_offsets()):
        target = place + sign * offset
        at = jnp.where((target >= 0) & (target < count), target, count)
        for number, row in enumerate(rows[slot]):
            pack_ref[at, number : number + 1, :] = row
    out_ref[...] = pack_ref[:count]


def landed(place, sign, got_ref, number):
    count = got_ref.shape[0]
    rows = []
    for offset in neighbour_offsets():
        source = place - sign * offset
        row = got_ref[jnp.clip(source, 0, count - 1), number : number + 1, :]
        there = jnp.broadcast_to((source >= 0) & (source < count), row.shape)
        rows.append(jnp.where(there, row, 0.0))
    return rows


def landed_wide(place, sign, got_ref, part):
    halves = [
        jnp.concatenate(landed(place, sign, got_ref, 2 * part + half), 0) for half in range(2)
    ]
    return jnp.concatenate(halves, 1)


def match16(row, count):
    width = row.shape[1]
    wide = jnp.broadcast_to(row.astype(f32), (16, width)).astype(bf16)
    numbers = lax.broadcasted_iota(i32, (count, width), 0).astype(f32).astype(bf16)
    numbers = numbers.reshape(count // 16, 16, width)
    return numbers == wide[None]


def one_hot(row, count):
    mask = match16(row, count)
    ones = jnp.ones(mask.shape, bf16)
    return jnp.where(mask, ones, jnp.zeros_like(ones)).reshape(count, row.shape[1])


def spread16(mask, row):
    wide = jnp.broadcast_to(row, (16, row.shape[1])).astype(bf16)[None]
    out = jnp.where(mask, jnp.broadcast_to(wide, mask.shape), jnp.zeros(mask.shape, bf16))
    return out.reshape(mask.shape[0] * 16, row.shape[1])


def pieces(x):
    high = x.astype(bf16)
    return high, (x - high.astype(f32)).astype(bf16)


def build_hot(column_ref, hot_ref):
    def body(block, carry):
        start = pl.multiple_of(block * 8, 8)
        for j in range(8):
            at = pl.multiple_of((start + j) * WIDE, WIDE)
            hot_ref[pl.ds(at, WIDE), :] = one_hot(column_ref[pl.ds(start + j, 1), :], WIDE)
        return carry

    lax.fori_loop(0, column_ref.shape[0] // 8, body, 0)


def hot_of(hot_ref, number):
    return hot_ref[pl.ds(pl.multiple_of(number * WIDE, WIDE), WIDE), :]


def two_pieces(table):
    return jnp.concatenate(pieces(table), 0)


def gather(table, rows, parts, row_ref, hot_ref, sums_ref):
    count, width = row_ref.shape
    numbers = lax.broadcasted_iota(i32, (rows, width), 0)
    half_table = parts * rows

    def body(block, carry):
        start = pl.multiple_of(block * 8, 8)
        for j in range(8):
            found = jnp.dot(table, hot_of(hot_ref, start + j), preferred_element_type=f32)
            found = found[:half_table] + found[half_table:]
            mask = numbers == jnp.broadcast_to(row_ref[pl.ds(start + j, 1), :], numbers.shape)
            for part in range(parts):
                kept = jnp.where(mask, found[part * rows : (part + 1) * rows], 0.0)
                kept = jnp.sum(kept.reshape(rows // 8, 8, width), 0)
                for half in range(width // LANES):
                    sums_ref[half, pl.ds(part * count * 8 + start * 8 + j * 8, 8), :] = kept[
                        :, half * LANES : (half + 1) * LANES
                    ]
        return carry

    lax.fori_loop(0, count // 8, body, 0)


def gathered(sums_ref, count, part):
    totals = []
    for half in range(sums_ref.shape[0]):
        rows = [sums_ref[half, pl.ds(part * count * 8 + s, count, stride=8), :] for s in range(8)]
        while len(rows) > 1:
            rows = [a + b for a, b in zip(rows[::2], rows[1::2])]
        totals.append(rows[0])
    return jnp.concatenate(totals, 1)


def halves(x):
    return [x[:, :LANES], x[:, LANES:]]


def scatter(high_ref, low_ref, rows, row_ref, hot_ref, sum_ref):
    count = row_ref.shape[0]
    sum_ref[...] = jnp.zeros_like(sum_ref)

    def body(block, carry):
        start = pl.multiple_of(block * 8, 8)
        masks = [match16(row_ref[pl.ds(start + j, 1), :], rows) for j in range(8)]
        hot = jnp.concatenate([hot_of(hot_ref, start + j) for j in range(8)], 1)
        stacked = [
            jnp.concatenate(
                [
                    spread16(mask, piece_ref[pl.ds(part * count + start + j, 1), :])
                    for j, mask in enumerate(masks)
                ],
                1,
            )
            for piece_ref in (high_ref, low_ref)
            for part in range(3)
        ]
        sum_ref[...] += lax.dot_general(
            jnp.concatenate(stacked, 0), hot, (((1,), (1,)), ((), ())), preferred_element_type=f32
        )
        return carry

    lax.fori_loop(0, count // 8, body, 0)


def split32(x):
    high = x.astype(bf16).astype(f32)
    return high, x - high


def add_pieces(sums):
    half = sums.shape[0] // 2
    return sums[:half] + sums[half:]


def scatter_few(values, rows, row_ref, hot_ref, scratch):
    high_ref, low_ref, sum_ref = scratch
    for part in range(3):
        high_ref[part * 8 : part * 8 + 8, :], low_ref[part * 8 : part * 8 + 8, :] = split32(
            values[part]
        )
    scatter(high_ref, low_ref, rows, row_ref, hot_ref, sum_ref)
    return add_pieces(sum_ref[...])


def few(rows):
    return [((24, WIDE), f32)] * 2 + [((6 * rows, WIDE), f32)]


def spread_hanging(held, weight, rows, row_ref, hot_ref, scratch):
    both = jnp.concatenate([held, held], 1)
    values = [weight * both[part : part + 1] for part in range(3)]
    return scatter_few(values, rows, row_ref, hot_ref, scratch)


def sum_masters(table, rows, weight, row_ref, hot_ref, sums_ref):
    gather(table, rows, 3, row_ref, hot_ref, sums_ref)
    totals = []
    for part in range(3):
        left, right = halves(weight * gathered(sums_ref, 8, part))
        totals.append(jnp.sum(left + right, 0, keepdims=True))
    return totals


def fill_table(x_ref, out_ref):
    count = x_ref.shape[1] // WIDE
    for part in range(3):
        out_ref[part * OWN + count : (part + 1) * OWN, :] = jnp.zeros((OWN - count, WIDE), f32)
    for row in range(count):
        block = x_ref[:, row * WIDE : (row + 1) * WIDE]
        for part in range(3):
            out_ref[part * OWN + row : part * OWN + row + 1, :] = block[part : part + 1]


def export_rows(table, parts, row_ref, hot_ref, sums_ref):
    gather(table, OWN, parts, row_ref, hot_ref, sums_ref)
    rows = [[] for _ in range(2 * REACH)]
    for part in range(parts):
        for tile in halves(gathered(sums_ref, 8, part)):
            for slot in range(2 * REACH):
                rows[slot].append(tile[slot : slot + 1])
    return rows


def copy_in(pairs, sems):
    copies = [
        pltpu.make_async_copy(source, target, sems.at[number])
        for number, (source, target) in enumerate(pairs)
    ]
    for copy in copies:
        copy.start()
    for copy in copies:
        copy.wait()


def first_export(
    place_ref, adjoint_hbm, primal_hbm, list_hbm, tab_a, tab_p, row_ref, hot_ref,
    out_ref, pack_ref, adjoint_ref, primal_ref, list_ref, column_ref, sums_ref, sems,
):
    copy_in(
        [(adjoint_hbm, adjoint_ref), (primal_hbm, primal_ref), (list_hbm, list_ref)], sems
    )
    owned = adjoint_ref.shape[1]
    fill_table(adjoint_ref, tab_a)
    fill_table(primal_ref, tab_p)
    codes = list_ref[...]
    node = lax.rem(17 * codes + lax.broadcasted_iota(i32, codes.shape, 1), owned)
    row_ref[...] = node >> 8
    column_ref[...] = node & 255
    build_hot(column_ref, hot_ref)
    table = two_pieces(jnp.concatenate([tab_a[...], tab_p[...]], 0))
    rows = export_rows(table, 6, row_ref, hot_ref, sums_ref)
    pack(place_ref[0], 1, rows, pack_ref, out_ref)


def setup(
    connect_hbm, node_hbm, master_hbm, weight_hbm, source_hbm, inverse_hbm,
    own_row, edge_row, hot_ref, master_own, master_edge, master_hot, weight_out,
    tab_source, tab_inverse,
    connect_ref, node_ref, master_ref, weight_ref, source_ref, inverse_ref, column_ref,
    master_column, sums_ref, sems,
):
    copy_in(
        [
            (connect_hbm, connect_ref),
            (node_hbm, node_ref),
            (master_hbm, master_ref),
            (weight_hbm, weight_ref),
            (source_hbm, source_ref),
            (inverse_hbm, inverse_ref),
        ],
        sems,
    )
    owned = source_ref.shape[1]
    extent = owned + 2 * REACH * WIDE
    fill_table(source_ref, tab_source)
    fill_table(inverse_ref, tab_inverse)
    codes = master_ref[...]
    master = lax.rem(17 * codes + 8 * lax.broadcasted_iota(i32, codes.shape, 1), extent)
    count = codes.shape[0] // 2
    master = jnp.concatenate([master[:count], master[count:]], 1)
    weight = weight_ref[...]
    weight_out[...] = jnp.concatenate([weight[:count], weight[count:]], 1)
    last = owned // WIDE
    row = master >> 8
    master_own[...] = jnp.where(row < last, row, NOWHERE)
    master_edge[...] = jnp.where(row < last, NOWHERE, row - last)
    master_column[...] = master & 255
    build_hot(master_column, master_hot)

    codes = node_ref[...]
    node = jnp.where(codes == pad_code, extent, lax.rem(13 * codes, owned))
    slot = (lax.broadcasted_iota(i32, codes.shape, 1) + 1).astype(f32)
    table = lax.dot_general(
        spread16(match16(node >> 8, OWN), slot),
        one_hot(node & 255, WIDE),
        (((1,), (1,)), ((), ())),
        preferred_element_type=f32,
    ).astype(bf16)

    codes = connect_ref[...]
    cells = lax.broadcasted_iota(i32, codes.shape, 1)
    slots = lax.rem(27 * cells + 17 * codes, extent)
    own_row[...] = slots >> 8
    column_ref[...] = slots & 255
    numbers = lax.broadcasted_iota(i32, (OWN, WIDE), 0)

    def body(block, carry):
        start = pl.multiple_of(block * 8, 8)
        for j in range(8):
            hot = one_hot(column_ref[pl.ds(start + j, 1), :], WIDE)
            found = jnp.dot(table, hot, preferred_element_type=f32)
            mask = numbers == jnp.broadcast_to(own_row[pl.ds(start + j, 1), :], numbers.shape)
            kept = jnp.sum(jnp.where(mask, found, 0.0).reshape(OWN // 8, 8, WIDE), 0)
            for half in range(2):
                sums_ref[half, pl.ds(start * 8 + j * 8, 8), :] = halves(kept)[half]
        return carry

    lax.fori_loop(0, codes.shape[0] // 8, body, 0)
    slot = gathered(sums_ref, codes.shape[0], 0).astype(i32)
    row = slots >> 8
    hanging = slot > 0
    outside = row >= last
    own_row[...] = jnp.where(hanging | outside, NOWHERE, row)
    edge_row[...] = jnp.where(hanging, 2 * REACH, jnp.where(outside, row - last, NOWHERE))
    column_ref[...] = jnp.where(hanging, slot - 1, slots & 255)
    build_hot(column_ref, hot_ref)


def own_gather(
    tab_ref, row_ref, hot_ref, master_row, master_hot, weight_ref, cells_ref, hang_ref, sums_ref
):
    table = two_pieces(tab_ref[...])
    found = sum_masters(table, OWN, weight_ref[...], master_row, master_hot, sums_ref)
    for part in range(3):
        hang_ref[part : part + 1, :] = found[part]
    gather(table, OWN, 3, row_ref, hot_ref, sums_ref)
    count = row_ref.shape[0]
    for part in range(3):
        cells_ref[part * count : (part + 1) * count, :] = gathered(sums_ref, count, part)


def edge_gather(
    place, got_ref, first, cells_ref, hang_ref, row_ref, hot_ref, master_row, master_hot,
    weight_ref, edge_ref, sums_ref, out_ref,
):
    slots = 2 * REACH
    edge_ref[...] = jnp.zeros_like(edge_ref)
    for part in range(3):
        edge_ref[part * EDGE : part * EDGE + slots, :] = landed_wide(
            place, 1, got_ref, first + part
        )
    found = sum_masters(
        two_pieces(edge_ref[...]), EDGE, weight_ref[...], master_row, master_hot, sums_ref
    )
    for part in range(3):
        at = part * EDGE + slots
        edge_ref[at : at + 1, :LANES] = found[part] + hang_ref[part : part + 1, :]
    gather(two_pieces(edge_ref[...]), EDGE, 3, row_ref, hot_ref, sums_ref)
    count = row_ref.shape[0]
    for part in range(3):
        rows = slice(part * count, (part + 1) * count)
        out_ref[rows, :] = cells_ref[rows, :] + gathered(sums_ref, count, part)


def edge_product(
    place_ref, got_ref, cells_ref, hang_ref, row_ref, hot_ref, master_row, master_hot,
    weight_ref, modulus_ref, stiffness_ref, out_ref,
    image_ref, held_ref, pack_ref, edge_ref, sums_ref, full_ref, low_ref, sum_ref, *scratch,
):
    place = place_ref[0]
    edge_gather(
        place, got_ref, 0, cells_ref, hang_ref, row_ref, hot_ref,
        master_row, master_hot, weight_ref, edge_ref, sums_ref, full_ref,
    )
    image = modulus_ref[...] * lax.dot_general(
        stiffness_ref[...],
        full_ref[...],
        (((0,), (0,)), ((), ())),
        precision=lax.Precision.HIGHEST,
        preferred_element_type=f32,
    )
    image_ref[...] = image
    full_ref[...], low_ref[...] = split32(image)
    scatter(full_ref, low_ref, EDGE, row_ref, hot_ref, sum_ref)
    sums = add_pieces(sum_ref[...])
    slots = 2 * REACH
    held = jnp.concatenate(
        [sums[part * EDGE + slots : part * EDGE + slots + 1, :LANES] for part in range(3)], 0
    )
    held_ref[...] = held
    sums += spread_hanging(held, weight_ref[...], EDGE, master_row, master_hot, scratch)
    rows = [
        [
            sums[part * EDGE + slot : part * EDGE + slot + 1, half * LANES : (half + 1) * LANES]
            for part in range(3)
            for half in range(2)
        ]
        for slot in range(slots)
    ]
    pack(place, -1, rows, pack_ref, out_ref)


def own_sums(
    image_ref, held_ref, row_ref, hot_ref, master_row, master_hot, weight_ref,
    tab_ref, source_ref, inverse_ref, out_ref, high_ref, low_ref, sum_ref, *scratch,
):
    high_ref[...], low_ref[...] = split32(image_ref[...])
    scatter(high_ref, low_ref, OWN, row_ref, hot_ref, sum_ref)
    applied = add_pieces(sum_ref[...]) + spread_hanging(
        held_ref[...], weight_ref[...], OWN, master_row, master_hot, scratch
    )
    out_ref[...] = tab_ref[...] + relaxation * inverse_ref[...] * (source_ref[...] - applied)


def update(
    place_ref, got_ref, row_ref, hot_ref, partial_ref, inverse_ref,
    out_ref, tab_ref, *rest,
):
    *final_ref, pack_ref, sums_ref = rest[:-3]
    place = place_ref[0]
    values = [landed_wide(place, -1, got_ref, part) for part in range(3)]
    returned = scatter_few(values, OWN, row_ref, hot_ref, rest[-3:])
    tab_ref[...] = partial_ref[...] - relaxation * inverse_ref[...] * returned
    rows = export_rows(two_pieces(tab_ref[...]), 3, row_ref, hot_ref, sums_ref)
    pack(place, 1, rows, pack_ref, out_ref)
    if final_ref:
        final_ref = final_ref[0]
        for row in range(final_ref.shape[1] // WIDE):
            for part in range(3):
                final_ref[part : part + 1, row * WIDE : (row + 1) * WIDE] = tab_ref[
                    part * OWN + row : part * OWN + row + 1, :
                ]


def primal_product(
    place_ref, got_ref, cells_ref, hang_ref, row_ref, hot_ref, master_row,
    master_hot, weight_ref, modulus_ref, stiffness_ref, out_ref, edge_ref, sums_ref, full_ref,
):
    edge_gather(
        place_ref[0], got_ref, 3, cells_ref, hang_ref, row_ref, hot_ref,
        master_row, master_hot, weight_ref, edge_ref, sums_ref, full_ref,
    )
    out_ref[...] = modulus_ref[...] * jnp.dot(
        stiffness_ref[...],
        full_ref[...],
        precision=lax.Precision.HIGHEST,
        preferred_element_type=f32,
    )


def fluxes(
    place_ref, got_ref, cells_ref, hang_ref, row_ref, hot_ref, master_row,
    master_hot, weight_ref, ku_ref, load_ref, sub_cell, sub_face, out_ref,
    term_ref, pack_ref, edge_ref, sums_ref, full_ref, face_hot, few_ref,
):
    place = place_ref[0]
    edge_gather(
        place, got_ref, 0, cells_ref, hang_ref, row_ref, hot_ref,
        master_row, master_hot, weight_ref, edge_ref, sums_ref, full_ref,
    )
    cells = full_ref[...]
    ku = ku_ref[...]
    term_ref[...] = jnp.sum(cells * (load_ref[...] - ku), 0, keepdims=True)
    face = lax.broadcasted_iota(i32, (8, ku.shape[0]), 0)
    node = lax.broadcasted_iota(i32, (8, ku.shape[0]), 1) & 63
    index = jnp.where(face < 2, node >> 4, jnp.where(face < 4, (node >> 2) & 3, node & 3))
    member = jnp.where((face < 6) & (index == 3 * (face & 1)), 1.0, 0.0).astype(f32)
    flux = jnp.dot(
        member, ku * cells, precision=lax.Precision.HIGHEST, preferred_element_type=f32
    )
    build_hot(sub_cell, face_hot)
    gather(two_pieces(flux), 8, 1, sub_face, face_hot, few_ref)
    found = gathered(few_ref, 8, 0)
    rows = [[found[slot : slot + 1]] for slot in range(2 * REACH)]
    pack(place, 1, rows, pack_ref, out_ref)


def collect(place_ref, got_ref, owner_ref, term_ref, out_ref):
    count = term_ref.shape[1]
    got = jnp.concatenate(landed(place_ref[0], 1, got_ref, 0), 1)
    hot = jnp.concatenate(
        [one_hot(owner_ref[slot : slot + 1, :], count) for slot in range(2 * REACH)], 1
    )
    values = jnp.concatenate(
        [jnp.broadcast_to(x, (16, got.shape[1])).astype(bf16) for x in split32(got)], 0
    )
    sums = lax.dot_general(values, hot, (((1,), (1,)), ((), ())), preferred_element_type=f32)
    face_term = sums[0:1] + sums[16:17]
    out_ref[...] = (jnp.abs(term_ref[...]) + jnp.abs(face_term)) / scale_down


SMALL = pl.BlockSpec(memory_space=pltpu.SMEM)
FAST = pl.BlockSpec(memory_space=pltpu.VMEM)
FAR = pl.BlockSpec(memory_space=pl.ANY)


def away(*arrays):
    return [pltpu.with_memory_space_constraint(x, pltpu.HBM) for x in arrays]


def call(kernel, outs, scratch=(), specs=None, sems=0):
    scratch = [pltpu.VMEM(shape, kind) for shape, kind in scratch]
    if sems:
        scratch.append(pltpu.SemaphoreType.DMA((sems,)))

    def run(*args):
        return pl.pallas_call(
            kernel,
            out_shape=[jax.ShapeDtypeStruct(shape, kind) for shape, kind in outs],
            in_specs=specs or [SMALL] + [FAST] * (len(args) - 1),
            scratch_shapes=scratch,
            compiler_params=pltpu.CompilerParams(vmem_limit_bytes=24 * 1024 * 1024),
        )(*args)

    return run


def local(
    adjoint_start,
    adjoint_source,
    inverse_diagonal,
    primal_field,
    cell_load,
    modulus,
    stiffness,
    connectivity,
    hang_node,
    hang_master,
    hang_weight,
    ghost_lists,
    subface_cell,
    subface_face,
    subface_owner,
):
    slots = 2 * REACH
    local_values, cell_count = cell_load.shape
    nodes = connectivity.shape[0]
    moduli = modulus.reshape(1, cell_count)
    place = lax.axis_index("dom").reshape(1).astype(i32)
    table = ((3 * OWN, WIDE), f32)
    index = ((nodes, cell_count), i32)
    cells_shape = ((local_values, cell_count), f32)
    hang_shape = ((3, hang_node.shape[0]), f32)
    master_shape = ((8, WIDE), i32)

    count = lax.axis_size("dom")

    def packed(height):
        return [((count, height, LANES), f32)]

    def room(height):
        return ((count + 1, height, LANES), f32)

    few_sums = ((2, 3 * 64, LANES), f32)
    many_sums = ((2, local_values * 8, LANES), f32)
    few_hot = ((8 * WIDE, WIDE), bf16)
    edge = [((3 * EDGE, WIDE), f32), many_sums, cells_shape]
    tab, tab_primal, list_row, list_hot, blocks = call(
        first_export,
        [table, table, (ghost_lists.shape, i32), few_hot] + packed(16),
        [
            room(16),
            (adjoint_start.shape, f32),
            (primal_field.shape, f32),
            (ghost_lists.shape, i32),
            (ghost_lists.shape, i32),
            ((2, 6 * 64, LANES), f32),
        ],
        [SMALL, FAR, FAR, FAR],
        sems=3,
    )(place, *away(adjoint_start, primal_field, ghost_lists))
    ghosts = first_ghosts = exchange(blocks)
    far = (
        connectivity, hang_node.reshape(1, -1), hang_master, hang_weight, adjoint_source,
        inverse_diagonal,
    )
    (
        own_row, edge_row, hot, master_own, master_edge, master_hot, weight, source, inverse,
    ) = call(
        setup,
        [index, index, ((nodes * WIDE, cell_count), bf16), master_shape, master_shape, few_hot]
        + [((8, WIDE), f32), table, table],
        [(x.shape, x.dtype) for x in far]
        + [index, master_shape, ((2, nodes * 8, LANES), f32)],
        [FAR] * 6,
        sems=6,
    )(*away(*far))

    def gather_own(values):
        return call(own_gather, [cells_shape, hang_shape], [many_sums], specs=[FAST] * 6)(
            values, own_row, hot, master_own, master_hot, weight
        )

    on_edge = (edge_row, hot, master_edge, master_hot, weight)
    for sweep in range(SWEEPS):
        cells, hang = gather_own(tab)
        if sweep == 1:
            (ku,) = call(primal_product, [cells_shape], edge)(
                place, first_ghosts, *primal_cells, *on_edge, moduli, stiffness
            )
            cells, ku = lax.optimization_barrier((cells, ku))
        blocks, image, held = call(
            edge_product,
            packed(8) + [cells_shape, hang_shape],
            [room(8)] + edge + [cells_shape, ((6 * EDGE, WIDE), f32)] + few(EDGE),
        )(place, ghosts, cells, hang, *on_edge, moduli, stiffness)
        returned = exchange(blocks)
        (partial,) = call(
            own_sums,
            [table],
            [cells_shape, cells_shape, ((6 * OWN, WIDE), f32)] + few(OWN),
            specs=[FAST] * 10,
        )(image, held, own_row, hot, master_own, master_hot, weight, tab, source, inverse)
        if sweep == 0:
            tab_primal, image = lax.optimization_barrier((tab_primal, image))
            primal_cells = gather_own(tab_primal)
            partial, *primal_cells = lax.optimization_barrier((partial, *primal_cells))
        last = sweep == SWEEPS - 1
        blocks, tab, *final = call(
            update,
            packed(8) + [table] + ([(adjoint_start.shape, f32)] if last else []),
            [room(8), few_sums] + few(OWN),
        )(place, returned, list_row, list_hot, partial, inverse)
        ghosts = exchange(blocks)
    cells, hang = gather_own(tab)
    blocks, term = call(
        fluxes,
        packed(1) + [((1, cell_count), f32)],
        [room(1)]
        + edge
        + [((8 * WIDE, subface_cell.shape[1]), bf16), ((1, 64, LANES), f32)],
    )(place, ghosts, cells, hang, *on_edge, ku, cell_load, subface_cell, subface_face)
    received = exchange(blocks)
    (indicator,) = call(collect, [((1, cell_count), f32)])(
        place, received, subface_owner, term
    )
    return (final[0], indicator.reshape(cell_count))


def solution(mesh):
    placed = (
        P(None, "dom"),
        P(None, "dom"),
        P(None, "dom"),
        P(None, "dom"),
        P(None, "dom"),
        P("dom"),
        P(),
        P(None, "dom"),
        P("dom"),
        P(None, "dom"),
        P(None, "dom"),
        P(None, "dom"),
        P(None, "dom"),
        P(None, "dom"),
        P(None, "dom"),
    )
    return jax.shard_map(
        local, mesh=mesh, in_specs=placed, out_specs=(P(None, "dom"), P("dom")), check_vma=False
    )
```

time: 105 us -> 136 us (1.30)
  local copies, waits for them, and re-layouts: 0.71 us -> 33.2 us
  waiting for transfers between devices: 12.4 us -> 1.51 us
  starting transfers between devices: 23.3 us -> 30.4 us
  blocking collectives: 8.85 us -> 11.6 us
    unnamed x12 -> x42, local copies, waits for them, and re-layouts: 0.71 us -> 33.2 us
    all_to_all x5, waiting for transfers between devices: 12.4 us -> 1.51 us  [exchange(): return lax.all_to_all(packed, 'dom', 0, 0, tiled=True)]
    all_to_all x5, starting transfers between devices: 23.3 us -> 30.4 us  [exchange(): return lax.all_to_all(packed, 'dom', 0, 0, tiled=True)]
    all_to_all x1, blocking collectives: 8.85 us -> 11.6 us  [exchange(): return lax.all_to_all(packed, 'dom', 0, 0, tiled=True)]
  transfers between devices with their start and end apart: 5 -> 5, of which waited for: 4 -> 2; matrix products, arithmetic and copies ran while one was open for 0% -> 0% of each run, Pallas kernels for 30% -> 24%
where the time goes in v5:
time: 136 us; the launch traced here: 135 us
  Pallas kernels  57.7 us (42%)
  local copies, waits for them, and re-layouts  33.2 us (24%)
  starting transfers between devices  30.4 us (22%)
  blocking collectives  11.6 us (9%)
  waiting for transfers between devices  1.51 us (1%)
    pallas_call x15, Pallas kernels, run(): pl.pallas_call(kernel, out_shape=[jax.ShapeDtypeStruct(shape, kind) for s...  57.7 us
    unnamed x42, local copies, waits for them, and re-layouts  33.2 us
    all_to_all x5, starting transfers between devices, exchange(): return lax.all_to_all(packed, 'dom', 0, 0, tiled=True)  30.4 us
    all_to_all x1, blocking collectives, exchange(): return lax.all_to_all(packed, 'dom', 0, 0, tiled=True)  11.6 us
  transfers between devices with their start and end apart: 5, of which 2 were waited for; matrix products, arithmetic and copies ran while one was open for 0% of the time, Pallas kernels for 24%

profile of v5, /device:TPU:0, one launch (start us, length us, event | category | flops | bytes accessed | tf_op | source)
XLA Modules:
  0.0 135.3 jit_solution(4290539083584111434)
XLA Ops:
  0.6 0.0 copy-start.9
  0.6 0.0 copy-start.17
  0.7 2.5 %shard_map.158 = (f32[96,256]{1,0:T(8,128)S(1)}, f32[96,256]{1,0:T(8,128)S(1)}, s32[8,256]{1,0:T(8,128)S(1)}, bf16[2048,256]{1,0:T(8,128)(2,1)S(1)}, f32[32,16,128]{2,1,0:T(8,128)}) custom-call(s32[1]{0:T(128)} %bitcast.place_ref, f32[3,6912]{1,0:T(4,128)} %adjoint_hbm.1, f32[3,6912]{1,0:T(4,128)} %primal_hbm.1, s32[8,256]{1,0:T(8,128)} %list_hbm.1), custom_call_target="tpu_custom_call" | custom-call | tf_op jit(solution)/shard_map/pallas_call | solution.py:512
  3.1 0.0 copy-start.15
  3.2 7.3 %all-to-all-start = ((f32[32,16,128]{2,1,0:T(8,128)}), f32[32,16,128]{2,1,0:T(8,128)S(1)}, u32[]{:S(2)}, u32[]{:S(2)}) async-start(f32[32,16,128]{2,1,0:T(8,128)} %get-tuple-element.43), calls=%async_computation | async-start | bytes 524288 | tf_op jit(solution)/shard_map/all_to_all | solution.py:30
  10.5 5.0 %shard_map.159 = (s32[64,256]{1,0:T(8,128)S(1)}, s32[64,256]{1,0:T(8,128)S(1)}, bf16[16384,256]{1,0:T(8,128)(2,1)S(1)}, s32[8,256]{1,0:T(8,128)S(1)}, s32[8,256]...) custom-call(s32[64,256]{1,0:T(8,128)} %connect_hbm.1, ...), custom_call_target="tpu_custom_call" | custom-call | tf_op jit(solution)/shard_map/pallas_call | solution.py:512
  15.5 3.6 %shard_map.160 = (f32[192,256]{1,0:T(8,128)S(1)}, f32[3,128]{1,0:T(4,128)S(1)}) custom-call(f32[96,256]{1,0:T(8,128)S(1)} %get-tuple-element.44.tab_ref, s32[64,256]{1,0:T(8,128)S(1)} %get-tuple-element.45.row_ref, bf16[16384,256]{1,0:T(8,128)(2,1)S(1)} %get-tuple-element.46.hot_ref, s32[8,256]{1,0:T(8,128)S(1)} %get-tuple-element.47.master_row, ...), custom_call_target="tpu_custom_call" | custom-call | tf_op jit(solution)/shard_map/pallas_call | solution.py:512
  19.1 0.0 copy-start
  19.1 3.3 %copy-done = bf16[16384,256]{1,0:T(8,128)(2,1)} copy-done((bf16[16384,256]{1,0:T(8,128)(2,1)}, bf16[16384,256]{1,0:T(8,128)(2,1)S(1)}, u32[]{:S(2)}) %copy-start) | copy-done | bytes 8388632
  22.4 0.0 all-to-all-done.got_ref
  22.4 0.0 copy-done.9
  22.4 3.4 %copy-done.1 = bf16[16384,256]{1,0:T(8,128)(2,1)S(1)} copy-done((bf16[16384,256]{1,0:T(8,128)(2,1)S(1)}, bf16[16384,256]{1,0:T(8,128)(2,1)}, u32[]{:S(2)}) %copy-start.1) | copy-done | bytes 8388632
  25.8 8.2 %shard_map.161 = (f32[32,8,128]{2,1,0:T(8,128)}, f32[192,256]{1,0:T(8,128)S(1)}, f32[3,128]{1,0:T(4,128)S(1)}) custom-call(s32[1]{0:T(128)} %bitcast.place_ref, f32[32,16,128]{2,1,0:T(8,128)S(1)} %all-to-all-done.got_ref, f32[192,256]{1,0:T(8,128)S(1)} %get-tuple-element.50.cells_ref, f32[3,128]{1,0:T(4,128)S(1)} %get-tuple-element.51.hang_ref, ...), custom_call_target="tpu_custom_call" | custom-call | tf_op jit(solution)/shard_map/pallas_call | solution.py:512
  34.0 0.7 copy-done.11
  34.7 5.8 %all-to-all-start.1 = ((f32[32,8,128]{2,1,0:T(8,128)}), f32[32,8,128]{2,1,0:T(8,128)S(1)}, u32[]{:S(2)}, u32[]{:S(2)}) async-start(f32[32,8,128]{2,1,0:T(8,128)} %get-tuple-element.54), calls=%async_computation.1 | async-start | bytes 262144 | tf_op jit(solution)/shard_map/all_to_all | solution.py:30
  40.5 3.4 %copy-done.2 = bf16[16384,256]{1,0:T(8,128)(2,1)S(1)} copy-done((bf16[16384,256]{1,0:T(8,128)(2,1)S(1)}, bf16[16384,256]{1,0:T(8,128)(2,1)}, u32[]{:S(2)}) %copy-start.2) | copy-done | bytes 8388632
  43.9 0.9 copy-done.16
  44.8 3.6 %shard_map.163 = (f32[192,256]{1,0:T(8,128)S(1)}, f32[3,128]{1,0:T(4,128)S(1)}) custom-call(f32[96,256]{1,0:T(8,128)S(1)} %copy-done.16, s32[64,256]{1,0:T(8,128)S(1)} %get-tuple-element.45.row_ref, bf16[16384,256]{1,0:T(8,128)(2,1)S(1)} %copy-done.2, s32[8,256]{1,0:T(8,128)S(1)} %get-tuple-element.47.master_row, ...), custom_call_target="tpu_custom_call" | custom-call | tf_op jit(solution)/shard_map/pallas_call | solution.py:512
  48.4 4.6 %shard_map.162.partial_ref = f32[96,256]{1,0:T(8,128)S(1)} custom-call(f32[192,256]{1,0:T(8,128)S(1)} %copy-done.12, f32[3,128]{1,0:T(4,128)S(1)} %get-tuple-element.58.held_ref, s32[64,256]{1,0:T(8,128)S(1)} %get-tuple-element.45.row_ref, bf16[16384,256]{1,0:T(8,128)(2,1)S(1)} %copy-done.2, s32[8,256]{1,0:T(8,128)S(1)} %get-tuple-element.47.master_row, ...), custom_call_target="tpu_custom_call" | custom-call | tf_op jit(solution)/shard_map/pallas_call | solution.py:512
  53.0 0.0 all-to-all-done.1.got_ref
  53.0 1.2 shard_map.164
  54.2 0.6 copy-done.13
  54.9 5.8 %all-to-all-start.2 = ((f32[32,8,128]{2,1,0:T(8,128)}), f32[32,8,128]{2,1,0:T(8,128)S(1)}, u32[]{:S(2)}, u32[]{:S(2)}) async-start(f32[32,8,128]{2,1,0:T(8,128)} %copy-done.13), calls=%async_computation.2 | async-start | bytes 262144 | tf_op jit(solution)/shard_map/all_to_all | solution.py:30
  60.7 3.4 %copy-done.3 = bf16[16384,256]{1,0:T(8,128)(2,1)S(1)} copy-done((bf16[16384,256]{1,0:T(8,128)(2,1)S(1)}, bf16[16384,256]{1,0:T(8,128)(2,1)}, u32[]{:S(2)}) %copy-start.3) | copy-done | bytes 8388632
  64.1 3.3 %shard_map.166.ku_ref = f32[192,256]{1,0:T(8,128)S(1)} custom-call(s32[1]{0:T(128)} %bitcast.place_ref, f32[32,16,128]{2,1,0:T(8,128)S(1)} %all-to-all-done.got_ref, f32[192,256]{1,0:T(8,128)S(1)} %get-tuple-element.69.cells_ref, f32[3,128]{1,0:T(4,128)S(1)} %get-tuple-element.70.hang_ref, s32[64,256]{1,0:T(8,128)S(1)} %get-tuple-element.52.row_ref, ...), custom_call_target="tpu_custom_call" | custom-call | tf_op jit(solution)/shard_map/pallas_call | solution.py:512
  67.5 3.4 %copy-done.4 = bf16[16384,256]{1,0:T(8,128)(2,1)S(1)} copy-done((bf16[16384,256]{1,0:T(8,128)(2,1)S(1)}, bf16[16384,256]{1,0:T(8,128)(2,1)}, u32[]{:S(2)}) %copy-start.4) | copy-done | bytes 8388632
  70.8 3.6 %shard_map.165 = (f32[192,256]{1,0:T(8,128)S(1)}, f32[3,128]{1,0:T(4,128)S(1)}) custom-call(f32[96,256]{1,0:T(8,128)S(1)} %get-tuple-element.67.tab_ref, s32[64,256]{1,0:T(8,128)S(1)} %get-tuple-element.45.row_ref, bf16[16384,256]{1,0:T(8,128)(2,1)S(1)} %copy-done.4, s32[8,256]{1,0:T(8,128)S(1)} %get-tuple-element.47.master_row, ...), custom_call_target="tpu_custom_call" | custom-call | tf_op jit(solution)/shard_map/pallas_call | solution.py:512
  74.4 0.0 all-to-all-done.2.got_ref
  74.4 3.4 %copy-done.5 = bf16[16384,256]{1,0:T(8,128)(2,1)S(1)} copy-done((bf16[16384,256]{1,0:T(8,128)(2,1)S(1)}, bf16[16384,256]{1,0:T(8,128)(2,1)}, u32[]{:S(2)}) %copy-start.5) | copy-done | bytes 8388632
  77.8 7.6 %shard_map.167 = (f32[32,8,128]{2,1,0:T(8,128)S(1)}, f32[192,256]{1,0:T(8,128)S(1)}, f32[3,128]{1,0:T(4,128)S(1)}) custom-call(s32[1]{0:T(128)} %bitcast.place_ref, f32[32,8,128]{2,1,0:T(8,128)S(1)} %all-to-all-done.2.got_ref, f32[192,256]{1,0:T(8,128)S(1)} %get-tuple-element.71.cells_ref, f32[3,128]{1,0:T(4,128)S(1)} %get-tuple-element.72.hang_ref, ...), custom_call_target="tpu_custom_call" | custom-call | tf_op jit(solution)/shard_map/pallas_call | solution.py:512
  85.4 0.0 copy-start.14
  85.4 0.6 copy-done.14
  86.0 5.8 %all-to-all-start.3 = ((f32[32,8,128]{2,1,0:T(8,128)}), f32[32,8,128]{2,1,0:T(8,128)S(1)}, u32[]{:S(2)}, u32[]{:S(2)}) async-start(f32[32,8,128]{2,1,0:T(8,128)} %copy-done.14), calls=%async_computation.3 | async-start | bytes 262144 | tf_op jit(solution)/shard_map/all_to_all | solution.py:30
  91.9 3.4 %copy-done.6 = bf16[16384,256]{1,0:T(8,128)(2,1)S(1)} copy-done((bf16[16384,256]{1,0:T(8,128)(2,1)S(1)}, bf16[16384,256]{1,0:T(8,128)(2,1)}, u32[]{:S(2)}) %copy-start.6) | copy-done | bytes 8388632
  95.3 4.6 %shard_map.168.partial_ref = f32[96,256]{1,0:T(8,128)S(1)} custom-call(f32[192,256]{1,0:T(8,128)S(1)} %get-tuple-element.74.image_ref, f32[3,128]{1,0:T(4,128)S(1)} %get-tuple-element.75.held_ref, s32[64,256]{1,0:T(8,128)S(1)} %get-tuple-element.45.row_ref, bf16[16384,256]{1,0:T(8,128)(2,1)S(1)} %copy-done.6, s32[8,256]{1,0:T(8,128)S(1)} %get-tuple-element.47.master_row, ...), custom_call_target="tpu_custom_call" | custom-call | tf_op jit(solution)/shard_map/pallas_call | solution.py:512
  99.8 0.3 all-to-all-done.3.got_ref
  100.1 1.9 %shard_map.169 = (f32[32,8,128]{2,1,0:T(8,128)}, f32[96,256]{1,0:T(8,128)S(1)}, f32[3,6912]{1,0:T(4,128)}) custom-call(s32[1]{0:T(128)} %bitcast.place_ref, f32[32,8,128]{2,1,0:T(8,128)S(1)} %all-to-all-done.3.got_ref, s32[8,256]{1,0:T(8,128)S(1)} %get-tuple-element.55.row_ref, bf16[2048,256]{1,0:T(8,128)(2,1)S(1)} %get-tuple-element.56.hot_ref, ...), custom_call_target="tpu_custom_call" | custom-call | tf_op jit(solution)/shard_map/pallas_call | solution.py:512
  102.0 5.6 %all-to-all-start.4 = ((f32[32,8,128]{2,1,0:T(8,128)}), f32[32,8,128]{2,1,0:T(8,128)S(1)}, u32[]{:S(2)}, u32[]{:S(2)}) async-start(f32[32,8,128]{2,1,0:T(8,128)} %get-tuple-element.77), calls=%async_computation.4 | async-start | bytes 262144 | tf_op jit(solution)/shard_map/all_to_all | solution.py:30
  107.6 0.0 copy-start.7
  107.6 3.4 %copy-done.7 = bf16[16384,256]{1,0:T(8,128)(2,1)S(1)} copy-done((bf16[16384,256]{1,0:T(8,128)(2,1)S(1)}, bf16[16384,256]{1,0:T(8,128)(2,1)}, u32[]{:S(2)}) %copy-start.7) | copy-done | bytes 8388632
  111.0 3.6 %shard_map.170 = (f32[192,256]{1,0:T(8,128)S(1)}, f32[3,128]{1,0:T(4,128)S(1)}) custom-call(f32[96,256]{1,0:T(8,128)S(1)} %get-tuple-element.78.tab_ref, s32[64,256]{1,0:T(8,128)S(1)} %get-tuple-element.45.row_ref, bf16[16384,256]{1,0:T(8,128)(2,1)S(1)} %copy-done.7, s32[8,256]{1,0:T(8,128)S(1)} %get-tuple-element.47.master_row, ...), custom_call_target="tpu_custom_call" | custom-call | tf_op jit(solution)/shard_map/pallas_call | solution.py:512
  114.6 1.2 all-to-all-done.4.got_ref
  115.8 0.0 copy-done.18
  115.9 3.4 %copy-done.8 = bf16[16384,256]{1,0:T(8,128)(2,1)S(1)} copy-done((bf16[16384,256]{1,0:T(8,128)(2,1)S(1)}, bf16[16384,256]{1,0:T(8,128)(2,1)}, u32[]{:S(2)}) %copy-start.8) | copy-done | bytes 8388632
  119.2 3.6 %shard_map.171 = (f32[32,1,128]{2,1,0:T(1,128)S(1)}, f32[1,256]{1,0:T(1,128)S(1)}) custom-call(s32[1]{0:T(128)} %bitcast.place_ref, f32[32,8,128]{2,1,0:T(8,128)S(1)} %all-to-all-done.4.got_ref, f32[192,256]{1,0:T(8,128)S(1)} %get-tuple-element.79.cells_ref, f32[3,128]{1,0:T(4,128)S(1)} %get-tuple-element.80.hang_ref, ...), custom_call_target="tpu_custom_call" | custom-call | tf_op jit(solution)/shard_map/pallas_call | solution.py:512
  122.9 11.6 %all_to_all.30.got_ref = f32[32,1,128]{2,1,0:T(1,128)S(1)} all-to-all(f32[32,1,128]{2,1,0:T(1,128)S(1)} %get-tuple-element.82), channel_id=1, replica_groups=mesh['dom'=32] {'dom'}, dimensions={0} | all-to-all | bytes 32768 | tf_op jit(solution)/shard_map/all_to_all | solution.py:30
  134.4 0.0 copy-done.20
  134.4 0.8 shard_map.172
  (20 shorter events, 0.0 us)
Async XLA Ops:
  0.6 21.8 %copy-start.9 = (f32[192,192]{1,0:T(8,128)S(1)}, f32[192,192]{1,0:T(8,128)}, u32[]{:S(2)}) copy-start(f32[192,192]{1,0:T(8,128)} %stiffness_ref.5) | copy-start | bytes 442372
  0.6 21.7 %copy-start.17 = (f32[256]{0:T(256)S(1)}, f32[256]{0:T(256)}, u32[]{:S(2)}) copy-start(f32[256]{0:T(256)} %param.20) | copy-start | bytes 3076
  3.1 7.3 %copy-start.15 = (f32[96,256]{1,0:T(8,128)}, f32[96,256]{1,0:T(8,128)S(1)}, u32[]{:S(2)}) copy-start(f32[96,256]{1,0:T(8,128)S(1)} %get-tuple-element.62.tab_ref) | copy-start | bytes 294916
  3.2 19.2 %all-to-all-start = ((f32[32,16,128]{2,1,0:T(8,128)}), f32[32,16,128]{2,1,0:T(8,128)S(1)}, u32[]{:S(2)}, u32[]{:S(2)}) async-start(f32[32,16,128]{2,1,0:T(8,128)} %get-tuple-element.43), calls=%async_computation | async-start | bytes 524288 | tf_op jit(solution)/shard_map/all_to_all | solution.py:30
  19.1 3.3 %copy-start = (bf16[16384,256]{1,0:T(8,128)(2,1)}, bf16[16384,256]{1,0:T(8,128)(2,1)S(1)}, u32[]{:S(2)}) copy-start(bf16[16384,256]{1,0:T(8,128)(2,1)S(1)} %get-tuple-element.46.hot_ref) | copy-start | bytes 25165828
  22.4 3.4 %copy-start.1 = (bf16[16384,256]{1,0:T(8,128)(2,1)S(1)}, bf16[16384,256]{1,0:T(8,128)(2,1)}, u32[]{:S(2)}) copy-start(bf16[16384,256]{1,0:T(8,128)(2,1)} %copy-done) | copy-start | bytes 25165828
  34.0 0.7 copy-start.11
  34.7 18.3 %all-to-all-start.1 = ((f32[32,8,128]{2,1,0:T(8,128)}), f32[32,8,128]{2,1,0:T(8,128)S(1)}, u32[]{:S(2)}, u32[]{:S(2)}) async-start(f32[32,8,128]{2,1,0:T(8,128)} %get-tuple-element.54), calls=%async_computation.1 | async-start | bytes 262144 | tf_op jit(solution)/shard_map/all_to_all | solution.py:30
  40.5 3.4 %copy-start.2 = (bf16[16384,256]{1,0:T(8,128)(2,1)S(1)}, bf16[16384,256]{1,0:T(8,128)(2,1)}, u32[]{:S(2)}) copy-start(bf16[16384,256]{1,0:T(8,128)(2,1)} %copy-done) | copy-start | bytes 25165828
  43.9 0.9 copy-start.16
  44.8 3.6 %copy-start.12 = (f32[192,256]{1,0:T(8,128)S(1)}, f32[192,256]{1,0:T(8,128)}, u32[]{:S(2)}) copy-start(f32[192,256]{1,0:T(8,128)} %copy-done.11) | copy-start | bytes 589828
  54.2 0.7 copy-start.13
  54.9 19.5 %all-to-all-start.2 = ((f32[32,8,128]{2,1,0:T(8,128)}), f32[32,8,128]{2,1,0:T(8,128)S(1)}, u32[]{:S(2)}, u32[]{:S(2)}) async-start(f32[32,8,128]{2,1,0:T(8,128)} %copy-done.13), calls=%async_computation.2 | async-start | bytes 262144 | tf_op jit(solution)/shard_map/all_to_all | solution.py:30
  60.7 3.4 %copy-start.3 = (bf16[16384,256]{1,0:T(8,128)(2,1)S(1)}, bf16[16384,256]{1,0:T(8,128)(2,1)}, u32[]{:S(2)}) copy-start(bf16[16384,256]{1,0:T(8,128)(2,1)} %copy-done) | copy-start | bytes 25165828
  67.4 3.4 %copy-start.4 = (bf16[16384,256]{1,0:T(8,128)(2,1)S(1)}, bf16[16384,256]{1,0:T(8,128)(2,1)}, u32[]{:S(2)}) copy-start(bf16[16384,256]{1,0:T(8,128)(2,1)} %copy-done) | copy-start | bytes 25165828
  74.4 3.4 %copy-start.5 = (bf16[16384,256]{1,0:T(8,128)(2,1)S(1)}, bf16[16384,256]{1,0:T(8,128)(2,1)}, u32[]{:S(2)}) copy-start(bf16[16384,256]{1,0:T(8,128)(2,1)} %copy-done) | copy-start | bytes 25165828
  85.4 0.7 copy-start.14
  86.0 14.1 %all-to-all-start.3 = ((f32[32,8,128]{2,1,0:T(8,128)}), f32[32,8,128]{2,1,0:T(8,128)S(1)}, u32[]{:S(2)}, u32[]{:S(2)}) async-start(f32[32,8,128]{2,1,0:T(8,128)} %copy-done.14), calls=%async_computation.3 | async-start | bytes 262144 | tf_op jit(solution)/shard_map/all_to_all | solution.py:30
  91.9 3.4 %copy-start.6 = (bf16[16384,256]{1,0:T(8,128)(2,1)S(1)}, bf16[16384,256]{1,0:T(8,128)(2,1)}, u32[]{:S(2)}) copy-start(bf16[16384,256]{1,0:T(8,128)(2,1)} %copy-done) | copy-start | bytes 25165828
  95.3 20.6 %copy-start.10 = (f32[192,256]{1,0:T(8,128)S(1)}, f32[192,256]{1,0:T(8,128)}, u32[]{:S(2)}) copy-start(f32[192,256]{1,0:T(8,128)} %load_ref.1) | copy-start | bytes 589828
  95.3 20.6 %copy-start.18 = (s32[8,128]{1,0:T(8,128)S(1)}, s32[8,128]{1,0:T(8,128)}, u32[]{:S(2)}) copy-start(s32[8,128]{1,0:T(8,128)} %sub_cell.1) | copy-start | bytes 12292
  95.3 20.6 %copy-start.19 = (s32[8,128]{1,0:T(8,128)S(1)}, s32[8,128]{1,0:T(8,128)}, u32[]{:S(2)}) copy-start(s32[8,128]{1,0:T(8,128)} %sub_face.1) | copy-start | bytes 12292
  102.0 13.8 %all-to-all-start.4 = ((f32[32,8,128]{2,1,0:T(8,128)}), f32[32,8,128]{2,1,0:T(8,128)S(1)}, u32[]{:S(2)}, u32[]{:S(2)}) async-start(f32[32,8,128]{2,1,0:T(8,128)} %get-tuple-element.77), calls=%async_computation.4 | async-start | bytes 262144 | tf_op jit(solution)/shard_map/all_to_all | solution.py:30
  107.6 3.4 %copy-start.7 = (bf16[16384,256]{1,0:T(8,128)(2,1)S(1)}, bf16[16384,256]{1,0:T(8,128)(2,1)}, u32[]{:S(2)}) copy-start(bf16[16384,256]{1,0:T(8,128)(2,1)} %copy-done) | copy-start | bytes 25165828
  111.0 23.5 %copy-start.20 = (s32[8,128]{1,0:T(8,128)S(1)}, s32[8,128]{1,0:T(8,128)}, u32[]{:S(2)}) copy-start(s32[8,128]{1,0:T(8,128)} %owner_ref.1) | copy-start | bytes 12292
  115.8 3.4 %copy-start.8 = (bf16[16384,256]{1,0:T(8,128)(2,1)S(1)}, bf16[16384,256]{1,0:T(8,128)(2,1)}, u32[]{:S(2)}) copy-start(bf16[16384,256]{1,0:T(8,128)(2,1)} %copy-done) | copy-start | bytes 25165828

commit v6 on v4

--- a/solution.py
+++ b/solution.py
@@ -87,27 +87,34 @@
     return high, (x - high.astype(f32)).astype(bf16)
 
 
-def gather(table, tall, parts, where_ref, lane_ref, sums_ref):
-    count = where_ref.shape[0]
-    width = where_ref.shape[1]
-    numbers = lax.broadcasted_iota(i32, (tall, width), 0)
+def gather(table, rows, parts, row_ref, column_ref, sums_ref, wide=False):
+    count, width = row_ref.shape
+    step = min(count, 32)
+    numbers = lax.broadcasted_iota(i32, (rows, width), 0)
 
     def body(block, carry):
-        start = pl.multiple_of(block * 8, 8)
-        for j in range(8):
-            hot = one_hot(lane_ref[pl.ds(start + j, 1), :], LANES)
-            found = jnp.dot(table, jnp.concatenate([hot, hot], 0), preferred_element_type=f32)
-            mask = numbers == jnp.broadcast_to(where_ref[pl.ds(start + j, 1), :], numbers.shape)
+        start = pl.multiple_of(block * step, step)
+        for j in range(step):
+            hot = one_hot(column_ref[pl.ds(start + j, 1), :], WIDE if wide else LANES)
+            if not wide:
+                hot = jnp.concatenate([hot, hot], 0)
+            found = jnp.dot(table, hot, preferred_element_type=f32)
+            if wide:
+                found = found[: parts * rows] + found[parts * rows :]
+            mask = numbers == jnp.broadcast_to(row_ref[pl.ds(start + j, 1), :], numbers.shape)
             for part in range(parts):
-                kept = jnp.where(mask, found[part * tall : (part + 1) * tall], 0.0)
-                kept = jnp.sum(kept.reshape(tall // 8, 8, width), 0)
+                kept = jnp.where(mask, found[part * rows : (part + 1) * rows], 0.0)
+                kept = jnp.sum(kept.reshape(rows // 8, 8, width), 0)
                 for half in range(width // LANES):
                     sums_ref[half, pl.ds(part * count * 8 + start * 8 + j * 8, 8), :] = kept[
                         :, half * LANES : (half + 1) * LANES
                     ]
         return carry
 
-    lax.fori_loop(0, count // 8, body, 0)
+    if count == step:
+        body(0, 0)
+    else:
+        lax.fori_loop(0, count // step, body, 0)
 
 
 def gathered(sums_ref, count, part):
@@ -128,38 +135,44 @@
     return where >> 1, (where & 1) * LANES + lane
 
 
-def scatter(high_ref, low_ref, rows, row_ref, column_ref, sum_ref, deep):
+def scatter(high_ref, low_ref, rows, row_ref, column_ref, sum_ref):
     count = row_ref.shape[0]
+    step = min(count, 16)
+
+    def product(start):
+        masks = [match16(row_ref[pl.ds(start + j, 1), :], rows) for j in range(8)]
+        hot = jnp.concatenate(
+            [one_hot(column_ref[pl.ds(start + j, 1), :], WIDE) for j in range(8)], 1
+        )
+        stacked = [
+            jnp.concatenate(
+                [
+                    spread16(mask, piece_ref[pl.ds(part * count + start + j, 1), :])
+                    for j, mask in enumerate(masks)
+                ],
+                1,
+            )
+            for piece_ref in (high_ref, low_ref)
+            for part in range(3)
+        ]
+        return lax.dot_general(
+            jnp.concatenate(stacked, 0), hot, (((1,), (1,)), ((), ())), preferred_element_type=f32
+        )
+
+    if count == 8:
+        sum_ref[...] = product(0)
+        return
     sum_ref[...] = jnp.zeros_like(sum_ref)
 
     def body(block, carry):
-        start = pl.multiple_of(block * 8, 8)
-        for first in range(0, 8, deep):
-            steps = range(first, first + deep)
-            masks = [match16(row_ref[pl.ds(start + j, 1), :], rows) for j in steps]
-            hot = jnp.concatenate(
-                [one_hot(column_ref[pl.ds(start + j, 1), :], WIDE) for j in steps], 1
-            )
-            stacked = [
-                jnp.concatenate(
-                    [
-                        spread16(mask, piece_ref[pl.ds(part * count + start + j, 1), :])
-                        for mask, j in zip(masks, steps)
-                    ],
-                    1,
-                )
-                for piece_ref in (high_ref, low_ref)
-                for part in range(3)
-            ]
-            sum_ref[...] += lax.dot_general(
-                jnp.concatenate(stacked, 0),
-                hot,
-                (((1,), (1,)), ((), ())),
-                preferred_element_type=f32,
-            )
+        start = pl.multiple_of(block * step, step)
+        total = product(start)
+        for first in range(8, step, 8):
+            total += product(start + first)
+        sum_ref[...] += total
         return carry
 
-    lax.fori_loop(0, count // 8, body, 0)
+    lax.fori_loop(0, count // step, body, 0)
 
 
 def split32(x):
@@ -172,25 +185,24 @@
     return sums[:half] + sums[half:]
 
 
-def scatter_few(values, rows, where, lane, scratch):
-    high_ref, low_ref, row_ref, column_ref, sum_ref = scratch
-    row_ref[...], column_ref[...] = rows_and_columns(where, lane)
+def scatter_few(values, rows, row_ref, column_ref, scratch):
+    high_ref, low_ref, sum_ref = scratch
     for part in range(3):
         high_ref[part * 8 : part * 8 + 8, :], low_ref[part * 8 : part * 8 + 8, :] = split32(
             values[part]
         )
-    scatter(high_ref, low_ref, rows, row_ref, column_ref, sum_ref, 8)
+    scatter(high_ref, low_ref, rows, row_ref, column_ref, sum_ref)
     return add_pieces(sum_ref[...])
 
 
 def few(rows):
-    return [((24, WIDE), f32)] * 2 + [((8, WIDE), i32)] * 2 + [((6 * rows, WIDE), f32)]
-
-
-def spread_hanging(held, weight, rows, where, lane, scratch):
+    return [((24, WIDE), f32)] * 2 + [((6 * rows, WIDE), f32)]
+
+
+def spread_hanging(held, weight, rows, row_ref, column_ref, scratch):
     both = jnp.concatenate([held, held], 1)
     values = [weight * both[part : part + 1] for part in range(3)]
-    return scatter_few(values, rows, where, lane, scratch)
+    return scatter_few(values, rows, row_ref, column_ref, scratch)
 
 
 def sum_masters(table, tall, weight, where_ref, lane_ref, sums_ref):
@@ -230,8 +242,9 @@
     return -(-count // 8) * 8
 
 
-def export_rows(table, tall, parts, where_ref, lane_ref, sums_ref):
-    gather(table, tall, parts, where_ref, lane_ref, sums_ref)
+def export_rows(table, parts, row_ref, column_ref, sums_ref):
+    table = jnp.concatenate(pieces(table), 0)
+    gather(table, OWN, parts, row_ref, column_ref, sums_ref, wide=True)
     rows = [[] for _ in range(2 * REACH)]
     for part in range(parts):
         for tile in halves(gathered(sums_ref, 8, part)):
@@ -252,8 +265,8 @@
 
 
 def first_export(
-    place_ref, adjoint_hbm, primal_hbm, list_hbm, tab_a, tab_p, where_ref, lane_ref,
-    out_ref, pack_ref, adjoint_ref, primal_ref, list_ref, tall_ref, sums_ref, sems,
+    place_ref, adjoint_hbm, primal_hbm, list_hbm, tab_a, tab_p, row_ref, column_ref,
+    out_ref, pack_ref, adjoint_ref, primal_ref, list_ref, sums_ref, sems,
 ):
     copy_in(
         [(adjoint_hbm, adjoint_ref), (primal_hbm, primal_ref), (list_hbm, list_ref)], sems
@@ -263,19 +276,18 @@
     fill_table(primal_ref, tab_p)
     codes = list_ref[...]
     node = lax.rem(17 * codes + lax.broadcasted_iota(i32, codes.shape, 1), owned)
-    where_ref[...] = node >> 7
-    lane_ref[...] = node & 127
-    half_rows = owned // LANES
-    table = tall_table([tab_a, tab_p], half_rows, tall_ref)
-    rows = export_rows(table, up8(half_rows), 6, where_ref, lane_ref, sums_ref)
+    row_ref[...] = node >> 8
+    column_ref[...] = node & 255
+    table = jnp.concatenate([tab_a[...], tab_p[...]], 0)
+    rows = export_rows(table, 6, row_ref, column_ref, sums_ref)
     pack(place_ref[0], 1, rows, pack_ref, out_ref)
 
 
 def setup(
-    connect_hbm, node_hbm, master_hbm, weight_hbm, source_hbm, inverse_hbm,
-    own_where, own_row, edge_where, edge_row, lane_ref, column_ref, edge_column, master_own, master_edge,
-    master_lane, weight_out,
-    tab_source, tab_inverse,
+    connect_hbm, node_hbm, master_hbm, weight_hbm, source_hbm, inverse_hbm, modulus_hbm,
+    own_where, own_row, edge_where, edge_row, lane_ref, column_ref, edge_column, master_own, master_own_row,
+    master_edge, master_edge_row, master_lane, master_column, weight_out, tab_source, tab_inverse,
+    modulus_out,
     connect_ref, node_ref, master_ref, weight_ref, source_ref, inverse_ref, map_ref, tall_ref, sums_ref,
     sems,
 ):
@@ -287,6 +299,7 @@
             (weight_hbm, weight_ref),
             (source_hbm, source_ref),
             (inverse_hbm, inverse_ref),
+            (modulus_hbm, modulus_out),
         ],
         sems,
     )
@@ -305,6 +318,10 @@
     master_own[...] = jnp.where(where < last, where, NOWHERE)
     master_edge[...] = jnp.where(where < last, NOWHERE, where - last)
     master_lane[...] = master & 127
+    row = master >> 8
+    master_own_row[...] = jnp.where(where < last, row, NOWHERE)
+    master_edge_row[...] = jnp.where(where < last, NOWHERE, row - last // 2)
+    master_column[...] = master & 255
 
     codes = node_ref[...]
     node = jnp.where(codes == pad_code, extent, lax.rem(13 * codes, owned))
@@ -345,8 +362,9 @@
 
 def own_gather(
     half_rows, tab_ref, where_ref, lane_ref, master_where, master_lane, weight_ref, cells_ref,
-    hang_ref, tall_ref, sums_ref,
-):
+    hang_ref, *rest,
+):
+    *final_ref, tall_ref, sums_ref = rest
     table = tall_table([tab_ref], half_rows, tall_ref)
     tall = up8(half_rows)
     found = sum_masters(table, tall, weight_ref[...], master_where, master_lane, sums_ref)
@@ -356,6 +374,13 @@
     count = where_ref.shape[0]
     for part in range(3):
         cells_ref[part * count : (part + 1) * count, :] = gathered(sums_ref, count, part)
+    if final_ref:
+        final_ref = final_ref[0]
+        for row in range(final_ref.shape[1] // WIDE):
+            for part in range(3):
+                final_ref[part : part + 1, row * WIDE : (row + 1) * WIDE] = tab_ref[
+                    part * OWN + row : part * OWN + row + 1, :
+                ]
 
 
 def edge_gather(
@@ -385,7 +410,7 @@
 
 def edge_product(
     place_ref, got_ref, cells_ref, hang_ref, where_ref, lane_ref, master_where, master_lane,
-    weight_ref, row_ref, column_ref, modulus_ref, stiffness_ref, out_ref,
+    weight_ref, row_ref, column_ref, master_row, master_column, modulus_ref, stiffness_ref, out_ref,
     image_ref, held_ref, pack_ref, edge_ref, sums_ref, full_ref, low_ref, sum_ref, *scratch,
 ):
     place = place_ref[0]
@@ -402,16 +427,14 @@
     )
     image_ref[...] = image
     full_ref[...], low_ref[...] = split32(image)
-    scatter(full_ref, low_ref, EDGE, row_ref, column_ref, sum_ref, 2)
+    scatter(full_ref, low_ref, EDGE, row_ref, column_ref, sum_ref)
     sums = add_pieces(sum_ref[...])
     slots = 2 * REACH
     held = jnp.concatenate(
         [sums[part * EDGE + slots : part * EDGE + slots + 1, :LANES] for part in range(3)], 0
     )
     held_ref[...] = held
-    sums += spread_hanging(
-        held, weight_ref[...], EDGE, master_where[...], master_lane[...], scratch
-    )
+    sums += spread_hanging(held, weight_ref[...], EDGE, master_row, master_column, scratch)
     rows = [
         [
             sums[part * EDGE + slot : part * EDGE + slot + 1, half * LANES : (half + 1) * LANES]
@@ -424,36 +447,28 @@
 
 
 def own_sums(
-    image_ref, held_ref, row_ref, column_ref, master_where, master_lane, weight_ref,
+    image_ref, held_ref, row_ref, column_ref, master_row, master_column, weight_ref,
     tab_ref, source_ref, inverse_ref, out_ref, high_ref, low_ref, sum_ref, *scratch,
 ):
     high_ref[...], low_ref[...] = split32(image_ref[...])
-    scatter(high_ref, low_ref, OWN, row_ref, column_ref, sum_ref, 8)
+    scatter(high_ref, low_ref, OWN, row_ref, column_ref, sum_ref)
     applied = add_pieces(sum_ref[...]) + spread_hanging(
-        held_ref[...], weight_ref[...], OWN, master_where[...], master_lane[...], scratch
+        held_ref[...], weight_ref[...], OWN, master_row, master_column, scratch
     )
     out_ref[...] = tab_ref[...] + relaxation * inverse_ref[...] * (source_ref[...] - applied)
 
 
 def update(
-    half_rows, place_ref, got_ref, where_ref, lane_ref, partial_ref, inverse_ref,
-    out_ref, tab_ref, *rest,
-):
-    *final_ref, pack_ref, tall_ref, sums_ref = rest[:-5]
+    place_ref, got_ref, row_ref, column_ref, partial_ref, inverse_ref, out_ref, tab_ref,
+    pack_ref, sums_ref, *scratch,
+):
     place = place_ref[0]
     values = [landed_wide(place, -1, got_ref, part) for part in range(3)]
-    returned = scatter_few(values, OWN, where_ref[...], lane_ref[...], rest[-5:])
-    tab_ref[...] = partial_ref[...] - relaxation * inverse_ref[...] * returned
-    table = tall_table([tab_ref], half_rows, tall_ref)
-    rows = export_rows(table, up8(half_rows), 3, where_ref, lane_ref, sums_ref)
+    returned = scatter_few(values, OWN, row_ref, column_ref, scratch)
+    fresh = partial_ref[...] - relaxation * inverse_ref[...] * returned
+    tab_ref[...] = fresh
+    rows = export_rows(fresh, 3, row_ref, column_ref, sums_ref)
     pack(place, 1, rows, pack_ref, out_ref)
-    if final_ref:
-        final_ref = final_ref[0]
-        for row in range(final_ref.shape[1] // WIDE):
-            for part in range(3):
-                final_ref[part : part + 1, row * WIDE : (row + 1) * WIDE] = tab_ref[
-                    part * OWN + row : part * OWN + row + 1, :
-                ]
 
 
 def primal_product(
@@ -570,7 +585,6 @@
     local_values, cell_count = cell_load.shape
     nodes = connectivity.shape[0]
     half_rows = adjoint_start.shape[1] // LANES
-    moduli = modulus.reshape(1, cell_count)
     place = lax.axis_index("dom").reshape(1).astype(i32)
     table = ((3 * OWN, WIDE), f32)
     index = ((nodes, cell_count), i32)
@@ -591,7 +605,7 @@
     many_sums = ((2, local_values * 8, LANES), f32)
     own_tall = ((3 * tall, LANES), f32)
     edge = [((3 * TALL, LANES), f32), many_sums, cells_shape]
-    tab, tab_primal, list_where, list_lane, blocks = call(
+    tab, tab_primal, list_row, list_column, blocks = call(
         first_export,
         [table, table] + [(ghost_lists.shape, i32)] * 2 + packed(16),
         [
@@ -599,7 +613,6 @@
             (adjoint_start.shape, f32),
             (primal_field.shape, f32),
             (ghost_lists.shape, i32),
-            ((6 * tall, LANES), f32),
             ((2, 6 * 64, LANES), f32),
         ],
         [SMALL, FAR, FAR, FAR],
@@ -612,20 +625,22 @@
     )
     (
         own_where, own_row, edge_where, edge_row, lane, own_column, edge_column, master_own,
-        master_edge, master_lane, weight, source, inverse,
+        master_own_row, master_edge, master_edge_row, master_lane, master_column, weight, source,
+        inverse, moduli,
     ) = call(
         setup,
-        [index] * 7 + [master_shape] * 3 + [((8, WIDE), f32), table, table],
+        [index] * 7 + [master_shape] * 6
+        + [((8, WIDE), f32), table, table, ((1, cell_count), f32)],
         [(x.shape, x.dtype) for x in far]
         + [((OWN, WIDE), f32), ((tall, LANES), f32), ((2, nodes * 8, LANES), f32)],
-        [FAR] * 6,
-        sems=6,
-    )(*away(*far))
-
-    def gather_own(values):
+        [FAR] * 7,
+        sems=7,
+    )(*away(*far, modulus.reshape(1, cell_count)))
+
+    def gather_own(values, final=()):
         return call(
             functools.partial(own_gather, half_rows),
-            [cells_shape, hang_shape],
+            [cells_shape, hang_shape, *final],
             [own_tall, many_sums],
             specs=[FAST] * 6,
         )(values, own_where, lane, master_own, master_lane, weight)
@@ -642,26 +657,29 @@
             edge_product,
             packed(8) + [cells_shape, hang_shape],
             [room(8)] + edge + [cells_shape, ((6 * EDGE, WIDE), f32)] + few(EDGE),
-        )(place, ghosts, cells, hang, *on_edge, edge_row, edge_column, moduli, stiffness)
+        )(
+            place, ghosts, cells, hang, *on_edge, edge_row, edge_column, master_edge_row,
+            master_column, moduli, stiffness,
+        )
         returned = exchange(blocks)
         (partial,) = call(
             own_sums,
             [table],
             [cells_shape, cells_shape, ((6 * OWN, WIDE), f32)] + few(OWN),
             specs=[FAST] * 10,
-        )(image, held, own_row, own_column, master_own, master_lane, weight, tab, source, inverse)
+        )(
+            image, held, own_row, own_column, master_own_row, master_column, weight, tab, source,
+            inverse,
+        )
         if sweep == 0:
             tab_primal, image = lax.optimization_barrier((tab_primal, image))
             primal_cells = gather_own(tab_primal)
             partial, *primal_cells = lax.optimization_barrier((partial, *primal_cells))
-        last = sweep == SWEEPS - 1
-        blocks, tab, *final = call(
-            functools.partial(update, half_rows),
-            packed(8) + [table] + ([(adjoint_start.shape, f32)] if last else []),
-            [room(8), own_tall, few_sums] + few(OWN),
-        )(place, returned, list_where, list_lane, partial, inverse)
+        blocks, tab = call(update, packed(8) + [table], [room(8), few_sums] + few(OWN))(
+            place, returned, list_row, list_column, partial, inverse
+        )
         ghosts = exchange(blocks)
-    cells, hang = gather_own(tab)
+    cells, hang, adjoint = gather_own(tab, [(adjoint_start.shape, f32)])
     blocks, term = call(
         fluxes,
         packed(1) + [((1, cell_count), f32)],
@@ -677,7 +695,7 @@
     (indicator,) = call(collect, [((1, cell_count), f32)])(
         place, received, subface_owner, term
     )
-    return (final[0], indicator.reshape(cell_count))
+    return (adjoint, indicator.reshape(cell_count))
 
 
 def solution(mesh):

time: 105 us -> 96.7 us (0.921)
  Pallas kernels: 58.2 us -> 48 us
  waiting for transfers between devices: 12.4 us -> 18.9 us
  starting transfers between devices: 23.3 us -> 19.7 us
    pallas_call x15, Pallas kernels: 58.2 us -> 48 us  [run(): pl.pallas_call(kernel, out_shape=[jax.ShapeDtypeStruct(shape, kind) for s...]
    all_to_all x5, waiting for transfers between devices: 12.4 us -> 18.9 us  [exchange(): return lax.all_to_all(packed, 'dom', 0, 0, tiled=True)]
    all_to_all x5, starting transfers between devices: 23.3 us -> 19.7 us  [exchange(): return lax.all_to_all(packed, 'dom', 0, 0, tiled=True)]
  transfers between devices with their start and end apart: 5 -> 5, of which waited for: 4 -> 5; matrix products, arithmetic and copies ran while one was open for 0% -> 0% of each run, Pallas kernels for 30% -> 25%
where the time goes in v6:
time: 96.7 us; the launch traced here: 96.2 us
  Pallas kernels  48 us (50%)
  starting transfers between devices  19.7 us (20%)
  waiting for transfers between devices  18.9 us (20%)
  blocking collectives  8.85 us (9%)
    pallas_call x15, Pallas kernels, run(): pl.pallas_call(kernel, out_shape=[jax.ShapeDtypeStruct(shape, kind) for s...  48 us
    all_to_all x5, starting transfers between devices, exchange(): return lax.all_to_all(packed, 'dom', 0, 0, tiled=True)  19.7 us
    all_to_all x5, waiting for transfers between devices, exchange(): return lax.all_to_all(packed, 'dom', 0, 0, tiled=True)  18.9 us
    all_to_all x1, blocking collectives, exchange(): return lax.all_to_all(packed, 'dom', 0, 0, tiled=True)  8.85 us
  transfers between devices with their start and end apart: 5, of which 5 were waited for; matrix products, arithmetic and copies ran while one was open for 0% of the time, Pallas kernels for 25%

profile of v6, /device:TPU:0, one launch (start us, length us, event | category | flops | bytes accessed | tf_op | source)
XLA Modules:
  0.0 96.2 jit_solution(16123456929327254702)
XLA Ops:
  0.6 2.4 %shard_map.158 = (f32[96,256]{1,0:T(8,128)S(1)}, f32[96,256]{1,0:T(8,128)S(1)}, s32[8,256]{1,0:T(8,128)S(1)}, s32[8,256]{1,0:T(8,128)S(1)}, f32[32,16,128]{2,1,0:T(8,128)}) custom-call(s32[1]{0:T(128)} %bitcast.place_ref, f32[3,6912]{1,0:T(4,128)} %adjoint_hbm.1, f32[3,6912]{1,0:T(4,128)} %primal_hbm.1, s32[8,256]{1,0:T(8,128)} %list_hbm.1), custom_call_target="tpu_custom_call" | custom-call | tf_op jit(solution)/shard_map/pallas_call | solution.py:556
  3.0 7.3 %all-to-all-start = ((f32[32,16,128]{2,1,0:T(8,128)}), f32[32,16,128]{2,1,0:T(8,128)S(1)}, u32[]{:S(2)}, u32[]{:S(2)}) async-start(f32[32,16,128]{2,1,0:T(8,128)} %get-tuple-element.51), calls=%async_computation | async-start | bytes 524288 | tf_op jit(solution)/shard_map/all_to_all | solution.py:33
  10.4 3.2 %shard_map.159 = (s32[64,256]{1,0:T(8,128)S(1)}, s32[64,256]{1,0:T(8,128)S(1)}, s32[64,256]{1,0:T(8,128)S(1)}, s32[64,256]{1,0:T(8,128)S(1)}, s32[64,256]{1,0:T(...) custom-call(s32[64,256]{1,0:T(8,128)} %connect_hbm.1, ...), custom_call_target="tpu_custom_call" | custom-call | tf_op jit(solution)/shard_map/pallas_call | solution.py:556
  13.6 0.0 copy-start
  13.6 2.5 %shard_map.160 = (f32[192,256]{1,0:T(8,128)S(1)}, f32[3,128]{1,0:T(4,128)S(1)}) custom-call(f32[96,256]{1,0:T(8,128)S(1)} %get-tuple-element.52.tab_ref, s32[64,256]{1,0:T(8,128)S(1)} %get-tuple-element.53.where_ref, s32[64,256]{1,0:T(8,128)S(1)} %get-tuple-element.54.lane_ref, s32[8,256]{1,0:T(8,128)S(1)} %get-tuple-element.55.master_where, ...), custom_call_target="tpu_custom_call" | custom-call | tf_op jit(solution)/shard_map/pallas_call | solution.py:556
  16.1 4.8 %all-to-all-done.got_ref = f32[32,16,128]{2,1,0:T(8,128)S(1)} async-done(((f32[32,16,128]{2,1,0:T(8,128)}), f32[32,16,128]{2,1,0:T(8,128)S(1)}, u32[]{:S(2)}, u32[]{:S(2)}) %all-to-all-start) | async-done | bytes 262176 | tf_op jit(solution)/shard_map/all_to_all | solution.py:33
  21.0 0.0 copy-done
  21.0 6.9 %shard_map.161 = (f32[32,8,128]{2,1,0:T(8,128)}, f32[192,256]{1,0:T(8,128)S(1)}, f32[3,128]{1,0:T(4,128)S(1)}) custom-call(s32[1]{0:T(128)} %bitcast.place_ref, f32[32,16,128]{2,1,0:T(8,128)S(1)} %all-to-all-done.got_ref, f32[192,256]{1,0:T(8,128)S(1)} %get-tuple-element.58.cells_ref, f32[3,128]{1,0:T(4,128)S(1)} %get-tuple-element.59.hang_ref, ...), custom_call_target="tpu_custom_call" | custom-call | tf_op jit(solution)/shard_map/pallas_call | solution.py:556
  27.9 2.6 %all-to-all-start.1 = ((f32[32,8,128]{2,1,0:T(8,128)}), f32[32,8,128]{2,1,0:T(8,128)S(1)}, u32[]{:S(2)}, u32[]{:S(2)}) async-start(f32[32,8,128]{2,1,0:T(8,128)} %get-tuple-element.67), calls=%async_computation.1 | async-start | bytes 262144 | tf_op jit(solution)/shard_map/all_to_all | solution.py:33
  30.5 2.5 %shard_map.163 = (f32[192,256]{1,0:T(8,128)S(1)}, f32[3,128]{1,0:T(4,128)S(1)}) custom-call(f32[96,256]{1,0:T(8,128)S(1)} %get-tuple-element.78.tab_ref, s32[64,256]{1,0:T(8,128)S(1)} %get-tuple-element.53.where_ref, s32[64,256]{1,0:T(8,128)S(1)} %get-tuple-element.54.lane_ref, s32[8,256]{1,0:T(8,128)S(1)} %get-tuple-element.55.master_where, ...), custom_call_target="tpu_custom_call" | custom-call | tf_op jit(solution)/shard_map/pallas_call | solution.py:556
  33.0 3.9 %shard_map.162.partial_ref = f32[96,256]{1,0:T(8,128)S(1)} custom-call(f32[192,256]{1,0:T(8,128)S(1)} %get-tuple-element.70.image_ref, f32[3,128]{1,0:T(4,128)S(1)} %get-tuple-element.71.held_ref, s32[64,256]{1,0:T(8,128)S(1)} %get-tuple-element.72.row_ref, s32[64,256]{1,0:T(8,128)S(1)} %get-tuple-element.73.column_ref, ...), custom_call_target="tpu_custom_call" | custom-call | tf_op jit(solution)/shard_map/pallas_call | solution.py:556
  36.9 1.7 %all-to-all-done.1.got_ref = f32[32,8,128]{2,1,0:T(8,128)S(1)} async-done(((f32[32,8,128]{2,1,0:T(8,128)}), f32[32,8,128]{2,1,0:T(8,128)S(1)}, u32[]{:S(2)}, u32[]{:S(2)}) %all-to-all-start.1) | async-done | bytes 131104 | tf_op jit(solution)/shard_map/all_to_all | solution.py:33
  38.7 1.9 %shard_map.164 = (f32[32,8,128]{2,1,0:T(8,128)}, f32[96,256]{1,0:T(8,128)S(1)}) custom-call(s32[1]{0:T(128)} %bitcast.place_ref, f32[32,8,128]{2,1,0:T(8,128)S(1)} %all-to-all-done.1.got_ref, s32[8,256]{1,0:T(8,128)S(1)} %get-tuple-element.68.row_ref, s32[8,256]{1,0:T(8,128)S(1)} %get-tuple-element.69.column_ref, f32[96,256]{1,0:T(8,128)S(1)} %shard_map.162.partial_ref, ...), custom_call_target="tpu_custom_call" | custom-call | tf_op jit(solution)/shard_map/pallas_call | solution.py:556
  40.5 4.3 %all-to-all-start.2 = ((f32[32,8,128]{2,1,0:T(8,128)}), f32[32,8,128]{2,1,0:T(8,128)S(1)}, u32[]{:S(2)}, u32[]{:S(2)}) async-start(f32[32,8,128]{2,1,0:T(8,128)} %get-tuple-element.82), calls=%async_computation.2 | async-start | bytes 262144 | tf_op jit(solution)/shard_map/all_to_all | solution.py:33
  44.8 2.6 %shard_map.166.ku_ref = f32[192,256]{1,0:T(8,128)S(1)} custom-call(s32[1]{0:T(128)} %bitcast.place_ref, f32[32,16,128]{2,1,0:T(8,128)S(1)} %all-to-all-done.got_ref, f32[192,256]{1,0:T(8,128)S(1)} %get-tuple-element.85.cells_ref, f32[3,128]{1,0:T(4,128)S(1)} %get-tuple-element.86.hang_ref, s32[64,256]{1,0:T(8,128)S(1)} %get-tuple-element.60.where_ref, ...), custom_call_target="tpu_custom_call" | custom-call | tf_op jit(solution)/shard_map/pallas_call | solution.py:556
  47.5 2.5 %shard_map.165 = (f32[192,256]{1,0:T(8,128)S(1)}, f32[3,128]{1,0:T(4,128)S(1)}) custom-call(f32[96,256]{1,0:T(8,128)S(1)} %get-tuple-element.83.tab_ref, s32[64,256]{1,0:T(8,128)S(1)} %get-tuple-element.53.where_ref, s32[64,256]{1,0:T(8,128)S(1)} %get-tuple-element.54.lane_ref, s32[8,256]{1,0:T(8,128)S(1)} %get-tuple-element.55.master_where, ...), custom_call_target="tpu_custom_call" | custom-call | tf_op jit(solution)/shard_map/pallas_call | solution.py:556
  50.0 2.9 %all-to-all-done.2.got_ref = f32[32,8,128]{2,1,0:T(8,128)S(1)} async-done(((f32[32,8,128]{2,1,0:T(8,128)}), f32[32,8,128]{2,1,0:T(8,128)S(1)}, u32[]{:S(2)}, u32[]{:S(2)}) %all-to-all-start.2) | async-done | bytes 131104 | tf_op jit(solution)/shard_map/all_to_all | solution.py:33
  52.9 6.9 %shard_map.167 = (f32[32,8,128]{2,1,0:T(8,128)}, f32[192,256]{1,0:T(8,128)S(1)}, f32[3,128]{1,0:T(4,128)S(1)}) custom-call(s32[1]{0:T(128)} %bitcast.place_ref, f32[32,8,128]{2,1,0:T(8,128)S(1)} %all-to-all-done.2.got_ref, f32[192,256]{1,0:T(8,128)S(1)} %get-tuple-element.87.cells_ref, f32[3,128]{1,0:T(4,128)S(1)} %get-tuple-element.88.hang_ref, ...), custom_call_target="tpu_custom_call" | custom-call | tf_op jit(solution)/shard_map/pallas_call | solution.py:556
  59.8 2.8 %all-to-all-start.3 = ((f32[32,8,128]{2,1,0:T(8,128)}), f32[32,8,128]{2,1,0:T(8,128)S(1)}, u32[]{:S(2)}, u32[]{:S(2)}) async-start(f32[32,8,128]{2,1,0:T(8,128)} %get-tuple-element.89), calls=%async_computation.3 | async-start | bytes 262144 | tf_op jit(solution)/shard_map/all_to_all | solution.py:33
  62.6 4.0 %shard_map.168.partial_ref = f32[96,256]{1,0:T(8,128)S(1)} custom-call(f32[192,256]{1,0:T(8,128)S(1)} %get-tuple-element.90.image_ref, f32[3,128]{1,0:T(4,128)S(1)} %get-tuple-element.91.held_ref, s32[64,256]{1,0:T(8,128)S(1)} %get-tuple-element.72.row_ref, s32[64,256]{1,0:T(8,128)S(1)} %get-tuple-element.73.column_ref, ...), custom_call_target="tpu_custom_call" | custom-call | tf_op jit(solution)/shard_map/pallas_call | solution.py:556
  66.6 4.3 %all-to-all-done.3.got_ref = f32[32,8,128]{2,1,0:T(8,128)S(1)} async-done(((f32[32,8,128]{2,1,0:T(8,128)}), f32[32,8,128]{2,1,0:T(8,128)S(1)}, u32[]{:S(2)}, u32[]{:S(2)}) %all-to-all-start.3) | async-done | bytes 131104 | tf_op jit(solution)/shard_map/all_to_all | solution.py:33
  70.8 1.9 %shard_map.169 = (f32[32,8,128]{2,1,0:T(8,128)}, f32[96,256]{1,0:T(8,128)S(1)}) custom-call(s32[1]{0:T(128)} %bitcast.place_ref, f32[32,8,128]{2,1,0:T(8,128)S(1)} %all-to-all-done.3.got_ref, s32[8,256]{1,0:T(8,128)S(1)} %get-tuple-element.68.row_ref, s32[8,256]{1,0:T(8,128)S(1)} %get-tuple-element.69.column_ref, f32[96,256]{1,0:T(8,128)S(1)} %shard_map.168.partial_ref, ...), custom_call_target="tpu_custom_call" | custom-call | tf_op jit(solution)/shard_map/pallas_call | solution.py:556
  72.7 0.0 copy-start.1
  72.7 2.7 %all-to-all-start.4 = ((f32[32,8,128]{2,1,0:T(8,128)}), f32[32,8,128]{2,1,0:T(8,128)S(1)}, u32[]{:S(2)}, u32[]{:S(2)}) async-start(f32[32,8,128]{2,1,0:T(8,128)} %get-tuple-element.94), calls=%async_computation.4 | async-start | bytes 262144 | tf_op jit(solution)/shard_map/all_to_all | solution.py:33
  75.4 0.0 copy-start.2
  75.4 0.0 copy-start.3
  75.4 3.0 %shard_map.170 = (f32[192,256]{1,0:T(8,128)S(1)}, f32[3,128]{1,0:T(4,128)S(1)}, f32[3,6912]{1,0:T(4,128)}) custom-call(f32[96,256]{1,0:T(8,128)S(1)} %get-tuple-element.92.tab_ref, s32[64,256]{1,0:T(8,128)S(1)} %get-tuple-element.53.where_ref, s32[64,256]{1,0:T(8,128)S(1)} %get-tuple-element.54.lane_ref, s32[8,256]{1,0:T(8,128)S(1)} %get-tuple-element.55.master_where, ...), custom_call_target="tpu_custom_call" | custom-call | tf_op jit(solution)/shard_map/pallas_call | solution.py:556
  78.4 5.2 %all-to-all-done.4.got_ref = f32[32,8,128]{2,1,0:T(8,128)S(1)} async-done(((f32[32,8,128]{2,1,0:T(8,128)}), f32[32,8,128]{2,1,0:T(8,128)S(1)}, u32[]{:S(2)}, u32[]{:S(2)}) %all-to-all-start.4) | async-done | bytes 131104 | tf_op jit(solution)/shard_map/all_to_all | solution.py:33
  83.6 0.0 copy-done.1
  83.6 0.0 copy-done.2
  83.6 0.0 copy-done.3
  83.6 0.0 copy-start.4
  83.7 2.9 %shard_map.171 = (f32[32,1,128]{2,1,0:T(1,128)S(1)}, f32[1,256]{1,0:T(1,128)S(1)}) custom-call(s32[1]{0:T(128)} %bitcast.place_ref, f32[32,8,128]{2,1,0:T(8,128)S(1)} %all-to-all-done.4.got_ref, f32[192,256]{1,0:T(8,128)S(1)} %get-tuple-element.95.cells_ref, f32[3,128]{1,0:T(4,128)S(1)} %get-tuple-element.96.hang_ref, ...), custom_call_target="tpu_custom_call" | custom-call | tf_op jit(solution)/shard_map/pallas_call | solution.py:556
  86.5 8.8 %all_to_all.30.got_ref = f32[32,1,128]{2,1,0:T(1,128)S(1)} all-to-all(f32[32,1,128]{2,1,0:T(1,128)S(1)} %get-tuple-element.98), channel_id=1, replica_groups=mesh['dom'=32] {'dom'}, dimensions={0} | all-to-all | bytes 32768 | tf_op jit(solution)/shard_map/all_to_all | solution.py:33
  95.4 0.0 copy-done.4
  95.4 0.8 shard_map.172
Async XLA Ops:
  3.0 17.9 %all-to-all-start = ((f32[32,16,128]{2,1,0:T(8,128)}), f32[32,16,128]{2,1,0:T(8,128)S(1)}, u32[]{:S(2)}, u32[]{:S(2)}) async-start(f32[32,16,128]{2,1,0:T(8,128)} %get-tuple-element.51), calls=%async_computation | async-start | bytes 524288 | tf_op jit(solution)/shard_map/all_to_all | solution.py:33
  13.6 7.4 %copy-start = (f32[192,192]{1,0:T(8,128)S(1)}, f32[192,192]{1,0:T(8,128)}, u32[]{:S(2)}) copy-start(f32[192,192]{1,0:T(8,128)} %stiffness_ref.5) | copy-start | bytes 442372
  27.9 10.8 %all-to-all-start.1 = ((f32[32,8,128]{2,1,0:T(8,128)}), f32[32,8,128]{2,1,0:T(8,128)S(1)}, u32[]{:S(2)}, u32[]{:S(2)}) async-start(f32[32,8,128]{2,1,0:T(8,128)} %get-tuple-element.67), calls=%async_computation.1 | async-start | bytes 262144 | tf_op jit(solution)/shard_map/all_to_all | solution.py:33
  40.5 12.3 %all-to-all-start.2 = ((f32[32,8,128]{2,1,0:T(8,128)}), f32[32,8,128]{2,1,0:T(8,128)S(1)}, u32[]{:S(2)}, u32[]{:S(2)}) async-start(f32[32,8,128]{2,1,0:T(8,128)} %get-tuple-element.82), calls=%async_computation.2 | async-start | bytes 262144 | tf_op jit(solution)/shard_map/all_to_all | solution.py:33
  59.8 11.0 %all-to-all-start.3 = ((f32[32,8,128]{2,1,0:T(8,128)}), f32[32,8,128]{2,1,0:T(8,128)S(1)}, u32[]{:S(2)}, u32[]{:S(2)}) async-start(f32[32,8,128]{2,1,0:T(8,128)} %get-tuple-element.89), calls=%async_computation.3 | async-start | bytes 262144 | tf_op jit(solution)/shard_map/all_to_all | solution.py:33
  72.7 10.9 %copy-start.1 = (f32[192,256]{1,0:T(8,128)S(1)}, f32[192,256]{1,0:T(8,128)}, u32[]{:S(2)}) copy-start(f32[192,256]{1,0:T(8,128)} %load_ref.1) | copy-start | bytes 589828
  72.7 10.9 %all-to-all-start.4 = ((f32[32,8,128]{2,1,0:T(8,128)}), f32[32,8,128]{2,1,0:T(8,128)S(1)}, u32[]{:S(2)}, u32[]{:S(2)}) async-start(f32[32,8,128]{2,1,0:T(8,128)} %get-tuple-element.94), calls=%async_computation.4 | async-start | bytes 262144 | tf_op jit(solution)/shard_map/all_to_all | solution.py:33
  75.4 8.2 %copy-start.2 = (s32[8,128]{1,0:T(8,128)S(1)}, s32[8,128]{1,0:T(8,128)}, u32[]{:S(2)}) copy-start(s32[8,128]{1,0:T(8,128)} %sub_cell.1) | copy-start | bytes 12292
  75.4 8.2 %copy-start.3 = (s32[8,128]{1,0:T(8,128)S(1)}, s32[8,128]{1,0:T(8,128)}, u32[]{:S(2)}) copy-start(s32[8,128]{1,0:T(8,128)} %sub_face.1) | copy-start | bytes 12292
  83.6 11.7 %copy-start.4 = (s32[8,128]{1,0:T(8,128)S(1)}, s32[8,128]{1,0:T(8,128)}, u32[]{:S(2)}) copy-start(s32[8,128]{1,0:T(8,128)} %owner_ref.1) | copy-start | bytes 12292

commit v7 on v6

--- a/solution.py
+++ b/solution.py
@@ -62,24 +62,21 @@
     return jnp.concatenate(halves, 1)
 
 
-def match16(row, count):
+def wide16(row):
+    return jnp.broadcast_to(row, (16, row.shape[1])).astype(bf16)[None]
+
+
+def one_hot(row, count):
     width = row.shape[1]
-    wide = jnp.broadcast_to(row.astype(f32), (16, width)).astype(bf16)
     numbers = lax.broadcasted_iota(i32, (count, width), 0).astype(f32).astype(bf16)
-    numbers = numbers.reshape(count // 16, 16, width)
-    return numbers == wide[None]
-
-
-def one_hot(row, count):
-    mask = match16(row, count)
-    ones = jnp.ones(mask.shape, bf16)
-    return jnp.where(mask, ones, jnp.zeros_like(ones)).reshape(count, row.shape[1])
-
-
-def spread16(mask, row):
-    wide = jnp.broadcast_to(row, (16, row.shape[1])).astype(bf16)[None]
-    out = jnp.where(mask, jnp.broadcast_to(wide, mask.shape), jnp.zeros(mask.shape, bf16))
-    return out.reshape(mask.shape[0] * 16, row.shape[1])
+    off = numbers.reshape(count // 16, 16, width) - wide16(row.astype(f32))
+    hot = jnp.maximum(jnp.ones_like(off) - off * off, jnp.zeros_like(off))
+    return hot.reshape(count, width)
+
+
+def spread16(hot, row):
+    count, width = hot.shape
+    return (hot.reshape(count // 16, 16, width) * wide16(row)).reshape(count, width)
 
 
 def pieces(x):
@@ -140,7 +137,7 @@
     step = min(count, 16)
 
     def product(start):
-        masks = [match16(row_ref[pl.ds(start + j, 1), :], rows) for j in range(8)]
+        masks = [one_hot(row_ref[pl.ds(start + j, 1), :], rows) for j in range(8)]
         hot = jnp.concatenate(
             [one_hot(column_ref[pl.ds(start + j, 1), :], WIDE) for j in range(8)], 1
         )
@@ -242,15 +239,23 @@
     return -(-count // 8) * 8
 
 
-def export_rows(table, parts, row_ref, column_ref, sums_ref):
+def export_tiles(table, row_ref, column_ref, sums_ref):
     table = jnp.concatenate(pieces(table), 0)
-    gather(table, OWN, parts, row_ref, column_ref, sums_ref, wide=True)
-    rows = [[] for _ in range(2 * REACH)]
-    for part in range(parts):
-        for tile in halves(gathered(sums_ref, 8, part)):
-            for slot in range(2 * REACH):
-                rows[slot].append(tile[slot : slot + 1])
-    return rows
+    gather(table, OWN, 3, row_ref, column_ref, sums_ref, wide=True)
+    return [tile for part in range(3) for tile in halves(gathered(sums_ref, 8, part))]
+
+
+def export_rows(table, row_ref, column_ref, sums_ref):
+    tiles = export_tiles(table, row_ref, column_ref, sums_ref)
+    return [[tile[slot : slot + 1] for tile in tiles] for slot in range(2 * REACH)]
+
+
+def add_primal(rows, sign, part, extra_ref):
+    slots = 2 * REACH
+    for slot in range(slots):
+        export = slot if sign > 0 else (slot + REACH) % slots
+        for half in range(2):
+            rows[slot].append(extra_ref[2 * part + half, export : export + 1, :])
 
 
 def copy_in(pairs, sems):
@@ -265,22 +270,28 @@
 
 
 def first_export(
-    place_ref, adjoint_hbm, primal_hbm, list_hbm, tab_a, tab_p, row_ref, column_ref,
-    out_ref, pack_ref, adjoint_ref, primal_ref, list_ref, sums_ref, sems,
-):
-    copy_in(
-        [(adjoint_hbm, adjoint_ref), (primal_hbm, primal_ref), (list_hbm, list_ref)], sems
-    )
+    place_ref, adjoint_hbm, list_hbm, tab_ref, row_ref, column_ref,
+    out_ref, pack_ref, adjoint_ref, list_ref, sums_ref, sems,
+):
+    copy_in([(adjoint_hbm, adjoint_ref), (list_hbm, list_ref)], sems)
     owned = adjoint_ref.shape[1]
-    fill_table(adjoint_ref, tab_a)
-    fill_table(primal_ref, tab_p)
+    fill_table(adjoint_ref, tab_ref)
     codes = list_ref[...]
     node = lax.rem(17 * codes + lax.broadcasted_iota(i32, codes.shape, 1), owned)
     row_ref[...] = node >> 8
     column_ref[...] = node & 255
-    table = jnp.concatenate([tab_a[...], tab_p[...]], 0)
-    rows = export_rows(table, 6, row_ref, column_ref, sums_ref)
+    rows = export_rows(tab_ref[...], row_ref, column_ref, sums_ref)
     pack(place_ref[0], 1, rows, pack_ref, out_ref)
+
+
+def primal_export(
+    primal_hbm, row_ref, column_ref, tab_ref, out_ref, primal_ref, sums_ref, sems
+):
+    copy_in([(primal_hbm, primal_ref)], sems)
+    fill_table(primal_ref, tab_ref)
+    tiles = export_tiles(tab_ref[...], row_ref, column_ref, sums_ref)
+    for number, tile in enumerate(tiles):
+        out_ref[number] = tile
 
 
 def setup(
@@ -327,7 +338,7 @@
     node = jnp.where(codes == pad_code, extent, lax.rem(13 * codes, owned))
     slot = (lax.broadcasted_iota(i32, codes.shape, 1) + 1).astype(f32)
     map_ref[...] = lax.dot_general(
-        spread16(match16(node >> 8, OWN), slot),
+        spread16(one_hot(node >> 8, OWN), slot),
         one_hot(node & 255, WIDE),
         (((1,), (1,)), ((), ())),
         preferred_element_type=f32,
@@ -384,14 +395,14 @@
 
 
 def edge_gather(
-    place, got_ref, first, cells_ref, hang_ref, where_ref, lane_ref, master_where, master_lane,
+    place, got_refs, first, cells_ref, hang_ref, where_ref, lane_ref, master_where, master_lane,
     weight_ref, edge_ref, sums_ref, out_ref,
 ):
     slots = 2 * REACH
     edge_ref[...] = jnp.zeros_like(edge_ref)
     for part in range(3):
         for half in range(2):
-            lines = landed(place, 1, got_ref, 2 * (first + part) + half)
+            lines = landed(place, 1, got_refs[part], first[part] + half)
             for slot in range(slots):
                 at = part * TALL + 2 * slot + half
                 edge_ref[at : at + 1, :] = lines[slot]
@@ -409,13 +420,14 @@
 
 
 def edge_product(
-    place_ref, got_ref, cells_ref, hang_ref, where_ref, lane_ref, master_where, master_lane,
-    weight_ref, row_ref, column_ref, master_row, master_column, modulus_ref, stiffness_ref, out_ref,
+    primal_part, place_ref, got_ref, cells_ref, hang_ref, where_ref, lane_ref, master_where, master_lane,
+    weight_ref, row_ref, column_ref, master_row, master_column, extra_ref, modulus_ref,
+    stiffness_ref, out_ref,
     image_ref, held_ref, pack_ref, edge_ref, sums_ref, full_ref, low_ref, sum_ref, *scratch,
 ):
     place = place_ref[0]
     edge_gather(
-        place, got_ref, 0, cells_ref, hang_ref, where_ref, lane_ref,
+        place, [got_ref] * 3, (0, 2, 4), cells_ref, hang_ref, where_ref, lane_ref,
         master_where, master_lane, weight_ref, edge_ref, sums_ref, full_ref,
     )
     image = modulus_ref[...] * lax.dot_general(
@@ -443,6 +455,7 @@
         ]
         for slot in range(slots)
     ]
+    add_primal(rows, -1, primal_part, extra_ref)
     pack(place, -1, rows, pack_ref, out_ref)
 
 
@@ -459,7 +472,8 @@
 
 
 def update(
-    place_ref, got_ref, row_ref, column_ref, partial_ref, inverse_ref, out_ref, tab_ref,
+    primal_part, place_ref, got_ref, row_ref, column_ref, partial_ref, inverse_ref, extra_ref,
+    out_ref, tab_ref,
     pack_ref, sums_ref, *scratch,
 ):
     place = place_ref[0]
@@ -467,16 +481,18 @@
     returned = scatter_few(values, OWN, row_ref, column_ref, scratch)
     fresh = partial_ref[...] - relaxation * inverse_ref[...] * returned
     tab_ref[...] = fresh
-    rows = export_rows(fresh, 3, row_ref, column_ref, sums_ref)
+    rows = export_rows(fresh, row_ref, column_ref, sums_ref)
+    if primal_part is not None:
+        add_primal(rows, 1, primal_part, extra_ref)
     pack(place, 1, rows, pack_ref, out_ref)
 
 
 def primal_product(
-    place_ref, got_ref, cells_ref, hang_ref, where_ref, lane_ref, master_where,
+    place_ref, got_a, got_b, got_c, cells_ref, hang_ref, where_ref, lane_ref, master_where,
     master_lane, weight_ref, modulus_ref, stiffness_ref, out_ref, edge_ref, sums_ref, full_ref,
 ):
     edge_gather(
-        place_ref[0], got_ref, 3, cells_ref, hang_ref, where_ref, lane_ref,
+        place_ref[0], (got_a, got_b, got_c), (6, 6, 6), cells_ref, hang_ref, where_ref, lane_ref,
         master_where, master_lane, weight_ref, edge_ref, sums_ref, full_ref,
     )
     out_ref[...] = modulus_ref[...] * jnp.dot(
@@ -494,7 +510,7 @@
 ):
     place = place_ref[0]
     edge_gather(
-        place, got_ref, 0, cells_ref, hang_ref, where_ref, lane_ref,
+        place, [got_ref] * 3, (0, 2, 4), cells_ref, hang_ref, where_ref, lane_ref,
         master_where, master_lane, weight_ref, edge_ref, sums_ref, full_ref,
     )
     cells = full_ref[...]
@@ -605,20 +621,21 @@
     many_sums = ((2, local_values * 8, LANES), f32)
     own_tall = ((3 * tall, LANES), f32)
     edge = [((3 * TALL, LANES), f32), many_sums, cells_shape]
-    tab, tab_primal, list_row, list_column, blocks = call(
+    tab, list_row, list_column, blocks = call(
         first_export,
-        [table, table] + [(ghost_lists.shape, i32)] * 2 + packed(16),
-        [
-            room(16),
-            (adjoint_start.shape, f32),
-            (primal_field.shape, f32),
-            (ghost_lists.shape, i32),
-            ((2, 6 * 64, LANES), f32),
-        ],
-        [SMALL, FAR, FAR, FAR],
-        sems=3,
-    )(place, *away(adjoint_start, primal_field, ghost_lists))
-    ghosts = first_ghosts = exchange(blocks)
+        [table] + [(ghost_lists.shape, i32)] * 2 + packed(8),
+        [room(8), (adjoint_start.shape, f32), (ghost_lists.shape, i32), few_sums],
+        [SMALL, FAR, FAR],
+        sems=2,
+    )(place, *away(adjoint_start, ghost_lists))
+    ghosts = exchange(blocks)
+    tab_primal, extra = call(
+        primal_export,
+        [table, ((6, slots, LANES), f32)],
+        [(primal_field.shape, f32), few_sums],
+        [FAR, FAST, FAST],
+        sems=1,
+    )(*away(primal_field), list_row, list_column)
     far = (
         connectivity, hang_node.reshape(1, -1), hang_master, hang_weight, adjoint_source,
         inverse_diagonal,
@@ -646,22 +663,23 @@
         )(values, own_where, lane, master_own, master_lane, weight)
 
     on_edge = (edge_where, lane, master_edge, master_lane, weight)
+    landings = []
     for sweep in range(SWEEPS):
         cells, hang = gather_own(tab)
         if sweep == 1:
-            (ku,) = call(primal_product, [cells_shape], edge)(
-                place, first_ghosts, *primal_cells, *on_edge, moduli, stiffness
-            )
-            cells, ku = lax.optimization_barrier((cells, ku))
+            tab_primal, tab = lax.optimization_barrier((tab_primal, tab))
+            primal_cells = gather_own(tab_primal)
+            cells, *primal_cells = lax.optimization_barrier((cells, *primal_cells))
         blocks, image, held = call(
-            edge_product,
+            functools.partial(edge_product, 2 * sweep),
             packed(8) + [cells_shape, hang_shape],
             [room(8)] + edge + [cells_shape, ((6 * EDGE, WIDE), f32)] + few(EDGE),
         )(
             place, ghosts, cells, hang, *on_edge, edge_row, edge_column, master_edge_row,
-            master_column, moduli, stiffness,
+            master_column, extra, moduli, stiffness,
         )
         returned = exchange(blocks)
+        landings.append(returned)
         (partial,) = call(
             own_sums,
             [table],
@@ -671,15 +689,18 @@
             image, held, own_row, own_column, master_own_row, master_column, weight, tab, source,
             inverse,
         )
-        if sweep == 0:
-            tab_primal, image = lax.optimization_barrier((tab_primal, image))
-            primal_cells = gather_own(tab_primal)
-            partial, *primal_cells = lax.optimization_barrier((partial, *primal_cells))
-        blocks, tab = call(update, packed(8) + [table], [room(8), few_sums] + few(OWN))(
-            place, returned, list_row, list_column, partial, inverse
-        )
+        blocks, tab = call(
+            functools.partial(update, 1 if sweep == 0 else None),
+            packed(8) + [table],
+            [room(8), few_sums] + few(OWN),
+        )(place, returned, list_row, list_column, partial, inverse, extra)
         ghosts = exchange(blocks)
+        landings.append(ghosts)
     cells, hang, adjoint = gather_own(tab, [(adjoint_start.shape, f32)])
+    tab, *primal_cells = lax.optimization_barrier((tab, *primal_cells))
+    (ku,) = call(primal_product, [cells_shape], edge)(
+        place, *landings[:3], *primal_cells, *on_edge, moduli, stiffness
+    )
     blocks, term = call(
         fluxes,
         packed(1) + [((1, cell_count), f32)],

time: 96.7 us -> 98 us (1.013)
  waiting for transfers between devices: 18.9 us -> 13 us
  Pallas kernels: 48 us -> 51.3 us
  starting transfers between devices: 19.7 us -> 21.7 us
  blocking collectives: 8.85 us -> 10.7 us
    all_to_all x5, waiting for transfers between devices: 18.9 us -> 13 us  [exchange(): return lax.all_to_all(packed, 'dom', 0, 0, tiled=True)]
    pallas_call x15 -> x16, Pallas kernels: 48 us -> 51.3 us  [run(): pl.pallas_call(kernel, out_shape=[jax.ShapeDtypeStruct(shape, kind) for s...]
    all_to_all x5, starting transfers between devices: 19.7 us -> 21.7 us  [exchange(): return lax.all_to_all(packed, 'dom', 0, 0, tiled=True)]
    all_to_all x1, blocking collectives: 8.85 us -> 10.7 us  [exchange(): return lax.all_to_all(packed, 'dom', 0, 0, tiled=True)]
  transfers between devices with their start and end apart: 5 -> 5, of which waited for: 5 -> 5; matrix products, arithmetic and copies ran while one was open for 0% -> 0% of each run, Pallas kernels for 25% -> 28%
where the time goes in v7:
time: 98 us; the launch traced here: 97.5 us
  Pallas kernels  51.3 us (52%)
  starting transfers between devices  21.7 us (22%)
  waiting for transfers between devices  13 us (13%)
  blocking collectives  10.7 us (11%)
    pallas_call x16, Pallas kernels, run(): pl.pallas_call(kernel, out_shape=[jax.ShapeDtypeStruct(shape, kind) for s...  51.3 us
    all_to_all x5, starting transfers between devices, exchange(): return lax.all_to_all(packed, 'dom', 0, 0, tiled=True)  21.7 us
    all_to_all x5, waiting for transfers between devices, exchange(): return lax.all_to_all(packed, 'dom', 0, 0, tiled=True)  13 us
    all_to_all x1, blocking collectives, exchange(): return lax.all_to_all(packed, 'dom', 0, 0, tiled=True)  10.7 us
  transfers between devices with their start and end apart: 5, of which 5 were waited for; matrix products, arithmetic and copies ran while one was open for 0% of the time, Pallas kernels for 28%

profile of v7, /device:TPU:0, one launch (start us, length us, event | category | flops | bytes accessed | tf_op | source)
XLA Modules:
  0.0 97.5 jit_solution(16707850092498626248)
XLA Ops:
  0.6 2.1 %shard_map.158 = (f32[96,256]{1,0:T(8,128)S(1)}, s32[8,256]{1,0:T(8,128)S(1)}, s32[8,256]{1,0:T(8,128)S(1)}, f32[32,8,128]{2,1,0:T(8,128)}) custom-call(s32[1]{0:T(128)} %bitcast.place_ref, f32[3,6912]{1,0:T(4,128)} %adjoint_hbm.1, s32[8,256]{1,0:T(8,128)} %list_hbm.1), custom_call_target="tpu_custom_call" | custom-call | tf_op jit(solution)/shard_map/pallas_call | solution.py:572
  2.7 7.3 %all-to-all-start = ((f32[32,8,128]{2,1,0:T(8,128)}), f32[32,8,128]{2,1,0:T(8,128)S(1)}, u32[]{:S(2)}, u32[]{:S(2)}) async-start(f32[32,8,128]{2,1,0:T(8,128)} %get-tuple-element.53), calls=%async_computation | async-start | bytes 262144 | tf_op jit(solution)/shard_map/all_to_all | solution.py:33
  10.0 1.4 %shard_map.161 = (f32[96,256]{1,0:T(8,128)S(1)}, f32[6,8,128]{2,1,0:T(8,128)S(1)}) custom-call(f32[3,6912]{1,0:T(4,128)} %primal_hbm.1, s32[8,256]{1,0:T(8,128)S(1)} %get-tuple-element.68.row_ref, s32[8,256]{1,0:T(8,128)S(1)} %get-tuple-element.69.column_ref), custom_call_target="tpu_custom_call" | custom-call | tf_op jit(solution)/shard_map/pallas_call | solution.py:572
  11.4 3.3 %shard_map.159 = (s32[64,256]{1,0:T(8,128)S(1)}, s32[64,256]{1,0:T(8,128)S(1)}, s32[64,256]{1,0:T(8,128)S(1)}, s32[64,256]{1,0:T(8,128)S(1)}, s32[64,256]{1,0:T(...) custom-call(s32[64,256]{1,0:T(8,128)} %connect_hbm.1, ...), custom_call_target="tpu_custom_call" | custom-call | tf_op jit(solution)/shard_map/pallas_call | solution.py:572
  14.7 0.0 copy-start
  14.7 3.0 %shard_map.160 = (f32[192,256]{1,0:T(8,128)S(1)}, f32[3,128]{1,0:T(4,128)S(1)}) custom-call(f32[96,256]{1,0:T(8,128)S(1)} %get-tuple-element.54.tab_ref, s32[64,256]{1,0:T(8,128)S(1)} %get-tuple-element.55.where_ref, s32[64,256]{1,0:T(8,128)S(1)} %get-tuple-element.56.lane_ref, s32[8,256]{1,0:T(8,128)S(1)} %get-tuple-element.57.master_where, ...), custom_call_target="tpu_custom_call" | custom-call | tf_op jit(solution)/shard_map/pallas_call | solution.py:572
  17.7 0.5 all-to-all-done.got_ref
  18.2 0.0 copy-done
  18.2 7.0 %shard_map.162 = (f32[32,8,128]{2,1,0:T(8,128)}, f32[192,256]{1,0:T(8,128)S(1)}, f32[3,128]{1,0:T(4,128)S(1)}) custom-call(s32[1]{0:T(128)} %bitcast.place_ref, f32[32,8,128]{2,1,0:T(8,128)S(1)} %all-to-all-done.got_ref, f32[192,256]{1,0:T(8,128)S(1)} %get-tuple-element.60.cells_ref, f32[3,128]{1,0:T(4,128)S(1)} %get-tuple-element.61.hang_ref, ...), custom_call_target="tpu_custom_call" | custom-call | tf_op jit(solution)/shard_map/pallas_call | solution.py:572
  25.3 5.3 %all-to-all-start.1 = ((f32[32,8,128]{2,1,0:T(8,128)}), f32[32,8,128]{2,1,0:T(8,128)S(1)}, u32[]{:S(2)}, u32[]{:S(2)}) async-start(f32[32,8,128]{2,1,0:T(8,128)} %get-tuple-element.72), calls=%async_computation.1 | async-start | bytes 262144 | tf_op jit(solution)/shard_map/all_to_all | solution.py:33
  30.6 4.0 %shard_map.163.partial_ref = f32[96,256]{1,0:T(8,128)S(1)} custom-call(f32[192,256]{1,0:T(8,128)S(1)} %get-tuple-element.73.image_ref, f32[3,128]{1,0:T(4,128)S(1)} %get-tuple-element.74.held_ref, s32[64,256]{1,0:T(8,128)S(1)} %get-tuple-element.75.row_ref, s32[64,256]{1,0:T(8,128)S(1)} %get-tuple-element.76.column_ref, ...), custom_call_target="tpu_custom_call" | custom-call | tf_op jit(solution)/shard_map/pallas_call | solution.py:572
  34.6 4.2 %all-to-all-done.1.got_ref.got_a = f32[32,8,128]{2,1,0:T(8,128)S(1)} async-done(((f32[32,8,128]{2,1,0:T(8,128)}), f32[32,8,128]{2,1,0:T(8,128)S(1)}, u32[]{:S(2)}, u32[]{:S(2)}) %all-to-all-start.1) | async-done | bytes 131104 | tf_op jit(solution)/shard_map/all_to_all | solution.py:33
  38.8 1.9 %shard_map.164 = (f32[32,8,128]{2,1,0:T(8,128)}, f32[96,256]{1,0:T(8,128)S(1)}) custom-call(s32[1]{0:T(128)} %bitcast.place_ref, f32[32,8,128]{2,1,0:T(8,128)S(1)} %all-to-all-done.1.got_ref.got_a, s32[8,256]{1,0:T(8,128)S(1)} %get-tuple-element.68.row_ref, s32[8,256]{1,0:T(8,128)S(1)} %get-tuple-element.69.column_ref, ...), custom_call_target="tpu_custom_call" | custom-call | tf_op jit(solution)/shard_map/pallas_call | solution.py:572
  40.7 2.8 %all-to-all-start.2 = ((f32[32,8,128]{2,1,0:T(8,128)}), f32[32,8,128]{2,1,0:T(8,128)S(1)}, u32[]{:S(2)}, u32[]{:S(2)}) async-start(f32[32,8,128]{2,1,0:T(8,128)} %get-tuple-element.80), calls=%async_computation.2 | async-start | bytes 262144 | tf_op jit(solution)/shard_map/all_to_all | solution.py:33
  43.5 3.0 %shard_map.165 = (f32[192,256]{1,0:T(8,128)S(1)}, f32[3,128]{1,0:T(4,128)S(1)}) custom-call(f32[96,256]{1,0:T(8,128)S(1)} %get-tuple-element.92.tab_ref, s32[64,256]{1,0:T(8,128)S(1)} %get-tuple-element.55.where_ref, s32[64,256]{1,0:T(8,128)S(1)} %get-tuple-element.56.lane_ref, s32[8,256]{1,0:T(8,128)S(1)} %get-tuple-element.57.master_where, ...), custom_call_target="tpu_custom_call" | custom-call | tf_op jit(solution)/shard_map/pallas_call | solution.py:572
  46.4 3.0 %shard_map.166 = (f32[192,256]{1,0:T(8,128)S(1)}, f32[3,128]{1,0:T(4,128)S(1)}) custom-call(f32[96,256]{1,0:T(8,128)S(1)} %get-tuple-element.84.tab_ref, s32[64,256]{1,0:T(8,128)S(1)} %get-tuple-element.55.where_ref, s32[64,256]{1,0:T(8,128)S(1)} %get-tuple-element.56.lane_ref, s32[8,256]{1,0:T(8,128)S(1)} %get-tuple-element.57.master_where, ...), custom_call_target="tpu_custom_call" | custom-call | tf_op jit(solution)/shard_map/pallas_call | solution.py:572
  49.4 2.1 %all-to-all-done.2.got_ref.got_b = f32[32,8,128]{2,1,0:T(8,128)S(1)} async-done(((f32[32,8,128]{2,1,0:T(8,128)}), f32[32,8,128]{2,1,0:T(8,128)S(1)}, u32[]{:S(2)}, u32[]{:S(2)}) %all-to-all-start.2) | async-done | bytes 131104 | tf_op jit(solution)/shard_map/all_to_all | solution.py:33
  51.5 7.0 %shard_map.167 = (f32[32,8,128]{2,1,0:T(8,128)}, f32[192,256]{1,0:T(8,128)S(1)}, f32[3,128]{1,0:T(4,128)S(1)}) custom-call(s32[1]{0:T(128)} %bitcast.place_ref, f32[32,8,128]{2,1,0:T(8,128)S(1)} %all-to-all-done.2.got_ref.got_b, f32[192,256]{1,0:T(8,128)S(1)} %get-tuple-element.87.cells_ref, f32[3,128]{1,0:T(4,128)S(1)} %get-tuple-element.88.hang_ref, ...), custom_call_target="tpu_custom_call" | custom-call | tf_op jit(solution)/shard_map/pallas_call | solution.py:572
  58.5 3.6 %all-to-all-start.3 = ((f32[32,8,128]{2,1,0:T(8,128)}), f32[32,8,128]{2,1,0:T(8,128)S(1)}, u32[]{:S(2)}, u32[]{:S(2)}) async-start(f32[32,8,128]{2,1,0:T(8,128)} %get-tuple-element.89), calls=%async_computation.3 | async-start | bytes 262144 | tf_op jit(solution)/shard_map/all_to_all | solution.py:33
  62.1 4.0 %shard_map.168.partial_ref = f32[96,256]{1,0:T(8,128)S(1)} custom-call(f32[192,256]{1,0:T(8,128)S(1)} %get-tuple-element.90.image_ref, f32[3,128]{1,0:T(4,128)S(1)} %get-tuple-element.91.held_ref, s32[64,256]{1,0:T(8,128)S(1)} %get-tuple-element.75.row_ref, s32[64,256]{1,0:T(8,128)S(1)} %get-tuple-element.76.column_ref, ...), custom_call_target="tpu_custom_call" | custom-call | tf_op jit(solution)/shard_map/pallas_call | solution.py:572
  66.1 4.2 %all-to-all-done.3.got_ref.got_c = f32[32,8,128]{2,1,0:T(8,128)S(1)} async-done(((f32[32,8,128]{2,1,0:T(8,128)}), f32[32,8,128]{2,1,0:T(8,128)S(1)}, u32[]{:S(2)}, u32[]{:S(2)}) %all-to-all-start.3) | async-done | bytes 131104 | tf_op jit(solution)/shard_map/all_to_all | solution.py:33
  70.3 1.9 %shard_map.169 = (f32[32,8,128]{2,1,0:T(8,128)}, f32[96,256]{1,0:T(8,128)S(1)}) custom-call(s32[1]{0:T(128)} %bitcast.place_ref, f32[32,8,128]{2,1,0:T(8,128)S(1)} %all-to-all-done.3.got_ref.got_c, s32[8,256]{1,0:T(8,128)S(1)} %get-tuple-element.68.row_ref, s32[8,256]{1,0:T(8,128)S(1)} %get-tuple-element.69.column_ref, ...), custom_call_target="tpu_custom_call" | custom-call | tf_op jit(solution)/shard_map/pallas_call | solution.py:572
  72.2 2.8 %all-to-all-start.4 = ((f32[32,8,128]{2,1,0:T(8,128)}), f32[32,8,128]{2,1,0:T(8,128)S(1)}, u32[]{:S(2)}, u32[]{:S(2)}) async-start(f32[32,8,128]{2,1,0:T(8,128)} %get-tuple-element.95), calls=%async_computation.4 | async-start | bytes 262144 | tf_op jit(solution)/shard_map/all_to_all | solution.py:33
  75.0 3.4 %shard_map.170 = (f32[192,256]{1,0:T(8,128)S(1)}, f32[3,128]{1,0:T(4,128)S(1)}, f32[3,6912]{1,0:T(4,128)}) custom-call(f32[96,256]{1,0:T(8,128)S(1)} %get-tuple-element.93.tab_ref, s32[64,256]{1,0:T(8,128)S(1)} %get-tuple-element.55.where_ref, s32[64,256]{1,0:T(8,128)S(1)} %get-tuple-element.56.lane_ref, s32[8,256]{1,0:T(8,128)S(1)} %get-tuple-element.57.master_where, ...), custom_call_target="tpu_custom_call" | custom-call | tf_op jit(solution)/shard_map/pallas_call | solution.py:572
  78.4 0.0 copy-start.1
  78.4 0.0 copy-start.2
  78.4 0.0 copy-start.3
  78.4 2.6 %shard_map.171.ku_ref = f32[192,256]{1,0:T(8,128)S(1)} custom-call(s32[1]{0:T(128)} %bitcast.place_ref, f32[32,8,128]{2,1,0:T(8,128)S(1)} %all-to-all-done.1.got_ref.got_a, f32[32,8,128]{2,1,0:T(8,128)S(1)} %all-to-all-done.2.got_ref.got_b, f32[32,8,128]{2,1,0:T(8,128)S(1)} %all-to-all-done.3.got_ref.got_c, f32[192,256]{1,0:T(8,128)S(1)} %get-tuple-element.100.cells_ref, ...), custom_call_target="tpu_custom_call" | custom-call | tf_op jit(solution)/shard_map/pallas_call | solution.py:572
  81.1 1.9 %all-to-all-done.4.got_ref = f32[32,8,128]{2,1,0:T(8,128)S(1)} async-done(((f32[32,8,128]{2,1,0:T(8,128)}), f32[32,8,128]{2,1,0:T(8,128)S(1)}, u32[]{:S(2)}, u32[]{:S(2)}) %all-to-all-start.4) | async-done | bytes 131104 | tf_op jit(solution)/shard_map/all_to_all | solution.py:33
  83.0 0.0 copy-done.1
  83.0 0.0 copy-done.2
  83.0 0.0 copy-done.3
  83.0 0.0 copy-start.4
  83.0 2.9 %shard_map.172 = (f32[32,1,128]{2,1,0:T(1,128)S(1)}, f32[1,256]{1,0:T(1,128)S(1)}) custom-call(s32[1]{0:T(128)} %bitcast.place_ref, f32[32,8,128]{2,1,0:T(8,128)S(1)} %all-to-all-done.4.got_ref, f32[192,256]{1,0:T(8,128)S(1)} %get-tuple-element.96.cells_ref, f32[3,128]{1,0:T(4,128)S(1)} %get-tuple-element.97.hang_ref, ...), custom_call_target="tpu_custom_call" | custom-call | tf_op jit(solution)/shard_map/pallas_call | solution.py:572
  86.0 10.7 %all_to_all.30.got_ref = f32[32,1,128]{2,1,0:T(1,128)S(1)} all-to-all(f32[32,1,128]{2,1,0:T(1,128)S(1)} %get-tuple-element.102), channel_id=1, replica_groups=mesh['dom'=32] {'dom'}, dimensions={0} | all-to-all | bytes 32768 | tf_op jit(solution)/shard_map/all_to_all | solution.py:33
  96.6 0.0 copy-done.4
  96.6 0.8 shard_map.173
Async XLA Ops:
  2.7 15.5 %all-to-all-start = ((f32[32,8,128]{2,1,0:T(8,128)}), f32[32,8,128]{2,1,0:T(8,128)S(1)}, u32[]{:S(2)}, u32[]{:S(2)}) async-start(f32[32,8,128]{2,1,0:T(8,128)} %get-tuple-element.53), calls=%async_computation | async-start | bytes 262144 | tf_op jit(solution)/shard_map/all_to_all | solution.py:33
  14.7 3.5 %copy-start = (f32[192,192]{1,0:T(8,128)S(1)}, f32[192,192]{1,0:T(8,128)}, u32[]{:S(2)}) copy-start(f32[192,192]{1,0:T(8,128)} %stiffness_ref.5) | copy-start | bytes 442372
  25.3 13.6 %all-to-all-start.1 = ((f32[32,8,128]{2,1,0:T(8,128)}), f32[32,8,128]{2,1,0:T(8,128)S(1)}, u32[]{:S(2)}, u32[]{:S(2)}) async-start(f32[32,8,128]{2,1,0:T(8,128)} %get-tuple-element.72), calls=%async_computation.1 | async-start | bytes 262144 | tf_op jit(solution)/shard_map/all_to_all | solution.py:33
  40.7 10.8 %all-to-all-start.2 = ((f32[32,8,128]{2,1,0:T(8,128)}), f32[32,8,128]{2,1,0:T(8,128)S(1)}, u32[]{:S(2)}, u32[]{:S(2)}) async-start(f32[32,8,128]{2,1,0:T(8,128)} %get-tuple-element.80), calls=%async_computation.2 | async-start | bytes 262144 | tf_op jit(solution)/shard_map/all_to_all | solution.py:33
  58.5 11.8 %all-to-all-start.3 = ((f32[32,8,128]{2,1,0:T(8,128)}), f32[32,8,128]{2,1,0:T(8,128)S(1)}, u32[]{:S(2)}, u32[]{:S(2)}) async-start(f32[32,8,128]{2,1,0:T(8,128)} %get-tuple-element.89), calls=%async_computation.3 | async-start | bytes 262144 | tf_op jit(solution)/shard_map/all_to_all | solution.py:33
  72.2 10.8 %all-to-all-start.4 = ((f32[32,8,128]{2,1,0:T(8,128)}), f32[32,8,128]{2,1,0:T(8,128)S(1)}, u32[]{:S(2)}, u32[]{:S(2)}) async-start(f32[32,8,128]{2,1,0:T(8,128)} %get-tuple-element.95), calls=%async_computation.4 | async-start | bytes 262144 | tf_op jit(solution)/shard_map/all_to_all | solution.py:33
  78.4 4.6 %copy-start.1 = (f32[192,256]{1,0:T(8,128)S(1)}, f32[192,256]{1,0:T(8,128)}, u32[]{:S(2)}) copy-start(f32[192,256]{1,0:T(8,128)} %load_ref.1) | copy-start | bytes 589828
  78.4 4.6 %copy-start.2 = (s32[8,128]{1,0:T(8,128)S(1)}, s32[8,128]{1,0:T(8,128)}, u32[]{:S(2)}) copy-start(s32[8,128]{1,0:T(8,128)} %sub_cell.1) | copy-start | bytes 12292
  78.4 4.6 %copy-start.3 = (s32[8,128]{1,0:T(8,128)S(1)}, s32[8,128]{1,0:T(8,128)}, u32[]{:S(2)}) copy-start(s32[8,128]{1,0:T(8,128)} %sub_face.1) | copy-start | bytes 12292
  83.0 13.6 %copy-start.4 = (s32[8,128]{1,0:T(8,128)S(1)}, s32[8,128]{1,0:T(8,128)}, u32[]{:S(2)}) copy-start(s32[8,128]{1,0:T(8,128)} %owner_ref.1) | copy-start | bytes 12292

commit v8 on v7

--- a/solution.py
+++ b/solution.py
@@ -62,21 +62,23 @@
     return jnp.concatenate(halves, 1)
 
 
-def wide16(row):
-    return jnp.broadcast_to(row, (16, row.shape[1])).astype(bf16)[None]
-
-
 def one_hot(row, count):
+    shape = (count, row.shape[1])
+    mask = lax.broadcasted_iota(i32, shape, 0) == jnp.broadcast_to(row, shape)
+    return jnp.where(mask, 1.0, 0.0).astype(bf16)
+
+
+def match16(row, count):
     width = row.shape[1]
+    wide = jnp.broadcast_to(row.astype(f32), (16, width)).astype(bf16)
     numbers = lax.broadcasted_iota(i32, (count, width), 0).astype(f32).astype(bf16)
-    off = numbers.reshape(count // 16, 16, width) - wide16(row.astype(f32))
-    hot = jnp.maximum(jnp.ones_like(off) - off * off, jnp.zeros_like(off))
-    return hot.reshape(count, width)
-
-
-def spread16(hot, row):
-    count, width = hot.shape
-    return (hot.reshape(count // 16, 16, width) * wide16(row)).reshape(count, width)
+    return numbers.reshape(count // 16, 16, width) == wide[None]
+
+
+def spread16(mask, row):
+    wide = jnp.broadcast_to(row, (16, row.shape[1])).astype(bf16)[None]
+    out = jnp.where(mask, jnp.broadcast_to(wide, mask.shape), jnp.zeros(mask.shape, bf16))
+    return out.reshape(mask.shape[0] * 16, row.shape[1])
 
 
 def pieces(x):
@@ -86,7 +88,7 @@
 
 def gather(table, rows, parts, row_ref, column_ref, sums_ref, wide=False):
     count, width = row_ref.shape
-    step = min(count, 32)
+    step = min(count, 64)
     numbers = lax.broadcasted_iota(i32, (rows, width), 0)
 
     def body(block, carry):
@@ -134,10 +136,10 @@
 
 def scatter(high_ref, low_ref, rows, row_ref, column_ref, sum_ref):
     count = row_ref.shape[0]
-    step = min(count, 16)
+    step = min(count, 32)
 
     def product(start):
-        masks = [one_hot(row_ref[pl.ds(start + j, 1), :], rows) for j in range(8)]
+        masks = [match16(row_ref[pl.ds(start + j, 1), :], rows) for j in range(8)]
         hot = jnp.concatenate(
             [one_hot(column_ref[pl.ds(start + j, 1), :], WIDE) for j in range(8)], 1
         )
@@ -239,14 +241,13 @@
     return -(-count // 8) * 8
 
 
-def export_tiles(table, row_ref, column_ref, sums_ref):
+def export_tiles(table, parts, row_ref, column_ref, sums_ref):
     table = jnp.concatenate(pieces(table), 0)
-    gather(table, OWN, 3, row_ref, column_ref, sums_ref, wide=True)
-    return [tile for part in range(3) for tile in halves(gathered(sums_ref, 8, part))]
-
-
-def export_rows(table, row_ref, column_ref, sums_ref):
-    tiles = export_tiles(table, row_ref, column_ref, sums_ref)
+    gather(table, OWN, parts, row_ref, column_ref, sums_ref, wide=True)
+    return [tile for part in range(parts) for tile in halves(gathered(sums_ref, 8, part))]
+
+
+def rows_of(tiles):
     return [[tile[slot : slot + 1] for tile in tiles] for slot in range(2 * REACH)]
 
 
@@ -270,28 +271,24 @@
 
 
 def first_export(
-    place_ref, adjoint_hbm, list_hbm, tab_ref, row_ref, column_ref,
-    out_ref, pack_ref, adjoint_ref, list_ref, sums_ref, sems,
-):
-    copy_in([(adjoint_hbm, adjoint_ref), (list_hbm, list_ref)], sems)
+    place_ref, adjoint_hbm, primal_hbm, list_hbm, tab_a, tab_p, row_ref, column_ref, extra_ref,
+    out_ref, pack_ref, adjoint_ref, primal_ref, list_ref, sums_ref, sems,
+):
+    copy_in(
+        [(adjoint_hbm, adjoint_ref), (primal_hbm, primal_ref), (list_hbm, list_ref)], sems
+    )
     owned = adjoint_ref.shape[1]
-    fill_table(adjoint_ref, tab_ref)
+    fill_table(adjoint_ref, tab_a)
+    fill_table(primal_ref, tab_p)
     codes = list_ref[...]
     node = lax.rem(17 * codes + lax.broadcasted_iota(i32, codes.shape, 1), owned)
     row_ref[...] = node >> 8
     column_ref[...] = node & 255
-    rows = export_rows(tab_ref[...], row_ref, column_ref, sums_ref)
-    pack(place_ref[0], 1, rows, pack_ref, out_ref)
-
-
-def primal_export(
-    primal_hbm, row_ref, column_ref, tab_ref, out_ref, primal_ref, sums_ref, sems
-):
-    copy_in([(primal_hbm, primal_ref)], sems)
-    fill_table(primal_ref, tab_ref)
-    tiles = export_tiles(tab_ref[...], row_ref, column_ref, sums_ref)
-    for number, tile in enumerate(tiles):
-        out_ref[number] = tile
+    table = jnp.concatenate([tab_a[...], tab_p[...]], 0)
+    tiles = export_tiles(table, 6, row_ref, column_ref, sums_ref)
+    for number in range(6):
+        extra_ref[number] = tiles[6 + number]
+    pack(place_ref[0], 1, rows_of(tiles[:6]), pack_ref, out_ref)
 
 
 def setup(
@@ -338,7 +335,7 @@
     node = jnp.where(codes == pad_code, extent, lax.rem(13 * codes, owned))
     slot = (lax.broadcasted_iota(i32, codes.shape, 1) + 1).astype(f32)
     map_ref[...] = lax.dot_general(
-        spread16(one_hot(node >> 8, OWN), slot),
+        spread16(match16(node >> 8, OWN), slot),
         one_hot(node & 255, WIDE),
         (((1,), (1,)), ((), ())),
         preferred_element_type=f32,
@@ -481,7 +478,7 @@
     returned = scatter_few(values, OWN, row_ref, column_ref, scratch)
     fresh = partial_ref[...] - relaxation * inverse_ref[...] * returned
     tab_ref[...] = fresh
-    rows = export_rows(fresh, row_ref, column_ref, sums_ref)
+    rows = rows_of(export_tiles(fresh, 3, row_ref, column_ref, sums_ref))
     if primal_part is not None:
         add_primal(rows, 1, primal_part, extra_ref)
     pack(place, 1, rows, pack_ref, out_ref)
@@ -621,21 +618,23 @@
     many_sums = ((2, local_values * 8, LANES), f32)
     own_tall = ((3 * tall, LANES), f32)
     edge = [((3 * TALL, LANES), f32), many_sums, cells_shape]
-    tab, list_row, list_column, blocks = call(
+    tab, tab_primal, list_row, list_column, extra, blocks = call(
         first_export,
-        [table] + [(ghost_lists.shape, i32)] * 2 + packed(8),
-        [room(8), (adjoint_start.shape, f32), (ghost_lists.shape, i32), few_sums],
-        [SMALL, FAR, FAR],
-        sems=2,
-    )(place, *away(adjoint_start, ghost_lists))
+        [table, table]
+        + [(ghost_lists.shape, i32)] * 2
+        + [((6, slots, LANES), f32)]
+        + packed(8),
+        [
+            room(8),
+            (adjoint_start.shape, f32),
+            (primal_field.shape, f32),
+            (ghost_lists.shape, i32),
+            ((2, 6 * 64, LANES), f32),
+        ],
+        [SMALL, FAR, FAR, FAR],
+        sems=3,
+    )(place, *away(adjoint_start, primal_field, ghost_lists))
     ghosts = exchange(blocks)
-    tab_primal, extra = call(
-        primal_export,
-        [table, ((6, slots, LANES), f32)],
-        [(primal_field.shape, f32), few_sums],
-        [FAR, FAST, FAST],
-        sems=1,
-    )(*away(primal_field), list_row, list_column)
     far = (
         connectivity, hang_node.reshape(1, -1), hang_master, hang_weight, adjoint_source,
         inverse_diagonal,

time: 98 us -> 101 us (1.031)
  Pallas kernels: 51.3 us -> 54.1 us
  waiting for transfers between devices: 13 us -> 11.4 us
  blocking collectives: 10.7 us -> 12 us
    pallas_call x16 -> x15, Pallas kernels: 51.3 us -> 54.1 us  [run(): pl.pallas_call(kernel, out_shape=[jax.ShapeDtypeStruct(shape, kind) for s...]
    all_to_all x5, waiting for transfers between devices: 13 us -> 11.4 us  [exchange(): return lax.all_to_all(packed, 'dom', 0, 0, tiled=True)]
    all_to_all x1, blocking collectives: 10.7 us -> 12 us  [exchange(): return lax.all_to_all(packed, 'dom', 0, 0, tiled=True)]
  transfers between devices with their start and end apart: 5 -> 5, of which waited for: 5 -> 5; matrix products, arithmetic and copies ran while one was open for 0% -> 0% of each run, Pallas kernels for 28% -> 29%
where the time goes in v8:
time: 101 us
  Pallas kernels  54.1 us (54%)
  starting transfers between devices  22.7 us (22%)
  blocking collectives  12 us (12%)
  waiting for transfers between devices  11.4 us (11%)
    pallas_call x15, Pallas kernels, run(): pl.pallas_call(kernel, out_shape=[jax.ShapeDtypeStruct(shape, kind) for s...  54.1 us
    all_to_all x5, starting transfers between devices, exchange(): return lax.all_to_all(packed, 'dom', 0, 0, tiled=True)  22.7 us
    all_to_all x1, blocking collectives, exchange(): return lax.all_to_all(packed, 'dom', 0, 0, tiled=True)  12 us
    all_to_all x5, waiting for transfers between devices, exchange(): return lax.all_to_all(packed, 'dom', 0, 0, tiled=True)  11.4 us
  transfers between devices with their start and end apart: 5, of which 5 were waited for; matrix products, arithmetic and copies ran while one was open for 0% of the time, Pallas kernels for 29%

profile of v8, /device:TPU:0, one launch (start us, length us, event | category | flops | bytes accessed | tf_op | source)
XLA Modules:
  0.0 101.0 jit_solution(4287271347772437013)
XLA Ops:
  0.6 2.4 %shard_map.158 = (f32[96,256]{1,0:T(8,128)S(1)}, f32[96,256]{1,0:T(8,128)S(1)}, s32[8,256]{1,0:T(8,128)S(1)}, s32[8,256]{1,0:T(8,128)S(1)}, f32[6,8,128]{2,1,0:T(8,128)S(1)}, /*index=5*/f32[32,8,128]{2,1,0:T(8,128)}) custom-call(s32[1]{0:T(128)} %bitcast.place_ref, f32[3,6912]{1,0:T(4,128)} %adjoint_hbm.1, f32[3,6912]{1,0:T(4,128)} %primal_hbm.1, ...), custom_call_target="tpu_custom_call" | custom-call | tf_op jit(solution)/shard_map/pallas_call | solution.py:569
  3.0 7.3 %all-to-all-start = ((f32[32,8,128]{2,1,0:T(8,128)}), f32[32,8,128]{2,1,0:T(8,128)S(1)}, u32[]{:S(2)}, u32[]{:S(2)}) async-start(f32[32,8,128]{2,1,0:T(8,128)} %get-tuple-element.53), calls=%async_computation | async-start | bytes 262144 | tf_op jit(solution)/shard_map/all_to_all | solution.py:33
  10.3 3.7 %shard_map.159 = (s32[64,256]{1,0:T(8,128)S(1)}, s32[64,256]{1,0:T(8,128)S(1)}, s32[64,256]{1,0:T(8,128)S(1)}, s32[64,256]{1,0:T(8,128)S(1)}, s32[64,256]{1,0:T(...) custom-call(s32[64,256]{1,0:T(8,128)} %connect_hbm.1, ...), custom_call_target="tpu_custom_call" | custom-call | tf_op jit(solution)/shard_map/pallas_call | solution.py:569
  14.1 0.0 copy-start
  14.1 3.6 %shard_map.160 = (f32[192,256]{1,0:T(8,128)S(1)}, f32[3,128]{1,0:T(4,128)S(1)}) custom-call(f32[96,256]{1,0:T(8,128)S(1)} %get-tuple-element.54.tab_ref, s32[64,256]{1,0:T(8,128)S(1)} %get-tuple-element.55.where_ref, s32[64,256]{1,0:T(8,128)S(1)} %get-tuple-element.56.lane_ref, s32[8,256]{1,0:T(8,128)S(1)} %get-tuple-element.57.master_where, ...), custom_call_target="tpu_custom_call" | custom-call | tf_op jit(solution)/shard_map/pallas_call | solution.py:569
  17.7 0.9 all-to-all-done.got_ref
  18.5 0.0 copy-done
  18.5 7.3 %shard_map.161 = (f32[32,8,128]{2,1,0:T(8,128)}, f32[192,256]{1,0:T(8,128)S(1)}, f32[3,128]{1,0:T(4,128)S(1)}) custom-call(s32[1]{0:T(128)} %bitcast.place_ref, f32[32,8,128]{2,1,0:T(8,128)S(1)} %all-to-all-done.got_ref, f32[192,256]{1,0:T(8,128)S(1)} %get-tuple-element.60.cells_ref, f32[3,128]{1,0:T(4,128)S(1)} %get-tuple-element.61.hang_ref, ...), custom_call_target="tpu_custom_call" | custom-call | tf_op jit(solution)/shard_map/pallas_call | solution.py:569
  25.8 5.2 %all-to-all-start.1 = ((f32[32,8,128]{2,1,0:T(8,128)}), f32[32,8,128]{2,1,0:T(8,128)S(1)}, u32[]{:S(2)}, u32[]{:S(2)}) async-start(f32[32,8,128]{2,1,0:T(8,128)} %get-tuple-element.70), calls=%async_computation.1 | async-start | bytes 262144 | tf_op jit(solution)/shard_map/all_to_all | solution.py:33
  31.0 3.7 %shard_map.162.partial_ref = f32[96,256]{1,0:T(8,128)S(1)} custom-call(f32[192,256]{1,0:T(8,128)S(1)} %get-tuple-element.73.image_ref, f32[3,128]{1,0:T(4,128)S(1)} %get-tuple-element.74.held_ref, s32[64,256]{1,0:T(8,128)S(1)} %get-tuple-element.75.row_ref, s32[64,256]{1,0:T(8,128)S(1)} %get-tuple-element.76.column_ref, ...), custom_call_target="tpu_custom_call" | custom-call | tf_op jit(solution)/shard_map/pallas_call | solution.py:569
  34.7 4.4 %all-to-all-done.1.got_ref.got_a = f32[32,8,128]{2,1,0:T(8,128)S(1)} async-done(((f32[32,8,128]{2,1,0:T(8,128)}), f32[32,8,128]{2,1,0:T(8,128)S(1)}, u32[]{:S(2)}, u32[]{:S(2)}) %all-to-all-start.1) | async-done | bytes 131104 | tf_op jit(solution)/shard_map/all_to_all | solution.py:33
  39.0 1.9 %shard_map.163 = (f32[32,8,128]{2,1,0:T(8,128)}, f32[96,256]{1,0:T(8,128)S(1)}) custom-call(s32[1]{0:T(128)} %bitcast.place_ref, f32[32,8,128]{2,1,0:T(8,128)S(1)} %all-to-all-done.1.got_ref.got_a, s32[8,256]{1,0:T(8,128)S(1)} %get-tuple-element.71.row_ref, s32[8,256]{1,0:T(8,128)S(1)} %get-tuple-element.72.column_ref, ...), custom_call_target="tpu_custom_call" | custom-call | tf_op jit(solution)/shard_map/pallas_call | solution.py:569
  40.9 2.6 %all-to-all-start.2 = ((f32[32,8,128]{2,1,0:T(8,128)}), f32[32,8,128]{2,1,0:T(8,128)S(1)}, u32[]{:S(2)}, u32[]{:S(2)}) async-start(f32[32,8,128]{2,1,0:T(8,128)} %get-tuple-element.80), calls=%async_computation.2 | async-start | bytes 262144 | tf_op jit(solution)/shard_map/all_to_all | solution.py:33
  43.5 3.6 %shard_map.164 = (f32[192,256]{1,0:T(8,128)S(1)}, f32[3,128]{1,0:T(4,128)S(1)}) custom-call(f32[96,256]{1,0:T(8,128)S(1)} %get-tuple-element.92.tab_ref, s32[64,256]{1,0:T(8,128)S(1)} %get-tuple-element.55.where_ref, s32[64,256]{1,0:T(8,128)S(1)} %get-tuple-element.56.lane_ref, s32[8,256]{1,0:T(8,128)S(1)} %get-tuple-element.57.master_where, ...), custom_call_target="tpu_custom_call" | custom-call | tf_op jit(solution)/shard_map/pallas_call | solution.py:569
  47.1 3.6 %shard_map.165 = (f32[192,256]{1,0:T(8,128)S(1)}, f32[3,128]{1,0:T(4,128)S(1)}) custom-call(f32[96,256]{1,0:T(8,128)S(1)} %get-tuple-element.84.tab_ref, s32[64,256]{1,0:T(8,128)S(1)} %get-tuple-element.55.where_ref, s32[64,256]{1,0:T(8,128)S(1)} %get-tuple-element.56.lane_ref, s32[8,256]{1,0:T(8,128)S(1)} %get-tuple-element.57.master_where, ...), custom_call_target="tpu_custom_call" | custom-call | tf_op jit(solution)/shard_map/pallas_call | solution.py:569
  50.7 1.0 all-to-all-done.2.got_ref.got_b
  51.7 7.3 %shard_map.166 = (f32[32,8,128]{2,1,0:T(8,128)}, f32[192,256]{1,0:T(8,128)S(1)}, f32[3,128]{1,0:T(4,128)S(1)}) custom-call(s32[1]{0:T(128)} %bitcast.place_ref, f32[32,8,128]{2,1,0:T(8,128)S(1)} %all-to-all-done.2.got_ref.got_b, f32[192,256]{1,0:T(8,128)S(1)} %get-tuple-element.87.cells_ref, f32[3,128]{1,0:T(4,128)S(1)} %get-tuple-element.88.hang_ref, ...), custom_call_target="tpu_custom_call" | custom-call | tf_op jit(solution)/shard_map/pallas_call | solution.py:569
  59.0 5.1 %all-to-all-start.3 = ((f32[32,8,128]{2,1,0:T(8,128)}), f32[32,8,128]{2,1,0:T(8,128)S(1)}, u32[]{:S(2)}, u32[]{:S(2)}) async-start(f32[32,8,128]{2,1,0:T(8,128)} %get-tuple-element.89), calls=%async_computation.3 | async-start | bytes 262144 | tf_op jit(solution)/shard_map/all_to_all | solution.py:33
  64.1 3.7 %shard_map.167.partial_ref = f32[96,256]{1,0:T(8,128)S(1)} custom-call(f32[192,256]{1,0:T(8,128)S(1)} %get-tuple-element.90.image_ref, f32[3,128]{1,0:T(4,128)S(1)} %get-tuple-element.91.held_ref, s32[64,256]{1,0:T(8,128)S(1)} %get-tuple-element.75.row_ref, s32[64,256]{1,0:T(8,128)S(1)} %get-tuple-element.76.column_ref, ...), custom_call_target="tpu_custom_call" | custom-call | tf_op jit(solution)/shard_map/pallas_call | solution.py:569
  67.7 4.3 %all-to-all-done.3.got_ref.got_c = f32[32,8,128]{2,1,0:T(8,128)S(1)} async-done(((f32[32,8,128]{2,1,0:T(8,128)}), f32[32,8,128]{2,1,0:T(8,128)S(1)}, u32[]{:S(2)}, u32[]{:S(2)}) %all-to-all-start.3) | async-done | bytes 131104 | tf_op jit(solution)/shard_map/all_to_all | solution.py:33
  72.1 1.9 %shard_map.168 = (f32[32,8,128]{2,1,0:T(8,128)}, f32[96,256]{1,0:T(8,128)S(1)}) custom-call(s32[1]{0:T(128)} %bitcast.place_ref, f32[32,8,128]{2,1,0:T(8,128)S(1)} %all-to-all-done.3.got_ref.got_c, s32[8,256]{1,0:T(8,128)S(1)} %get-tuple-element.71.row_ref, s32[8,256]{1,0:T(8,128)S(1)} %get-tuple-element.72.column_ref, ...), custom_call_target="tpu_custom_call" | custom-call | tf_op jit(solution)/shard_map/pallas_call | solution.py:569
  73.9 2.6 %all-to-all-start.4 = ((f32[32,8,128]{2,1,0:T(8,128)}), f32[32,8,128]{2,1,0:T(8,128)S(1)}, u32[]{:S(2)}, u32[]{:S(2)}) async-start(f32[32,8,128]{2,1,0:T(8,128)} %get-tuple-element.95), calls=%async_computation.4 | async-start | bytes 262144 | tf_op jit(solution)/shard_map/all_to_all | solution.py:33
  76.5 4.3 %shard_map.169 = (f32[192,256]{1,0:T(8,128)S(1)}, f32[3,128]{1,0:T(4,128)S(1)}, f32[3,6912]{1,0:T(4,128)}) custom-call(f32[96,256]{1,0:T(8,128)S(1)} %get-tuple-element.93.tab_ref, s32[64,256]{1,0:T(8,128)S(1)} %get-tuple-element.55.where_ref, s32[64,256]{1,0:T(8,128)S(1)} %get-tuple-element.56.lane_ref, s32[8,256]{1,0:T(8,128)S(1)} %get-tuple-element.57.master_where, ...), custom_call_target="tpu_custom_call" | custom-call | tf_op jit(solution)/shard_map/pallas_call | solution.py:569
  80.8 0.0 copy-start.1
  80.8 0.0 copy-start.2
  80.8 0.0 copy-start.3
  80.8 3.1 %shard_map.170.ku_ref = f32[192,256]{1,0:T(8,128)S(1)} custom-call(s32[1]{0:T(128)} %bitcast.place_ref, f32[32,8,128]{2,1,0:T(8,128)S(1)} %all-to-all-done.1.got_ref.got_a, f32[32,8,128]{2,1,0:T(8,128)S(1)} %all-to-all-done.2.got_ref.got_b, f32[32,8,128]{2,1,0:T(8,128)S(1)} %all-to-all-done.3.got_ref.got_c, f32[192,256]{1,0:T(8,128)S(1)} %get-tuple-element.100.cells_ref, ...), custom_call_target="tpu_custom_call" | custom-call | tf_op jit(solution)/shard_map/pallas_call | solution.py:569
  83.9 0.9 all-to-all-done.4.got_ref
  84.8 0.0 copy-done.1
  84.8 0.0 copy-done.2
  84.8 0.0 copy-done.3
  84.8 0.0 copy-start.4
  84.8 3.3 %shard_map.171 = (f32[32,1,128]{2,1,0:T(1,128)S(1)}, f32[1,256]{1,0:T(1,128)S(1)}) custom-call(s32[1]{0:T(128)} %bitcast.place_ref, f32[32,8,128]{2,1,0:T(8,128)S(1)} %all-to-all-done.4.got_ref, f32[192,256]{1,0:T(8,128)S(1)} %get-tuple-element.96.cells_ref, f32[3,128]{1,0:T(4,128)S(1)} %get-tuple-element.97.hang_ref, ...), custom_call_target="tpu_custom_call" | custom-call | tf_op jit(solution)/shard_map/pallas_call | solution.py:569
  88.1 12.0 %all_to_all.30.got_ref = f32[32,1,128]{2,1,0:T(1,128)S(1)} all-to-all(f32[32,1,128]{2,1,0:T(1,128)S(1)} %get-tuple-element.102), channel_id=1, replica_groups=mesh['dom'=32] {'dom'}, dimensions={0} | all-to-all | bytes 32768 | tf_op jit(solution)/shard_map/all_to_all | solution.py:33
  100.1 0.0 copy-done.4
  100.1 0.9 shard_map.172
Async XLA Ops:
  3.0 15.5 %all-to-all-start = ((f32[32,8,128]{2,1,0:T(8,128)}), f32[32,8,128]{2,1,0:T(8,128)S(1)}, u32[]{:S(2)}, u32[]{:S(2)}) async-start(f32[32,8,128]{2,1,0:T(8,128)} %get-tuple-element.53), calls=%async_computation | async-start | bytes 262144 | tf_op jit(solution)/shard_map/all_to_all | solution.py:33
  14.1 4.5 %copy-start = (f32[192,192]{1,0:T(8,128)S(1)}, f32[192,192]{1,0:T(8,128)}, u32[]{:S(2)}) copy-start(f32[192,192]{1,0:T(8,128)} %stiffness_ref.5) | copy-start | bytes 442372
  25.8 13.2 %all-to-all-start.1 = ((f32[32,8,128]{2,1,0:T(8,128)}), f32[32,8,128]{2,1,0:T(8,128)S(1)}, u32[]{:S(2)}, u32[]{:S(2)}) async-start(f32[32,8,128]{2,1,0:T(8,128)} %get-tuple-element.70), calls=%async_computation.1 | async-start | bytes 262144 | tf_op jit(solution)/shard_map/all_to_all | solution.py:33
  40.9 10.8 %all-to-all-start.2 = ((f32[32,8,128]{2,1,0:T(8,128)}), f32[32,8,128]{2,1,0:T(8,128)S(1)}, u32[]{:S(2)}, u32[]{:S(2)}) async-start(f32[32,8,128]{2,1,0:T(8,128)} %get-tuple-element.80), calls=%async_computation.2 | async-start | bytes 262144 | tf_op jit(solution)/shard_map/all_to_all | solution.py:33
  59.0 13.1 %all-to-all-start.3 = ((f32[32,8,128]{2,1,0:T(8,128)}), f32[32,8,128]{2,1,0:T(8,128)S(1)}, u32[]{:S(2)}, u32[]{:S(2)}) async-start(f32[32,8,128]{2,1,0:T(8,128)} %get-tuple-element.89), calls=%async_computation.3 | async-start | bytes 262144 | tf_op jit(solution)/shard_map/all_to_all | solution.py:33
  73.9 10.8 %all-to-all-start.4 = ((f32[32,8,128]{2,1,0:T(8,128)}), f32[32,8,128]{2,1,0:T(8,128)S(1)}, u32[]{:S(2)}, u32[]{:S(2)}) async-start(f32[32,8,128]{2,1,0:T(8,128)} %get-tuple-element.95), calls=%async_computation.4 | async-start | bytes 262144 | tf_op jit(solution)/shard_map/all_to_all | solution.py:33
  80.8 4.0 %copy-start.1 = (f32[192,256]{1,0:T(8,128)S(1)}, f32[192,256]{1,0:T(8,128)}, u32[]{:S(2)}) copy-start(f32[192,256]{1,0:T(8,128)} %load_ref.1) | copy-start | bytes 589828
  80.8 4.0 %copy-start.2 = (s32[8,128]{1,0:T(8,128)S(1)}, s32[8,128]{1,0:T(8,128)}, u32[]{:S(2)}) copy-start(s32[8,128]{1,0:T(8,128)} %sub_cell.1) | copy-start | bytes 12292
  80.8 4.0 %copy-start.3 = (s32[8,128]{1,0:T(8,128)S(1)}, s32[8,128]{1,0:T(8,128)}, u32[]{:S(2)}) copy-start(s32[8,128]{1,0:T(8,128)} %sub_face.1) | copy-start | bytes 12292
  84.8 15.3 %copy-start.4 = (s32[8,128]{1,0:T(8,128)S(1)}, s32[8,128]{1,0:T(8,128)}, u32[]{:S(2)}) copy-start(s32[8,128]{1,0:T(8,128)} %owner_ref.1) | copy-start | bytes 12292

commit v9 on v8

--- a/solution.py
+++ b/solution.py
@@ -12,7 +12,7 @@
 LANES = 128
 WIDE = 2 * LANES
 OWN = 32
-EDGE = 16
+EDGE = 32
 TALL = 24
 NOWHERE = 126
 
@@ -62,12 +62,6 @@
     return jnp.concatenate(halves, 1)
 
 
-def one_hot(row, count):
-    shape = (count, row.shape[1])
-    mask = lax.broadcasted_iota(i32, shape, 0) == jnp.broadcast_to(row, shape)
-    return jnp.where(mask, 1.0, 0.0).astype(bf16)
-
-
 def match16(row, count):
     width = row.shape[1]
     wide = jnp.broadcast_to(row.astype(f32), (16, width)).astype(bf16)
@@ -75,6 +69,12 @@
     return numbers.reshape(count // 16, 16, width) == wide[None]
 
 
+def one_hot(row, count):
+    mask = match16(row, count)
+    ones = jnp.ones(mask.shape, bf16)
+    return jnp.where(mask, ones, jnp.zeros_like(ones)).reshape(count, row.shape[1])
+
+
 def spread16(mask, row):
     wide = jnp.broadcast_to(row, (16, row.shape[1])).astype(bf16)[None]
     out = jnp.where(mask, jnp.broadcast_to(wide, mask.shape), jnp.zeros(mask.shape, bf16))
@@ -86,10 +86,12 @@
     return high, (x - high.astype(f32)).astype(bf16)
 
 
-def gather(table, rows, parts, row_ref, column_ref, sums_ref, wide=False):
-    count, width = row_ref.shape
-    step = min(count, 64)
-    numbers = lax.broadcasted_iota(i32, (rows, width), 0)
+def gather(jobs, column_ref, wide=False):
+    count, width = column_ref.shape
+    tables = jnp.concatenate([job[0] for job in jobs], 0)
+    high = tables.shape[0]
+    numbers = lax.broadcasted_iota(i32, (max(job[1] for job in jobs), width), 0)
+    step = min(count, 32 if sum(job[1] * job[2] for job in jobs) <= 192 else 16)
 
     def body(block, carry):
         start = pl.multiple_of(block * step, step)
@@ -97,17 +99,23 @@
             hot = one_hot(column_ref[pl.ds(start + j, 1), :], WIDE if wide else LANES)
             if not wide:
                 hot = jnp.concatenate([hot, hot], 0)
-            found = jnp.dot(table, hot, preferred_element_type=f32)
+            all_found = jnp.dot(tables, hot, preferred_element_type=f32)
             if wide:
-                found = found[: parts * rows] + found[parts * rows :]
-            mask = numbers == jnp.broadcast_to(row_ref[pl.ds(start + j, 1), :], numbers.shape)
-            for part in range(parts):
-                kept = jnp.where(mask, found[part * rows : (part + 1) * rows], 0.0)
-                kept = jnp.sum(kept.reshape(rows // 8, 8, width), 0)
-                for half in range(width // LANES):
-                    sums_ref[half, pl.ds(part * count * 8 + start * 8 + j * 8, 8), :] = kept[
-                        :, half * LANES : (half + 1) * LANES
-                    ]
+                all_found = all_found[: high // 2] + all_found[high // 2 :]
+            top = 0
+            for _, rows, parts, row_ref, sums_ref in jobs:
+                found = all_found[top : top + parts * rows]
+                top += parts * rows
+                mask = numbers[:rows] == jnp.broadcast_to(
+                    row_ref[pl.ds(start + j, 1), :], (rows, width)
+                )
+                for part in range(parts):
+                    kept = jnp.where(mask, found[part * rows : (part + 1) * rows], 0.0)
+                    kept = jnp.sum(kept.reshape(rows // 8, 8, width), 0)
+                    for half in range(width // LANES):
+                        sums_ref[half, pl.ds(part * count * 8 + start * 8 + j * 8, 8), :] = kept[
+                            :, half * LANES : (half + 1) * LANES
+                        ]
         return carry
 
     if count == step:
@@ -141,7 +149,7 @@
     def product(start):
         masks = [match16(row_ref[pl.ds(start + j, 1), :], rows) for j in range(8)]
         hot = jnp.concatenate(
-            [one_hot(column_ref[pl.ds(start + j, 1), :], WIDE) for j in range(8)], 1
+            [one_hot(column_ref[pl.ds(start + j, 1), :], sum_ref.shape[1]) for j in range(8)], 1
         )
         stacked = [
             jnp.concatenate(
@@ -194,8 +202,8 @@
     return add_pieces(sum_ref[...])
 
 
-def few(rows):
-    return [((24, WIDE), f32)] * 2 + [((6 * rows, WIDE), f32)]
+def few(rows, columns):
+    return [((24, WIDE), f32)] * 2 + [((6 * rows, columns), f32)]
 
 
 def spread_hanging(held, weight, rows, row_ref, column_ref, scratch):
@@ -204,10 +212,9 @@
     return scatter_few(values, rows, row_ref, column_ref, scratch)
 
 
-def sum_masters(table, tall, weight, where_ref, lane_ref, sums_ref):
-    gather(table, tall, 3, where_ref, lane_ref, sums_ref)
+def sum_masters(sums_ref, first, weight):
     totals = []
-    for part in range(3):
+    for part in range(first, first + 3):
         left, right = halves(weight * gathered(sums_ref, 8, part))
         totals.append(jnp.sum(left + right, 0, keepdims=True))
     return totals
@@ -243,7 +250,7 @@
 
 def export_tiles(table, parts, row_ref, column_ref, sums_ref):
     table = jnp.concatenate(pieces(table), 0)
-    gather(table, OWN, parts, row_ref, column_ref, sums_ref, wide=True)
+    gather([(table, OWN, parts, row_ref, sums_ref)], column_ref, wide=True)
     return [tile for part in range(parts) for tile in halves(gathered(sums_ref, 8, part))]
 
 
@@ -292,29 +299,13 @@
 
 
 def setup(
-    connect_hbm, node_hbm, master_hbm, weight_hbm, source_hbm, inverse_hbm, modulus_hbm,
-    own_where, own_row, edge_where, edge_row, lane_ref, column_ref, edge_column, master_own, master_own_row,
-    master_edge, master_edge_row, master_lane, master_column, weight_out, tab_source, tab_inverse,
-    modulus_out,
-    connect_ref, node_ref, master_ref, weight_ref, source_ref, inverse_ref, map_ref, tall_ref, sums_ref,
-    sems,
-):
-    copy_in(
-        [
-            (connect_hbm, connect_ref),
-            (node_hbm, node_ref),
-            (master_hbm, master_ref),
-            (weight_hbm, weight_ref),
-            (source_hbm, source_ref),
-            (inverse_hbm, inverse_ref),
-            (modulus_hbm, modulus_out),
-        ],
-        sems,
-    )
-    owned = source_ref.shape[1]
+    owned, connect_ref, node_ref, master_ref, weight_ref, modulus_ref,
+    own_where, own_row, edge_where, lane_ref, column_ref, master_own, master_own_row,
+    master_edge, master_lane, master_column, weight_out, modulus_out,
+    map_ref, tall_ref, sums_ref,
+):
     extent = owned + 2 * REACH * WIDE
-    fill_table(source_ref, tab_source)
-    fill_table(inverse_ref, tab_inverse)
+    modulus_out[...] = modulus_ref[...]
     codes = master_ref[...]
     master = lax.rem(17 * codes + 8 * lax.broadcasted_iota(i32, codes.shape, 1), extent)
     count = codes.shape[0] // 2
@@ -326,9 +317,7 @@
     master_own[...] = jnp.where(where < last, where, NOWHERE)
     master_edge[...] = jnp.where(where < last, NOWHERE, where - last)
     master_lane[...] = master & 127
-    row = master >> 8
-    master_own_row[...] = jnp.where(where < last, row, NOWHERE)
-    master_edge_row[...] = jnp.where(where < last, NOWHERE, row - last // 2)
+    master_own_row[...] = jnp.where(where < last, master >> 8, NOWHERE)
     master_column[...] = master & 255
 
     codes = node_ref[...]
@@ -353,7 +342,7 @@
             row : row + 1, half * LANES : (half + 1) * LANES
         ]
     table = jnp.concatenate(pieces(tall_ref[...]), 1)
-    gather(table, tall_ref.shape[0], 1, own_where, lane_ref, sums_ref)
+    gather([(table, tall_ref.shape[0], 1, own_where, sums_ref)], lane_ref)
     slot = gathered(sums_ref, codes.shape[0], 0).astype(i32)
     where = slots >> 7
     hanging = slot > 0
@@ -363,69 +352,75 @@
     where_own = jnp.where(hanging | outside, NOWHERE, where)
     own_where[...] = where_own
     own_row[...], column_ref[...] = rows_and_columns(where_own, lane)
-    where_edge = jnp.where(hanging, 4 * REACH, jnp.where(outside, where - last, NOWHERE))
-    edge_where[...] = where_edge
-    edge_row[...], edge_column[...] = rows_and_columns(where_edge, lane)
+    edge_where[...] = jnp.where(hanging, 4 * REACH, jnp.where(outside, where - last, NOWHERE))
 
 
 def own_gather(
-    half_rows, tab_ref, where_ref, lane_ref, master_where, master_lane, weight_ref, cells_ref,
-    hang_ref, *rest,
-):
-    *final_ref, tall_ref, sums_ref = rest
-    table = tall_table([tab_ref], half_rows, tall_ref)
+    half_rows, fields, row_ref, lane_ref, master_row, master_lane, weight_ref, *refs
+):
+    tab_refs, refs = refs[:fields], refs[fields:]
+    outs, (tall_ref, sums_ref) = refs[:-2], refs[-2:]
     tall = up8(half_rows)
-    found = sum_masters(table, tall, weight_ref[...], master_where, master_lane, sums_ref)
-    for part in range(3):
-        hang_ref[part : part + 1, :] = found[part]
-    gather(table, tall, 3, where_ref, lane_ref, sums_ref)
-    count = where_ref.shape[0]
-    for part in range(3):
-        cells_ref[part * count : (part + 1) * count, :] = gathered(sums_ref, count, part)
-    if final_ref:
-        final_ref = final_ref[0]
-        for row in range(final_ref.shape[1] // WIDE):
-            for part in range(3):
-                final_ref[part : part + 1, row * WIDE : (row + 1) * WIDE] = tab_ref[
-                    part * OWN + row : part * OWN + row + 1, :
-                ]
-
-
-def edge_gather(
-    place, got_refs, first, cells_ref, hang_ref, where_ref, lane_ref, master_where, master_lane,
-    weight_ref, edge_ref, sums_ref, out_ref,
-):
-    slots = 2 * REACH
+    table = tall_table(tab_refs, half_rows, tall_ref)
+    parts = 3 * fields
+    gather([(table, tall, parts, master_row, sums_ref)], master_lane)
+    found = sum_masters(sums_ref, 0, weight_ref[...])
+    if fields == 2:
+        found += sum_masters(sums_ref, 3, weight_ref[...])
+    for field in range(fields):
+        for part in range(3):
+            outs[2 * field + 1][part : part + 1, :] = found[3 * field + part]
+    gather([(table, tall, parts, row_ref, sums_ref)], lane_ref)
+    count = row_ref.shape[0]
+    for field in range(fields):
+        cells_ref = outs[2 * field]
+        for part in range(3):
+            cells_ref[part * count : (part + 1) * count, :] = gathered(
+                sums_ref, count, 3 * field + part
+            )
+
+
+def ghost_rows(place, got_refs, first, edge_ref):
     edge_ref[...] = jnp.zeros_like(edge_ref)
     for part in range(3):
         for half in range(2):
             lines = landed(place, 1, got_refs[part], first[part] + half)
-            for slot in range(slots):
+            for slot in range(2 * REACH):
                 at = part * TALL + 2 * slot + half
                 edge_ref[at : at + 1, :] = lines[slot]
-    table = jnp.concatenate(pieces(edge_ref[...]), 1)
-    found = sum_masters(table, TALL, weight_ref[...], master_where, master_lane, sums_ref)
+    return jnp.concatenate(pieces(edge_ref[...]), 1)
+
+
+def hanging_rows(found, hang_ref, edge_ref):
     for part in range(3):
-        at = part * TALL + 2 * slots
+        at = part * TALL + 4 * REACH
         edge_ref[at : at + 1, :] = found[part] + hang_ref[part : part + 1, :]
-    table = jnp.concatenate(pieces(edge_ref[...]), 1)
-    gather(table, TALL, 3, where_ref, lane_ref, sums_ref)
-    count = where_ref.shape[0]
+    return jnp.concatenate(pieces(edge_ref[...]), 1)
+
+
+def edge_gather(
+    place, got_refs, first, cells_ref, hang_ref, row_ref, lane_ref, master_row, master_lane,
+    weight_ref, edge_ref, sums_ref, out_ref,
+):
+    table = ghost_rows(place, got_refs, first, edge_ref)
+    gather([(table, TALL, 3, master_row, sums_ref)], master_lane)
+    table = hanging_rows(sum_masters(sums_ref, 0, weight_ref[...]), hang_ref, edge_ref)
+    gather([(table, TALL, 3, row_ref, sums_ref)], lane_ref)
+    count = row_ref.shape[0]
     for part in range(3):
         rows = slice(part * count, (part + 1) * count)
         out_ref[rows, :] = cells_ref[rows, :] + gathered(sums_ref, count, part)
 
 
 def edge_product(
-    primal_part, place_ref, got_ref, cells_ref, hang_ref, where_ref, lane_ref, master_where, master_lane,
-    weight_ref, row_ref, column_ref, master_row, master_column, extra_ref, modulus_ref,
-    stiffness_ref, out_ref,
+    primal_part, place_ref, got_ref, cells_ref, hang_ref, row_ref, lane_ref, master_row,
+    master_lane, weight_ref, extra_ref, modulus_ref, stiffness_ref, out_ref,
     image_ref, held_ref, pack_ref, edge_ref, sums_ref, full_ref, low_ref, sum_ref, *scratch,
 ):
     place = place_ref[0]
     edge_gather(
-        place, [got_ref] * 3, (0, 2, 4), cells_ref, hang_ref, where_ref, lane_ref,
-        master_where, master_lane, weight_ref, edge_ref, sums_ref, full_ref,
+        place, [got_ref] * 3, (0, 2, 4), cells_ref, hang_ref, row_ref, lane_ref,
+        master_row, master_lane, weight_ref, edge_ref, sums_ref, full_ref,
     )
     image = modulus_ref[...] * lax.dot_general(
         stiffness_ref[...],
@@ -436,17 +431,17 @@
     )
     image_ref[...] = image
     full_ref[...], low_ref[...] = split32(image)
-    scatter(full_ref, low_ref, EDGE, row_ref, column_ref, sum_ref)
+    scatter(full_ref, low_ref, EDGE, row_ref, lane_ref, sum_ref)
     sums = add_pieces(sum_ref[...])
     slots = 2 * REACH
     held = jnp.concatenate(
-        [sums[part * EDGE + slots : part * EDGE + slots + 1, :LANES] for part in range(3)], 0
+        [sums[part * EDGE + 2 * slots : part * EDGE + 2 * slots + 1] for part in range(3)], 0
     )
     held_ref[...] = held
-    sums += spread_hanging(held, weight_ref[...], EDGE, master_row, master_column, scratch)
+    sums += spread_hanging(held, weight_ref[...], EDGE, master_row, master_lane, scratch)
     rows = [
         [
-            sums[part * EDGE + slot : part * EDGE + slot + 1, half * LANES : (half + 1) * LANES]
+            sums[part * EDGE + 2 * slot + half : part * EDGE + 2 * slot + half + 1]
             for part in range(3)
             for half in range(2)
         ]
@@ -458,12 +453,18 @@
 
 def own_sums(
     image_ref, held_ref, row_ref, column_ref, master_row, master_column, weight_ref,
-    tab_ref, source_ref, inverse_ref, out_ref, high_ref, low_ref, sum_ref, *scratch,
-):
+    tab_ref, source_ref, inverse_ref, out_ref, *rest,
+):
+    *tables, high_ref, low_ref, sum_ref = rest[:-3]
+    if tables:
+        tab_source, tab_inverse = tables
+        fill_table(source_ref, tab_source)
+        fill_table(inverse_ref, tab_inverse)
+        source_ref, inverse_ref = tab_source, tab_inverse
     high_ref[...], low_ref[...] = split32(image_ref[...])
     scatter(high_ref, low_ref, OWN, row_ref, column_ref, sum_ref)
     applied = add_pieces(sum_ref[...]) + spread_hanging(
-        held_ref[...], weight_ref[...], OWN, master_row, master_column, scratch
+        held_ref[...], weight_ref[...], OWN, master_row, master_column, rest[-3:]
     )
     out_ref[...] = tab_ref[...] + relaxation * inverse_ref[...] * (source_ref[...] - applied)
 
@@ -484,31 +485,54 @@
     pack(place, 1, rows, pack_ref, out_ref)
 
 
-def primal_product(
-    place_ref, got_a, got_b, got_c, cells_ref, hang_ref, where_ref, lane_ref, master_where,
-    master_lane, weight_ref, modulus_ref, stiffness_ref, out_ref, edge_ref, sums_ref, full_ref,
-):
-    edge_gather(
-        place_ref[0], (got_a, got_b, got_c), (6, 6, 6), cells_ref, hang_ref, where_ref, lane_ref,
-        master_where, master_lane, weight_ref, edge_ref, sums_ref, full_ref,
-    )
-    out_ref[...] = modulus_ref[...] * jnp.dot(
+def last_gather(
+    half_rows, place_ref, tab_ref, own_where, lane_ref, master_own, master_lane, weight_ref,
+    got_a, got_b, got_c, primal_cells, primal_hang, edge_where, master_edge, modulus_ref,
+    stiffness_ref, cells_ref, hang_ref, ku_ref, final_ref,
+    tall_ref, sums_ref, edge_ref, edge_sums, full_ref,
+):
+    tall = up8(half_rows)
+    own = tall_table([tab_ref], half_rows, tall_ref)
+    edge = ghost_rows(place_ref[0], (got_a, got_b, got_c), (6, 6, 6), edge_ref)
+    gather(
+        [(own, tall, 3, master_own, sums_ref), (edge, TALL, 3, master_edge, edge_sums)],
+        master_lane,
+    )
+    weight = weight_ref[...]
+    found = sum_masters(sums_ref, 0, weight)
+    for part in range(3):
+        hang_ref[part : part + 1, :] = found[part]
+    edge = hanging_rows(sum_masters(edge_sums, 0, weight), primal_hang, edge_ref)
+    gather(
+        [(own, tall, 3, own_where, sums_ref), (edge, TALL, 3, edge_where, edge_sums)], lane_ref
+    )
+    count = lane_ref.shape[0]
+    for part in range(3):
+        rows = slice(part * count, (part + 1) * count)
+        cells_ref[rows, :] = gathered(sums_ref, count, part)
+        full_ref[rows, :] = primal_cells[rows, :] + gathered(edge_sums, count, part)
+    ku_ref[...] = modulus_ref[...] * jnp.dot(
         stiffness_ref[...],
         full_ref[...],
         precision=lax.Precision.HIGHEST,
         preferred_element_type=f32,
     )
+    for row in range(final_ref.shape[1] // WIDE):
+        for part in range(3):
+            final_ref[part : part + 1, row * WIDE : (row + 1) * WIDE] = tab_ref[
+                part * OWN + row : part * OWN + row + 1, :
+            ]
 
 
 def fluxes(
-    place_ref, got_ref, cells_ref, hang_ref, where_ref, lane_ref, master_where,
+    place_ref, got_ref, cells_ref, hang_ref, row_ref, lane_ref, master_row,
     master_lane, weight_ref, ku_ref, load_ref, sub_cell, sub_face, out_ref,
     term_ref, pack_ref, edge_ref, sums_ref, full_ref, tall_ref, code_ref, few_ref,
 ):
     place = place_ref[0]
     edge_gather(
-        place, [got_ref] * 3, (0, 2, 4), cells_ref, hang_ref, where_ref, lane_ref,
-        master_where, master_lane, weight_ref, edge_ref, sums_ref, full_ref,
+        place, [got_ref] * 3, (0, 2, 4), cells_ref, hang_ref, row_ref, lane_ref,
+        master_row, master_lane, weight_ref, edge_ref, sums_ref, full_ref,
     )
     cells = full_ref[...]
     ku = ku_ref[...]
@@ -531,7 +555,7 @@
     code_ref[:8, :] = 2 * sub_face[...] + (cell >> 7)
     code_ref[8:, :] = cell & 127
     table = jnp.concatenate(pieces(tall_ref[...]), 1)
-    gather(table, 16, 1, code_ref.at[:8, :], code_ref.at[8:, :], few_ref)
+    gather([(table, 16, 1, code_ref.at[:8, :], few_ref)], code_ref.at[8:, :])
     found = gathered(few_ref, 8, 0)
     rows = [[found[slot : slot + 1]] for slot in range(2 * REACH)]
     pack(place, 1, rows, pack_ref, out_ref)
@@ -635,70 +659,71 @@
         sems=3,
     )(place, *away(adjoint_start, primal_field, ghost_lists))
     ghosts = exchange(blocks)
-    far = (
-        connectivity, hang_node.reshape(1, -1), hang_master, hang_weight, adjoint_source,
-        inverse_diagonal,
-    )
     (
-        own_where, own_row, edge_where, edge_row, lane, own_column, edge_column, master_own,
-        master_own_row, master_edge, master_edge_row, master_lane, master_column, weight, source,
-        inverse, moduli,
+        own_where, own_row, edge_where, lane, own_column, master_own, master_own_row, master_edge,
+        master_lane, master_column, weight, moduli,
     ) = call(
-        setup,
-        [index] * 7 + [master_shape] * 6
-        + [((8, WIDE), f32), table, table, ((1, cell_count), f32)],
-        [(x.shape, x.dtype) for x in far]
-        + [((OWN, WIDE), f32), ((tall, LANES), f32), ((2, nodes * 8, LANES), f32)],
-        [FAR] * 7,
-        sems=7,
-    )(*away(*far, modulus.reshape(1, cell_count)))
-
-    def gather_own(values, final=()):
+        functools.partial(setup, adjoint_start.shape[1]),
+        [index] * 5 + [master_shape] * 5 + [((8, WIDE), f32), ((1, cell_count), f32)],
+        [((OWN, WIDE), f32), ((tall, LANES), f32), ((2, nodes * 8, LANES), f32)],
+        [FAST] * 5,
+    )(
+        connectivity, hang_node.reshape(1, -1), hang_master, hang_weight,
+        modulus.reshape(1, cell_count),
+    )
+
+    def gather_own(*fields):
+        number = len(fields)
         return call(
-            functools.partial(own_gather, half_rows),
-            [cells_shape, hang_shape, *final],
-            [own_tall, many_sums],
-            specs=[FAST] * 6,
-        )(values, own_where, lane, master_own, master_lane, weight)
+            functools.partial(own_gather, half_rows, number),
+            [cells_shape, hang_shape] * number,
+            [
+                ((3 * number * tall, LANES), f32),
+                ((2, number * local_values * 8, LANES), f32),
+            ],
+            specs=[FAST] * (5 + number),
+        )(own_where, lane, master_own, master_lane, weight, *fields)
 
     on_edge = (edge_where, lane, master_edge, master_lane, weight)
     landings = []
+    source, inverse = adjoint_source, inverse_diagonal
     for sweep in range(SWEEPS):
-        cells, hang = gather_own(tab)
         if sweep == 1:
-            tab_primal, tab = lax.optimization_barrier((tab_primal, tab))
-            primal_cells = gather_own(tab_primal)
-            cells, *primal_cells = lax.optimization_barrier((cells, *primal_cells))
+            cells, hang, *primal_cells = gather_own(tab, tab_primal)
+        else:
+            cells, hang = gather_own(tab)
         blocks, image, held = call(
             functools.partial(edge_product, 2 * sweep),
             packed(8) + [cells_shape, hang_shape],
-            [room(8)] + edge + [cells_shape, ((6 * EDGE, WIDE), f32)] + few(EDGE),
-        )(
-            place, ghosts, cells, hang, *on_edge, edge_row, edge_column, master_edge_row,
-            master_column, extra, moduli, stiffness,
-        )
+            [room(8)] + edge + [cells_shape, ((6 * EDGE, LANES), f32)] + few(EDGE, LANES),
+        )(place, ghosts, cells, hang, *on_edge, extra, moduli, stiffness)
         returned = exchange(blocks)
         landings.append(returned)
-        (partial,) = call(
+        partial, *tables = call(
             own_sums,
-            [table],
-            [cells_shape, cells_shape, ((6 * OWN, WIDE), f32)] + few(OWN),
+            [table] * (3 if sweep == 0 else 1),
+            [cells_shape, cells_shape, ((6 * OWN, WIDE), f32)] + few(OWN, WIDE),
             specs=[FAST] * 10,
         )(
             image, held, own_row, own_column, master_own_row, master_column, weight, tab, source,
             inverse,
         )
+        if tables:
+            source, inverse = tables
         blocks, tab = call(
             functools.partial(update, 1 if sweep == 0 else None),
             packed(8) + [table],
-            [room(8), few_sums] + few(OWN),
+            [room(8), few_sums] + few(OWN, WIDE),
         )(place, returned, list_row, list_column, partial, inverse, extra)
         ghosts = exchange(blocks)
         landings.append(ghosts)
-    cells, hang, adjoint = gather_own(tab, [(adjoint_start.shape, f32)])
-    tab, *primal_cells = lax.optimization_barrier((tab, *primal_cells))
-    (ku,) = call(primal_product, [cells_shape], edge)(
-        place, *landings[:3], *primal_cells, *on_edge, moduli, stiffness
+    cells, hang, ku, adjoint = call(
+        functools.partial(last_gather, half_rows),
+        [cells_shape, hang_shape, cells_shape, (adjoint_start.shape, f32)],
+        [own_tall, many_sums] + edge,
+    )(
+        place, tab, own_where, lane, master_own, master_lane, weight, *landings[:3], *primal_cells,
+        edge_where, master_edge, moduli, stiffness,
     )
     blocks, term = call(
         fluxes,

time: 101 us -> 91.1 us (0.902)
  Pallas kernels: 54.1 us -> 42.4 us
  waiting for transfers between devices: 11.4 us -> 19.5 us
  starting transfers between devices: 22.7 us -> 17.9 us
  blocking collectives: 12 us -> 9.94 us
    pallas_call x15 -> x13, Pallas kernels: 54.1 us -> 42.4 us  [run(): pl.pallas_call(kernel, out_shape=[jax.ShapeDtypeStruct(shape, kind) for s...]
    all_to_all x5, waiting for transfers between devices: 11.4 us -> 19.5 us  [exchange(): return lax.all_to_all(packed, 'dom', 0, 0, tiled=True)]
    all_to_all x5, starting transfers between devices: 22.7 us -> 17.9 us  [exchange(): return lax.all_to_all(packed, 'dom', 0, 0, tiled=True)]
    all_to_all x1, blocking collectives: 12 us -> 9.94 us  [exchange(): return lax.all_to_all(packed, 'dom', 0, 0, tiled=True)]
  transfers between devices with their start and end apart: 5 -> 5, of which waited for: 5 -> 5; matrix products, arithmetic and copies ran while one was open for 0% -> 0% of each run, Pallas kernels for 29% -> 24%
where the time goes in v9:
time: 91.1 us; the launch traced here: 90.6 us
  Pallas kernels  42.4 us (47%)
  waiting for transfers between devices  19.5 us (21%)
  starting transfers between devices  17.9 us (20%)
  blocking collectives  9.94 us (11%)
    pallas_call x13, Pallas kernels, run(): pl.pallas_call(kernel, out_shape=[jax.ShapeDtypeStruct(shape, kind) for s...  42.4 us
    all_to_all x5, waiting for transfers between devices, exchange(): return lax.all_to_all(packed, 'dom', 0, 0, tiled=True)  19.5 us
    all_to_all x5, starting transfers between devices, exchange(): return lax.all_to_all(packed, 'dom', 0, 0, tiled=True)  17.9 us
    all_to_all x1, blocking collectives, exchange(): return lax.all_to_all(packed, 'dom', 0, 0, tiled=True)  9.94 us
  transfers between devices with their start and end apart: 5, of which 5 were waited for; matrix products, arithmetic and copies ran while one was open for 0% of the time, Pallas kernels for 24%

profile of v9, /device:TPU:0, one launch (start us, length us, event | category | flops | bytes accessed | tf_op | source)
XLA Modules:
  0.0 90.6 jit_solution(17491844507139390091)
XLA Ops:
  0.6 2.3 %shard_map.158 = (f32[96,256]{1,0:T(8,128)S(1)}, f32[96,256]{1,0:T(8,128)S(1)}, s32[8,256]{1,0:T(8,128)S(1)}, s32[8,256]{1,0:T(8,128)S(1)}, f32[6,8,128]{2,1,0:T(8,128)S(1)}, /*index=5*/f32[32,8,128]{2,1,0:T(8,128)}) custom-call(s32[1]{0:T(128)} %bitcast.place_ref, f32[3,6912]{1,0:T(4,128)} %adjoint_hbm.1, f32[3,6912]{1,0:T(4,128)} %primal_hbm.1, ...), custom_call_target="tpu_custom_call" | custom-call | tf_op jit(solution)/shard_map/pallas_call | solution.py:593
  3.0 0.0 copy-start.4
  3.0 0.0 copy-start.5
  3.0 0.0 copy-start.6
  3.0 0.0 copy-start.10
  3.0 0.0 copy-start.11
  3.0 7.3 %all-to-all-start = ((f32[32,8,128]{2,1,0:T(8,128)}), f32[32,8,128]{2,1,0:T(8,128)S(1)}, u32[]{:S(2)}, u32[]{:S(2)}) async-start(f32[32,8,128]{2,1,0:T(8,128)} %get-tuple-element.45), calls=%async_computation | async-start | bytes 262144 | tf_op jit(solution)/shard_map/all_to_all | solution.py:33
  10.3 0.0 copy-start
  10.3 0.0 copy-done.4
  10.4 0.0 copy-done.5
  10.4 0.0 copy-done.6
  10.4 0.0 copy-done.10
  10.4 0.0 copy-done.11
  10.4 2.0 %shard_map.159 = (s32[64,256]{1,0:T(8,128)S(1)}, s32[64,256]{1,0:T(8,128)S(1)}, s32[64,256]{1,0:T(8,128)S(1)}, s32[64,256]{1,0:T(8,128)S(1)}, s32[64,256]{1,0:T(...) custom-call(s32[64,256]{1,0:T(8,128)S(1)} %copy-done.4, ...), custom_call_target="tpu_custom_call" | custom-call | tf_op jit(solution)/shard_map/pallas_call | solution.py:593
  12.4 2.5 %shard_map.160 = (f32[192,256]{1,0:T(8,128)S(1)}, f32[3,128]{1,0:T(4,128)S(1)}) custom-call(s32[64,256]{1,0:T(8,128)S(1)} %get-tuple-element.46.row_ref.own_where, s32[64,256]{1,0:T(8,128)S(1)} %get-tuple-element.47.lane_ref, s32[8,256]{1,0:T(8,128)S(1)} %get-tuple-element.48.master_row.master_own, s32[8,256]{1,0:T(8,128)S(1)} %get-tuple-element.49.master_lane, ...), custom_call_target="tpu_custom_call" | custom-call | tf_op jit(solution)/shard_map/pallas_call | solution.py:593
  15.0 3.6 %all-to-all-done.got_ref = f32[32,8,128]{2,1,0:T(8,128)S(1)} async-done(((f32[32,8,128]{2,1,0:T(8,128)}), f32[32,8,128]{2,1,0:T(8,128)S(1)}, u32[]{:S(2)}, u32[]{:S(2)}) %all-to-all-start) | async-done | bytes 131104 | tf_op jit(solution)/shard_map/all_to_all | solution.py:33
  18.6 0.0 copy-done
  18.6 5.7 %shard_map.161 = (f32[32,8,128]{2,1,0:T(8,128)}, f32[192,256]{1,0:T(8,128)S(1)}, f32[3,128]{1,0:T(4,128)S(1)}) custom-call(s32[1]{0:T(128)} %bitcast.place_ref, f32[32,8,128]{2,1,0:T(8,128)S(1)} %all-to-all-done.got_ref, f32[192,256]{1,0:T(8,128)S(1)} %get-tuple-element.52.cells_ref, f32[3,128]{1,0:T(4,128)S(1)} %get-tuple-element.53.hang_ref, ...), custom_call_target="tpu_custom_call" | custom-call | tf_op jit(solution)/shard_map/pallas_call | solution.py:593
  24.2 0.0 copy-start.2
  24.2 0.0 copy-start.3
  24.2 2.7 %all-to-all-start.1 = ((f32[32,8,128]{2,1,0:T(8,128)}), f32[32,8,128]{2,1,0:T(8,128)S(1)}, u32[]{:S(2)}, u32[]{:S(2)}) async-start(f32[32,8,128]{2,1,0:T(8,128)} %get-tuple-element.58), calls=%async_computation.1 | async-start | bytes 262144 | tf_op jit(solution)/shard_map/all_to_all | solution.py:33
  26.9 0.0 copy-done.2
  27.0 0.0 copy-done.3
  27.0 3.7 %shard_map.162 = (f32[96,256]{1,0:T(8,128)S(1)}, f32[96,256]{1,0:T(8,128)S(1)}, f32[96,256]{1,0:T(8,128)S(1)}) custom-call(f32[192,256]{1,0:T(8,128)S(1)} %get-tuple-element.61.image_ref, f32[3,128]{1,0:T(4,128)S(1)} %get-tuple-element.62.held_ref, s32[64,256]{1,0:T(8,128)S(1)} %get-tuple-element.63.row_ref, s32[64,256]{1,0:T(8,128)S(1)} %get-tuple-element.64.column_ref, ...), custom_call_target="tpu_custom_call" | custom-call | tf_op jit(solution)/shard_map/pallas_call | solution.py:593
  30.7 4.5 %all-to-all-done.1.got_ref.got_a = f32[32,8,128]{2,1,0:T(8,128)S(1)} async-done(((f32[32,8,128]{2,1,0:T(8,128)}), f32[32,8,128]{2,1,0:T(8,128)S(1)}, u32[]{:S(2)}, u32[]{:S(2)}) %all-to-all-start.1) | async-done | bytes 131104 | tf_op jit(solution)/shard_map/all_to_all | solution.py:33
  35.2 1.9 %shard_map.163 = (f32[32,8,128]{2,1,0:T(8,128)}, f32[96,256]{1,0:T(8,128)S(1)}) custom-call(s32[1]{0:T(128)} %bitcast.place_ref, f32[32,8,128]{2,1,0:T(8,128)S(1)} %all-to-all-done.1.got_ref.got_a, s32[8,256]{1,0:T(8,128)S(1)} %get-tuple-element.59.row_ref, s32[8,256]{1,0:T(8,128)S(1)} %get-tuple-element.60.column_ref, ...), custom_call_target="tpu_custom_call" | custom-call | tf_op jit(solution)/shard_map/pallas_call | solution.py:593
  37.0 2.7 %all-to-all-start.2 = ((f32[32,8,128]{2,1,0:T(8,128)}), f32[32,8,128]{2,1,0:T(8,128)S(1)}, u32[]{:S(2)}, u32[]{:S(2)}) async-start(f32[32,8,128]{2,1,0:T(8,128)} %get-tuple-element.69), calls=%async_computation.2 | async-start | bytes 262144 | tf_op jit(solution)/shard_map/all_to_all | solution.py:33
  39.8 4.7 %shard_map.164 = (f32[192,256]{1,0:T(8,128)S(1)}, f32[3,128]{1,0:T(4,128)S(1)}, f32[192,256]{1,0:T(8,128)S(1)}, f32[3,128]{1,0:T(4,128)S(1)}) custom-call(s32[64,256]{1,0:T(8,128)S(1)} %get-tuple-element.46.row_ref.own_where, s32[64,256]{1,0:T(8,128)S(1)} %get-tuple-element.47.lane_ref, s32[8,256]{1,0:T(8,128)S(1)} %get-tuple-element.48.master_row.master_own, ...), custom_call_target="tpu_custom_call" | custom-call | tf_op jit(solution)/shard_map/pallas_call | solution.py:593
  44.5 3.3 %all-to-all-done.2.got_ref.got_b = f32[32,8,128]{2,1,0:T(8,128)S(1)} async-done(((f32[32,8,128]{2,1,0:T(8,128)}), f32[32,8,128]{2,1,0:T(8,128)S(1)}, u32[]{:S(2)}, u32[]{:S(2)}) %all-to-all-start.2) | async-done | bytes 131104 | tf_op jit(solution)/shard_map/all_to_all | solution.py:33
  47.8 5.7 %shard_map.165 = (f32[32,8,128]{2,1,0:T(8,128)}, f32[192,256]{1,0:T(8,128)S(1)}, f32[3,128]{1,0:T(4,128)S(1)}) custom-call(s32[1]{0:T(128)} %bitcast.place_ref, f32[32,8,128]{2,1,0:T(8,128)S(1)} %all-to-all-done.2.got_ref.got_b, f32[192,256]{1,0:T(8,128)S(1)} %get-tuple-element.72.cells_ref, f32[3,128]{1,0:T(4,128)S(1)} %get-tuple-element.73.hang_ref, ...), custom_call_target="tpu_custom_call" | custom-call | tf_op jit(solution)/shard_map/pallas_call | solution.py:593
  53.5 2.6 %all-to-all-start.3 = ((f32[32,8,128]{2,1,0:T(8,128)}), f32[32,8,128]{2,1,0:T(8,128)S(1)}, u32[]{:S(2)}, u32[]{:S(2)}) async-start(f32[32,8,128]{2,1,0:T(8,128)} %get-tuple-element.74), calls=%async_computation.3 | async-start | bytes 262144 | tf_op jit(solution)/shard_map/all_to_all | solution.py:33
  56.1 3.6 %shard_map.166.partial_ref = f32[96,256]{1,0:T(8,128)S(1)} custom-call(f32[192,256]{1,0:T(8,128)S(1)} %get-tuple-element.75.image_ref, f32[3,128]{1,0:T(4,128)S(1)} %get-tuple-element.76.held_ref, s32[64,256]{1,0:T(8,128)S(1)} %get-tuple-element.63.row_ref, s32[64,256]{1,0:T(8,128)S(1)} %get-tuple-element.64.column_ref, ...), custom_call_target="tpu_custom_call" | custom-call | tf_op jit(solution)/shard_map/pallas_call | solution.py:593
  59.7 4.6 %all-to-all-done.3.got_ref.got_c = f32[32,8,128]{2,1,0:T(8,128)S(1)} async-done(((f32[32,8,128]{2,1,0:T(8,128)}), f32[32,8,128]{2,1,0:T(8,128)S(1)}, u32[]{:S(2)}, u32[]{:S(2)}) %all-to-all-start.3) | async-done | bytes 131104 | tf_op jit(solution)/shard_map/all_to_all | solution.py:33
  64.3 1.9 %shard_map.167 = (f32[32,8,128]{2,1,0:T(8,128)}, f32[96,256]{1,0:T(8,128)S(1)}) custom-call(s32[1]{0:T(128)} %bitcast.place_ref, f32[32,8,128]{2,1,0:T(8,128)S(1)} %all-to-all-done.3.got_ref.got_c, s32[8,256]{1,0:T(8,128)S(1)} %get-tuple-element.59.row_ref, s32[8,256]{1,0:T(8,128)S(1)} %get-tuple-element.60.column_ref, ...), custom_call_target="tpu_custom_call" | custom-call | tf_op jit(solution)/shard_map/pallas_call | solution.py:593
  66.2 2.6 %all-to-all-start.4 = ((f32[32,8,128]{2,1,0:T(8,128)}), f32[32,8,128]{2,1,0:T(8,128)S(1)}, u32[]{:S(2)}, u32[]{:S(2)}) async-start(f32[32,8,128]{2,1,0:T(8,128)} %get-tuple-element.82), calls=%async_computation.4 | async-start | bytes 262144 | tf_op jit(solution)/shard_map/all_to_all | solution.py:33
  68.7 0.0 copy-start.1
  68.8 0.0 copy-start.8
  68.8 4.7 %shard_map.168 = (f32[192,256]{1,0:T(8,128)S(1)}, f32[3,128]{1,0:T(4,128)S(1)}, f32[192,256]{1,0:T(8,128)S(1)}, f32[3,6912]{1,0:T(4,128)}) custom-call(s32[1]{0:T(128)} %bitcast.place_ref, f32[96,256]{1,0:T(8,128)S(1)} %get-tuple-element.78.tab_ref, s32[64,256]{1,0:T(8,128)S(1)} %get-tuple-element.46.row_ref.own_where, ...), custom_call_target="tpu_custom_call" | custom-call | tf_op jit(solution)/shard_map/pallas_call | solution.py:593
  73.5 0.0 copy-start.7
  73.5 3.5 %all-to-all-done.4.got_ref = f32[32,8,128]{2,1,0:T(8,128)S(1)} async-done(((f32[32,8,128]{2,1,0:T(8,128)}), f32[32,8,128]{2,1,0:T(8,128)S(1)}, u32[]{:S(2)}, u32[]{:S(2)}) %all-to-all-start.4) | async-done | bytes 131104 | tf_op jit(solution)/shard_map/all_to_all | solution.py:33
  77.0 0.0 copy-done.1
  77.0 0.0 copy-done.8
  77.0 0.0 copy-done.7
  77.0 0.0 copy-start.9
  77.0 2.9 %shard_map.169 = (f32[32,1,128]{2,1,0:T(1,128)S(1)}, f32[1,256]{1,0:T(1,128)S(1)}) custom-call(s32[1]{0:T(128)} %bitcast.place_ref, f32[32,8,128]{2,1,0:T(8,128)S(1)} %all-to-all-done.4.got_ref, f32[192,256]{1,0:T(8,128)S(1)} %get-tuple-element.83.cells_ref, f32[3,128]{1,0:T(4,128)S(1)} %get-tuple-element.84.hang_ref, ...), custom_call_target="tpu_custom_call" | custom-call | tf_op jit(solution)/shard_map/pallas_call | solution.py:593
  79.9 9.9 %all_to_all.30.got_ref = f32[32,1,128]{2,1,0:T(1,128)S(1)} all-to-all(f32[32,1,128]{2,1,0:T(1,128)S(1)} %get-tuple-element.86), channel_id=1, replica_groups=mesh['dom'=32] {'dom'}, dimensions={0} | all-to-all | bytes 32768 | tf_op jit(solution)/shard_map/all_to_all | solution.py:33
  89.8 0.0 copy-done.9
  89.8 0.8 shard_map.170
Async XLA Ops:
  3.0 7.4 %copy-start.4 = (s32[64,256]{1,0:T(8,128)S(1)}, s32[64,256]{1,0:T(8,128)}, u32[]{:S(2)}) copy-start(s32[64,256]{1,0:T(8,128)} %connect_ref.1) | copy-start | bytes 196612
  3.0 7.4 %copy-start.5 = (s32[16,128]{1,0:T(8,128)S(1)}, s32[16,128]{1,0:T(8,128)}, u32[]{:S(2)}) copy-start(s32[16,128]{1,0:T(8,128)} %master_ref.1) | copy-start | bytes 24580
  3.0 7.4 %copy-start.6 = (f32[16,128]{1,0:T(8,128)S(1)}, f32[16,128]{1,0:T(8,128)}, u32[]{:S(2)}) copy-start(f32[16,128]{1,0:T(8,128)} %weight_ref.1) | copy-start | bytes 24580
  3.0 7.4 %copy-start.10 = (f32[256]{0:T(256)S(1)}, f32[256]{0:T(256)}, u32[]{:S(2)}) copy-start(f32[256]{0:T(256)} %param.20) | copy-start | bytes 3076
  3.0 7.4 %copy-start.11 = (s32[128]{0:T(128)S(1)}, s32[128]{0:T(128)}, u32[]{:S(2)}) copy-start(s32[128]{0:T(128)} %param.23) | copy-start | bytes 1540
  3.0 15.5 %all-to-all-start = ((f32[32,8,128]{2,1,0:T(8,128)}), f32[32,8,128]{2,1,0:T(8,128)S(1)}, u32[]{:S(2)}, u32[]{:S(2)}) async-start(f32[32,8,128]{2,1,0:T(8,128)} %get-tuple-element.45), calls=%async_computation | async-start | bytes 262144 | tf_op jit(solution)/shard_map/all_to_all | solution.py:33
  10.3 8.2 %copy-start = (f32[192,192]{1,0:T(8,128)S(1)}, f32[192,192]{1,0:T(8,128)}, u32[]{:S(2)}) copy-start(f32[192,192]{1,0:T(8,128)} %stiffness_ref.5) | copy-start | bytes 442372
  24.2 2.7 %copy-start.2 = (f32[3,6912]{1,0:T(4,128)S(1)}, f32[3,6912]{1,0:T(4,128)}, u32[]{:S(2)}) copy-start(f32[3,6912]{1,0:T(4,128)} %source_ref.1) | copy-start | bytes 248836
  24.2 2.7 %copy-start.3 = (f32[3,6912]{1,0:T(4,128)S(1)}, f32[3,6912]{1,0:T(4,128)}, u32[]{:S(2)}) copy-start(f32[3,6912]{1,0:T(4,128)} %inverse_ref.1) | copy-start | bytes 248836
  24.2 10.9 %all-to-all-start.1 = ((f32[32,8,128]{2,1,0:T(8,128)}), f32[32,8,128]{2,1,0:T(8,128)S(1)}, u32[]{:S(2)}, u32[]{:S(2)}) async-start(f32[32,8,128]{2,1,0:T(8,128)} %get-tuple-element.58), calls=%async_computation.1 | async-start | bytes 262144 | tf_op jit(solution)/shard_map/all_to_all | solution.py:33
  37.0 10.8 %all-to-all-start.2 = ((f32[32,8,128]{2,1,0:T(8,128)}), f32[32,8,128]{2,1,0:T(8,128)S(1)}, u32[]{:S(2)}, u32[]{:S(2)}) async-start(f32[32,8,128]{2,1,0:T(8,128)} %get-tuple-element.69), calls=%async_computation.2 | async-start | bytes 262144 | tf_op jit(solution)/shard_map/all_to_all | solution.py:33
  53.5 10.8 %all-to-all-start.3 = ((f32[32,8,128]{2,1,0:T(8,128)}), f32[32,8,128]{2,1,0:T(8,128)S(1)}, u32[]{:S(2)}, u32[]{:S(2)}) async-start(f32[32,8,128]{2,1,0:T(8,128)} %get-tuple-element.74), calls=%async_computation.3 | async-start | bytes 262144 | tf_op jit(solution)/shard_map/all_to_all | solution.py:33
  66.2 10.8 %all-to-all-start.4 = ((f32[32,8,128]{2,1,0:T(8,128)}), f32[32,8,128]{2,1,0:T(8,128)S(1)}, u32[]{:S(2)}, u32[]{:S(2)}) async-start(f32[32,8,128]{2,1,0:T(8,128)} %get-tuple-element.82), calls=%async_computation.4 | async-start | bytes 262144 | tf_op jit(solution)/shard_map/all_to_all | solution.py:33
  68.7 8.2 %copy-start.1 = (f32[192,256]{1,0:T(8,128)S(1)}, f32[192,256]{1,0:T(8,128)}, u32[]{:S(2)}) copy-start(f32[192,256]{1,0:T(8,128)} %load_ref.1) | copy-start | bytes 589828
  68.8 8.2 %copy-start.8 = (s32[8,128]{1,0:T(8,128)S(1)}, s32[8,128]{1,0:T(8,128)}, u32[]{:S(2)}) copy-start(s32[8,128]{1,0:T(8,128)} %sub_face.1) | copy-start | bytes 12292
  73.5 3.5 %copy-start.7 = (s32[8,128]{1,0:T(8,128)S(1)}, s32[8,128]{1,0:T(8,128)}, u32[]{:S(2)}) copy-start(s32[8,128]{1,0:T(8,128)} %sub_cell.1) | copy-start | bytes 12292
  77.0 12.8 %copy-start.9 = (s32[8,128]{1,0:T(8,128)S(1)}, s32[8,128]{1,0:T(8,128)}, u32[]{:S(2)}) copy-start(s32[8,128]{1,0:T(8,128)} %owner_ref.1) | copy-start | bytes 12292

commit v10 on v9

--- a/solution.py
+++ b/solution.py
@@ -86,8 +86,21 @@
     return high, (x - high.astype(f32)).astype(bf16)
 
 
+def build_hot(column_ref, hot_ref):
+    count = column_ref.shape[0]
+    high = hot_ref.shape[0] // count
+    for j in range(count):
+        hot_ref[j * high : (j + 1) * high, :] = one_hot(column_ref[j : j + 1, :], high)
+
+
+def hot_at(column_ref, number, high):
+    if column_ref.dtype == bf16:
+        return column_ref[pl.ds(pl.multiple_of(number * high, high), high), :]
+    return one_hot(column_ref[pl.ds(number, 1), :], high)
+
+
 def gather(jobs, column_ref, wide=False):
-    count, width = column_ref.shape
+    count, width = jobs[0][3].shape
     tables = jnp.concatenate([job[0] for job in jobs], 0)
     high = tables.shape[0]
     numbers = lax.broadcasted_iota(i32, (max(job[1] for job in jobs), width), 0)
@@ -96,7 +109,7 @@
     def body(block, carry):
         start = pl.multiple_of(block * step, step)
         for j in range(step):
-            hot = one_hot(column_ref[pl.ds(start + j, 1), :], WIDE if wide else LANES)
+            hot = hot_at(column_ref, start + j, WIDE if wide else LANES)
             if not wide:
                 hot = jnp.concatenate([hot, hot], 0)
             all_found = jnp.dot(tables, hot, preferred_element_type=f32)
@@ -149,7 +162,7 @@
     def product(start):
         masks = [match16(row_ref[pl.ds(start + j, 1), :], rows) for j in range(8)]
         hot = jnp.concatenate(
-            [one_hot(column_ref[pl.ds(start + j, 1), :], sum_ref.shape[1]) for j in range(8)], 1
+            [hot_at(column_ref, start + j, sum_ref.shape[1]) for j in range(8)], 1
         )
         stacked = [
             jnp.concatenate(
@@ -220,6 +233,13 @@
     return totals
 
 
+def product(threefold, cells):
+    high, low = pieces(cells)
+    return jnp.dot(
+        threefold, jnp.concatenate([high, low, high], 0), preferred_element_type=f32
+    )
+
+
 def fill_table(x_ref, out_ref):
     count = x_ref.shape[1] // WIDE
     for part in range(3):
@@ -266,46 +286,49 @@
             rows[slot].append(extra_ref[2 * part + half, export : export + 1, :])
 
 
-def copy_in(pairs, sems):
+def first_export(
+    place_ref, adjoint_hbm, primal_hbm, list_hbm, tab_a, tab_p, row_ref, hot_ref, extra_ref,
+    out_ref, pack_ref, adjoint_ref, primal_ref, list_ref, column_ref, sums_ref, sems,
+):
+    pairs = [(list_hbm, list_ref), (adjoint_hbm, adjoint_ref), (primal_hbm, primal_ref)]
     copies = [
         pltpu.make_async_copy(source, target, sems.at[number])
         for number, (source, target) in enumerate(pairs)
     ]
     for copy in copies:
         copy.start()
-    for copy in copies:
-        copy.wait()
-
-
-def first_export(
-    place_ref, adjoint_hbm, primal_hbm, list_hbm, tab_a, tab_p, row_ref, column_ref, extra_ref,
-    out_ref, pack_ref, adjoint_ref, primal_ref, list_ref, sums_ref, sems,
-):
-    copy_in(
-        [(adjoint_hbm, adjoint_ref), (primal_hbm, primal_ref), (list_hbm, list_ref)], sems
-    )
     owned = adjoint_ref.shape[1]
-    fill_table(adjoint_ref, tab_a)
-    fill_table(primal_ref, tab_p)
+    copies[0].wait()
     codes = list_ref[...]
     node = lax.rem(17 * codes + lax.broadcasted_iota(i32, codes.shape, 1), owned)
     row_ref[...] = node >> 8
     column_ref[...] = node & 255
+    build_hot(column_ref, hot_ref)
+    copies[1].wait()
+    fill_table(adjoint_ref, tab_a)
+    copies[2].wait()
+    fill_table(primal_ref, tab_p)
     table = jnp.concatenate([tab_a[...], tab_p[...]], 0)
-    tiles = export_tiles(table, 6, row_ref, column_ref, sums_ref)
+    tiles = export_tiles(table, 6, row_ref, hot_ref, sums_ref)
     for number in range(6):
         extra_ref[number] = tiles[6 + number]
     pack(place_ref[0], 1, rows_of(tiles[:6]), pack_ref, out_ref)
 
 
 def setup(
-    owned, connect_ref, node_ref, master_ref, weight_ref, modulus_ref,
+    owned, connect_ref, node_ref, master_ref, weight_ref, modulus_ref, stiffness_ref,
     own_where, own_row, edge_where, lane_ref, column_ref, master_own, master_own_row,
-    master_edge, master_lane, master_column, weight_out, modulus_out,
-    map_ref, tall_ref, sums_ref,
+    master_edge, master_hot, master_column, weight_out, modulus_out, forward_out, adjoint_out,
+    map_ref, tall_ref, sums_ref, master_lane,
 ):
     extent = owned + 2 * REACH * WIDE
     modulus_out[...] = modulus_ref[...]
+    for out_ref, matrix in (
+        (forward_out, stiffness_ref[...]),
+        (adjoint_out, jnp.transpose(stiffness_ref[...])),
+    ):
+        high, low = pieces(matrix)
+        out_ref[...] = jnp.concatenate([high, high, low], 1)
     codes = master_ref[...]
     master = lax.rem(17 * codes + 8 * lax.broadcasted_iota(i32, codes.shape, 1), extent)
     count = codes.shape[0] // 2
@@ -317,6 +340,7 @@
     master_own[...] = jnp.where(where < last, where, NOWHERE)
     master_edge[...] = jnp.where(where < last, NOWHERE, where - last)
     master_lane[...] = master & 127
+    build_hot(master_lane, master_hot)
     master_own_row[...] = jnp.where(where < last, master >> 8, NOWHERE)
     master_column[...] = master & 255
 
@@ -422,13 +446,7 @@
         place, [got_ref] * 3, (0, 2, 4), cells_ref, hang_ref, row_ref, lane_ref,
         master_row, master_lane, weight_ref, edge_ref, sums_ref, full_ref,
     )
-    image = modulus_ref[...] * lax.dot_general(
-        stiffness_ref[...],
-        full_ref[...],
-        (((0,), (0,)), ((), ())),
-        precision=lax.Precision.HIGHEST,
-        preferred_element_type=f32,
-    )
+    image = modulus_ref[...] * product(stiffness_ref[...], full_ref[...])
     image_ref[...] = image
     full_ref[...], low_ref[...] = split32(image)
     scatter(full_ref, low_ref, EDGE, row_ref, lane_ref, sum_ref)
@@ -511,12 +529,7 @@
         rows = slice(part * count, (part + 1) * count)
         cells_ref[rows, :] = gathered(sums_ref, count, part)
         full_ref[rows, :] = primal_cells[rows, :] + gathered(edge_sums, count, part)
-    ku_ref[...] = modulus_ref[...] * jnp.dot(
-        stiffness_ref[...],
-        full_ref[...],
-        precision=lax.Precision.HIGHEST,
-        preferred_element_type=f32,
-    )
+    ku_ref[...] = modulus_ref[...] * product(stiffness_ref[...], full_ref[...])
     for row in range(final_ref.shape[1] // WIDE):
         for part in range(3):
             final_ref[part : part + 1, row * WIDE : (row + 1) * WIDE] = tab_ref[
@@ -526,8 +539,8 @@
 
 def fluxes(
     place_ref, got_ref, cells_ref, hang_ref, row_ref, lane_ref, master_row,
-    master_lane, weight_ref, ku_ref, load_ref, sub_cell, sub_face, out_ref,
-    term_ref, pack_ref, edge_ref, sums_ref, full_ref, tall_ref, code_ref, few_ref,
+    master_lane, weight_ref, ku_ref, load_ref, sub_where, sub_hot, out_ref,
+    term_ref, pack_ref, edge_ref, sums_ref, full_ref, tall_ref, few_ref,
 ):
     place = place_ref[0]
     edge_gather(
@@ -551,21 +564,26 @@
             tall_ref[at : at + 1, :] = flux[
                 number : number + 1, half * LANES : (half + 1) * LANES
             ]
-    cell = sub_cell[...]
-    code_ref[:8, :] = 2 * sub_face[...] + (cell >> 7)
-    code_ref[8:, :] = cell & 127
     table = jnp.concatenate(pieces(tall_ref[...]), 1)
-    gather([(table, 16, 1, code_ref.at[:8, :], few_ref)], code_ref.at[8:, :])
+    gather([(table, 16, 1, sub_where, few_ref)], sub_hot)
     found = gathered(few_ref, 8, 0)
     rows = [[found[slot : slot + 1]] for slot in range(2 * REACH)]
     pack(place, 1, rows, pack_ref, out_ref)
 
 
-def collect(place_ref, got_ref, owner_ref, term_ref, out_ref):
+def keep_subfaces(cell_ref, face_ref, owner_ref, where_ref, hot_ref, owner_hot, lane_ref):
+    cell = cell_ref[...]
+    where_ref[...] = 2 * face_ref[...] + (cell >> 7)
+    lane_ref[...] = cell & 127
+    build_hot(lane_ref, hot_ref)
+    build_hot(owner_ref, owner_hot)
+
+
+def collect(place_ref, got_ref, owner_hot, term_ref, out_ref):
     count = term_ref.shape[1]
     got = jnp.concatenate(landed(place_ref[0], 1, got_ref, 0), 1)
     hot = jnp.concatenate(
-        [one_hot(owner_ref[slot : slot + 1, :], count) for slot in range(2 * REACH)], 1
+        [owner_hot[slot * count : (slot + 1) * count, :] for slot in range(2 * REACH)], 1
     )
     values = jnp.concatenate(
         [jnp.broadcast_to(x, (16, got.shape[1])).astype(bf16) for x in split32(got)], 0
@@ -642,10 +660,9 @@
     many_sums = ((2, local_values * 8, LANES), f32)
     own_tall = ((3 * tall, LANES), f32)
     edge = [((3 * TALL, LANES), f32), many_sums, cells_shape]
-    tab, tab_primal, list_row, list_column, extra, blocks = call(
+    tab, tab_primal, list_row, list_hot, extra, blocks = call(
         first_export,
-        [table, table]
-        + [(ghost_lists.shape, i32)] * 2
+        [table, table, (ghost_lists.shape, i32), ((8 * WIDE, WIDE), bf16)]
         + [((6, slots, LANES), f32)]
         + packed(8),
         [
@@ -653,23 +670,28 @@
             (adjoint_start.shape, f32),
             (primal_field.shape, f32),
             (ghost_lists.shape, i32),
+            (ghost_lists.shape, i32),
             ((2, 6 * 64, LANES), f32),
         ],
         [SMALL, FAR, FAR, FAR],
         sems=3,
     )(place, *away(adjoint_start, primal_field, ghost_lists))
     ghosts = exchange(blocks)
+    connectivity, list_row = lax.optimization_barrier((connectivity, list_row))
     (
         own_where, own_row, edge_where, lane, own_column, master_own, master_own_row, master_edge,
-        master_lane, master_column, weight, moduli,
+        master_hot, master_column, weight, moduli, forward, backward,
     ) = call(
         functools.partial(setup, adjoint_start.shape[1]),
-        [index] * 5 + [master_shape] * 5 + [((8, WIDE), f32), ((1, cell_count), f32)],
-        [((OWN, WIDE), f32), ((tall, LANES), f32), ((2, nodes * 8, LANES), f32)],
-        [FAST] * 5,
+        [index] * 5
+        + [master_shape] * 3
+        + [((8 * LANES, WIDE), bf16), master_shape, ((8, WIDE), f32), ((1, cell_count), f32)]
+        + [((local_values, 3 * local_values), bf16)] * 2,
+        [((OWN, WIDE), f32), ((tall, LANES), f32), ((2, nodes * 8, LANES), f32), master_shape],
+        [FAST] * 6,
     )(
         connectivity, hang_node.reshape(1, -1), hang_master, hang_weight,
-        modulus.reshape(1, cell_count),
+        modulus.reshape(1, cell_count), stiffness,
     )
 
     def gather_own(*fields):
@@ -682,9 +704,9 @@
                 ((2, number * local_values * 8, LANES), f32),
             ],
             specs=[FAST] * (5 + number),
-        )(own_where, lane, master_own, master_lane, weight, *fields)
-
-    on_edge = (edge_where, lane, master_edge, master_lane, weight)
+        )(own_where, lane, master_own, master_hot, weight, *fields)
+
+    on_edge = (edge_where, lane, master_edge, master_hot, weight)
     landings = []
     source, inverse = adjoint_source, inverse_diagonal
     for sweep in range(SWEEPS):
@@ -696,7 +718,7 @@
             functools.partial(edge_product, 2 * sweep),
             packed(8) + [cells_shape, hang_shape],
             [room(8)] + edge + [cells_shape, ((6 * EDGE, LANES), f32)] + few(EDGE, LANES),
-        )(place, ghosts, cells, hang, *on_edge, extra, moduli, stiffness)
+        )(place, ghosts, cells, hang, *on_edge, extra, moduli, backward)
         returned = exchange(blocks)
         landings.append(returned)
         partial, *tables = call(
@@ -710,11 +732,26 @@
         )
         if tables:
             source, inverse = tables
+        else:
+            subs, image = lax.optimization_barrier(
+                ((subface_cell, subface_face, subface_owner), image)
+            )
+            kept = call(
+                keep_subfaces,
+                [
+                    (subface_cell.shape, i32),
+                    ((slots * LANES, subface_cell.shape[1]), bf16),
+                    ((slots * cell_count, subface_cell.shape[1]), bf16),
+                ],
+                [(subface_cell.shape, i32)],
+                [FAST] * 3,
+            )(*subs)
+            partial, (sub_where, sub_hot, owner_hot) = lax.optimization_barrier((partial, kept))
         blocks, tab = call(
             functools.partial(update, 1 if sweep == 0 else None),
             packed(8) + [table],
             [room(8), few_sums] + few(OWN, WIDE),
-        )(place, returned, list_row, list_column, partial, inverse, extra)
+        )(place, returned, list_row, list_hot, partial, inverse, extra)
         ghosts = exchange(blocks)
         landings.append(ghosts)
     cells, hang, ku, adjoint = call(
@@ -722,8 +759,8 @@
         [cells_shape, hang_shape, cells_shape, (adjoint_start.shape, f32)],
         [own_tall, many_sums] + edge,
     )(
-        place, tab, own_where, lane, master_own, master_lane, weight, *landings[:3], *primal_cells,
-        edge_where, master_edge, moduli, stiffness,
+        place, tab, own_where, lane, master_own, master_hot, weight, *landings[:3], *primal_cells,
+        edge_where, master_edge, moduli, forward,
     )
     blocks, term = call(
         fluxes,
@@ -732,13 +769,12 @@
         + edge
         + [
             ((16, LANES), f32),
-            ((16, subface_cell.shape[1]), i32),
             ((1, 64, LANES), f32),
         ],
-    )(place, ghosts, cells, hang, *on_edge, ku, cell_load, subface_cell, subface_face)
+    )(place, ghosts, cells, hang, *on_edge, ku, cell_load, sub_where, sub_hot)
     received = exchange(blocks)
     (indicator,) = call(collect, [((1, cell_count), f32)])(
-        place, received, subface_owner, term
+        place, received, owner_hot, term
     )
     return (adjoint, indicator.reshape(cell_count))
 

time: 91.1 us -> 92 us (level)
  local copies, waits for them, and re-layouts: 0.07 us -> 2.22 us
  waiting for transfers between devices: 19.5 us -> 17.9 us
    unnamed x24 -> x32, local copies, waits for them, and re-layouts: 0.07 us -> 2.22 us
    all_to_all x5, waiting for transfers between devices: 19.5 us -> 17.9 us  [exchange(): return lax.all_to_all(packed, 'dom', 0, 0, tiled=True)]
    pallas_call x13 -> x14, Pallas kernels: 42.4 us -> 42.2 us  [run(): pl.pallas_call(kernel, out_shape=[jax.ShapeDtypeStruct(shape, kind) for s...]
  transfers between devices with their start and end apart: 5 -> 5, of which waited for: 5 -> 5; matrix products, arithmetic and copies ran while one was open for 0% -> 0% of each run, Pallas kernels for 24% -> 23%
where the time goes in v10:
time: 92 us; the launch traced here: 91.5 us
  Pallas kernels  42.2 us (46%)
  starting transfers between devices  18.2 us (20%)
  waiting for transfers between devices  17.9 us (19%)
  blocking collectives  10.1 us (11%)
  local copies, waits for them, and re-layouts  2.22 us (2%)
  between operations  0.92 us (1%)
    pallas_call x14, Pallas kernels, run(): pl.pallas_call(kernel, out_shape=[jax.ShapeDtypeStruct(shape, kind) for s...  42.2 us
    all_to_all x5, starting transfers between devices, exchange(): return lax.all_to_all(packed, 'dom', 0, 0, tiled=True)  18.2 us
    all_to_all x5, waiting for transfers between devices, exchange(): return lax.all_to_all(packed, 'dom', 0, 0, tiled=True)  17.9 us
    all_to_all x1, blocking collectives, exchange(): return lax.all_to_all(packed, 'dom', 0, 0, tiled=True)  10.1 us
    unnamed x32, local copies, waits for them, and re-layouts  2.22 us
  transfers between devices with their start and end apart: 5, of which 5 were waited for; matrix products, arithmetic and copies ran while one was open for 0% of the time, Pallas kernels for 23%

profile of v10, /device:TPU:0, one launch (start us, length us, event | category | flops | bytes accessed | tf_op | source)
XLA Modules:
  0.0 91.5 jit_solution(4785073887317880847)
XLA Ops:
  0.6 0.0 copy-start.3
  0.6 2.3 %shard_map.158 = (f32[96,256]{1,0:T(8,128)S(1)}, f32[96,256]{1,0:T(8,128)S(1)}, s32[8,256]{1,0:T(8,128)S(1)}, bf16[2048,256]{1,0:T(8,128)(2,1)S(1)}, f32[6,8,128]{2,1,0:T(8,128)S(1)}, /*index=5*/f32[32,8,128]{2,1,0:T(8,128)}) custom-call(s32[1]{0:T(128)} %bitcast.place_ref, f32[3,6912]{1,0:T(4,128)} %adjoint_hbm.1, f32[3,6912]{1,0:T(4,128)} %primal_hbm.1, ...), custom_call_target="tpu_custom_call" | custom-call | tf_op jit(solution)/shard_map/pallas_call | solution.py:611
  3.0 0.0 copy-start.8
  3.0 0.0 copy-start.9
  3.0 0.0 copy-start.10
  3.0 7.3 %all-to-all-start = ((f32[32,8,128]{2,1,0:T(8,128)}), f32[32,8,128]{2,1,0:T(8,128)S(1)}, u32[]{:S(2)}, u32[]{:S(2)}) async-start(f32[32,8,128]{2,1,0:T(8,128)} %get-tuple-element.59), calls=%async_computation | async-start | bytes 262144 | tf_op jit(solution)/shard_map/all_to_all | solution.py:33
  10.3 0.0 copy-start.14
  10.3 0.0 copy-start.15
  10.3 0.0 copy-done.3
  10.4 0.0 copy-done.8
  10.4 0.0 copy-done.9
  10.4 0.0 copy-done.10
  10.4 0.6 copy-done.14
  11.0 0.0 copy-done.15
  11.0 2.1 %shard_map.159 = (s32[64,256]{1,0:T(8,128)S(1)}, s32[64,256]{1,0:T(8,128)S(1)}, s32[64,256]{1,0:T(8,128)S(1)}, s32[64,256]{1,0:T(8,128)S(1)}, s32[64,256]{1,0:T(...) custom-call(s32[64,256]{1,0:T(8,128)S(1)} %copy-done.8, ...), custom_call_target="tpu_custom_call" | custom-call | tf_op jit(solution)/shard_map/pallas_call | solution.py:611
  13.1 0.0 copy-start
  13.1 2.5 %shard_map.160 = (f32[192,256]{1,0:T(8,128)S(1)}, f32[3,128]{1,0:T(4,128)S(1)}) custom-call(s32[64,256]{1,0:T(8,128)S(1)} %get-tuple-element.62.row_ref.own_where, s32[64,256]{1,0:T(8,128)S(1)} %get-tuple-element.63.lane_ref, s32[8,256]{1,0:T(8,128)S(1)} %get-tuple-element.64.master_row.master_own, bf16[1024,256]{1,0:T(8,128)(2,1)S(1)} %get-tuple-element.65.master_lane, ...), custom_call_target="tpu_custom_call" | custom-call | tf_op jit(solution)/shard_map/pallas_call | solution.py:611
  15.6 0.0 copy-done
  15.6 2.9 %all-to-all-done.got_ref = f32[32,8,128]{2,1,0:T(8,128)S(1)} async-done(((f32[32,8,128]{2,1,0:T(8,128)}), f32[32,8,128]{2,1,0:T(8,128)S(1)}, u32[]{:S(2)}, u32[]{:S(2)}) %all-to-all-start) | async-done | bytes 131104 | tf_op jit(solution)/shard_map/all_to_all | solution.py:33
  18.5 5.6 %shard_map.161 = (f32[32,8,128]{2,1,0:T(8,128)}, f32[192,256]{1,0:T(8,128)S(1)}, f32[3,128]{1,0:T(4,128)S(1)}) custom-call(s32[1]{0:T(128)} %bitcast.place_ref, f32[32,8,128]{2,1,0:T(8,128)S(1)} %all-to-all-done.got_ref, f32[192,256]{1,0:T(8,128)S(1)} %get-tuple-element.68.cells_ref, f32[3,128]{1,0:T(4,128)S(1)} %get-tuple-element.69.hang_ref, ...), custom_call_target="tpu_custom_call" | custom-call | tf_op jit(solution)/shard_map/pallas_call | solution.py:611
  24.1 2.9 %all-to-all-start.1 = ((f32[32,8,128]{2,1,0:T(8,128)}), f32[32,8,128]{2,1,0:T(8,128)S(1)}, u32[]{:S(2)}, u32[]{:S(2)}) async-start(f32[32,8,128]{2,1,0:T(8,128)} %get-tuple-element.75), calls=%async_computation.1 | async-start | bytes 262144 | tf_op jit(solution)/shard_map/all_to_all | solution.py:33
  27.0 0.0 copy-done.4
  27.0 0.0 copy-done.5
  27.1 3.7 %shard_map.162 = (f32[96,256]{1,0:T(8,128)S(1)}, f32[96,256]{1,0:T(8,128)S(1)}, f32[96,256]{1,0:T(8,128)S(1)}) custom-call(f32[192,256]{1,0:T(8,128)S(1)} %get-tuple-element.78.image_ref, f32[3,128]{1,0:T(4,128)S(1)} %get-tuple-element.79.held_ref, s32[64,256]{1,0:T(8,128)S(1)} %get-tuple-element.80.row_ref, s32[64,256]{1,0:T(8,128)S(1)} %get-tuple-element.81.column_ref, ...), custom_call_target="tpu_custom_call" | custom-call | tf_op jit(solution)/shard_map/pallas_call | solution.py:611
  30.8 4.5 %all-to-all-done.1.got_ref.got_a = f32[32,8,128]{2,1,0:T(8,128)S(1)} async-done(((f32[32,8,128]{2,1,0:T(8,128)}), f32[32,8,128]{2,1,0:T(8,128)S(1)}, u32[]{:S(2)}, u32[]{:S(2)}) %all-to-all-start.1) | async-done | bytes 131104 | tf_op jit(solution)/shard_map/all_to_all | solution.py:33
  35.3 1.9 %shard_map.163 = (f32[32,8,128]{2,1,0:T(8,128)}, f32[96,256]{1,0:T(8,128)S(1)}) custom-call(s32[1]{0:T(128)} %bitcast.place_ref, f32[32,8,128]{2,1,0:T(8,128)S(1)} %all-to-all-done.1.got_ref.got_a, s32[8,256]{1,0:T(8,128)S(1)} %get-tuple-element.76.row_ref, bf16[2048,256]{1,0:T(8,128)(2,1)S(1)} %get-tuple-element.77.column_ref, ...), custom_call_target="tpu_custom_call" | custom-call | tf_op jit(solution)/shard_map/pallas_call | solution.py:611
  37.1 2.7 %all-to-all-start.2 = ((f32[32,8,128]{2,1,0:T(8,128)}), f32[32,8,128]{2,1,0:T(8,128)S(1)}, u32[]{:S(2)}, u32[]{:S(2)}) async-start(f32[32,8,128]{2,1,0:T(8,128)} %get-tuple-element.86), calls=%async_computation.2 | async-start | bytes 262144 | tf_op jit(solution)/shard_map/all_to_all | solution.py:33
  39.9 4.7 %shard_map.164 = (f32[192,256]{1,0:T(8,128)S(1)}, f32[3,128]{1,0:T(4,128)S(1)}, f32[192,256]{1,0:T(8,128)S(1)}, f32[3,128]{1,0:T(4,128)S(1)}) custom-call(s32[64,256]{1,0:T(8,128)S(1)} %get-tuple-element.62.row_ref.own_where, s32[64,256]{1,0:T(8,128)S(1)} %get-tuple-element.63.lane_ref, s32[8,256]{1,0:T(8,128)S(1)} %get-tuple-element.64.master_row.master_own, ...), custom_call_target="tpu_custom_call" | custom-call | tf_op jit(solution)/shard_map/pallas_call | solution.py:611
  44.6 3.3 %all-to-all-done.2.got_ref.got_b = f32[32,8,128]{2,1,0:T(8,128)S(1)} async-done(((f32[32,8,128]{2,1,0:T(8,128)}), f32[32,8,128]{2,1,0:T(8,128)S(1)}, u32[]{:S(2)}, u32[]{:S(2)}) %all-to-all-start.2) | async-done | bytes 131104 | tf_op jit(solution)/shard_map/all_to_all | solution.py:33
  47.9 5.6 %shard_map.165 = (f32[32,8,128]{2,1,0:T(8,128)}, f32[192,256]{1,0:T(8,128)S(1)}, f32[3,128]{1,0:T(4,128)S(1)}) custom-call(s32[1]{0:T(128)} %bitcast.place_ref, f32[32,8,128]{2,1,0:T(8,128)S(1)} %all-to-all-done.2.got_ref.got_b, f32[192,256]{1,0:T(8,128)S(1)} %get-tuple-element.89.cells_ref, f32[3,128]{1,0:T(4,128)S(1)} %get-tuple-element.90.hang_ref, ...), custom_call_target="tpu_custom_call" | custom-call | tf_op jit(solution)/shard_map/pallas_call | solution.py:611
  53.5 2.6 %all-to-all-start.3 = ((f32[32,8,128]{2,1,0:T(8,128)}), f32[32,8,128]{2,1,0:T(8,128)S(1)}, u32[]{:S(2)}, u32[]{:S(2)}) async-start(f32[32,8,128]{2,1,0:T(8,128)} %get-tuple-element.91), calls=%async_computation.3 | async-start | bytes 262144 | tf_op jit(solution)/shard_map/all_to_all | solution.py:33
  56.1 0.0 copy-start.11
  56.1 0.0 copy-start.12
  56.1 0.0 copy-start.13
  56.1 3.6 %shard_map.166.partial_ref = f32[96,256]{1,0:T(8,128)S(1)} custom-call(f32[192,256]{1,0:T(8,128)S(1)} %get-tuple-element.92.image_ref, f32[3,128]{1,0:T(4,128)S(1)} %get-tuple-element.93.held_ref, s32[64,256]{1,0:T(8,128)S(1)} %get-tuple-element.80.row_ref, s32[64,256]{1,0:T(8,128)S(1)} %get-tuple-element.81.column_ref, ...), custom_call_target="tpu_custom_call" | custom-call | tf_op jit(solution)/shard_map/pallas_call | solution.py:611
  59.8 0.1 shard_map.167
  59.9 4.4 %all-to-all-done.3.got_ref.got_c = f32[32,8,128]{2,1,0:T(8,128)S(1)} async-done(((f32[32,8,128]{2,1,0:T(8,128)}), f32[32,8,128]{2,1,0:T(8,128)S(1)}, u32[]{:S(2)}, u32[]{:S(2)}) %all-to-all-start.3) | async-done | bytes 131104 | tf_op jit(solution)/shard_map/all_to_all | solution.py:33
  64.3 1.9 %shard_map.168 = (f32[32,8,128]{2,1,0:T(8,128)}, f32[96,256]{1,0:T(8,128)S(1)}) custom-call(s32[1]{0:T(128)} %bitcast.place_ref, f32[32,8,128]{2,1,0:T(8,128)S(1)} %all-to-all-done.3.got_ref.got_c, s32[8,256]{1,0:T(8,128)S(1)} %get-tuple-element.76.row_ref, bf16[2048,256]{1,0:T(8,128)(2,1)S(1)} %get-tuple-element.77.column_ref, ...), custom_call_target="tpu_custom_call" | custom-call | tf_op jit(solution)/shard_map/pallas_call | solution.py:611
  66.2 0.6 copy-done.6
  66.8 2.7 %all-to-all-start.4 = ((f32[32,8,128]{2,1,0:T(8,128)}), f32[32,8,128]{2,1,0:T(8,128)S(1)}, u32[]{:S(2)}, u32[]{:S(2)}) async-start(f32[32,8,128]{2,1,0:T(8,128)} %get-tuple-element.107), calls=%async_computation.4 | async-start | bytes 262144 | tf_op jit(solution)/shard_map/all_to_all | solution.py:33
  69.5 0.0 copy-done.1
  69.5 0.0 copy-start.7
  69.5 0.9 copy-done.7
  70.4 4.6 %shard_map.169 = (f32[192,256]{1,0:T(8,128)S(1)}, f32[3,128]{1,0:T(4,128)S(1)}, f32[192,256]{1,0:T(8,128)S(1)}, f32[3,6912]{1,0:T(4,128)}) custom-call(s32[1]{0:T(128)} %bitcast.place_ref, f32[96,256]{1,0:T(8,128)S(1)} %copy-done.7, s32[64,256]{1,0:T(8,128)S(1)} %get-tuple-element.62.row_ref.own_where, s32[64,256]{1,0:T(8,128)S(1)} %get-tuple-element.63.lane_ref, ...), custom_call_target="tpu_custom_call" | custom-call | tf_op jit(solution)/shard_map/pallas_call | solution.py:611
  75.0 2.7 %all-to-all-done.4.got_ref = f32[32,8,128]{2,1,0:T(8,128)S(1)} async-done(((f32[32,8,128]{2,1,0:T(8,128)}), f32[32,8,128]{2,1,0:T(8,128)S(1)}, u32[]{:S(2)}, u32[]{:S(2)}) %all-to-all-start.4) | async-done | bytes 131104 | tf_op jit(solution)/shard_map/all_to_all | solution.py:33
  77.7 2.8 %shard_map.170 = (f32[32,1,128]{2,1,0:T(1,128)S(1)}, f32[1,256]{1,0:T(1,128)S(1)}) custom-call(s32[1]{0:T(128)} %bitcast.place_ref, f32[32,8,128]{2,1,0:T(8,128)S(1)} %all-to-all-done.4.got_ref, f32[192,256]{1,0:T(8,128)S(1)} %get-tuple-element.108.cells_ref, f32[3,128]{1,0:T(4,128)S(1)} %get-tuple-element.109.hang_ref, ...), custom_call_target="tpu_custom_call" | custom-call | tf_op jit(solution)/shard_map/pallas_call | solution.py:611
  80.6 10.1 %all_to_all.30.got_ref = f32[32,1,128]{2,1,0:T(1,128)S(1)} all-to-all(f32[32,1,128]{2,1,0:T(1,128)S(1)} %get-tuple-element.113), channel_id=1, replica_groups=mesh['dom'=32] {'dom'}, dimensions={0} | all-to-all | bytes 32768 | tf_op jit(solution)/shard_map/all_to_all | solution.py:33
  90.7 0.8 shard_map.171
  (9 shorter events, 0.0 us)
Async XLA Ops:
  0.6 9.7 %copy-start.3 = (f32[192,192]{1,0:T(8,128)S(1)}, f32[192,192]{1,0:T(8,128)}, u32[]{:S(2)}) copy-start(f32[192,192]{1,0:T(8,128)} %stiffness_ref.1) | copy-start | bytes 442372
  3.0 7.4 %copy-start.8 = (s32[64,256]{1,0:T(8,128)S(1)}, s32[64,256]{1,0:T(8,128)}, u32[]{:S(2)}) copy-start(s32[64,256]{1,0:T(8,128)} %connect_ref) | copy-start | bytes 196612
  3.0 7.4 %copy-start.9 = (s32[16,128]{1,0:T(8,128)S(1)}, s32[16,128]{1,0:T(8,128)}, u32[]{:S(2)}) copy-start(s32[16,128]{1,0:T(8,128)} %master_ref.1) | copy-start | bytes 24580
  3.0 7.4 %copy-start.10 = (f32[16,128]{1,0:T(8,128)S(1)}, f32[16,128]{1,0:T(8,128)}, u32[]{:S(2)}) copy-start(f32[16,128]{1,0:T(8,128)} %weight_ref.1) | copy-start | bytes 24580
  3.0 15.5 %all-to-all-start = ((f32[32,8,128]{2,1,0:T(8,128)}), f32[32,8,128]{2,1,0:T(8,128)S(1)}, u32[]{:S(2)}, u32[]{:S(2)}) async-start(f32[32,8,128]{2,1,0:T(8,128)} %get-tuple-element.59), calls=%async_computation | async-start | bytes 262144 | tf_op jit(solution)/shard_map/all_to_all | solution.py:33
  10.3 0.7 copy-start.14
  10.3 0.7 copy-start.15
  13.1 2.5 %copy-start = (bf16[192,576]{1,0:T(8,128)(2,1)}, bf16[192,576]{1,0:T(8,128)(2,1)S(1)}, u32[]{:S(2)}) copy-start(bf16[192,576]{1,0:T(8,128)(2,1)S(1)} %get-tuple-element.105.stiffness_ref) | copy-start | bytes 663556
  24.1 2.9 %copy-start.4 = (f32[3,6912]{1,0:T(4,128)S(1)}, f32[3,6912]{1,0:T(4,128)}, u32[]{:S(2)}) copy-start(f32[3,6912]{1,0:T(4,128)} %source_ref.1) | copy-start | bytes 248836
  24.1 2.9 %copy-start.5 = (f32[3,6912]{1,0:T(4,128)S(1)}, f32[3,6912]{1,0:T(4,128)}, u32[]{:S(2)}) copy-start(f32[3,6912]{1,0:T(4,128)} %inverse_ref.1) | copy-start | bytes 248836
  24.1 11.2 %all-to-all-start.1 = ((f32[32,8,128]{2,1,0:T(8,128)}), f32[32,8,128]{2,1,0:T(8,128)S(1)}, u32[]{:S(2)}, u32[]{:S(2)}) async-start(f32[32,8,128]{2,1,0:T(8,128)} %get-tuple-element.75), calls=%async_computation.1 | async-start | bytes 262144 | tf_op jit(solution)/shard_map/all_to_all | solution.py:33
  37.1 10.8 %all-to-all-start.2 = ((f32[32,8,128]{2,1,0:T(8,128)}), f32[32,8,128]{2,1,0:T(8,128)S(1)}, u32[]{:S(2)}, u32[]{:S(2)}) async-start(f32[32,8,128]{2,1,0:T(8,128)} %get-tuple-element.86), calls=%async_computation.2 | async-start | bytes 262144 | tf_op jit(solution)/shard_map/all_to_all | solution.py:33
  53.5 10.8 %all-to-all-start.3 = ((f32[32,8,128]{2,1,0:T(8,128)}), f32[32,8,128]{2,1,0:T(8,128)S(1)}, u32[]{:S(2)}, u32[]{:S(2)}) async-start(f32[32,8,128]{2,1,0:T(8,128)} %get-tuple-element.91), calls=%async_computation.3 | async-start | bytes 262144 | tf_op jit(solution)/shard_map/all_to_all | solution.py:33
  56.1 3.7 %copy-start.11 = (s32[8,128]{1,0:T(8,128)S(1)}, s32[8,128]{1,0:T(8,128)}, u32[]{:S(2)}) copy-start(s32[8,128]{1,0:T(8,128)} %cell_ref) | copy-start | bytes 12292
  56.1 3.7 %copy-start.12 = (s32[8,128]{1,0:T(8,128)S(1)}, s32[8,128]{1,0:T(8,128)}, u32[]{:S(2)}) copy-start(s32[8,128]{1,0:T(8,128)} %face_ref) | copy-start | bytes 12292
  56.1 3.7 %copy-start.13 = (s32[8,128]{1,0:T(8,128)S(1)}, s32[8,128]{1,0:T(8,128)}, u32[]{:S(2)}) copy-start(s32[8,128]{1,0:T(8,128)} %owner_ref) | copy-start | bytes 12292
  66.2 0.6 copy-start.6
  66.8 2.7 %copy-start.1 = (bf16[192,576]{1,0:T(8,128)(2,1)S(1)}, bf16[192,576]{1,0:T(8,128)(2,1)}, u32[]{:S(2)}) copy-start(bf16[192,576]{1,0:T(8,128)(2,1)} %copy-done) | copy-start | bytes 663556
  66.8 10.9 %all-to-all-start.4 = ((f32[32,8,128]{2,1,0:T(8,128)}), f32[32,8,128]{2,1,0:T(8,128)S(1)}, u32[]{:S(2)}, u32[]{:S(2)}) async-start(f32[32,8,128]{2,1,0:T(8,128)} %get-tuple-element.107), calls=%async_computation.4 | async-start | bytes 262144 | tf_op jit(solution)/shard_map/all_to_all | solution.py:33
  69.5 0.9 copy-start.7
  70.4 7.3 %copy-start.2 = (f32[192,256]{1,0:T(8,128)S(1)}, f32[192,256]{1,0:T(8,128)}, u32[]{:S(2)}) copy-start(f32[192,256]{1,0:T(8,128)} %load_ref.1) | copy-start | bytes 589828

commit v11 on v9

--- a/solution.py
+++ b/solution.py
@@ -220,6 +220,13 @@
     return totals
 
 
+def product(threefold, cells):
+    high, low = pieces(cells)
+    return jnp.dot(
+        threefold, jnp.concatenate([high, low, high], 0), preferred_element_type=f32
+    )
+
+
 def fill_table(x_ref, out_ref):
     count = x_ref.shape[1] // WIDE
     for part in range(3):
@@ -278,7 +285,7 @@
 
 
 def first_export(
-    place_ref, adjoint_hbm, primal_hbm, list_hbm, tab_a, tab_p, row_ref, column_ref, extra_ref,
+    adjoint_hbm, primal_hbm, list_hbm, tab_a, tab_p, row_ref, column_ref, extra_ref,
     out_ref, pack_ref, adjoint_ref, primal_ref, list_ref, sums_ref, sems,
 ):
     copy_in(
@@ -295,17 +302,23 @@
     tiles = export_tiles(table, 6, row_ref, column_ref, sums_ref)
     for number in range(6):
         extra_ref[number] = tiles[6 + number]
-    pack(place_ref[0], 1, rows_of(tiles[:6]), pack_ref, out_ref)
+    pack(lax.axis_index("dom"), 1, rows_of(tiles[:6]), pack_ref, out_ref)
 
 
 def setup(
-    owned, connect_ref, node_ref, master_ref, weight_ref, modulus_ref,
+    owned, connect_ref, node_ref, master_ref, weight_ref, modulus_ref, stiffness_ref,
     own_where, own_row, edge_where, lane_ref, column_ref, master_own, master_own_row,
-    master_edge, master_lane, master_column, weight_out, modulus_out,
+    master_edge, master_lane, master_column, weight_out, modulus_out, forward_out, adjoint_out,
     map_ref, tall_ref, sums_ref,
 ):
     extent = owned + 2 * REACH * WIDE
     modulus_out[...] = modulus_ref[...]
+    for out_ref, matrix in (
+        (forward_out, stiffness_ref[...]),
+        (adjoint_out, jnp.transpose(stiffness_ref[...])),
+    ):
+        high, low = pieces(matrix)
+        out_ref[...] = jnp.concatenate([high, high, low], 1)
     codes = master_ref[...]
     master = lax.rem(17 * codes + 8 * lax.broadcasted_iota(i32, codes.shape, 1), extent)
     count = codes.shape[0] // 2
@@ -413,22 +426,16 @@
 
 
 def edge_product(
-    primal_part, place_ref, got_ref, cells_ref, hang_ref, row_ref, lane_ref, master_row,
+    primal_part, got_ref, cells_ref, hang_ref, row_ref, lane_ref, master_row,
     master_lane, weight_ref, extra_ref, modulus_ref, stiffness_ref, out_ref,
     image_ref, held_ref, pack_ref, edge_ref, sums_ref, full_ref, low_ref, sum_ref, *scratch,
 ):
-    place = place_ref[0]
+    place = lax.axis_index("dom")
     edge_gather(
         place, [got_ref] * 3, (0, 2, 4), cells_ref, hang_ref, row_ref, lane_ref,
         master_row, master_lane, weight_ref, edge_ref, sums_ref, full_ref,
     )
-    image = modulus_ref[...] * lax.dot_general(
-        stiffness_ref[...],
-        full_ref[...],
-        (((0,), (0,)), ((), ())),
-        precision=lax.Precision.HIGHEST,
-        preferred_element_type=f32,
-    )
+    image = modulus_ref[...] * product(stiffness_ref[...], full_ref[...])
     image_ref[...] = image
     full_ref[...], low_ref[...] = split32(image)
     scatter(full_ref, low_ref, EDGE, row_ref, lane_ref, sum_ref)
@@ -470,11 +477,11 @@
 
 
 def update(
-    primal_part, place_ref, got_ref, row_ref, column_ref, partial_ref, inverse_ref, extra_ref,
+    primal_part, got_ref, row_ref, column_ref, partial_ref, inverse_ref, extra_ref,
     out_ref, tab_ref,
     pack_ref, sums_ref, *scratch,
 ):
-    place = place_ref[0]
+    place = lax.axis_index("dom")
     values = [landed_wide(place, -1, got_ref, part) for part in range(3)]
     returned = scatter_few(values, OWN, row_ref, column_ref, scratch)
     fresh = partial_ref[...] - relaxation * inverse_ref[...] * returned
@@ -486,14 +493,14 @@
 
 
 def last_gather(
-    half_rows, place_ref, tab_ref, own_where, lane_ref, master_own, master_lane, weight_ref,
+    half_rows, tab_ref, own_where, lane_ref, master_own, master_lane, weight_ref,
     got_a, got_b, got_c, primal_cells, primal_hang, edge_where, master_edge, modulus_ref,
     stiffness_ref, cells_ref, hang_ref, ku_ref, final_ref,
     tall_ref, sums_ref, edge_ref, edge_sums, full_ref,
 ):
     tall = up8(half_rows)
     own = tall_table([tab_ref], half_rows, tall_ref)
-    edge = ghost_rows(place_ref[0], (got_a, got_b, got_c), (6, 6, 6), edge_ref)
+    edge = ghost_rows(lax.axis_index("dom"), (got_a, got_b, got_c), (6, 6, 6), edge_ref)
     gather(
         [(own, tall, 3, master_own, sums_ref), (edge, TALL, 3, master_edge, edge_sums)],
         master_lane,
@@ -511,12 +518,7 @@
         rows = slice(part * count, (part + 1) * count)
         cells_ref[rows, :] = gathered(sums_ref, count, part)
         full_ref[rows, :] = primal_cells[rows, :] + gathered(edge_sums, count, part)
-    ku_ref[...] = modulus_ref[...] * jnp.dot(
-        stiffness_ref[...],
-        full_ref[...],
-        precision=lax.Precision.HIGHEST,
-        preferred_element_type=f32,
-    )
+    ku_ref[...] = modulus_ref[...] * product(stiffness_ref[...], full_ref[...])
     for row in range(final_ref.shape[1] // WIDE):
         for part in range(3):
             final_ref[part : part + 1, row * WIDE : (row + 1) * WIDE] = tab_ref[
@@ -525,11 +527,11 @@
 
 
 def fluxes(
-    place_ref, got_ref, cells_ref, hang_ref, row_ref, lane_ref, master_row,
+    got_ref, cells_ref, hang_ref, row_ref, lane_ref, master_row,
     master_lane, weight_ref, ku_ref, load_ref, sub_cell, sub_face, out_ref,
     term_ref, pack_ref, edge_ref, sums_ref, full_ref, tall_ref, code_ref, few_ref,
 ):
-    place = place_ref[0]
+    place = lax.axis_index("dom")
     edge_gather(
         place, [got_ref] * 3, (0, 2, 4), cells_ref, hang_ref, row_ref, lane_ref,
         master_row, master_lane, weight_ref, edge_ref, sums_ref, full_ref,
@@ -561,9 +563,9 @@
     pack(place, 1, rows, pack_ref, out_ref)
 
 
-def collect(place_ref, got_ref, owner_ref, term_ref, out_ref):
+def collect(got_ref, owner_ref, term_ref, out_ref):
     count = term_ref.shape[1]
-    got = jnp.concatenate(landed(place_ref[0], 1, got_ref, 0), 1)
+    got = jnp.concatenate(landed(lax.axis_index("dom"), 1, got_ref, 0), 1)
     hot = jnp.concatenate(
         [one_hot(owner_ref[slot : slot + 1, :], count) for slot in range(2 * REACH)], 1
     )
@@ -575,7 +577,6 @@
     out_ref[...] = (jnp.abs(term_ref[...]) + jnp.abs(face_term)) / scale_down
 
 
-SMALL = pl.BlockSpec(memory_space=pltpu.SMEM)
 FAST = pl.BlockSpec(memory_space=pltpu.VMEM)
 FAR = pl.BlockSpec(memory_space=pl.ANY)
 
@@ -592,8 +593,8 @@
     def run(*args):
         return pl.pallas_call(
             kernel,
-            out_shape=[jax.ShapeDtypeStruct(shape, kind) for shape, kind in outs],
-            in_specs=specs or [SMALL] + [FAST] * (len(args) - 1),
+            out_shape=[out if hasattr(out, "memory_space") else jax.ShapeDtypeStruct(*out) for out in outs],
+            in_specs=specs or [FAST] * len(args),
             scratch_shapes=scratch,
             compiler_params=pltpu.CompilerParams(vmem_limit_bytes=40 * 1024 * 1024),
         )(*args)
@@ -622,7 +623,6 @@
     local_values, cell_count = cell_load.shape
     nodes = connectivity.shape[0]
     half_rows = adjoint_start.shape[1] // LANES
-    place = lax.axis_index("dom").reshape(1).astype(i32)
     table = ((3 * OWN, WIDE), f32)
     index = ((nodes, cell_count), i32)
     cells_shape = ((local_values, cell_count), f32)
@@ -632,7 +632,7 @@
     count = lax.axis_size("dom")
 
     def packed(height):
-        return [((count, height, LANES), f32)]
+        return [pltpu.VMEM((count, height, LANES), f32)]
 
     def room(height):
         return ((count + 1, height, LANES), f32)
@@ -655,21 +655,24 @@
             (ghost_lists.shape, i32),
             ((2, 6 * 64, LANES), f32),
         ],
-        [SMALL, FAR, FAR, FAR],
+        [FAR, FAR, FAR],
         sems=3,
-    )(place, *away(adjoint_start, primal_field, ghost_lists))
+    )(*away(adjoint_start, primal_field, ghost_lists))
     ghosts = exchange(blocks)
     (
         own_where, own_row, edge_where, lane, own_column, master_own, master_own_row, master_edge,
-        master_lane, master_column, weight, moduli,
+        master_lane, master_column, weight, moduli, forward, backward,
     ) = call(
         functools.partial(setup, adjoint_start.shape[1]),
-        [index] * 5 + [master_shape] * 5 + [((8, WIDE), f32), ((1, cell_count), f32)],
+        [index] * 5
+        + [master_shape] * 5
+        + [((8, WIDE), f32), ((1, cell_count), f32)]
+        + [((local_values, 3 * local_values), bf16)] * 2,
         [((OWN, WIDE), f32), ((tall, LANES), f32), ((2, nodes * 8, LANES), f32)],
-        [FAST] * 5,
+        [FAST] * 6,
     )(
         connectivity, hang_node.reshape(1, -1), hang_master, hang_weight,
-        modulus.reshape(1, cell_count),
+        modulus.reshape(1, cell_count), stiffness,
     )
 
     def gather_own(*fields):
@@ -696,7 +699,7 @@
             functools.partial(edge_product, 2 * sweep),
             packed(8) + [cells_shape, hang_shape],
             [room(8)] + edge + [cells_shape, ((6 * EDGE, LANES), f32)] + few(EDGE, LANES),
-        )(place, ghosts, cells, hang, *on_edge, extra, moduli, stiffness)
+        )(ghosts, cells, hang, *on_edge, extra, moduli, backward)
         returned = exchange(blocks)
         landings.append(returned)
         partial, *tables = call(
@@ -714,7 +717,7 @@
             functools.partial(update, 1 if sweep == 0 else None),
             packed(8) + [table],
             [room(8), few_sums] + few(OWN, WIDE),
-        )(place, returned, list_row, list_column, partial, inverse, extra)
+        )(returned, list_row, list_column, partial, inverse, extra)
         ghosts = exchange(blocks)
         landings.append(ghosts)
     cells, hang, ku, adjoint = call(
@@ -722,8 +725,8 @@
         [cells_shape, hang_shape, cells_shape, (adjoint_start.shape, f32)],
         [own_tall, many_sums] + edge,
     )(
-        place, tab, own_where, lane, master_own, master_lane, weight, *landings[:3], *primal_cells,
-        edge_where, master_edge, moduli, stiffness,
+        tab, own_where, lane, master_own, master_lane, weight, *landings[:3], *primal_cells,
+        edge_where, master_edge, moduli, forward,
     )
     blocks, term = call(
         fluxes,
@@ -735,10 +738,10 @@
             ((16, subface_cell.shape[1]), i32),
             ((1, 64, LANES), f32),
         ],
-    )(place, ghosts, cells, hang, *on_edge, ku, cell_load, subface_cell, subface_face)
+    )(ghosts, cells, hang, *on_edge, ku, cell_load, subface_cell, subface_face)
     received = exchange(blocks)
     (indicator,) = call(collect, [((1, cell_count), f32)])(
-        place, received, subface_owner, term
+        received, subface_owner, term
     )
     return (adjoint, indicator.reshape(cell_count))
 

time: 91.1 us -> 91.1 us (level)
  transfers between devices with their start and end apart: 5 -> 5, of which waited for: 5 -> 5; matrix products, arithmetic and copies ran while one was open for 0% -> 0% of each run, Pallas kernels for 24% -> 23%
where the time goes in v11:
time: 91.1 us; the launch traced here: 90.6 us
  Pallas kernels  42.2 us (46%)
  waiting for transfers between devices  18.9 us (21%)
  starting transfers between devices  18 us (20%)
  blocking collectives  9.9 us (11%)
    pallas_call x13, Pallas kernels, run(): pl.pallas_call(kernel, out_shape=[out if hasattr(out, 'memory_space') els...  42.2 us
    all_to_all x5, waiting for transfers between devices, exchange(): return lax.all_to_all(packed, 'dom', 0, 0, tiled=True)  18.9 us
    all_to_all x5, starting transfers between devices, exchange(): return lax.all_to_all(packed, 'dom', 0, 0, tiled=True)  18 us
    all_to_all x1, blocking collectives, exchange(): return lax.all_to_all(packed, 'dom', 0, 0, tiled=True)  9.9 us
  transfers between devices with their start and end apart: 5, of which 5 were waited for; matrix products, arithmetic and copies ran while one was open for 0% of the time, Pallas kernels for 23%

profile of v11, /device:TPU:0, one launch (start us, length us, event | category | flops | bytes accessed | tf_op | source)
XLA Modules:
  0.0 90.6 jit_solution(18042613020450330817)
XLA Ops:
  0.6 0.0 copy-start.1
  0.6 2.4 %shard_map.158 = (f32[96,256]{1,0:T(8,128)S(1)}, f32[96,256]{1,0:T(8,128)S(1)}, s32[8,256]{1,0:T(8,128)S(1)}, s32[8,256]{1,0:T(8,128)S(1)}, f32[6,8,128]{2,1,0:T(8,128)S(1)}, /*index=5*/f32[32,8,128]{2,1,0:T(8,128)}) custom-call(f32[3,6912]{1,0:T(4,128)} %adjoint_hbm.1, f32[3,6912]{1,0:T(4,128)} %primal_hbm.1, s32[8,256]{1,0:T(8,128)} %list_hbm.1), custom_call_target="tpu_custom_call" | custom-call | tf_op jit(solution)/shard_map/pallas_call | solution.py:594
  3.0 0.0 copy-start.4
  3.0 0.0 copy-start.5
  3.0 0.0 copy-start.6
  3.0 7.3 %all-to-all-start = ((f32[32,8,128]{2,1,0:T(8,128)}), f32[32,8,128]{2,1,0:T(8,128)S(1)}, u32[]{:S(2)}, u32[]{:S(2)}) async-start(f32[32,8,128]{2,1,0:T(8,128)} %get-tuple-element.47), calls=%async_computation | async-start | bytes 262144 | tf_op jit(solution)/shard_map/all_to_all | solution.py:33
  10.3 0.0 copy-start.10
  10.4 0.0 copy-start.11
  10.4 0.0 copy-done.1
  10.4 0.0 copy-done.4
  10.4 0.0 copy-done.5
  10.4 0.0 copy-done.6
  10.4 0.6 copy-done.10
  11.0 0.0 copy-done.11
  11.0 2.0 %shard_map.159 = (s32[64,256]{1,0:T(8,128)S(1)}, s32[64,256]{1,0:T(8,128)S(1)}, s32[64,256]{1,0:T(8,128)S(1)}, s32[64,256]{1,0:T(8,128)S(1)}, s32[64,256]{1,0:T(...) custom-call(s32[64,256]{1,0:T(8,128)S(1)} %copy-done.4, ...), custom_call_target="tpu_custom_call" | custom-call | tf_op jit(solution)/shard_map/pallas_call | solution.py:594
  13.1 2.5 %shard_map.160 = (f32[192,256]{1,0:T(8,128)S(1)}, f32[3,128]{1,0:T(4,128)S(1)}) custom-call(s32[64,256]{1,0:T(8,128)S(1)} %get-tuple-element.48.row_ref.own_where, s32[64,256]{1,0:T(8,128)S(1)} %get-tuple-element.49.lane_ref, s32[8,256]{1,0:T(8,128)S(1)} %get-tuple-element.50.master_row.master_own, s32[8,256]{1,0:T(8,128)S(1)} %get-tuple-element.51.master_lane, ...), custom_call_target="tpu_custom_call" | custom-call | tf_op jit(solution)/shard_map/pallas_call | solution.py:594
  15.6 3.0 %all-to-all-done.got_ref = f32[32,8,128]{2,1,0:T(8,128)S(1)} async-done(((f32[32,8,128]{2,1,0:T(8,128)}), f32[32,8,128]{2,1,0:T(8,128)S(1)}, u32[]{:S(2)}, u32[]{:S(2)}) %all-to-all-start) | async-done | bytes 131104 | tf_op jit(solution)/shard_map/all_to_all | solution.py:33
  18.6 5.6 %shard_map.161 = (f32[32,8,128]{2,1,0:T(8,128)}, f32[192,256]{1,0:T(8,128)S(1)}, f32[3,128]{1,0:T(4,128)S(1)}) custom-call(f32[32,8,128]{2,1,0:T(8,128)S(1)} %all-to-all-done.got_ref, f32[192,256]{1,0:T(8,128)S(1)} %get-tuple-element.54.cells_ref, f32[3,128]{1,0:T(4,128)S(1)} %get-tuple-element.55.hang_ref, ...), custom_call_target="tpu_custom_call" | custom-call | tf_op jit(solution)/shard_map/pallas_call | solution.py:594
  24.2 0.0 copy-start.2
  24.2 0.0 copy-start.3
  24.2 2.9 %all-to-all-start.1 = ((f32[32,8,128]{2,1,0:T(8,128)}), f32[32,8,128]{2,1,0:T(8,128)S(1)}, u32[]{:S(2)}, u32[]{:S(2)}) async-start(f32[32,8,128]{2,1,0:T(8,128)} %get-tuple-element.61), calls=%async_computation.1 | async-start | bytes 262144 | tf_op jit(solution)/shard_map/all_to_all | solution.py:33
  27.1 0.0 copy-done.2
  27.1 0.0 copy-done.3
  27.1 3.7 %shard_map.162 = (f32[96,256]{1,0:T(8,128)S(1)}, f32[96,256]{1,0:T(8,128)S(1)}, f32[96,256]{1,0:T(8,128)S(1)}) custom-call(f32[192,256]{1,0:T(8,128)S(1)} %get-tuple-element.64.image_ref, f32[3,128]{1,0:T(4,128)S(1)} %get-tuple-element.65.held_ref, s32[64,256]{1,0:T(8,128)S(1)} %get-tuple-element.66.row_ref, s32[64,256]{1,0:T(8,128)S(1)} %get-tuple-element.67.column_ref, ...), custom_call_target="tpu_custom_call" | custom-call | tf_op jit(solution)/shard_map/pallas_call | solution.py:594
  30.8 4.5 %all-to-all-done.1.got_ref.got_a = f32[32,8,128]{2,1,0:T(8,128)S(1)} async-done(((f32[32,8,128]{2,1,0:T(8,128)}), f32[32,8,128]{2,1,0:T(8,128)S(1)}, u32[]{:S(2)}, u32[]{:S(2)}) %all-to-all-start.1) | async-done | bytes 131104 | tf_op jit(solution)/shard_map/all_to_all | solution.py:33
  35.3 1.9 %shard_map.163 = (f32[32,8,128]{2,1,0:T(8,128)}, f32[96,256]{1,0:T(8,128)S(1)}) custom-call(f32[32,8,128]{2,1,0:T(8,128)S(1)} %all-to-all-done.1.got_ref.got_a, s32[8,256]{1,0:T(8,128)S(1)} %get-tuple-element.62.row_ref, s32[8,256]{1,0:T(8,128)S(1)} %get-tuple-element.63.column_ref, f32[96,256]{1,0:T(8,128)S(1)} %get-tuple-element.70.partial_ref, ...), custom_call_target="tpu_custom_call" | custom-call | tf_op jit(solution)/shard_map/pallas_call | solution.py:594
  37.2 2.7 %all-to-all-start.2 = ((f32[32,8,128]{2,1,0:T(8,128)}), f32[32,8,128]{2,1,0:T(8,128)S(1)}, u32[]{:S(2)}, u32[]{:S(2)}) async-start(f32[32,8,128]{2,1,0:T(8,128)} %get-tuple-element.72), calls=%async_computation.2 | async-start | bytes 262144 | tf_op jit(solution)/shard_map/all_to_all | solution.py:33
  39.9 4.7 %shard_map.164 = (f32[192,256]{1,0:T(8,128)S(1)}, f32[3,128]{1,0:T(4,128)S(1)}, f32[192,256]{1,0:T(8,128)S(1)}, f32[3,128]{1,0:T(4,128)S(1)}) custom-call(s32[64,256]{1,0:T(8,128)S(1)} %get-tuple-element.48.row_ref.own_where, s32[64,256]{1,0:T(8,128)S(1)} %get-tuple-element.49.lane_ref, s32[8,256]{1,0:T(8,128)S(1)} %get-tuple-element.50.master_row.master_own, ...), custom_call_target="tpu_custom_call" | custom-call | tf_op jit(solution)/shard_map/pallas_call | solution.py:594
  44.6 3.3 %all-to-all-done.2.got_ref.got_b = f32[32,8,128]{2,1,0:T(8,128)S(1)} async-done(((f32[32,8,128]{2,1,0:T(8,128)}), f32[32,8,128]{2,1,0:T(8,128)S(1)}, u32[]{:S(2)}, u32[]{:S(2)}) %all-to-all-start.2) | async-done | bytes 131104 | tf_op jit(solution)/shard_map/all_to_all | solution.py:33
  48.0 5.6 %shard_map.165 = (f32[32,8,128]{2,1,0:T(8,128)}, f32[192,256]{1,0:T(8,128)S(1)}, f32[3,128]{1,0:T(4,128)S(1)}) custom-call(f32[32,8,128]{2,1,0:T(8,128)S(1)} %all-to-all-done.2.got_ref.got_b, f32[192,256]{1,0:T(8,128)S(1)} %get-tuple-element.75.cells_ref, f32[3,128]{1,0:T(4,128)S(1)} %get-tuple-element.76.hang_ref, ...), custom_call_target="tpu_custom_call" | custom-call | tf_op jit(solution)/shard_map/pallas_call | solution.py:594
  53.5 2.6 %all-to-all-start.3 = ((f32[32,8,128]{2,1,0:T(8,128)}), f32[32,8,128]{2,1,0:T(8,128)S(1)}, u32[]{:S(2)}, u32[]{:S(2)}) async-start(f32[32,8,128]{2,1,0:T(8,128)} %get-tuple-element.77), calls=%async_computation.3 | async-start | bytes 262144 | tf_op jit(solution)/shard_map/all_to_all | solution.py:33
  56.1 3.6 %shard_map.166.partial_ref = f32[96,256]{1,0:T(8,128)S(1)} custom-call(f32[192,256]{1,0:T(8,128)S(1)} %get-tuple-element.78.image_ref, f32[3,128]{1,0:T(4,128)S(1)} %get-tuple-element.79.held_ref, s32[64,256]{1,0:T(8,128)S(1)} %get-tuple-element.66.row_ref, s32[64,256]{1,0:T(8,128)S(1)} %get-tuple-element.67.column_ref, ...), custom_call_target="tpu_custom_call" | custom-call | tf_op jit(solution)/shard_map/pallas_call | solution.py:594
  59.7 4.6 %all-to-all-done.3.got_ref.got_c = f32[32,8,128]{2,1,0:T(8,128)S(1)} async-done(((f32[32,8,128]{2,1,0:T(8,128)}), f32[32,8,128]{2,1,0:T(8,128)S(1)}, u32[]{:S(2)}, u32[]{:S(2)}) %all-to-all-start.3) | async-done | bytes 131104 | tf_op jit(solution)/shard_map/all_to_all | solution.py:33
  64.3 1.9 %shard_map.167 = (f32[32,8,128]{2,1,0:T(8,128)}, f32[96,256]{1,0:T(8,128)S(1)}) custom-call(f32[32,8,128]{2,1,0:T(8,128)S(1)} %all-to-all-done.3.got_ref.got_c, s32[8,256]{1,0:T(8,128)S(1)} %get-tuple-element.62.row_ref, s32[8,256]{1,0:T(8,128)S(1)} %get-tuple-element.63.column_ref, f32[96,256]{1,0:T(8,128)S(1)} %shard_map.166.partial_ref, ...), custom_call_target="tpu_custom_call" | custom-call | tf_op jit(solution)/shard_map/pallas_call | solution.py:594
  66.2 2.6 %all-to-all-start.4 = ((f32[32,8,128]{2,1,0:T(8,128)}), f32[32,8,128]{2,1,0:T(8,128)S(1)}, u32[]{:S(2)}, u32[]{:S(2)}) async-start(f32[32,8,128]{2,1,0:T(8,128)} %get-tuple-element.86), calls=%async_computation.4 | async-start | bytes 262144 | tf_op jit(solution)/shard_map/all_to_all | solution.py:33
  68.8 0.0 copy-start
  68.8 0.0 copy-start.8
  68.8 4.6 %shard_map.168 = (f32[192,256]{1,0:T(8,128)S(1)}, f32[3,128]{1,0:T(4,128)S(1)}, f32[192,256]{1,0:T(8,128)S(1)}, f32[3,6912]{1,0:T(4,128)}) custom-call(f32[96,256]{1,0:T(8,128)S(1)} %get-tuple-element.81.tab_ref, s32[64,256]{1,0:T(8,128)S(1)} %get-tuple-element.48.row_ref.own_where, s32[64,256]{1,0:T(8,128)S(1)} %get-tuple-element.49.lane_ref, ...), custom_call_target="tpu_custom_call" | custom-call | tf_op jit(solution)/shard_map/pallas_call | solution.py:594
  73.4 0.0 copy-start.7
  73.4 3.6 %all-to-all-done.4.got_ref = f32[32,8,128]{2,1,0:T(8,128)S(1)} async-done(((f32[32,8,128]{2,1,0:T(8,128)}), f32[32,8,128]{2,1,0:T(8,128)S(1)}, u32[]{:S(2)}, u32[]{:S(2)}) %all-to-all-start.4) | async-done | bytes 131104 | tf_op jit(solution)/shard_map/all_to_all | solution.py:33
  77.0 0.0 copy-done
  77.0 0.0 copy-done.8
  77.0 0.0 copy-done.7
  77.0 0.0 copy-start.9
  77.0 2.9 %shard_map.169 = (f32[32,1,128]{2,1,0:T(1,128)S(1)}, f32[1,256]{1,0:T(1,128)S(1)}) custom-call(f32[32,8,128]{2,1,0:T(8,128)S(1)} %all-to-all-done.4.got_ref, f32[192,256]{1,0:T(8,128)S(1)} %get-tuple-element.87.cells_ref, f32[3,128]{1,0:T(4,128)S(1)} %get-tuple-element.88.hang_ref, s32[64,256]{1,0:T(8,128)S(1)} %get-tuple-element.56.row_ref.edge_where, ...), custom_call_target="tpu_custom_call" | custom-call | tf_op jit(solution)/shard_map/pallas_call | solution.py:594
  79.9 9.9 %all_to_all.30.got_ref = f32[32,1,128]{2,1,0:T(1,128)S(1)} all-to-all(f32[32,1,128]{2,1,0:T(1,128)S(1)} %get-tuple-element.90), channel_id=1, replica_groups=mesh['dom'=32] {'dom'}, dimensions={0} | all-to-all | bytes 32768 | tf_op jit(solution)/shard_map/all_to_all | solution.py:33
  89.8 0.0 copy-done.9
  89.8 0.8 shard_map.170
Async XLA Ops:
  0.6 9.7 %copy-start.1 = (f32[192,192]{1,0:T(8,128)S(1)}, f32[192,192]{1,0:T(8,128)}, u32[]{:S(2)}) copy-start(f32[192,192]{1,0:T(8,128)} %stiffness_ref.1) | copy-start | bytes 442372
  3.0 7.4 %copy-start.4 = (s32[64,256]{1,0:T(8,128)S(1)}, s32[64,256]{1,0:T(8,128)}, u32[]{:S(2)}) copy-start(s32[64,256]{1,0:T(8,128)} %connect_ref.1) | copy-start | bytes 196612
  3.0 7.4 %copy-start.5 = (s32[16,128]{1,0:T(8,128)S(1)}, s32[16,128]{1,0:T(8,128)}, u32[]{:S(2)}) copy-start(s32[16,128]{1,0:T(8,128)} %master_ref.1) | copy-start | bytes 24580
  3.0 7.4 %copy-start.6 = (f32[16,128]{1,0:T(8,128)S(1)}, f32[16,128]{1,0:T(8,128)}, u32[]{:S(2)}) copy-start(f32[16,128]{1,0:T(8,128)} %weight_ref.1) | copy-start | bytes 24580
  3.0 15.5 %all-to-all-start = ((f32[32,8,128]{2,1,0:T(8,128)}), f32[32,8,128]{2,1,0:T(8,128)S(1)}, u32[]{:S(2)}, u32[]{:S(2)}) async-start(f32[32,8,128]{2,1,0:T(8,128)} %get-tuple-element.47), calls=%async_computation | async-start | bytes 262144 | tf_op jit(solution)/shard_map/all_to_all | solution.py:33
  10.3 0.7 copy-start.10
  10.4 0.7 copy-start.11
  24.2 2.9 %copy-start.2 = (f32[3,6912]{1,0:T(4,128)S(1)}, f32[3,6912]{1,0:T(4,128)}, u32[]{:S(2)}) copy-start(f32[3,6912]{1,0:T(4,128)} %source_ref.1) | copy-start | bytes 248836
  24.2 2.9 %copy-start.3 = (f32[3,6912]{1,0:T(4,128)S(1)}, f32[3,6912]{1,0:T(4,128)}, u32[]{:S(2)}) copy-start(f32[3,6912]{1,0:T(4,128)} %inverse_ref.1) | copy-start | bytes 248836
  24.2 11.1 %all-to-all-start.1 = ((f32[32,8,128]{2,1,0:T(8,128)}), f32[32,8,128]{2,1,0:T(8,128)S(1)}, u32[]{:S(2)}, u32[]{:S(2)}) async-start(f32[32,8,128]{2,1,0:T(8,128)} %get-tuple-element.61), calls=%async_computation.1 | async-start | bytes 262144 | tf_op jit(solution)/shard_map/all_to_all | solution.py:33
  37.2 10.8 %all-to-all-start.2 = ((f32[32,8,128]{2,1,0:T(8,128)}), f32[32,8,128]{2,1,0:T(8,128)S(1)}, u32[]{:S(2)}, u32[]{:S(2)}) async-start(f32[32,8,128]{2,1,0:T(8,128)} %get-tuple-element.72), calls=%async_computation.2 | async-start | bytes 262144 | tf_op jit(solution)/shard_map/all_to_all | solution.py:33
  53.5 10.8 %all-to-all-start.3 = ((f32[32,8,128]{2,1,0:T(8,128)}), f32[32,8,128]{2,1,0:T(8,128)S(1)}, u32[]{:S(2)}, u32[]{:S(2)}) async-start(f32[32,8,128]{2,1,0:T(8,128)} %get-tuple-element.77), calls=%async_computation.3 | async-start | bytes 262144 | tf_op jit(solution)/shard_map/all_to_all | solution.py:33
  66.2 10.8 %all-to-all-start.4 = ((f32[32,8,128]{2,1,0:T(8,128)}), f32[32,8,128]{2,1,0:T(8,128)S(1)}, u32[]{:S(2)}, u32[]{:S(2)}) async-start(f32[32,8,128]{2,1,0:T(8,128)} %get-tuple-element.86), calls=%async_computation.4 | async-start | bytes 262144 | tf_op jit(solution)/shard_map/all_to_all | solution.py:33
  68.8 8.2 %copy-start = (f32[192,256]{1,0:T(8,128)S(1)}, f32[192,256]{1,0:T(8,128)}, u32[]{:S(2)}) copy-start(f32[192,256]{1,0:T(8,128)} %load_ref.1) | copy-start | bytes 589828
  68.8 8.2 %copy-start.8 = (s32[8,128]{1,0:T(8,128)S(1)}, s32[8,128]{1,0:T(8,128)}, u32[]{:S(2)}) copy-start(s32[8,128]{1,0:T(8,128)} %sub_face.1) | copy-start | bytes 12292
  73.4 3.6 %copy-start.7 = (s32[8,128]{1,0:T(8,128)S(1)}, s32[8,128]{1,0:T(8,128)}, u32[]{:S(2)}) copy-start(s32[8,128]{1,0:T(8,128)} %sub_cell.1) | copy-start | bytes 12292
  77.0 12.8 %copy-start.9 = (s32[8,128]{1,0:T(8,128)S(1)}, s32[8,128]{1,0:T(8,128)}, u32[]{:S(2)}) copy-start(s32[8,128]{1,0:T(8,128)} %owner_ref.1) | copy-start | bytes 12292

commit v12 on v11

--- a/solution.py
+++ b/solution.py
@@ -86,8 +86,14 @@
     return high, (x - high.astype(f32)).astype(bf16)
 
 
+def hot_at(column_ref, number, high):
+    if column_ref.dtype == bf16:
+        return column_ref[pl.ds(pl.multiple_of(number * high, high), high), :]
+    return one_hot(column_ref[pl.ds(number, 1), :], high)
+
+
 def gather(jobs, column_ref, wide=False):
-    count, width = column_ref.shape
+    count, width = jobs[0][3].shape
     tables = jnp.concatenate([job[0] for job in jobs], 0)
     high = tables.shape[0]
     numbers = lax.broadcasted_iota(i32, (max(job[1] for job in jobs), width), 0)
@@ -96,7 +102,7 @@
     def body(block, carry):
         start = pl.multiple_of(block * step, step)
         for j in range(step):
-            hot = one_hot(column_ref[pl.ds(start + j, 1), :], WIDE if wide else LANES)
+            hot = hot_at(column_ref, start + j, WIDE if wide else LANES)
             if not wide:
                 hot = jnp.concatenate([hot, hot], 0)
             all_found = jnp.dot(tables, hot, preferred_element_type=f32)
@@ -149,7 +155,7 @@
     def product(start):
         masks = [match16(row_ref[pl.ds(start + j, 1), :], rows) for j in range(8)]
         hot = jnp.concatenate(
-            [one_hot(column_ref[pl.ds(start + j, 1), :], sum_ref.shape[1]) for j in range(8)], 1
+            [hot_at(column_ref, start + j, sum_ref.shape[1]) for j in range(8)], 1
         )
         stacked = [
             jnp.concatenate(
@@ -306,13 +312,14 @@
 
 
 def setup(
-    owned, connect_ref, node_ref, master_ref, weight_ref, modulus_ref, stiffness_ref,
-    own_where, own_row, edge_where, lane_ref, column_ref, master_own, master_own_row,
+    owned, connect_ref, node_ref, master_ref, weight_ref, modulus_hbm, stiffness_ref,
+    own_where, own_row, edge_where, hot_ref, column_ref, master_own, master_own_row,
     master_edge, master_lane, master_column, weight_out, modulus_out, forward_out, adjoint_out,
-    map_ref, tall_ref, sums_ref,
+    map_ref, tall_ref, sums_ref, lane_ref, sems,
 ):
     extent = owned + 2 * REACH * WIDE
-    modulus_out[...] = modulus_ref[...]
+    copy = pltpu.make_async_copy(modulus_hbm, modulus_out, sems.at[0])
+    copy.start()
     for out_ref, matrix in (
         (forward_out, stiffness_ref[...]),
         (adjoint_out, jnp.transpose(stiffness_ref[...])),
@@ -367,6 +374,16 @@
     own_row[...], column_ref[...] = rows_and_columns(where_own, lane)
     edge_where[...] = jnp.where(hanging, 4 * REACH, jnp.where(outside, where - last, NOWHERE))
 
+    def body(block, carry):
+        start = pl.multiple_of(block * 16, 16)
+        for j in range(16):
+            at = pl.multiple_of((start + j) * LANES, LANES)
+            hot_ref[pl.ds(at, LANES), :] = one_hot(lane_ref[pl.ds(start + j, 1), :], LANES)
+        return carry
+
+    lax.fori_loop(0, codes.shape[0] // 16, body, 0)
+    copy.wait()
+
 
 def own_gather(
     half_rows, fields, row_ref, lane_ref, master_row, master_lane, weight_ref, *refs
@@ -513,7 +530,7 @@
     gather(
         [(own, tall, 3, own_where, sums_ref), (edge, TALL, 3, edge_where, edge_sums)], lane_ref
     )
-    count = lane_ref.shape[0]
+    count = own_where.shape[0]
     for part in range(3):
         rows = slice(part * count, (part + 1) * count)
         cells_ref[rows, :] = gathered(sums_ref, count, part)
@@ -593,10 +610,10 @@
     def run(*args):
         return pl.pallas_call(
             kernel,
-            out_shape=[out if hasattr(out, "memory_space") else jax.ShapeDtypeStruct(*out) for out in outs],
+            out_shape=[jax.ShapeDtypeStruct(*out) for out in outs],
             in_specs=specs or [FAST] * len(args),
             scratch_shapes=scratch,
-            compiler_params=pltpu.CompilerParams(vmem_limit_bytes=40 * 1024 * 1024),
+            compiler_params=pltpu.CompilerParams(vmem_limit_bytes=16 * 1024 * 1024),
         )(*args)
 
     return run
@@ -632,7 +649,7 @@
     count = lax.axis_size("dom")
 
     def packed(height):
-        return [pltpu.VMEM((count, height, LANES), f32)]
+        return [((count, height, LANES), f32)]
 
     def room(height):
         return ((count + 1, height, LANES), f32)
@@ -660,19 +677,21 @@
     )(*away(adjoint_start, primal_field, ghost_lists))
     ghosts = exchange(blocks)
     (
-        own_where, own_row, edge_where, lane, own_column, master_own, master_own_row, master_edge,
+        own_where, own_row, edge_where, hot, own_column, master_own, master_own_row, master_edge,
         master_lane, master_column, weight, moduli, forward, backward,
     ) = call(
         functools.partial(setup, adjoint_start.shape[1]),
-        [index] * 5
+        [index] * 3
+        + [((nodes * LANES, cell_count), bf16), index]
         + [master_shape] * 5
         + [((8, WIDE), f32), ((1, cell_count), f32)]
         + [((local_values, 3 * local_values), bf16)] * 2,
-        [((OWN, WIDE), f32), ((tall, LANES), f32), ((2, nodes * 8, LANES), f32)],
-        [FAST] * 6,
+        [((OWN, WIDE), f32), ((tall, LANES), f32), ((2, nodes * 8, LANES), f32), index],
+        [FAST] * 4 + [FAR, FAST],
+        sems=1,
     )(
         connectivity, hang_node.reshape(1, -1), hang_master, hang_weight,
-        modulus.reshape(1, cell_count), stiffness,
+        *away(modulus.reshape(1, cell_count)), stiffness,
     )
 
     def gather_own(*fields):
@@ -685,9 +704,9 @@
                 ((2, number * local_values * 8, LANES), f32),
             ],
             specs=[FAST] * (5 + number),
-        )(own_where, lane, master_own, master_lane, weight, *fields)
-
-    on_edge = (edge_where, lane, master_edge, master_lane, weight)
+        )(own_where, hot, master_own, master_lane, weight, *fields)
+
+    on_edge = (edge_where, hot, master_edge, master_lane, weight)
     landings = []
     source, inverse = adjoint_source, inverse_diagonal
     for sweep in range(SWEEPS):
@@ -725,7 +744,7 @@
         [cells_shape, hang_shape, cells_shape, (adjoint_start.shape, f32)],
         [own_tall, many_sums] + edge,
     )(
-        tab, own_where, lane, master_own, master_lane, weight, *landings[:3], *primal_cells,
+        tab, own_where, hot, master_own, master_lane, weight, *landings[:3], *primal_cells,
         edge_where, master_edge, moduli, forward,
     )
     blocks, term = call(

time: 91.1 us -> 107 us (1.17)
  local copies, waits for them, and re-layouts: 0.68 us -> 16.7 us
  waiting for transfers between devices: 18.9 us -> 11.8 us
  starting transfers between devices: 18 us -> 22.9 us
  blocking collectives: 9.9 us -> 11.3 us
    unnamed x24 -> x34, local copies, waits for them, and re-layouts: 0.68 us -> 16.7 us
    all_to_all x5, waiting for transfers between devices: 18.9 us -> 11.8 us  [exchange(): return lax.all_to_all(packed, 'dom', 0, 0, tiled=True)]
    all_to_all x5, starting transfers between devices: 18 us -> 22.9 us  [exchange(): return lax.all_to_all(packed, 'dom', 0, 0, tiled=True)]
    all_to_all x1, blocking collectives: 9.9 us -> 11.3 us  [exchange(): return lax.all_to_all(packed, 'dom', 0, 0, tiled=True)]
  transfers between devices with their start and end apart: 5 -> 5, of which waited for: 5 -> 4; matrix products, arithmetic and copies ran while one was open for 0% -> 0% of each run, Pallas kernels for 23% -> 20%
where the time goes in v12:
time: 107 us; the launch traced here: 106 us
  Pallas kernels  42.5 us (40%)
  starting transfers between devices  22.9 us (21%)
  local copies, waits for them, and re-layouts  16.7 us (16%)
  waiting for transfers between devices  11.8 us (11%)
  blocking collectives  11.3 us (11%)
    pallas_call x13, Pallas kernels, run(): pl.pallas_call(kernel, out_shape=[jax.ShapeDtypeStruct(*out) for out in o...  42.5 us
    all_to_all x5, starting transfers between devices, exchange(): return lax.all_to_all(packed, 'dom', 0, 0, tiled=True)  22.9 us
    unnamed x34, local copies, waits for them, and re-layouts  16.7 us
    all_to_all x5, waiting for transfers between devices, exchange(): return lax.all_to_all(packed, 'dom', 0, 0, tiled=True)  11.8 us
    all_to_all x1, blocking collectives, exchange(): return lax.all_to_all(packed, 'dom', 0, 0, tiled=True)  11.3 us
  transfers between devices with their start and end apart: 5, of which 4 were waited for; matrix products, arithmetic and copies ran while one was open for 0% of the time, Pallas kernels for 20%

profile of v12, /device:TPU:0, one launch (start us, length us, event | category | flops | bytes accessed | tf_op | source)
XLA Modules:
  0.0 106.1 jit_solution(17386787170160523895)
XLA Ops:
  0.6 2.3 %shard_map.158 = (f32[96,256]{1,0:T(8,128)S(1)}, f32[96,256]{1,0:T(8,128)S(1)}, s32[8,256]{1,0:T(8,128)S(1)}, s32[8,256]{1,0:T(8,128)S(1)}, f32[6,8,128]{2,1,0:T(8,128)S(1)}, /*index=5*/f32[32,8,128]{2,1,0:T(8,128)}) custom-call(f32[3,6912]{1,0:T(4,128)} %adjoint_hbm.1, f32[3,6912]{1,0:T(4,128)} %primal_hbm.1, s32[8,256]{1,0:T(8,128)} %list_hbm.1), custom_call_target="tpu_custom_call" | custom-call | tf_op jit(solution)/shard_map/pallas_call | solution.py:611
  2.9 7.3 %all-to-all-start = ((f32[32,8,128]{2,1,0:T(8,128)}), f32[32,8,128]{2,1,0:T(8,128)S(1)}, u32[]{:S(2)}, u32[]{:S(2)}) async-start(f32[32,8,128]{2,1,0:T(8,128)} %get-tuple-element.47), calls=%async_computation | async-start | bytes 262144 | tf_op jit(solution)/shard_map/all_to_all | solution.py:33
  10.3 0.0 copy-start.7
  10.3 0.9 copy-done.7
  11.2 0.8 copy-done.10
  12.0 0.7 copy-done.11
  12.7 0.7 copy-done.12
  13.4 0.7 copy-done.16
  14.1 2.7 %shard_map.159 = (s32[64,256]{1,0:T(8,128)S(1)}, s32[64,256]{1,0:T(8,128)S(1)}, s32[64,256]{1,0:T(8,128)S(1)}, bf16[8192,256]{1,0:T(8,128)(2,1)S(1)}, s32[64,256...) custom-call(s32[64,256]{1,0:T(8,128)S(1)} %copy-done.10, ...), custom_call_target="tpu_custom_call" | custom-call | tf_op jit(solution)/shard_map/pallas_call | solution.py:611
  16.7 0.0 copy-start.8
  16.8 0.0 copy-start.9
  16.8 2.5 %shard_map.160 = (f32[192,256]{1,0:T(8,128)S(1)}, f32[3,128]{1,0:T(4,128)S(1)}) custom-call(s32[64,256]{1,0:T(8,128)S(1)} %get-tuple-element.48.row_ref.own_where, bf16[8192,256]{1,0:T(8,128)(2,1)S(1)} %get-tuple-element.49.lane_ref, s32[8,256]{1,0:T(8,128)S(1)} %get-tuple-element.50.master_row.master_own, s32[8,256]{1,0:T(8,128)S(1)} %get-tuple-element.51.master_lane, ...), custom_call_target="tpu_custom_call" | custom-call | tf_op jit(solution)/shard_map/pallas_call | solution.py:611
  19.3 0.0 copy-start
  19.3 2.0 %copy-done = bf16[8192,256]{1,0:T(8,128)(2,1)} copy-done((bf16[8192,256]{1,0:T(8,128)(2,1)}, bf16[8192,256]{1,0:T(8,128)(2,1)S(1)}, u32[]{:S(2)}) %copy-start) | copy-done | bytes 4194328
  21.2 0.0 all-to-all-done.got_ref
  21.2 2.2 %copy-done.1 = bf16[8192,256]{1,0:T(8,128)(2,1)S(1)} copy-done((bf16[8192,256]{1,0:T(8,128)(2,1)S(1)}, bf16[8192,256]{1,0:T(8,128)(2,1)}, u32[]{:S(2)}) %copy-start.1) | copy-done | bytes 4194328
  23.4 5.6 %shard_map.161 = (f32[32,8,128]{2,1,0:T(8,128)}, f32[192,256]{1,0:T(8,128)S(1)}, f32[3,128]{1,0:T(4,128)S(1)}) custom-call(f32[32,8,128]{2,1,0:T(8,128)S(1)} %all-to-all-done.got_ref, f32[192,256]{1,0:T(8,128)S(1)} %get-tuple-element.54.cells_ref, f32[3,128]{1,0:T(4,128)S(1)} %get-tuple-element.55.hang_ref, ...), custom_call_target="tpu_custom_call" | custom-call | tf_op jit(solution)/shard_map/pallas_call | solution.py:611
  29.0 5.8 %all-to-all-start.1 = ((f32[32,8,128]{2,1,0:T(8,128)}), f32[32,8,128]{2,1,0:T(8,128)S(1)}, u32[]{:S(2)}, u32[]{:S(2)}) async-start(f32[32,8,128]{2,1,0:T(8,128)} %get-tuple-element.61), calls=%async_computation.1 | async-start | bytes 262144 | tf_op jit(solution)/shard_map/all_to_all | solution.py:33
  34.8 0.0 copy-done.8
  34.8 0.0 copy-done.9
  34.9 3.7 %shard_map.162 = (f32[96,256]{1,0:T(8,128)S(1)}, f32[96,256]{1,0:T(8,128)S(1)}, f32[96,256]{1,0:T(8,128)S(1)}) custom-call(f32[192,256]{1,0:T(8,128)S(1)} %get-tuple-element.64.image_ref, f32[3,128]{1,0:T(4,128)S(1)} %get-tuple-element.65.held_ref, s32[64,256]{1,0:T(8,128)S(1)} %get-tuple-element.66.row_ref, s32[64,256]{1,0:T(8,128)S(1)} %get-tuple-element.67.column_ref, ...), custom_call_target="tpu_custom_call" | custom-call | tf_op jit(solution)/shard_map/pallas_call | solution.py:611
  38.6 4.5 %all-to-all-done.1.got_ref.got_a = f32[32,8,128]{2,1,0:T(8,128)S(1)} async-done(((f32[32,8,128]{2,1,0:T(8,128)}), f32[32,8,128]{2,1,0:T(8,128)S(1)}, u32[]{:S(2)}, u32[]{:S(2)}) %all-to-all-start.1) | async-done | bytes 131104 | tf_op jit(solution)/shard_map/all_to_all | solution.py:33
  43.1 1.9 %shard_map.163 = (f32[32,8,128]{2,1,0:T(8,128)}, f32[96,256]{1,0:T(8,128)S(1)}) custom-call(f32[32,8,128]{2,1,0:T(8,128)S(1)} %all-to-all-done.1.got_ref.got_a, s32[8,256]{1,0:T(8,128)S(1)} %get-tuple-element.62.row_ref, s32[8,256]{1,0:T(8,128)S(1)} %get-tuple-element.63.column_ref, f32[96,256]{1,0:T(8,128)S(1)} %get-tuple-element.70.partial_ref, ...), custom_call_target="tpu_custom_call" | custom-call | tf_op jit(solution)/shard_map/pallas_call | solution.py:611
  44.9 2.7 %all-to-all-start.2 = ((f32[32,8,128]{2,1,0:T(8,128)}), f32[32,8,128]{2,1,0:T(8,128)S(1)}, u32[]{:S(2)}, u32[]{:S(2)}) async-start(f32[32,8,128]{2,1,0:T(8,128)} %get-tuple-element.72), calls=%async_computation.2 | async-start | bytes 262144 | tf_op jit(solution)/shard_map/all_to_all | solution.py:33
  47.7 0.0 copy-start.2
  47.7 2.2 %copy-done.2 = bf16[8192,256]{1,0:T(8,128)(2,1)S(1)} copy-done((bf16[8192,256]{1,0:T(8,128)(2,1)S(1)}, bf16[8192,256]{1,0:T(8,128)(2,1)}, u32[]{:S(2)}) %copy-start.2) | copy-done | bytes 4194328
  49.9 4.6 %shard_map.164 = (f32[192,256]{1,0:T(8,128)S(1)}, f32[3,128]{1,0:T(4,128)S(1)}, f32[192,256]{1,0:T(8,128)S(1)}, f32[3,128]{1,0:T(4,128)S(1)}) custom-call(s32[64,256]{1,0:T(8,128)S(1)} %get-tuple-element.48.row_ref.own_where, bf16[8192,256]{1,0:T(8,128)(2,1)S(1)} %copy-done.2, s32[8,256]{1,0:T(8,128)S(1)} %get-tuple-element.50.master_row.master_own, ...), custom_call_target="tpu_custom_call" | custom-call | tf_op jit(solution)/shard_map/pallas_call | solution.py:611
  54.5 1.2 %all-to-all-done.2.got_ref.got_b = f32[32,8,128]{2,1,0:T(8,128)S(1)} async-done(((f32[32,8,128]{2,1,0:T(8,128)}), f32[32,8,128]{2,1,0:T(8,128)S(1)}, u32[]{:S(2)}, u32[]{:S(2)}) %all-to-all-start.2) | async-done | bytes 131104 | tf_op jit(solution)/shard_map/all_to_all | solution.py:33
  55.7 2.2 %copy-done.3 = bf16[8192,256]{1,0:T(8,128)(2,1)S(1)} copy-done((bf16[8192,256]{1,0:T(8,128)(2,1)S(1)}, bf16[8192,256]{1,0:T(8,128)(2,1)}, u32[]{:S(2)}) %copy-start.3) | copy-done | bytes 4194328
  57.9 5.6 %shard_map.165 = (f32[32,8,128]{2,1,0:T(8,128)}, f32[192,256]{1,0:T(8,128)S(1)}, f32[3,128]{1,0:T(4,128)S(1)}) custom-call(f32[32,8,128]{2,1,0:T(8,128)S(1)} %all-to-all-done.2.got_ref.got_b, f32[192,256]{1,0:T(8,128)S(1)} %get-tuple-element.75.cells_ref, f32[3,128]{1,0:T(4,128)S(1)} %get-tuple-element.76.hang_ref, ...), custom_call_target="tpu_custom_call" | custom-call | tf_op jit(solution)/shard_map/pallas_call | solution.py:611
  63.5 4.5 %all-to-all-start.3 = ((f32[32,8,128]{2,1,0:T(8,128)}), f32[32,8,128]{2,1,0:T(8,128)S(1)}, u32[]{:S(2)}, u32[]{:S(2)}) async-start(f32[32,8,128]{2,1,0:T(8,128)} %get-tuple-element.77), calls=%async_computation.3 | async-start | bytes 262144 | tf_op jit(solution)/shard_map/all_to_all | solution.py:33
  68.0 3.6 %shard_map.166.partial_ref = f32[96,256]{1,0:T(8,128)S(1)} custom-call(f32[192,256]{1,0:T(8,128)S(1)} %get-tuple-element.78.image_ref, f32[3,128]{1,0:T(4,128)S(1)} %get-tuple-element.79.held_ref, s32[64,256]{1,0:T(8,128)S(1)} %get-tuple-element.66.row_ref, s32[64,256]{1,0:T(8,128)S(1)} %get-tuple-element.67.column_ref, ...), custom_call_target="tpu_custom_call" | custom-call | tf_op jit(solution)/shard_map/pallas_call | solution.py:611
  71.6 4.6 %all-to-all-done.3.got_ref.got_c = f32[32,8,128]{2,1,0:T(8,128)S(1)} async-done(((f32[32,8,128]{2,1,0:T(8,128)}), f32[32,8,128]{2,1,0:T(8,128)S(1)}, u32[]{:S(2)}, u32[]{:S(2)}) %all-to-all-start.3) | async-done | bytes 131104 | tf_op jit(solution)/shard_map/all_to_all | solution.py:33
  76.2 1.9 %shard_map.167 = (f32[32,8,128]{2,1,0:T(8,128)}, f32[96,256]{1,0:T(8,128)S(1)}) custom-call(f32[32,8,128]{2,1,0:T(8,128)S(1)} %all-to-all-done.3.got_ref.got_c, s32[8,256]{1,0:T(8,128)S(1)} %get-tuple-element.62.row_ref, s32[8,256]{1,0:T(8,128)S(1)} %get-tuple-element.63.column_ref, f32[96,256]{1,0:T(8,128)S(1)} %shard_map.166.partial_ref, ...), custom_call_target="tpu_custom_call" | custom-call | tf_op jit(solution)/shard_map/pallas_call | solution.py:611
  78.1 2.6 %all-to-all-start.4 = ((f32[32,8,128]{2,1,0:T(8,128)}), f32[32,8,128]{2,1,0:T(8,128)S(1)}, u32[]{:S(2)}, u32[]{:S(2)}) async-start(f32[32,8,128]{2,1,0:T(8,128)} %get-tuple-element.86), calls=%async_computation.4 | async-start | bytes 262144 | tf_op jit(solution)/shard_map/all_to_all | solution.py:33
  80.6 0.0 copy-start.4
  80.6 2.2 %copy-done.4 = bf16[8192,256]{1,0:T(8,128)(2,1)S(1)} copy-done((bf16[8192,256]{1,0:T(8,128)(2,1)S(1)}, bf16[8192,256]{1,0:T(8,128)(2,1)}, u32[]{:S(2)}) %copy-start.4) | copy-done | bytes 4194328
  82.8 4.6 %shard_map.168 = (f32[192,256]{1,0:T(8,128)S(1)}, f32[3,128]{1,0:T(4,128)S(1)}, f32[192,256]{1,0:T(8,128)S(1)}, f32[3,6912]{1,0:T(4,128)}) custom-call(f32[96,256]{1,0:T(8,128)S(1)} %get-tuple-element.81.tab_ref, s32[64,256]{1,0:T(8,128)S(1)} %get-tuple-element.48.row_ref.own_where, bf16[8192,256]{1,0:T(8,128)(2,1)S(1)} %copy-done.4, ...), custom_call_target="tpu_custom_call" | custom-call | tf_op jit(solution)/shard_map/pallas_call | solution.py:611
  87.4 1.5 %all-to-all-done.4.got_ref = f32[32,8,128]{2,1,0:T(8,128)S(1)} async-done(((f32[32,8,128]{2,1,0:T(8,128)}), f32[32,8,128]{2,1,0:T(8,128)S(1)}, u32[]{:S(2)}, u32[]{:S(2)}) %all-to-all-start.4) | async-done | bytes 131104 | tf_op jit(solution)/shard_map/all_to_all | solution.py:33
  88.8 0.0 copy-done.6
  88.8 0.0 copy-done.13
  88.8 0.0 copy-done.14
  88.9 0.0 copy-start.5
  88.9 2.2 %copy-done.5 = bf16[8192,256]{1,0:T(8,128)(2,1)S(1)} copy-done((bf16[8192,256]{1,0:T(8,128)(2,1)S(1)}, bf16[8192,256]{1,0:T(8,128)(2,1)}, u32[]{:S(2)}) %copy-start.5) | copy-done | bytes 4194328
  91.0 2.8 %shard_map.169 = (f32[32,1,128]{2,1,0:T(1,128)S(1)}, f32[1,256]{1,0:T(1,128)S(1)}) custom-call(f32[32,8,128]{2,1,0:T(8,128)S(1)} %all-to-all-done.4.got_ref, f32[192,256]{1,0:T(8,128)S(1)} %get-tuple-element.87.cells_ref, f32[3,128]{1,0:T(4,128)S(1)} %get-tuple-element.88.hang_ref, s32[64,256]{1,0:T(8,128)S(1)} %get-tuple-element.56.row_ref.edge_where, ...), custom_call_target="tpu_custom_call" | custom-call | tf_op jit(solution)/shard_map/pallas_call | solution.py:611
  93.9 11.3 %all_to_all.30.got_ref = f32[32,1,128]{2,1,0:T(1,128)S(1)} all-to-all(f32[32,1,128]{2,1,0:T(1,128)S(1)} %get-tuple-element.90), channel_id=1, replica_groups=mesh['dom'=32] {'dom'}, dimensions={0} | all-to-all | bytes 32768 | tf_op jit(solution)/shard_map/all_to_all | solution.py:33
  105.2 0.0 copy-done.15
  105.2 0.8 shard_map.170
  (10 shorter events, 0.0 us)
Async XLA Ops:
  2.9 18.3 %all-to-all-start = ((f32[32,8,128]{2,1,0:T(8,128)}), f32[32,8,128]{2,1,0:T(8,128)S(1)}, u32[]{:S(2)}, u32[]{:S(2)}) async-start(f32[32,8,128]{2,1,0:T(8,128)} %get-tuple-element.47), calls=%async_computation | async-start | bytes 262144 | tf_op jit(solution)/shard_map/all_to_all | solution.py:33
  10.3 0.9 copy-start.7
  11.2 0.8 copy-start.10
  12.0 0.7 copy-start.11
  12.7 0.7 copy-start.12
  13.4 0.7 copy-start.16
  16.7 18.1 %copy-start.8 = (f32[3,6912]{1,0:T(4,128)S(1)}, f32[3,6912]{1,0:T(4,128)}, u32[]{:S(2)}) copy-start(f32[3,6912]{1,0:T(4,128)} %source_ref.1) | copy-start | bytes 248836
  16.8 18.1 %copy-start.9 = (f32[3,6912]{1,0:T(4,128)S(1)}, f32[3,6912]{1,0:T(4,128)}, u32[]{:S(2)}) copy-start(f32[3,6912]{1,0:T(4,128)} %inverse_ref.1) | copy-start | bytes 248836
  19.3 2.0 %copy-start = (bf16[8192,256]{1,0:T(8,128)(2,1)}, bf16[8192,256]{1,0:T(8,128)(2,1)S(1)}, u32[]{:S(2)}) copy-start(bf16[8192,256]{1,0:T(8,128)(2,1)S(1)} %get-tuple-element.49.lane_ref) | copy-start | bytes 12582916
  21.2 2.2 %copy-start.1 = (bf16[8192,256]{1,0:T(8,128)(2,1)S(1)}, bf16[8192,256]{1,0:T(8,128)(2,1)}, u32[]{:S(2)}) copy-start(bf16[8192,256]{1,0:T(8,128)(2,1)} %copy-done) | copy-start | bytes 12582916
  29.0 14.1 %all-to-all-start.1 = ((f32[32,8,128]{2,1,0:T(8,128)}), f32[32,8,128]{2,1,0:T(8,128)S(1)}, u32[]{:S(2)}, u32[]{:S(2)}) async-start(f32[32,8,128]{2,1,0:T(8,128)} %get-tuple-element.61), calls=%async_computation.1 | async-start | bytes 262144 | tf_op jit(solution)/shard_map/all_to_all | solution.py:33
  44.9 10.8 %all-to-all-start.2 = ((f32[32,8,128]{2,1,0:T(8,128)}), f32[32,8,128]{2,1,0:T(8,128)S(1)}, u32[]{:S(2)}, u32[]{:S(2)}) async-start(f32[32,8,128]{2,1,0:T(8,128)} %get-tuple-element.72), calls=%async_computation.2 | async-start | bytes 262144 | tf_op jit(solution)/shard_map/all_to_all | solution.py:33
  47.7 2.2 %copy-start.2 = (bf16[8192,256]{1,0:T(8,128)(2,1)S(1)}, bf16[8192,256]{1,0:T(8,128)(2,1)}, u32[]{:S(2)}) copy-start(bf16[8192,256]{1,0:T(8,128)(2,1)} %copy-done) | copy-start | bytes 12582916
  55.7 2.2 %copy-start.3 = (bf16[8192,256]{1,0:T(8,128)(2,1)S(1)}, bf16[8192,256]{1,0:T(8,128)(2,1)}, u32[]{:S(2)}) copy-start(bf16[8192,256]{1,0:T(8,128)(2,1)} %copy-done) | copy-start | bytes 12582916
  63.5 25.4 %copy-start.6 = (f32[192,256]{1,0:T(8,128)S(1)}, f32[192,256]{1,0:T(8,128)}, u32[]{:S(2)}) copy-start(f32[192,256]{1,0:T(8,128)} %load_ref.1) | copy-start | bytes 589828
  63.5 25.4 %copy-start.13 = (s32[8,128]{1,0:T(8,128)S(1)}, s32[8,128]{1,0:T(8,128)}, u32[]{:S(2)}) copy-start(s32[8,128]{1,0:T(8,128)} %sub_cell.1) | copy-start | bytes 12292
  63.5 25.4 %copy-start.14 = (s32[8,128]{1,0:T(8,128)S(1)}, s32[8,128]{1,0:T(8,128)}, u32[]{:S(2)}) copy-start(s32[8,128]{1,0:T(8,128)} %sub_face.1) | copy-start | bytes 12292
  63.5 12.7 %all-to-all-start.3 = ((f32[32,8,128]{2,1,0:T(8,128)}), f32[32,8,128]{2,1,0:T(8,128)S(1)}, u32[]{:S(2)}, u32[]{:S(2)}) async-start(f32[32,8,128]{2,1,0:T(8,128)} %get-tuple-element.77), calls=%async_computation.3 | async-start | bytes 262144 | tf_op jit(solution)/shard_map/all_to_all | solution.py:33
  78.1 10.8 %all-to-all-start.4 = ((f32[32,8,128]{2,1,0:T(8,128)}), f32[32,8,128]{2,1,0:T(8,128)S(1)}, u32[]{:S(2)}, u32[]{:S(2)}) async-start(f32[32,8,128]{2,1,0:T(8,128)} %get-tuple-element.86), calls=%async_computation.4 | async-start | bytes 262144 | tf_op jit(solution)/shard_map/all_to_all | solution.py:33
  80.6 2.2 %copy-start.4 = (bf16[8192,256]{1,0:T(8,128)(2,1)S(1)}, bf16[8192,256]{1,0:T(8,128)(2,1)}, u32[]{:S(2)}) copy-start(bf16[8192,256]{1,0:T(8,128)(2,1)} %copy-done) | copy-start | bytes 12582916
  82.8 22.4 %copy-start.15 = (s32[8,128]{1,0:T(8,128)S(1)}, s32[8,128]{1,0:T(8,128)}, u32[]{:S(2)}) copy-start(s32[8,128]{1,0:T(8,128)} %owner_ref.1) | copy-start | bytes 12292
  88.9 2.2 %copy-start.5 = (bf16[8192,256]{1,0:T(8,128)(2,1)S(1)}, bf16[8192,256]{1,0:T(8,128)(2,1)}, u32[]{:S(2)}) copy-start(bf16[8192,256]{1,0:T(8,128)(2,1)} %copy-done) | copy-start | bytes 12582916

commit v13 on v11

--- a/solution.py
+++ b/solution.py
@@ -12,7 +12,7 @@
 LANES = 128
 WIDE = 2 * LANES
 OWN = 32
-EDGE = 32
+EDGE = 16
 TALL = 24
 NOWHERE = 126
 
@@ -86,22 +86,22 @@
     return high, (x - high.astype(f32)).astype(bf16)
 
 
-def gather(jobs, column_ref, wide=False):
+def gather(jobs, column_ref, high=2 * LANES, stacked=False):
     count, width = column_ref.shape
     tables = jnp.concatenate([job[0] for job in jobs], 0)
-    high = tables.shape[0]
+    tall = tables.shape[0] // 2
     numbers = lax.broadcasted_iota(i32, (max(job[1] for job in jobs), width), 0)
     step = min(count, 32 if sum(job[1] * job[2] for job in jobs) <= 192 else 16)
 
     def body(block, carry):
         start = pl.multiple_of(block * step, step)
         for j in range(step):
-            hot = one_hot(column_ref[pl.ds(start + j, 1), :], WIDE if wide else LANES)
-            if not wide:
+            hot = one_hot(column_ref[pl.ds(start + j, 1), :], high if stacked else LANES)
+            if not stacked:
                 hot = jnp.concatenate([hot, hot], 0)
             all_found = jnp.dot(tables, hot, preferred_element_type=f32)
-            if wide:
-                all_found = all_found[: high // 2] + all_found[high // 2 :]
+            if stacked:
+                all_found = all_found[:tall] + all_found[tall:]
             top = 0
             for _, rows, parts, row_ref, sums_ref in jobs:
                 found = all_found[top : top + parts * rows]
@@ -142,9 +142,21 @@
     return where >> 1, (where & 1) * LANES + lane
 
 
-def scatter(high_ref, low_ref, rows, row_ref, column_ref, sum_ref):
+def scatter(high_ref, low_ref, rows, row_ref, column_ref, sum_ref, hanging=None):
     count = row_ref.shape[0]
     step = min(count, 32)
+
+    def hanging_tile(number):
+        at_row = row_ref[pl.ds(number, 1), :]
+        shape = (8, at_row.shape[1])
+        numbers = lax.broadcasted_iota(i32, shape, 0)
+        tile = jnp.zeros(shape, f32)
+        for piece, piece_ref in enumerate((high_ref, low_ref)):
+            for part in range(3):
+                value = jnp.broadcast_to(piece_ref[pl.ds(part * count + number, 1), :], shape)
+                tile = jnp.where(numbers == 3 * piece + part, value, tile)
+        tile = jnp.where(jnp.broadcast_to(at_row, shape) == hanging, tile, 0.0)
+        return jnp.concatenate([tile, jnp.zeros_like(tile)], 0).astype(bf16)
 
     def product(start):
         masks = [match16(row_ref[pl.ds(start + j, 1), :], rows) for j in range(8)]
@@ -162,6 +174,8 @@
             for piece_ref in (high_ref, low_ref)
             for part in range(3)
         ]
+        if hanging is not None:
+            stacked.append(jnp.concatenate([hanging_tile(start + j) for j in range(8)], 1))
         return lax.dot_general(
             jnp.concatenate(stacked, 0), hot, (((1,), (1,)), ((), ())), preferred_element_type=f32
         )
@@ -257,7 +271,7 @@
 
 def export_tiles(table, parts, row_ref, column_ref, sums_ref):
     table = jnp.concatenate(pieces(table), 0)
-    gather([(table, OWN, parts, row_ref, sums_ref)], column_ref, wide=True)
+    gather([(table, OWN, parts, row_ref, sums_ref)], column_ref, WIDE, stacked=True)
     return [tile for part in range(parts) for tile in halves(gathered(sums_ref, 8, part))]
 
 
@@ -285,11 +299,18 @@
 
 
 def first_export(
-    adjoint_hbm, primal_hbm, list_hbm, tab_a, tab_p, row_ref, column_ref, extra_ref,
-    out_ref, pack_ref, adjoint_ref, primal_ref, list_ref, sums_ref, sems,
+    adjoint_hbm, primal_hbm, list_hbm, modulus_hbm, node_hbm, tab_a, tab_p, row_ref,
+    column_ref, extra_ref, modulus_ref, node_ref, out_ref, pack_ref, adjoint_ref, primal_ref, list_ref, sums_ref, sems,
 ):
     copy_in(
-        [(adjoint_hbm, adjoint_ref), (primal_hbm, primal_ref), (list_hbm, list_ref)], sems
+        [
+            (adjoint_hbm, adjoint_ref),
+            (primal_hbm, primal_ref),
+            (list_hbm, list_ref),
+            (modulus_hbm, modulus_ref),
+            (node_hbm, node_ref),
+        ],
+        sems,
     )
     owned = adjoint_ref.shape[1]
     fill_table(adjoint_ref, tab_a)
@@ -306,13 +327,12 @@
 
 
 def setup(
-    owned, connect_ref, node_ref, master_ref, weight_ref, modulus_ref, stiffness_ref,
+    owned, connect_ref, node_ref, master_ref, weight_ref, stiffness_ref,
     own_where, own_row, edge_where, lane_ref, column_ref, master_own, master_own_row,
-    master_edge, master_lane, master_column, weight_out, modulus_out, forward_out, adjoint_out,
+    master_edge, master_lane, master_column, weight_out, forward_out, adjoint_out,
     map_ref, tall_ref, sums_ref,
 ):
     extent = owned + 2 * REACH * WIDE
-    modulus_out[...] = modulus_ref[...]
     for out_ref, matrix in (
         (forward_out, stiffness_ref[...]),
         (adjoint_out, jnp.transpose(stiffness_ref[...])),
@@ -393,7 +413,7 @@
             )
 
 
-def ghost_rows(place, got_refs, first, edge_ref):
+def ghost_rows(place, got_refs, first, edge_ref, axis=1):
     edge_ref[...] = jnp.zeros_like(edge_ref)
     for part in range(3):
         for half in range(2):
@@ -401,24 +421,24 @@
             for slot in range(2 * REACH):
                 at = part * TALL + 2 * slot + half
                 edge_ref[at : at + 1, :] = lines[slot]
-    return jnp.concatenate(pieces(edge_ref[...]), 1)
-
-
-def hanging_rows(found, hang_ref, edge_ref):
+    return jnp.concatenate(pieces(edge_ref[...]), axis)
+
+
+def hanging_rows(found, hang_ref, edge_ref, axis=1):
     for part in range(3):
         at = part * TALL + 4 * REACH
         edge_ref[at : at + 1, :] = found[part] + hang_ref[part : part + 1, :]
-    return jnp.concatenate(pieces(edge_ref[...]), 1)
+    return jnp.concatenate(pieces(edge_ref[...]), axis)
 
 
 def edge_gather(
     place, got_refs, first, cells_ref, hang_ref, row_ref, lane_ref, master_row, master_lane,
     weight_ref, edge_ref, sums_ref, out_ref,
 ):
-    table = ghost_rows(place, got_refs, first, edge_ref)
-    gather([(table, TALL, 3, master_row, sums_ref)], master_lane)
-    table = hanging_rows(sum_masters(sums_ref, 0, weight_ref[...]), hang_ref, edge_ref)
-    gather([(table, TALL, 3, row_ref, sums_ref)], lane_ref)
+    table = ghost_rows(place, got_refs, first, edge_ref, 0)
+    gather([(table, TALL, 3, master_row, sums_ref)], master_lane, LANES, stacked=True)
+    table = hanging_rows(sum_masters(sums_ref, 0, weight_ref[...]), hang_ref, edge_ref, 0)
+    gather([(table, TALL, 3, row_ref, sums_ref)], lane_ref, LANES, stacked=True)
     count = row_ref.shape[0]
     for part in range(3):
         rows = slice(part * count, (part + 1) * count)
@@ -438,12 +458,10 @@
     image = modulus_ref[...] * product(stiffness_ref[...], full_ref[...])
     image_ref[...] = image
     full_ref[...], low_ref[...] = split32(image)
-    scatter(full_ref, low_ref, EDGE, row_ref, lane_ref, sum_ref)
-    sums = add_pieces(sum_ref[...])
     slots = 2 * REACH
-    held = jnp.concatenate(
-        [sums[part * EDGE + 2 * slots : part * EDGE + 2 * slots + 1] for part in range(3)], 0
-    )
+    scatter(full_ref, low_ref, EDGE, row_ref, lane_ref, sum_ref, hanging=2 * slots)
+    sums = add_pieces(sum_ref[: 6 * EDGE, :])
+    held = sum_ref[6 * EDGE : 6 * EDGE + 3, :] + sum_ref[6 * EDGE + 3 : 6 * EDGE + 6, :]
     held_ref[...] = held
     sums += spread_hanging(held, weight_ref[...], EDGE, master_row, master_lane, scratch)
     rows = [
@@ -593,7 +611,7 @@
     def run(*args):
         return pl.pallas_call(
             kernel,
-            out_shape=[out if hasattr(out, "memory_space") else jax.ShapeDtypeStruct(*out) for out in outs],
+            out_shape=[jax.ShapeDtypeStruct(*out) for out in outs],
             in_specs=specs or [FAST] * len(args),
             scratch_shapes=scratch,
             compiler_params=pltpu.CompilerParams(vmem_limit_bytes=40 * 1024 * 1024),
@@ -632,7 +650,7 @@
     count = lax.axis_size("dom")
 
     def packed(height):
-        return [pltpu.VMEM((count, height, LANES), f32)]
+        return [((count, height, LANES), f32)]
 
     def room(height):
         return ((count + 1, height, LANES), f32)
@@ -642,11 +660,11 @@
     many_sums = ((2, local_values * 8, LANES), f32)
     own_tall = ((3 * tall, LANES), f32)
     edge = [((3 * TALL, LANES), f32), many_sums, cells_shape]
-    tab, tab_primal, list_row, list_column, extra, blocks = call(
+    tab, tab_primal, list_row, list_column, extra, moduli, hang_node, blocks = call(
         first_export,
         [table, table]
         + [(ghost_lists.shape, i32)] * 2
-        + [((6, slots, LANES), f32)]
+        + [((6, slots, LANES), f32), ((1, cell_count), f32), ((1, hang_node.shape[0]), i32)]
         + packed(8),
         [
             room(8),
@@ -655,25 +673,27 @@
             (ghost_lists.shape, i32),
             ((2, 6 * 64, LANES), f32),
         ],
-        [FAR, FAR, FAR],
-        sems=3,
-    )(*away(adjoint_start, primal_field, ghost_lists))
+        [FAR] * 5,
+        sems=5,
+    )(
+        *away(
+            adjoint_start, primal_field, ghost_lists, modulus.reshape(1, -1),
+            hang_node.reshape(1, -1),
+        )
+    )
     ghosts = exchange(blocks)
     (
         own_where, own_row, edge_where, lane, own_column, master_own, master_own_row, master_edge,
-        master_lane, master_column, weight, moduli, forward, backward,
+        master_lane, master_column, weight, forward, backward,
     ) = call(
         functools.partial(setup, adjoint_start.shape[1]),
         [index] * 5
         + [master_shape] * 5
-        + [((8, WIDE), f32), ((1, cell_count), f32)]
+        + [((8, WIDE), f32)]
         + [((local_values, 3 * local_values), bf16)] * 2,
         [((OWN, WIDE), f32), ((tall, LANES), f32), ((2, nodes * 8, LANES), f32)],
-        [FAST] * 6,
-    )(
-        connectivity, hang_node.reshape(1, -1), hang_master, hang_weight,
-        modulus.reshape(1, cell_count), stiffness,
-    )
+        [FAST] * 5,
+    )(connectivity, hang_node, hang_master, hang_weight, stiffness)
 
     def gather_own(*fields):
         number = len(fields)
@@ -698,7 +718,7 @@
         blocks, image, held = call(
             functools.partial(edge_product, 2 * sweep),
             packed(8) + [cells_shape, hang_shape],
-            [room(8)] + edge + [cells_shape, ((6 * EDGE, LANES), f32)] + few(EDGE, LANES),
+            [room(8)] + edge + [cells_shape, ((6 * EDGE + 16, LANES), f32)] + few(EDGE, LANES),
         )(ghosts, cells, hang, *on_edge, extra, moduli, backward)
         returned = exchange(blocks)
         landings.append(returned)

time: 91.1 us -> 89.4 us (0.981)
  Pallas kernels: 42.2 us -> 40.7 us
    pallas_call x13, Pallas kernels: 42.2 us -> 40.7 us  [run(): pl.pallas_call(kernel, out_shape=[jax.ShapeDtypeStruct(*out) for out in o...]
  transfers between devices with their start and end apart: 5 -> 5, of which waited for: 5 -> 5; matrix products, arithmetic and copies ran while one was open for 0% -> 0% of each run, Pallas kernels for 23% -> 24%
where the time goes in v13:
time: 89.4 us; the launch traced here: 88.9 us
  Pallas kernels  40.7 us (46%)
  waiting for transfers between devices  19.5 us (22%)
  starting transfers between devices  17.9 us (20%)
  blocking collectives  9.93 us (11%)
    pallas_call x13, Pallas kernels, run(): pl.pallas_call(kernel, out_shape=[jax.ShapeDtypeStruct(*out) for out in o...  40.7 us
    all_to_all x5, waiting for transfers between devices, exchange(): return lax.all_to_all(packed, 'dom', 0, 0, tiled=True)  19.5 us
    all_to_all x5, starting transfers between devices, exchange(): return lax.all_to_all(packed, 'dom', 0, 0, tiled=True)  17.9 us
    all_to_all x1, blocking collectives, exchange(): return lax.all_to_all(packed, 'dom', 0, 0, tiled=True)  9.93 us
  transfers between devices with their start and end apart: 5, of which 5 were waited for; matrix products, arithmetic and copies ran while one was open for 0% of the time, Pallas kernels for 24%

profile of v13, /device:TPU:0, one launch (start us, length us, event | category | flops | bytes accessed | tf_op | source)
XLA Modules:
  0.0 88.9 jit_solution(9950321401345656163)
XLA Ops:
  0.6 0.0 copy-start.1
  0.6 2.4 %shard_map.158 = (f32[96,256]{1,0:T(8,128)S(1)}, f32[96,256]{1,0:T(8,128)S(1)}, s32[8,256]{1,0:T(8,128)S(1)}, s32[8,256]{1,0:T(8,128)S(1)}, f32[6,8,128]{2,1,0:T...) custom-call(f32[3,6912]{1,0:T(4,128)} %adjoint_hbm.1, f32[3,6912]{1,0:T(4,128)} %primal_hbm.1, ...), custom_call_target="tpu_custom_call" | custom-call | tf_op jit(solution)/shard_map/pallas_call | solution.py:612
  3.0 0.0 copy-start.4
  3.0 0.0 copy-start.5
  3.0 0.0 copy-start.6
  3.1 7.3 %all-to-all-start = ((f32[32,8,128]{2,1,0:T(8,128)}), f32[32,8,128]{2,1,0:T(8,128)S(1)}, u32[]{:S(2)}, u32[]{:S(2)}) async-start(f32[32,8,128]{2,1,0:T(8,128)} %get-tuple-element.48), calls=%async_computation | async-start | bytes 262144 | tf_op jit(solution)/shard_map/all_to_all | solution.py:33
  10.4 0.0 copy-done.1
  10.4 0.0 copy-done.4
  10.4 0.0 copy-done.5
  10.4 0.0 copy-done.6
  10.4 2.0 %shard_map.159 = (s32[64,256]{1,0:T(8,128)S(1)}, s32[64,256]{1,0:T(8,128)S(1)}, s32[64,256]{1,0:T(8,128)S(1)}, s32[64,256]{1,0:T(8,128)S(1)}, s32[64,256]{1,0:T(...) custom-call(s32[64,256]{1,0:T(8,128)S(1)} %copy-done.4, ...), custom_call_target="tpu_custom_call" | custom-call | tf_op jit(solution)/shard_map/pallas_call | solution.py:612
  12.5 2.5 %shard_map.160 = (f32[192,256]{1,0:T(8,128)S(1)}, f32[3,128]{1,0:T(4,128)S(1)}) custom-call(s32[64,256]{1,0:T(8,128)S(1)} %get-tuple-element.50.row_ref.own_where, s32[64,256]{1,0:T(8,128)S(1)} %get-tuple-element.51.lane_ref, s32[8,256]{1,0:T(8,128)S(1)} %get-tuple-element.52.master_row.master_own, s32[8,256]{1,0:T(8,128)S(1)} %get-tuple-element.53.master_lane, ...), custom_call_target="tpu_custom_call" | custom-call | tf_op jit(solution)/shard_map/pallas_call | solution.py:612
  15.0 3.6 %all-to-all-done.got_ref = f32[32,8,128]{2,1,0:T(8,128)S(1)} async-done(((f32[32,8,128]{2,1,0:T(8,128)}), f32[32,8,128]{2,1,0:T(8,128)S(1)}, u32[]{:S(2)}, u32[]{:S(2)}) %all-to-all-start) | async-done | bytes 131104 | tf_op jit(solution)/shard_map/all_to_all | solution.py:33
  18.6 4.9 %shard_map.161 = (f32[32,8,128]{2,1,0:T(8,128)}, f32[192,256]{1,0:T(8,128)S(1)}, f32[3,128]{1,0:T(4,128)S(1)}) custom-call(f32[32,8,128]{2,1,0:T(8,128)S(1)} %all-to-all-done.got_ref, f32[192,256]{1,0:T(8,128)S(1)} %get-tuple-element.56.cells_ref, f32[3,128]{1,0:T(4,128)S(1)} %get-tuple-element.57.hang_ref, ...), custom_call_target="tpu_custom_call" | custom-call | tf_op jit(solution)/shard_map/pallas_call | solution.py:612
  23.5 0.0 copy-start.2
  23.5 0.0 copy-start.3
  23.5 2.7 %all-to-all-start.1 = ((f32[32,8,128]{2,1,0:T(8,128)}), f32[32,8,128]{2,1,0:T(8,128)S(1)}, u32[]{:S(2)}, u32[]{:S(2)}) async-start(f32[32,8,128]{2,1,0:T(8,128)} %get-tuple-element.63), calls=%async_computation.1 | async-start | bytes 262144 | tf_op jit(solution)/shard_map/all_to_all | solution.py:33
  26.2 0.0 copy-done.2
  26.2 0.0 copy-done.3
  26.2 3.7 %shard_map.162 = (f32[96,256]{1,0:T(8,128)S(1)}, f32[96,256]{1,0:T(8,128)S(1)}, f32[96,256]{1,0:T(8,128)S(1)}) custom-call(f32[192,256]{1,0:T(8,128)S(1)} %get-tuple-element.66.image_ref, f32[3,128]{1,0:T(4,128)S(1)} %get-tuple-element.67.held_ref, s32[64,256]{1,0:T(8,128)S(1)} %get-tuple-element.68.row_ref, s32[64,256]{1,0:T(8,128)S(1)} %get-tuple-element.69.column_ref, ...), custom_call_target="tpu_custom_call" | custom-call | tf_op jit(solution)/shard_map/pallas_call | solution.py:612
  29.9 4.5 %all-to-all-done.1.got_ref.got_a = f32[32,8,128]{2,1,0:T(8,128)S(1)} async-done(((f32[32,8,128]{2,1,0:T(8,128)}), f32[32,8,128]{2,1,0:T(8,128)S(1)}, u32[]{:S(2)}, u32[]{:S(2)}) %all-to-all-start.1) | async-done | bytes 131104 | tf_op jit(solution)/shard_map/all_to_all | solution.py:33
  34.4 1.9 %shard_map.163 = (f32[32,8,128]{2,1,0:T(8,128)}, f32[96,256]{1,0:T(8,128)S(1)}) custom-call(f32[32,8,128]{2,1,0:T(8,128)S(1)} %all-to-all-done.1.got_ref.got_a, s32[8,256]{1,0:T(8,128)S(1)} %get-tuple-element.64.row_ref, s32[8,256]{1,0:T(8,128)S(1)} %get-tuple-element.65.column_ref, f32[96,256]{1,0:T(8,128)S(1)} %get-tuple-element.72.partial_ref, ...), custom_call_target="tpu_custom_call" | custom-call | tf_op jit(solution)/shard_map/pallas_call | solution.py:612
  36.3 2.7 %all-to-all-start.2 = ((f32[32,8,128]{2,1,0:T(8,128)}), f32[32,8,128]{2,1,0:T(8,128)S(1)}, u32[]{:S(2)}, u32[]{:S(2)}) async-start(f32[32,8,128]{2,1,0:T(8,128)} %get-tuple-element.74), calls=%async_computation.2 | async-start | bytes 262144 | tf_op jit(solution)/shard_map/all_to_all | solution.py:33
  39.0 4.7 %shard_map.164 = (f32[192,256]{1,0:T(8,128)S(1)}, f32[3,128]{1,0:T(4,128)S(1)}, f32[192,256]{1,0:T(8,128)S(1)}, f32[3,128]{1,0:T(4,128)S(1)}) custom-call(s32[64,256]{1,0:T(8,128)S(1)} %get-tuple-element.50.row_ref.own_where, s32[64,256]{1,0:T(8,128)S(1)} %get-tuple-element.51.lane_ref, s32[8,256]{1,0:T(8,128)S(1)} %get-tuple-element.52.master_row.master_own, ...), custom_call_target="tpu_custom_call" | custom-call | tf_op jit(solution)/shard_map/pallas_call | solution.py:612
  43.7 3.3 %all-to-all-done.2.got_ref.got_b = f32[32,8,128]{2,1,0:T(8,128)S(1)} async-done(((f32[32,8,128]{2,1,0:T(8,128)}), f32[32,8,128]{2,1,0:T(8,128)S(1)}, u32[]{:S(2)}, u32[]{:S(2)}) %all-to-all-start.2) | async-done | bytes 131104 | tf_op jit(solution)/shard_map/all_to_all | solution.py:33
  47.1 4.9 %shard_map.165 = (f32[32,8,128]{2,1,0:T(8,128)}, f32[192,256]{1,0:T(8,128)S(1)}, f32[3,128]{1,0:T(4,128)S(1)}) custom-call(f32[32,8,128]{2,1,0:T(8,128)S(1)} %all-to-all-done.2.got_ref.got_b, f32[192,256]{1,0:T(8,128)S(1)} %get-tuple-element.77.cells_ref, f32[3,128]{1,0:T(4,128)S(1)} %get-tuple-element.78.hang_ref, ...), custom_call_target="tpu_custom_call" | custom-call | tf_op jit(solution)/shard_map/pallas_call | solution.py:612
  51.9 2.6 %all-to-all-start.3 = ((f32[32,8,128]{2,1,0:T(8,128)}), f32[32,8,128]{2,1,0:T(8,128)S(1)}, u32[]{:S(2)}, u32[]{:S(2)}) async-start(f32[32,8,128]{2,1,0:T(8,128)} %get-tuple-element.79), calls=%async_computation.3 | async-start | bytes 262144 | tf_op jit(solution)/shard_map/all_to_all | solution.py:33
  54.5 3.6 %shard_map.166.partial_ref = f32[96,256]{1,0:T(8,128)S(1)} custom-call(f32[192,256]{1,0:T(8,128)S(1)} %get-tuple-element.80.image_ref, f32[3,128]{1,0:T(4,128)S(1)} %get-tuple-element.81.held_ref, s32[64,256]{1,0:T(8,128)S(1)} %get-tuple-element.68.row_ref, s32[64,256]{1,0:T(8,128)S(1)} %get-tuple-element.69.column_ref, ...), custom_call_target="tpu_custom_call" | custom-call | tf_op jit(solution)/shard_map/pallas_call | solution.py:612
  58.1 4.6 %all-to-all-done.3.got_ref.got_c = f32[32,8,128]{2,1,0:T(8,128)S(1)} async-done(((f32[32,8,128]{2,1,0:T(8,128)}), f32[32,8,128]{2,1,0:T(8,128)S(1)}, u32[]{:S(2)}, u32[]{:S(2)}) %all-to-all-start.3) | async-done | bytes 131104 | tf_op jit(solution)/shard_map/all_to_all | solution.py:33
  62.7 1.9 %shard_map.167 = (f32[32,8,128]{2,1,0:T(8,128)}, f32[96,256]{1,0:T(8,128)S(1)}) custom-call(f32[32,8,128]{2,1,0:T(8,128)S(1)} %all-to-all-done.3.got_ref.got_c, s32[8,256]{1,0:T(8,128)S(1)} %get-tuple-element.64.row_ref, s32[8,256]{1,0:T(8,128)S(1)} %get-tuple-element.65.column_ref, f32[96,256]{1,0:T(8,128)S(1)} %shard_map.166.partial_ref, ...), custom_call_target="tpu_custom_call" | custom-call | tf_op jit(solution)/shard_map/pallas_call | solution.py:612
  64.6 2.6 %all-to-all-start.4 = ((f32[32,8,128]{2,1,0:T(8,128)}), f32[32,8,128]{2,1,0:T(8,128)S(1)}, u32[]{:S(2)}, u32[]{:S(2)}) async-start(f32[32,8,128]{2,1,0:T(8,128)} %get-tuple-element.88), calls=%async_computation.4 | async-start | bytes 262144 | tf_op jit(solution)/shard_map/all_to_all | solution.py:33
  67.2 0.0 copy-start
  67.2 0.0 copy-start.8
  67.2 4.7 %shard_map.168 = (f32[192,256]{1,0:T(8,128)S(1)}, f32[3,128]{1,0:T(4,128)S(1)}, f32[192,256]{1,0:T(8,128)S(1)}, f32[3,6912]{1,0:T(4,128)}) custom-call(f32[96,256]{1,0:T(8,128)S(1)} %get-tuple-element.83.tab_ref, s32[64,256]{1,0:T(8,128)S(1)} %get-tuple-element.50.row_ref.own_where, s32[64,256]{1,0:T(8,128)S(1)} %get-tuple-element.51.lane_ref, ...), custom_call_target="tpu_custom_call" | custom-call | tf_op jit(solution)/shard_map/pallas_call | solution.py:612
  71.9 0.0 copy-start.7
  71.9 3.5 %all-to-all-done.4.got_ref = f32[32,8,128]{2,1,0:T(8,128)S(1)} async-done(((f32[32,8,128]{2,1,0:T(8,128)}), f32[32,8,128]{2,1,0:T(8,128)S(1)}, u32[]{:S(2)}, u32[]{:S(2)}) %all-to-all-start.4) | async-done | bytes 131104 | tf_op jit(solution)/shard_map/all_to_all | solution.py:33
  75.4 0.0 copy-done
  75.4 0.0 copy-done.8
  75.4 0.0 copy-done.7
  75.4 0.0 copy-start.9
  75.4 2.7 %shard_map.169 = (f32[32,1,128]{2,1,0:T(1,128)S(1)}, f32[1,256]{1,0:T(1,128)S(1)}) custom-call(f32[32,8,128]{2,1,0:T(8,128)S(1)} %all-to-all-done.4.got_ref, f32[192,256]{1,0:T(8,128)S(1)} %get-tuple-element.89.cells_ref, f32[3,128]{1,0:T(4,128)S(1)} %get-tuple-element.90.hang_ref, s32[64,256]{1,0:T(8,128)S(1)} %get-tuple-element.58.row_ref.edge_where, ...), custom_call_target="tpu_custom_call" | custom-call | tf_op jit(solution)/shard_map/pallas_call | solution.py:612
  78.2 9.9 %all_to_all.30.got_ref = f32[32,1,128]{2,1,0:T(1,128)S(1)} all-to-all(f32[32,1,128]{2,1,0:T(1,128)S(1)} %get-tuple-element.92), channel_id=1, replica_groups=mesh['dom'=32] {'dom'}, dimensions={0} | all-to-all | bytes 32768 | tf_op jit(solution)/shard_map/all_to_all | solution.py:33
  88.1 0.0 copy-done.9
  88.1 0.8 shard_map.170
Async XLA Ops:
  0.6 9.7 %copy-start.1 = (f32[192,192]{1,0:T(8,128)S(1)}, f32[192,192]{1,0:T(8,128)}, u32[]{:S(2)}) copy-start(f32[192,192]{1,0:T(8,128)} %stiffness_ref.1) | copy-start | bytes 442372
  3.0 7.4 %copy-start.4 = (s32[64,256]{1,0:T(8,128)S(1)}, s32[64,256]{1,0:T(8,128)}, u32[]{:S(2)}) copy-start(s32[64,256]{1,0:T(8,128)} %connect_ref.1) | copy-start | bytes 196612
  3.0 7.4 %copy-start.5 = (s32[16,128]{1,0:T(8,128)S(1)}, s32[16,128]{1,0:T(8,128)}, u32[]{:S(2)}) copy-start(s32[16,128]{1,0:T(8,128)} %master_ref.1) | copy-start | bytes 24580
  3.0 7.4 %copy-start.6 = (f32[16,128]{1,0:T(8,128)S(1)}, f32[16,128]{1,0:T(8,128)}, u32[]{:S(2)}) copy-start(f32[16,128]{1,0:T(8,128)} %weight_ref.1) | copy-start | bytes 24580
  3.1 15.5 %all-to-all-start = ((f32[32,8,128]{2,1,0:T(8,128)}), f32[32,8,128]{2,1,0:T(8,128)S(1)}, u32[]{:S(2)}, u32[]{:S(2)}) async-start(f32[32,8,128]{2,1,0:T(8,128)} %get-tuple-element.48), calls=%async_computation | async-start | bytes 262144 | tf_op jit(solution)/shard_map/all_to_all | solution.py:33
  23.5 2.7 %copy-start.2 = (f32[3,6912]{1,0:T(4,128)S(1)}, f32[3,6912]{1,0:T(4,128)}, u32[]{:S(2)}) copy-start(f32[3,6912]{1,0:T(4,128)} %source_ref.1) | copy-start | bytes 248836
  23.5 2.7 %copy-start.3 = (f32[3,6912]{1,0:T(4,128)S(1)}, f32[3,6912]{1,0:T(4,128)}, u32[]{:S(2)}) copy-start(f32[3,6912]{1,0:T(4,128)} %inverse_ref.1) | copy-start | bytes 248836
  23.5 10.9 %all-to-all-start.1 = ((f32[32,8,128]{2,1,0:T(8,128)}), f32[32,8,128]{2,1,0:T(8,128)S(1)}, u32[]{:S(2)}, u32[]{:S(2)}) async-start(f32[32,8,128]{2,1,0:T(8,128)} %get-tuple-element.63), calls=%async_computation.1 | async-start | bytes 262144 | tf_op jit(solution)/shard_map/all_to_all | solution.py:33
  36.3 10.8 %all-to-all-start.2 = ((f32[32,8,128]{2,1,0:T(8,128)}), f32[32,8,128]{2,1,0:T(8,128)S(1)}, u32[]{:S(2)}, u32[]{:S(2)}) async-start(f32[32,8,128]{2,1,0:T(8,128)} %get-tuple-element.74), calls=%async_computation.2 | async-start | bytes 262144 | tf_op jit(solution)/shard_map/all_to_all | solution.py:33
  51.9 10.8 %all-to-all-start.3 = ((f32[32,8,128]{2,1,0:T(8,128)}), f32[32,8,128]{2,1,0:T(8,128)S(1)}, u32[]{:S(2)}, u32[]{:S(2)}) async-start(f32[32,8,128]{2,1,0:T(8,128)} %get-tuple-element.79), calls=%async_computation.3 | async-start | bytes 262144 | tf_op jit(solution)/shard_map/all_to_all | solution.py:33
  64.6 10.8 %all-to-all-start.4 = ((f32[32,8,128]{2,1,0:T(8,128)}), f32[32,8,128]{2,1,0:T(8,128)S(1)}, u32[]{:S(2)}, u32[]{:S(2)}) async-start(f32[32,8,128]{2,1,0:T(8,128)} %get-tuple-element.88), calls=%async_computation.4 | async-start | bytes 262144 | tf_op jit(solution)/shard_map/all_to_all | solution.py:33
  67.2 8.2 %copy-start = (f32[192,256]{1,0:T(8,128)S(1)}, f32[192,256]{1,0:T(8,128)}, u32[]{:S(2)}) copy-start(f32[192,256]{1,0:T(8,128)} %load_ref.1) | copy-start | bytes 589828
  67.2 8.2 %copy-start.8 = (s32[8,128]{1,0:T(8,128)S(1)}, s32[8,128]{1,0:T(8,128)}, u32[]{:S(2)}) copy-start(s32[8,128]{1,0:T(8,128)} %sub_face.1) | copy-start | bytes 12292
  71.9 3.5 %copy-start.7 = (s32[8,128]{1,0:T(8,128)S(1)}, s32[8,128]{1,0:T(8,128)}, u32[]{:S(2)}) copy-start(s32[8,128]{1,0:T(8,128)} %sub_cell.1) | copy-start | bytes 12292
  75.4 12.7 %copy-start.9 = (s32[8,128]{1,0:T(8,128)S(1)}, s32[8,128]{1,0:T(8,128)}, u32[]{:S(2)}) copy-start(s32[8,128]{1,0:T(8,128)} %owner_ref.1) | copy-start | bytes 12292

commit v14 on v13

--- a/solution.py
+++ b/solution.py
@@ -42,6 +42,23 @@
         for number, row in enumerate(rows[slot]):
             pack_ref[at, number : number + 1, :] = row
     out_ref[...] = pack_ref[:count]
+
+
+def send_off(place, sign, rows, pack_ref, out_ref, sems):
+    count = out_ref.shape[0]
+    copies = []
+    for slot, offset in enumerate(neighbour_offsets()):
+        for number, row in enumerate(rows[slot]):
+            pack_ref[slot, number : number + 1, :] = row
+        target = place + sign * offset
+        inside = (target >= 0) & (target < count)
+        copy = pltpu.make_async_copy(
+            pack_ref.at[slot], out_ref.at[jnp.clip(target, 0, count - 1)], sems.at[slot]
+        )
+        copies.append((inside, copy))
+        pl.when(inside)(copy.start)
+    for inside, copy in copies:
+        pl.when(inside)(copy.wait)
 
 
 def landed(place, sign, got_ref, number):
@@ -323,7 +340,8 @@
     tiles = export_tiles(table, 6, row_ref, column_ref, sums_ref)
     for number in range(6):
         extra_ref[number] = tiles[6 + number]
-    pack(lax.axis_index("dom"), 1, rows_of(tiles[:6]), pack_ref, out_ref)
+    sent = sems.at[pl.ds(5, 2 * REACH)]
+    send_off(lax.axis_index("dom"), 1, rows_of(tiles[:6]), pack_ref, out_ref, sent)
 
 
 def setup(
@@ -463,7 +481,7 @@
     sums = add_pieces(sum_ref[: 6 * EDGE, :])
     held = sum_ref[6 * EDGE : 6 * EDGE + 3, :] + sum_ref[6 * EDGE + 3 : 6 * EDGE + 6, :]
     held_ref[...] = held
-    sums += spread_hanging(held, weight_ref[...], EDGE, master_row, master_lane, scratch)
+    sums += spread_hanging(held, weight_ref[...], EDGE, master_row, master_lane, scratch[:-1])
     rows = [
         [
             sums[part * EDGE + 2 * slot + half : part * EDGE + 2 * slot + half + 1]
@@ -473,7 +491,7 @@
         for slot in range(slots)
     ]
     add_primal(rows, -1, primal_part, extra_ref)
-    pack(place, -1, rows, pack_ref, out_ref)
+    send_off(place, -1, rows, pack_ref, out_ref, scratch[-1])
 
 
 def own_sums(
@@ -501,21 +519,28 @@
 ):
     place = lax.axis_index("dom")
     values = [landed_wide(place, -1, got_ref, part) for part in range(3)]
-    returned = scatter_few(values, OWN, row_ref, column_ref, scratch)
+    returned = scatter_few(values, OWN, row_ref, column_ref, scratch[:-1])
     fresh = partial_ref[...] - relaxation * inverse_ref[...] * returned
     tab_ref[...] = fresh
     rows = rows_of(export_tiles(fresh, 3, row_ref, column_ref, sums_ref))
     if primal_part is not None:
         add_primal(rows, 1, primal_part, extra_ref)
-    pack(place, 1, rows, pack_ref, out_ref)
+    send_off(place, 1, rows, pack_ref, out_ref, scratch[-1])
 
 
 def last_gather(
     half_rows, tab_ref, own_where, lane_ref, master_own, master_lane, weight_ref,
     got_a, got_b, got_c, primal_cells, primal_hang, edge_where, master_edge, modulus_ref,
     stiffness_ref, cells_ref, hang_ref, ku_ref, final_ref,
-    tall_ref, sums_ref, edge_ref, edge_sums, full_ref,
-):
+    tall_ref, sums_ref, edge_ref, edge_sums, full_ref, whole_ref, sems,
+):
+    for row in range(whole_ref.shape[1] // WIDE):
+        for part in range(3):
+            whole_ref[part : part + 1, row * WIDE : (row + 1) * WIDE] = tab_ref[
+                part * OWN + row : part * OWN + row + 1, :
+            ]
+    copy = pltpu.make_async_copy(whole_ref, final_ref, sems.at[0])
+    copy.start()
     tall = up8(half_rows)
     own = tall_table([tab_ref], half_rows, tall_ref)
     edge = ghost_rows(lax.axis_index("dom"), (got_a, got_b, got_c), (6, 6, 6), edge_ref)
@@ -537,11 +562,7 @@
         cells_ref[rows, :] = gathered(sums_ref, count, part)
         full_ref[rows, :] = primal_cells[rows, :] + gathered(edge_sums, count, part)
     ku_ref[...] = modulus_ref[...] * product(stiffness_ref[...], full_ref[...])
-    for row in range(final_ref.shape[1] // WIDE):
-        for part in range(3):
-            final_ref[part : part + 1, row * WIDE : (row + 1) * WIDE] = tab_ref[
-                part * OWN + row : part * OWN + row + 1, :
-            ]
+    copy.wait()
 
 
 def fluxes(
@@ -611,7 +632,8 @@
     def run(*args):
         return pl.pallas_call(
             kernel,
-            out_shape=[jax.ShapeDtypeStruct(*out) for out in outs],
+            out_shape=[jax.ShapeDtypeStruct(*out[:2]) for out in outs],
+            out_specs=[out[2] if len(out) > 2 else FAST for out in outs],
             in_specs=specs or [FAST] * len(args),
             scratch_shapes=scratch,
             compiler_params=pltpu.CompilerParams(vmem_limit_bytes=40 * 1024 * 1024),
@@ -649,13 +671,14 @@
 
     count = lax.axis_size("dom")
 
-    def packed(height):
-        return [((count, height, LANES), f32)]
+    def packed(height, *where):
+        return [((count, height, LANES), f32, *where)]
 
     def room(height):
         return ((count + 1, height, LANES), f32)
 
     tall = up8(half_rows)
+    pack_room = ((slots, 8, LANES), f32)
     few_sums = ((2, 3 * 64, LANES), f32)
     many_sums = ((2, local_values * 8, LANES), f32)
     own_tall = ((3 * tall, LANES), f32)
@@ -665,16 +688,16 @@
         [table, table]
         + [(ghost_lists.shape, i32)] * 2
         + [((6, slots, LANES), f32), ((1, cell_count), f32), ((1, hang_node.shape[0]), i32)]
-        + packed(8),
+        + packed(8, FAR),
         [
-            room(8),
+            pack_room,
             (adjoint_start.shape, f32),
             (primal_field.shape, f32),
             (ghost_lists.shape, i32),
             ((2, 6 * 64, LANES), f32),
         ],
         [FAR] * 5,
-        sems=5,
+        sems=5 + slots,
     )(
         *away(
             adjoint_start, primal_field, ghost_lists, modulus.reshape(1, -1),
@@ -717,8 +740,9 @@
             cells, hang = gather_own(tab)
         blocks, image, held = call(
             functools.partial(edge_product, 2 * sweep),
-            packed(8) + [cells_shape, hang_shape],
-            [room(8)] + edge + [cells_shape, ((6 * EDGE + 16, LANES), f32)] + few(EDGE, LANES),
+            packed(8, FAR) + [cells_shape, hang_shape],
+            [pack_room] + edge + [cells_shape, ((6 * EDGE + 16, LANES), f32)] + few(EDGE, LANES),
+            sems=slots,
         )(ghosts, cells, hang, *on_edge, extra, moduli, backward)
         returned = exchange(blocks)
         landings.append(returned)
@@ -735,15 +759,17 @@
             source, inverse = tables
         blocks, tab = call(
             functools.partial(update, 1 if sweep == 0 else None),
-            packed(8) + [table],
-            [room(8), few_sums] + few(OWN, WIDE),
+            packed(8, FAR) + [table],
+            [pack_room, few_sums] + few(OWN, WIDE),
+            sems=slots,
         )(returned, list_row, list_column, partial, inverse, extra)
         ghosts = exchange(blocks)
         landings.append(ghosts)
     cells, hang, ku, adjoint = call(
         functools.partial(last_gather, half_rows),
-        [cells_shape, hang_shape, cells_shape, (adjoint_start.shape, f32)],
-        [own_tall, many_sums] + edge,
+        [cells_shape, hang_shape, cells_shape, (adjoint_start.shape, f32, FAR)],
+        [own_tall, many_sums] + edge + [(adjoint_start.shape, f32)],
+        sems=1,
     )(
         tab, own_where, lane, master_own, master_lane, weight, *landings[:3], *primal_cells,
         edge_where, master_edge, moduli, forward,

time: 89.4 us -> 88.9 us (level)
  transfers between devices with their start and end apart: 5 -> 5, of which waited for: 5 -> 5; matrix products, arithmetic and copies ran while one was open for 0% -> 0% of each run, Pallas kernels for 24% -> 23%
where the time goes in v14:
time: 88.9 us; the launch traced here: 88.5 us
  Pallas kernels  40.1 us (45%)
  waiting for transfers between devices  20.2 us (23%)
  starting transfers between devices  17.9 us (20%)
  blocking collectives  9.31 us (10%)
  between operations  0.9 us (1%)
    pallas_call x13, Pallas kernels, run(): pl.pallas_call(kernel, out_shape=[jax.ShapeDtypeStruct(*out[:2]) for out...  40.1 us
    all_to_all x5, waiting for transfers between devices, exchange(): return lax.all_to_all(packed, 'dom', 0, 0, tiled=True)  20.2 us
    all_to_all x5, starting transfers between devices, exchange(): return lax.all_to_all(packed, 'dom', 0, 0, tiled=True)  17.9 us
    all_to_all x1, blocking collectives, exchange(): return lax.all_to_all(packed, 'dom', 0, 0, tiled=True)  9.31 us
  transfers between devices with their start and end apart: 5, of which 5 were waited for; matrix products, arithmetic and copies ran while one was open for 0% of the time, Pallas kernels for 23%

profile of v14, /device:TPU:0, one launch (start us, length us, event | category | flops | bytes accessed | tf_op | source)
XLA Modules:
  0.0 88.5 jit_solution(10301188311307493983)
XLA Ops:
  0.6 0.0 copy-start.1
  0.6 2.4 %shard_map.158 = (f32[96,256]{1,0:T(8,128)S(1)}, f32[96,256]{1,0:T(8,128)S(1)}, s32[8,256]{1,0:T(8,128)S(1)}, s32[8,256]{1,0:T(8,128)S(1)}, f32[6,8,128]{2,1,0:T...) custom-call(f32[3,6912]{1,0:T(4,128)} %adjoint_hbm.1, f32[3,6912]{1,0:T(4,128)} %primal_hbm.1, ...), custom_call_target="tpu_custom_call" | custom-call | tf_op jit(solution)/shard_map/pallas_call | solution.py:633
  3.0 0.0 copy-start.4
  3.0 0.0 copy-start.5
  3.0 0.0 copy-start.6
  3.1 7.3 %all-to-all-start = ((f32[32,8,128]{2,1,0:T(8,128)}), f32[32,8,128]{2,1,0:T(8,128)S(1)}, u32[]{:S(2)}, u32[]{:S(2)}) async-start(f32[32,8,128]{2,1,0:T(8,128)} %get-tuple-element.48), calls=%async_computation | async-start | bytes 262144 | tf_op jit(solution)/shard_map/all_to_all | solution.py:33
  10.4 0.0 copy-done.1
  10.4 0.0 copy-done.4
  10.4 0.0 copy-done.5
  10.4 0.0 copy-done.6
  10.4 2.0 %shard_map.159 = (s32[64,256]{1,0:T(8,128)S(1)}, s32[64,256]{1,0:T(8,128)S(1)}, s32[64,256]{1,0:T(8,128)S(1)}, s32[64,256]{1,0:T(8,128)S(1)}, s32[64,256]{1,0:T(...) custom-call(s32[64,256]{1,0:T(8,128)S(1)} %copy-done.4, ...), custom_call_target="tpu_custom_call" | custom-call | tf_op jit(solution)/shard_map/pallas_call | solution.py:633
  12.5 2.5 %shard_map.160 = (f32[192,256]{1,0:T(8,128)S(1)}, f32[3,128]{1,0:T(4,128)S(1)}) custom-call(s32[64,256]{1,0:T(8,128)S(1)} %get-tuple-element.50.row_ref.own_where, s32[64,256]{1,0:T(8,128)S(1)} %get-tuple-element.51.lane_ref, s32[8,256]{1,0:T(8,128)S(1)} %get-tuple-element.52.master_row.master_own, s32[8,256]{1,0:T(8,128)S(1)} %get-tuple-element.53.master_lane, ...), custom_call_target="tpu_custom_call" | custom-call | tf_op jit(solution)/shard_map/pallas_call | solution.py:633
  15.0 3.6 %all-to-all-done.got_ref = f32[32,8,128]{2,1,0:T(8,128)S(1)} async-done(((f32[32,8,128]{2,1,0:T(8,128)}), f32[32,8,128]{2,1,0:T(8,128)S(1)}, u32[]{:S(2)}, u32[]{:S(2)}) %all-to-all-start) | async-done | bytes 131104 | tf_op jit(solution)/shard_map/all_to_all | solution.py:33
  18.6 4.9 %shard_map.161 = (f32[32,8,128]{2,1,0:T(8,128)}, f32[192,256]{1,0:T(8,128)S(1)}, f32[3,128]{1,0:T(4,128)S(1)}) custom-call(f32[32,8,128]{2,1,0:T(8,128)S(1)} %all-to-all-done.got_ref, f32[192,256]{1,0:T(8,128)S(1)} %get-tuple-element.56.cells_ref, f32[3,128]{1,0:T(4,128)S(1)} %get-tuple-element.57.hang_ref, ...), custom_call_target="tpu_custom_call" | custom-call | tf_op jit(solution)/shard_map/pallas_call | solution.py:633
  23.5 0.0 copy-start.2
  23.5 0.0 copy-start.3
  23.5 2.7 %all-to-all-start.1 = ((f32[32,8,128]{2,1,0:T(8,128)}), f32[32,8,128]{2,1,0:T(8,128)S(1)}, u32[]{:S(2)}, u32[]{:S(2)}) async-start(f32[32,8,128]{2,1,0:T(8,128)} %get-tuple-element.63), calls=%async_computation.1 | async-start | bytes 262144 | tf_op jit(solution)/shard_map/all_to_all | solution.py:33
  26.2 0.0 copy-done.2
  26.2 0.0 copy-done.3
  26.2 3.7 %shard_map.162 = (f32[96,256]{1,0:T(8,128)S(1)}, f32[96,256]{1,0:T(8,128)S(1)}, f32[96,256]{1,0:T(8,128)S(1)}) custom-call(f32[192,256]{1,0:T(8,128)S(1)} %get-tuple-element.66.image_ref, f32[3,128]{1,0:T(4,128)S(1)} %get-tuple-element.67.held_ref, s32[64,256]{1,0:T(8,128)S(1)} %get-tuple-element.68.row_ref, s32[64,256]{1,0:T(8,128)S(1)} %get-tuple-element.69.column_ref, ...), custom_call_target="tpu_custom_call" | custom-call | tf_op jit(solution)/shard_map/pallas_call | solution.py:633
  29.9 4.5 %all-to-all-done.1.got_ref.got_a = f32[32,8,128]{2,1,0:T(8,128)S(1)} async-done(((f32[32,8,128]{2,1,0:T(8,128)}), f32[32,8,128]{2,1,0:T(8,128)S(1)}, u32[]{:S(2)}, u32[]{:S(2)}) %all-to-all-start.1) | async-done | bytes 131104 | tf_op jit(solution)/shard_map/all_to_all | solution.py:33
  34.4 1.9 %shard_map.163 = (f32[32,8,128]{2,1,0:T(8,128)}, f32[96,256]{1,0:T(8,128)S(1)}) custom-call(f32[32,8,128]{2,1,0:T(8,128)S(1)} %all-to-all-done.1.got_ref.got_a, s32[8,256]{1,0:T(8,128)S(1)} %get-tuple-element.64.row_ref, s32[8,256]{1,0:T(8,128)S(1)} %get-tuple-element.65.column_ref, f32[96,256]{1,0:T(8,128)S(1)} %get-tuple-element.72.partial_ref, ...), custom_call_target="tpu_custom_call" | custom-call | tf_op jit(solution)/shard_map/pallas_call | solution.py:633
  36.3 2.8 %all-to-all-start.2 = ((f32[32,8,128]{2,1,0:T(8,128)}), f32[32,8,128]{2,1,0:T(8,128)S(1)}, u32[]{:S(2)}, u32[]{:S(2)}) async-start(f32[32,8,128]{2,1,0:T(8,128)} %get-tuple-element.74), calls=%async_computation.2 | async-start | bytes 262144 | tf_op jit(solution)/shard_map/all_to_all | solution.py:33
  39.1 4.7 %shard_map.164 = (f32[192,256]{1,0:T(8,128)S(1)}, f32[3,128]{1,0:T(4,128)S(1)}, f32[192,256]{1,0:T(8,128)S(1)}, f32[3,128]{1,0:T(4,128)S(1)}) custom-call(s32[64,256]{1,0:T(8,128)S(1)} %get-tuple-element.50.row_ref.own_where, s32[64,256]{1,0:T(8,128)S(1)} %get-tuple-element.51.lane_ref, s32[8,256]{1,0:T(8,128)S(1)} %get-tuple-element.52.master_row.master_own, ...), custom_call_target="tpu_custom_call" | custom-call | tf_op jit(solution)/shard_map/pallas_call | solution.py:633
  43.8 3.3 %all-to-all-done.2.got_ref.got_b = f32[32,8,128]{2,1,0:T(8,128)S(1)} async-done(((f32[32,8,128]{2,1,0:T(8,128)}), f32[32,8,128]{2,1,0:T(8,128)S(1)}, u32[]{:S(2)}, u32[]{:S(2)}) %all-to-all-start.2) | async-done | bytes 131104 | tf_op jit(solution)/shard_map/all_to_all | solution.py:33
  47.1 4.9 %shard_map.165 = (f32[32,8,128]{2,1,0:T(8,128)}, f32[192,256]{1,0:T(8,128)S(1)}, f32[3,128]{1,0:T(4,128)S(1)}) custom-call(f32[32,8,128]{2,1,0:T(8,128)S(1)} %all-to-all-done.2.got_ref.got_b, f32[192,256]{1,0:T(8,128)S(1)} %get-tuple-element.77.cells_ref, f32[3,128]{1,0:T(4,128)S(1)} %get-tuple-element.78.hang_ref, ...), custom_call_target="tpu_custom_call" | custom-call | tf_op jit(solution)/shard_map/pallas_call | solution.py:633
  52.0 2.6 %all-to-all-start.3 = ((f32[32,8,128]{2,1,0:T(8,128)}), f32[32,8,128]{2,1,0:T(8,128)S(1)}, u32[]{:S(2)}, u32[]{:S(2)}) async-start(f32[32,8,128]{2,1,0:T(8,128)} %get-tuple-element.79), calls=%async_computation.3 | async-start | bytes 262144 | tf_op jit(solution)/shard_map/all_to_all | solution.py:33
  54.6 3.6 %shard_map.166.partial_ref = f32[96,256]{1,0:T(8,128)S(1)} custom-call(f32[192,256]{1,0:T(8,128)S(1)} %get-tuple-element.80.image_ref, f32[3,128]{1,0:T(4,128)S(1)} %get-tuple-element.81.held_ref, s32[64,256]{1,0:T(8,128)S(1)} %get-tuple-element.68.row_ref, s32[64,256]{1,0:T(8,128)S(1)} %get-tuple-element.69.column_ref, ...), custom_call_target="tpu_custom_call" | custom-call | tf_op jit(solution)/shard_map/pallas_call | solution.py:633
  58.2 4.6 %all-to-all-done.3.got_ref.got_c = f32[32,8,128]{2,1,0:T(8,128)S(1)} async-done(((f32[32,8,128]{2,1,0:T(8,128)}), f32[32,8,128]{2,1,0:T(8,128)S(1)}, u32[]{:S(2)}, u32[]{:S(2)}) %all-to-all-start.3) | async-done | bytes 131104 | tf_op jit(solution)/shard_map/all_to_all | solution.py:33
  62.8 1.9 %shard_map.167 = (f32[32,8,128]{2,1,0:T(8,128)}, f32[96,256]{1,0:T(8,128)S(1)}) custom-call(f32[32,8,128]{2,1,0:T(8,128)S(1)} %all-to-all-done.3.got_ref.got_c, s32[8,256]{1,0:T(8,128)S(1)} %get-tuple-element.64.row_ref, s32[8,256]{1,0:T(8,128)S(1)} %get-tuple-element.65.column_ref, f32[96,256]{1,0:T(8,128)S(1)} %shard_map.166.partial_ref, ...), custom_call_target="tpu_custom_call" | custom-call | tf_op jit(solution)/shard_map/pallas_call | solution.py:633
  64.7 2.6 %all-to-all-start.4 = ((f32[32,8,128]{2,1,0:T(8,128)}), f32[32,8,128]{2,1,0:T(8,128)S(1)}, u32[]{:S(2)}, u32[]{:S(2)}) async-start(f32[32,8,128]{2,1,0:T(8,128)} %get-tuple-element.88), calls=%async_computation.4 | async-start | bytes 262144 | tf_op jit(solution)/shard_map/all_to_all | solution.py:33
  67.3 0.0 copy-start
  67.3 0.0 copy-start.8
  67.3 4.1 %shard_map.168 = (f32[192,256]{1,0:T(8,128)S(1)}, f32[3,128]{1,0:T(4,128)S(1)}, f32[192,256]{1,0:T(8,128)S(1)}, f32[3,6912]{1,0:T(4,128)}) custom-call(f32[96,256]{1,0:T(8,128)S(1)} %get-tuple-element.83.tab_ref, s32[64,256]{1,0:T(8,128)S(1)} %get-tuple-element.50.row_ref.own_where, s32[64,256]{1,0:T(8,128)S(1)} %get-tuple-element.51.lane_ref, ...), custom_call_target="tpu_custom_call" | custom-call | tf_op jit(solution)/shard_map/pallas_call | solution.py:633
  71.4 0.0 copy-start.7
  71.4 4.1 %all-to-all-done.4.got_ref = f32[32,8,128]{2,1,0:T(8,128)S(1)} async-done(((f32[32,8,128]{2,1,0:T(8,128)}), f32[32,8,128]{2,1,0:T(8,128)S(1)}, u32[]{:S(2)}, u32[]{:S(2)}) %all-to-all-start.4) | async-done | bytes 131104 | tf_op jit(solution)/shard_map/all_to_all | solution.py:33
  75.5 0.0 copy-done
  75.5 0.0 copy-done.8
  75.5 0.0 copy-done.7
  75.5 0.0 copy-start.9
  75.6 2.7 %shard_map.169 = (f32[32,1,128]{2,1,0:T(1,128)S(1)}, f32[1,256]{1,0:T(1,128)S(1)}) custom-call(f32[32,8,128]{2,1,0:T(8,128)S(1)} %all-to-all-done.4.got_ref, f32[192,256]{1,0:T(8,128)S(1)} %get-tuple-element.89.cells_ref, f32[3,128]{1,0:T(4,128)S(1)} %get-tuple-element.90.hang_ref, s32[64,256]{1,0:T(8,128)S(1)} %get-tuple-element.58.row_ref.edge_where, ...), custom_call_target="tpu_custom_call" | custom-call | tf_op jit(solution)/shard_map/pallas_call | solution.py:633
  78.3 9.3 %all_to_all.30.got_ref = f32[32,1,128]{2,1,0:T(1,128)S(1)} all-to-all(f32[32,1,128]{2,1,0:T(1,128)S(1)} %get-tuple-element.92), channel_id=1, replica_groups=mesh['dom'=32] {'dom'}, dimensions={0} | all-to-all | bytes 32768 | tf_op jit(solution)/shard_map/all_to_all | solution.py:33
  87.6 0.0 copy-done.9
  87.6 0.8 shard_map.170
Async XLA Ops:
  0.6 9.7 %copy-start.1 = (f32[192,192]{1,0:T(8,128)S(1)}, f32[192,192]{1,0:T(8,128)}, u32[]{:S(2)}) copy-start(f32[192,192]{1,0:T(8,128)} %stiffness_ref.1) | copy-start | bytes 442372
  3.0 7.4 %copy-start.4 = (s32[64,256]{1,0:T(8,128)S(1)}, s32[64,256]{1,0:T(8,128)}, u32[]{:S(2)}) copy-start(s32[64,256]{1,0:T(8,128)} %connect_ref.1) | copy-start | bytes 196612
  3.0 7.4 %copy-start.5 = (s32[16,128]{1,0:T(8,128)S(1)}, s32[16,128]{1,0:T(8,128)}, u32[]{:S(2)}) copy-start(s32[16,128]{1,0:T(8,128)} %master_ref.1) | copy-start | bytes 24580
  3.0 7.4 %copy-start.6 = (f32[16,128]{1,0:T(8,128)S(1)}, f32[16,128]{1,0:T(8,128)}, u32[]{:S(2)}) copy-start(f32[16,128]{1,0:T(8,128)} %weight_ref.1) | copy-start | bytes 24580
  3.1 15.5 %all-to-all-start = ((f32[32,8,128]{2,1,0:T(8,128)}), f32[32,8,128]{2,1,0:T(8,128)S(1)}, u32[]{:S(2)}, u32[]{:S(2)}) async-start(f32[32,8,128]{2,1,0:T(8,128)} %get-tuple-element.48), calls=%async_computation | async-start | bytes 262144 | tf_op jit(solution)/shard_map/all_to_all | solution.py:33
  23.5 2.7 %copy-start.2 = (f32[3,6912]{1,0:T(4,128)S(1)}, f32[3,6912]{1,0:T(4,128)}, u32[]{:S(2)}) copy-start(f32[3,6912]{1,0:T(4,128)} %source_ref.1) | copy-start | bytes 248836
  23.5 2.7 %copy-start.3 = (f32[3,6912]{1,0:T(4,128)S(1)}, f32[3,6912]{1,0:T(4,128)}, u32[]{:S(2)}) copy-start(f32[3,6912]{1,0:T(4,128)} %inverse_ref.1) | copy-start | bytes 248836
  23.5 10.9 %all-to-all-start.1 = ((f32[32,8,128]{2,1,0:T(8,128)}), f32[32,8,128]{2,1,0:T(8,128)S(1)}, u32[]{:S(2)}, u32[]{:S(2)}) async-start(f32[32,8,128]{2,1,0:T(8,128)} %get-tuple-element.63), calls=%async_computation.1 | async-start | bytes 262144 | tf_op jit(solution)/shard_map/all_to_all | solution.py:33
  36.3 10.8 %all-to-all-start.2 = ((f32[32,8,128]{2,1,0:T(8,128)}), f32[32,8,128]{2,1,0:T(8,128)S(1)}, u32[]{:S(2)}, u32[]{:S(2)}) async-start(f32[32,8,128]{2,1,0:T(8,128)} %get-tuple-element.74), calls=%async_computation.2 | async-start | bytes 262144 | tf_op jit(solution)/shard_map/all_to_all | solution.py:33
  52.0 10.8 %all-to-all-start.3 = ((f32[32,8,128]{2,1,0:T(8,128)}), f32[32,8,128]{2,1,0:T(8,128)S(1)}, u32[]{:S(2)}, u32[]{:S(2)}) async-start(f32[32,8,128]{2,1,0:T(8,128)} %get-tuple-element.79), calls=%async_computation.3 | async-start | bytes 262144 | tf_op jit(solution)/shard_map/all_to_all | solution.py:33
  64.7 10.8 %all-to-all-start.4 = ((f32[32,8,128]{2,1,0:T(8,128)}), f32[32,8,128]{2,1,0:T(8,128)S(1)}, u32[]{:S(2)}, u32[]{:S(2)}) async-start(f32[32,8,128]{2,1,0:T(8,128)} %get-tuple-element.88), calls=%async_computation.4 | async-start | bytes 262144 | tf_op jit(solution)/shard_map/all_to_all | solution.py:33
  67.3 8.2 %copy-start = (f32[192,256]{1,0:T(8,128)S(1)}, f32[192,256]{1,0:T(8,128)}, u32[]{:S(2)}) copy-start(f32[192,256]{1,0:T(8,128)} %load_ref.1) | copy-start | bytes 589828
  67.3 8.2 %copy-start.8 = (s32[8,128]{1,0:T(8,128)S(1)}, s32[8,128]{1,0:T(8,128)}, u32[]{:S(2)}) copy-start(s32[8,128]{1,0:T(8,128)} %sub_face.1) | copy-start | bytes 12292
  71.4 4.1 %copy-start.7 = (s32[8,128]{1,0:T(8,128)S(1)}, s32[8,128]{1,0:T(8,128)}, u32[]{:S(2)}) copy-start(s32[8,128]{1,0:T(8,128)} %sub_cell.1) | copy-start | bytes 12292
  75.5 12.1 %copy-start.9 = (s32[8,128]{1,0:T(8,128)S(1)}, s32[8,128]{1,0:T(8,128)}, u32[]{:S(2)}) copy-start(s32[8,128]{1,0:T(8,128)} %owner_ref.1) | copy-start | bytes 12292
